TPU v7x, 32 devices: a whole 2x2x4 slice. The times are simulated.
32 devices in a mesh: dp: 4 (over x, core), seq: 2 (over y), tensor: 4 (over z).
Axes of the slice: x: 2, y: 2, z: 4, core: 2. Of those that a mesh axis runs over, the one named last changes fastest.
Arguments:
- hidden_in: bfloat16 [8192, 2048], P(('dp', 'seq', 'tensor')), may hold values from -6 to 6
- teacher: bfloat16 [8192, 2048], P(('dp', 'seq', 'tensor')), may hold values from -6 to 6
- segment_ids: int32 [8192], P(('dp', 'seq')), may hold values from 0 to 3, as said below
- norm_gain: bfloat16 [2048], P('tensor'), may hold values from 0.5 to 1.5
- input_projection_weight: bfloat16 [2048, 2, 4096], P(('dp', 'seq'), None, 'tensor'), may hold values from -0.125 to 0.125
- conv_weight: bfloat16 [4, 4096], P(None, 'tensor'), may hold values from -3 to 3
- conv_bias: bfloat16 [4096], P('tensor'), may hold values from -3 to 3
- xproj_weight: bfloat16 [4096, 160], P('tensor', ('dp', 'seq')), may hold values from -0.09375 to 0.09375
- dtproj_weight: bfloat16 [128, 4096], P(('dp', 'seq'), 'tensor'), may hold values from -0.5 to 0.5
- dt_bias: float32 [4096], P('tensor'), may hold values from -4.6 to -2.2
- a_log: float32 [16, 4096], P(None, 'tensor'), may hold values from -4 to 2.8
- d_skip: float32 [4096], P('tensor'), may hold values from 0.5 to 1.5
- output_projection_weight: bfloat16 [4096, 2048], P('tensor', ('dp', 'seq')), may hold values from -0.25 to 0.25
Outputs:
- output: bfloat16 [8192, 2048], P(('dp', 'seq', 'tensor'))
- input_grad: float32 [8192, 2048], P(('dp', 'seq', 'tensor'))
- gain_grad: float32 [2048], P('tensor')
- in_weight_grad: float32 [2048, 2, 4096], P(('dp', 'seq'), None, 'tensor')
- conv_weight_grad: float32 [4, 4096], P(None, 'tensor')
- conv_bias_grad: float32 [4096], P('tensor')
- xproj_grad: float32 [4096, 128], P('tensor', ('dp', 'seq'))
- xproj_state_grad: float32 [4096, 32], P('tensor', ('dp', 'seq'))
- dtproj_grad: float32 [128, 4096], P(('dp', 'seq'), 'tensor')
- dt_bias_grad: float32 [4096], P('tensor')
- a_log_grad: float32 [16, 4096], P(None, 'tensor')
- d_skip_grad: float32 [4096], P('tensor')
- out_weight_grad: float32 [4096, 2048], P('tensor', ('dp', 'seq'))
Inputs may be any that keep to these rules, and one draw needn't show every extreme that they name: `segment_ids`: in each sequence of 2048 tokens the ids are 1, 2, 3 in runs in that order, then a final run of 0 of 1 to 2048 / 20 tokens; document 1 has 2048 / 10 to 512 tokens, and document 2 covers the tokens from 512 to 1280.
All inputs are finite; a program needn't handle non-finite values.
Results may differ from a plain program's by a relative error of at most 0.0075.
Values may be sent and summed in bfloat16 or wider, within the bound.
A program may use at most 896 MiB of HBM per device.

v0:
```python
import functools

import jax
import jax.numpy as jnp
from jax import lax
from jax.experimental import pallas as pl
from jax.experimental.pallas import tpu as pltpu
from jax.sharding import PartitionSpec as P

EPS = 1e-05
LOG2E = 1.4426950408889634
LN2 = 0.6931471805599453
FAR = 1e30


def passed_along(x, axis, by):
    size = lax.axis_size(axis)
    pairs = [(i, i + by) for i in range(size) if 0 <= i + by < size]
    return lax.ppermute(x, axis, pairs)


def silu_slope(values):
    logistic = jax.nn.sigmoid(values)
    return logistic * (1.0 + values * (1.0 - logistic))


F32, BF16 = jnp.float32, jnp.bfloat16
N = 16
CH = 16

def fwd_kernel(stepd_ref, u_ref, bc_ref, cdiag_ref, rate_ref, y_ref, ckpt_ref, last_ref, state_ref, sbf_ref, *, unroll):
    @pl.when(pl.program_id(1) == 0)
    def _():
        state_ref[...] = jnp.zeros_like(state_ref)
    ckpt_ref[0] = state_ref[...]
    rate = rate_ref[...]
    tb = stepd_ref.shape[0]

    def chunk(c, s):
        base = pl.multiple_of(c * CH, CH)
        bc = bc_ref[c]
        for k in range(CH):
            dec = jnp.exp2(rate * stepd_ref[pl.ds(base + k, 1), :])
            s = dec * s + bc[:, k:k + 1] * u_ref[pl.ds(base + k, 1), :]
            sbf_ref[k * N:(k + 1) * N, :] = s.astype(BF16)
        y_ref[pl.ds(base, CH), :] = jnp.dot(cdiag_ref[pl.ds(base, CH), :], sbf_ref[...], preferred_element_type=F32)
        return s

    s = lax.fori_loop(0, tb // CH, chunk, state_ref[...], unroll=unroll)
    state_ref[...] = s
    last_ref[...] = s

def fwd(stepd, u, bc, cdiag, rate, tb=128, w=512, unroll=1):
    t, c = stepd.shape
    w = min(w, c)
    grid = (c // w, t // tb)
    return pl.pallas_call(
        functools.partial(fwd_kernel, unroll=unroll),
        grid=grid,
        in_specs=[
            pl.BlockSpec((tb, w), lambda j, i: (i, j)),
            pl.BlockSpec((tb, w), lambda j, i: (i, j)),
            pl.BlockSpec((tb // CH, N, 2 * CH), lambda j, i: (i, 0, 0)),
            pl.BlockSpec((tb, CH * N), lambda j, i: (i, 0)),
            pl.BlockSpec((N, w), lambda j, i: (0, j)),
        ],
        out_specs=[
            pl.BlockSpec((tb, w), lambda j, i: (i, j)),
            pl.BlockSpec((1, N, w), lambda j, i: (i, 0, j)),
            pl.BlockSpec((N, w), lambda j, i: (0, j)),
        ],
        out_shape=[
            jax.ShapeDtypeStruct((t, c), F32),
            jax.ShapeDtypeStruct((t // tb, N, c), F32),
            jax.ShapeDtypeStruct((N, c), F32),
        ],
        scratch_shapes=[pltpu.VMEM((N, w), F32), pltpu.VMEM((CH * N, w), BF16)],
        compiler_params=pltpu.CompilerParams(vmem_limit_bytes=48 << 20),
        name="scan_forward",
    )(stepd, u, bc, cdiag, rate)

def bwd_kernel(stepd_ref, u_ref, ds_ref, bc_ref, bdiag_ref, ones_ref, rate_ref, ckpt_ref, gin_ref,
               wb_ref, dn_ref, db_ref, dc_ref, acc_ref, g_ref, sbf_ref, abf_ref, rbf_ref, *, unroll):
    @pl.when(pl.program_id(1) == 0)
    def _():
        g_ref[...] = gin_ref[...]
        acc_ref[...] = jnp.zeros_like(acc_ref)
    rate = rate_ref[...]
    tb = stepd_ref.shape[0]
    nc = tb // CH
    row = lax.broadcasted_iota(jnp.int32, (CH, CH * N), 0)
    lane = lax.broadcasted_iota(jnp.int32, (CH, CH * N), 1)
    diag = (row == lane // N).astype(F32)
    sbf_ref[0:N, :] = ckpt_ref[0].astype(BF16)

    def forward(c, s):
        base = pl.multiple_of(c * CH, CH)
        bc = bc_ref[c]
        for k in range(CH):
            dec = jnp.exp2(rate * stepd_ref[pl.ds(base + k, 1), :])
            s = dec * s + bc[:, k:k + 1] * u_ref[pl.ds(base + k, 1), :]
            sbf_ref[pl.ds(pl.multiple_of((base + k + 1) * N, N), N), :] = s.astype(BF16)
        return s

    lax.fori_loop(0, nc, forward, ckpt_ref[0])

    def backward(c, carry):
        g, acc = carry
        c = nc - 1 - c
        base = pl.multiple_of(c * CH, CH)
        bc = bc_ref[c]
        for k in range(CH - 1, -1, -1):
            sd = stepd_ref[pl.ds(base + k, 1), :]
            adj = g + bc[:, CH + k:CH + k + 1] * ds_ref[pl.ds(base + k, 1), :]
            abf_ref[k * N:(k + 1) * N, :] = adj.astype(BF16)
            g = jnp.exp2(rate * sd) * adj
            before = sbf_ref[pl.ds(pl.multiple_of((base + k) * N, N), N), :].astype(F32)
            r = g * before * rate
            rbf_ref[k * N:(k + 1) * N, :] = r.astype(BF16)
            acc = acc + r * sd
        wb_ref[pl.ds(base, CH), :] = jnp.dot(bdiag_ref[pl.ds(base, CH), :], abf_ref[...], preferred_element_type=F32)
        dn_ref[pl.ds(base, CH), :] = jnp.dot(ones_ref[...], rbf_ref[...], preferred_element_type=F32)
        nt = (((1,), (1,)), ((), ()))
        now = sbf_ref[pl.ds(pl.multiple_of((base + 1) * N, N), CH * N), :]
        db = lax.dot_general(u_ref[pl.ds(base, CH), :].astype(BF16), abf_ref[...], nt, preferred_element_type=F32)
        dc = lax.dot_general(ds_ref[pl.ds(base, CH), :].astype(BF16), now, nt, preferred_element_type=F32)
        db_ref[0, pl.ds(c, 1), :] = jnp.sum(db * diag, axis=0, keepdims=True)
        dc_ref[0, pl.ds(c, 1), :] = jnp.sum(dc * diag, axis=0, keepdims=True)
        return g, acc

    g, acc = lax.fori_loop(0, nc, backward, (g_ref[...], acc_ref[...]), unroll=unroll)
    g_ref[...] = g
    acc_ref[...] = acc

def bwd(stepd, u, ds, bc, bdiag, ones, rate, ckpt, gin, tb=128, w=512, unroll=1):
    t, c = stepd.shape
    w = min(w, c)
    nb = t // tb
    grid = (c // w, nb)
    rows = pl.BlockSpec((tb, w), lambda j, i: (nb - 1 - i, j))
    return pl.pallas_call(
        functools.partial(bwd_kernel, unroll=unroll),
        grid=grid,
        in_specs=[
            rows, rows, rows,
            pl.BlockSpec((tb // CH, N, 2 * CH), lambda j, i: (nb - 1 - i, 0, 0)),
            pl.BlockSpec((tb, CH * N), lambda j, i: (nb - 1 - i, 0)),
            pl.BlockSpec((CH, CH * N), lambda j, i: (0, 0)),
            pl.BlockSpec((N, w), lambda j, i: (0, j)),
            pl.BlockSpec((1, N, w), lambda j, i: (nb - 1 - i, 0, j)),
            pl.BlockSpec((N, w), lambda j, i: (0, j)),
        ],
        out_specs=[
            rows, rows,
            pl.BlockSpec((1, tb // CH, CH * N), lambda j, i: (j, nb - 1 - i, 0)),
            pl.BlockSpec((1, tb // CH, CH * N), lambda j, i: (j, nb - 1 - i, 0)),
            pl.BlockSpec((N, w), lambda j, i: (0, j)),
        ],
        out_shape=[
            jax.ShapeDtypeStruct((t, c), F32),
            jax.ShapeDtypeStruct((t, c), F32),
            jax.ShapeDtypeStruct((c // w, t // CH, CH * N), F32),
            jax.ShapeDtypeStruct((c // w, t // CH, CH * N), F32),
            jax.ShapeDtypeStruct((N, c), F32),
        ],
        scratch_shapes=[pltpu.VMEM((N, w), F32), pltpu.VMEM(((tb + 1) * N, w), BF16),
                        pltpu.VMEM((CH * N, w), BF16), pltpu.VMEM((CH * N, w), BF16)],
        compiler_params=pltpu.CompilerParams(vmem_limit_bytes=48 << 20),
        name="scan_backward",
    )(stepd, u, ds, bc, bdiag, ones, rate, ckpt, gin)


def correct_kernel(alive_ref, y_ref, stepd_ref, cdiag_ref, rate_ref, ckpt_ref, sin_ref, yo_ref, ckpto_ref, state_ref, sbf_ref):
    i = pl.program_id(1)

    @pl.when(i == 0)
    def _():
        state_ref[...] = sin_ref[...]

    alive = alive_ref[i] != 0

    @pl.when(alive)
    def _():
        rate = rate_ref[...]
        ckpto_ref[0] = ckpt_ref[0] + state_ref[...]

        def chunk(c, s):
            base = pl.multiple_of(c * CH, CH)
            for k in range(CH):
                s = jnp.exp2(rate * stepd_ref[pl.ds(base + k, 1), :]) * s
                sbf_ref[k * N:(k + 1) * N, :] = s.astype(BF16)
            yo_ref[pl.ds(base, CH), :] = y_ref[pl.ds(base, CH), :] + jnp.dot(
                cdiag_ref[pl.ds(base, CH), :], sbf_ref[...], preferred_element_type=F32
            )
            return s

        state_ref[...] = lax.fori_loop(0, y_ref.shape[0] // CH, chunk, state_ref[...])

    @pl.when(jnp.logical_not(alive))
    def _():
        yo_ref[...] = y_ref[...]
        ckpto_ref[...] = ckpt_ref[...]


def correct(alive, y, stepd, cdiag, rate, ckpt, state_in, tb=128, w=512):
    t, c = stepd.shape
    w = min(w, c)
    rows = pl.BlockSpec((tb, w), lambda j, i, _: (i, j))
    lanes = pl.BlockSpec((N, w), lambda j, i, _: (0, j))
    marks = pl.BlockSpec((1, N, w), lambda j, i, _: (i, 0, j))
    return pl.pallas_call(
        correct_kernel,
        grid_spec=pltpu.PrefetchScalarGridSpec(
            num_scalar_prefetch=1,
            grid=(c // w, t // tb),
            in_specs=[rows, rows, pl.BlockSpec((tb, CH * N), lambda j, i, _: (i, 0)), lanes, marks, lanes],
            out_specs=[rows, marks],
            scratch_shapes=[pltpu.VMEM((N, w), F32), pltpu.VMEM((CH * N, w), BF16)],
        ),
        out_shape=[jax.ShapeDtypeStruct((t, c), F32), jax.ShapeDtypeStruct(ckpt.shape, F32)],
        compiler_params=pltpu.CompilerParams(vmem_limit_bytes=48 << 20),
        name="scan_correct",
    )(alive, y, stepd, cdiag, rate, ckpt, state_in)


def entry_kernel(alive_ref, stepd_ref, ds_ref, bc_ref, rate_ref, g_ref):
    i = pl.program_id(1)

    @pl.when(i == 0)
    def _():
        g_ref[...] = jnp.zeros_like(g_ref)

    @pl.when(alive_ref[pl.num_programs(1) - 1 - i] != 0)
    def _():
        rate = rate_ref[...]
        nc = stepd_ref.shape[0] // CH

        def chunk(c, g):
            c = nc - 1 - c
            base = pl.multiple_of(c * CH, CH)
            bc = bc_ref[c]
            for k in range(CH - 1, -1, -1):
                adj = g + bc[:, CH + k:CH + k + 1] * ds_ref[pl.ds(base + k, 1), :]
                g = jnp.exp2(rate * stepd_ref[pl.ds(base + k, 1), :]) * adj
            return g

        g_ref[...] = lax.fori_loop(0, nc, chunk, g_ref[...])


def entry(alive, stepd, ds, bc, rate, tb=128, w=512):
    t, c = stepd.shape
    w = min(w, c)
    nb = t // tb
    rows = pl.BlockSpec((tb, w), lambda j, i, _: (nb - 1 - i, j))
    lanes = pl.BlockSpec((N, w), lambda j, i, _: (0, j))
    return pl.pallas_call(
        entry_kernel,
        grid_spec=pltpu.PrefetchScalarGridSpec(
            num_scalar_prefetch=1,
            grid=(c // w, nb),
            in_specs=[rows, rows, pl.BlockSpec((tb // CH, N, 2 * CH), lambda j, i, _: (nb - 1 - i, 0, 0)), lanes],
            out_specs=lanes,
        ),
        out_shape=jax.ShapeDtypeStruct((N, c), F32),
        compiler_params=pltpu.CompilerParams(vmem_limit_bytes=48 << 20),
        name="scan_entry",
    )(alive, stepd, ds, bc, rate)


def carried(local, reach, axis, by):
    found = jnp.zeros_like(local)
    for _ in range(lax.axis_size(axis) - 1):
        found = passed_along(local + reach * found, axis, by)
    return found


def columns(values):
    tokens = values.shape[0]
    return values.reshape(tokens // CH, CH, N).transpose(0, 2, 1)


def diagonal(values):
    tokens = values.shape[0]
    mine = jnp.arange(CH * N)[None] // N == jnp.arange(tokens)[:, None] % CH
    return jnp.where(mine, jnp.tile(values.astype(BF16), (1, CH)), 0)


def on_device(
    hidden_in,
    teacher,
    segment_ids,
    norm_gain,
    input_projection_weight,
    conv_weight,
    conv_bias,
    xproj_weight,
    dtproj_weight,
    dt_bias,
    a_log,
    d_skip,
    output_projection_weight,
):
    tok_rows = segment_ids.shape[0]
    row_share = hidden_in.shape[0]
    model_width = hidden_in.shape[1]
    conv_taps = conv_weight.shape[0]
    chan_lanes = conv_weight.shape[1]
    back_rows = conv_taps - 1
    row_start = lax.axis_index("tensor") * row_share
    valid_mask = (segment_ids != 0).astype(jnp.float32)
    count_here = jnp.sum((segment_ids != 0).astype(jnp.int32))
    count_pair = (
        jnp.stack([count_here // 32, count_here % 32]).astype(jnp.float32).astype(jnp.bfloat16)
    )
    w_in, w_x, w_dt, w_out, count_pairs = (
        lax.all_gather(input_projection_weight, ("dp", "seq"), axis=0, tiled=True),
        lax.all_gather(xproj_weight, ("dp", "seq"), axis=1, tiled=True),
        lax.all_gather(dtproj_weight, ("dp", "seq"), axis=0, tiled=True),
        lax.all_gather(output_projection_weight, ("dp", "seq"), axis=1, tiled=True),
        lax.all_gather(count_pair, ("dp", "seq"), axis=0, tiled=True),
    )
    count_pairs = count_pairs.astype(jnp.float32).reshape(-1, 2)
    total_count = 32.0 * jnp.sum(count_pairs[:, 0]) + jnp.sum(count_pairs[:, 1])
    full_rows_b, full_gain_b = (
        lax.all_gather(hidden_in, "tensor", axis=0, tiled=True),
        lax.all_gather(norm_gain, "tensor", axis=0, tiled=True),
    )
    full_rows = full_rows_b.astype(jnp.float32)
    full_gain = full_gain_b.astype(jnp.float32)
    inv_rms = lax.rsqrt(jnp.mean(full_rows * full_rows, axis=1, keepdims=True) + EPS)
    normalized_rows = (full_rows * inv_rms * full_gain[None]).astype(jnp.bfloat16)
    projected_input_gate = jnp.einsum(
        "td,dke->tke", normalized_rows, w_in, preferred_element_type=jnp.float32
    )
    x_inner = projected_input_gate[:, 0]
    z_gate = projected_input_gate[:, 1]
    seg_float = segment_ids.astype(jnp.float32)
    prev_x, prev_seg = passed_along(
        (x_inner[tok_rows - back_rows :], seg_float[tok_rows - back_rows :]), "seq", 1
    )
    ext_x = jnp.concatenate([prev_x, x_inner], 0)
    ext_seg = jnp.concatenate([prev_seg, seg_float], 0)
    tap_keeps = []
    conv_sum = jnp.broadcast_to(conv_bias.astype(jnp.float32)[None], (tok_rows, chan_lanes))
    for offset in range(conv_taps):
        keep_tap = (ext_seg[offset : offset + tok_rows] == seg_float).astype(jnp.float32)[:, None]
        tap_keeps.append(keep_tap)
        conv_sum = (
            conv_sum
            + conv_weight[offset].astype(jnp.float32)[None]
            * ext_x[offset : offset + tok_rows]
            * keep_tap
        )
    x_low = jax.nn.silu(conv_sum).astype(jnp.bfloat16)
    x_float = x_low.astype(jnp.float32)
    mixed_rows = lax.psum(jnp.dot(x_low, w_x, preferred_element_type=jnp.float32), "tensor")
    rank_width = w_dt.shape[0]
    state_width = (mixed_rows.shape[1] - rank_width) // 2
    step_low = mixed_rows[:, :rank_width].astype(jnp.bfloat16)
    b_in = mixed_rows[:, rank_width : rank_width + state_width]
    c_out = mixed_rows[:, rank_width + state_width :]
    pre_act = jnp.dot(step_low, w_dt, preferred_element_type=jnp.float32) + dt_bias[None]
    step_size = jax.nn.softplus(pre_act)
    decay_rates = -jnp.exp(a_log)
    same_doc = (seg_float == ext_seg[back_rows - 1 : back_rows - 1 + tok_rows]).astype(jnp.float32)
    rates = decay_rates * LOG2E
    block = 128
    stepd = jnp.where(same_doc[:, None] != 0, step_size, FAR)
    inject = step_size * x_float
    col_pair = jnp.concatenate([columns(b_in), columns(c_out)], -1)
    b_diag, c_diag = diagonal(b_in), diagonal(c_out)
    resets = jnp.sum((same_doc == 0).astype(jnp.int32).reshape(-1, block), axis=1)
    alive = (jnp.cumsum(resets) - resets == 0).astype(jnp.int32)
    y_local, marks, state_last = fwd(stepd, inject, col_pair, c_diag, rates, tb=block, unroll=2)
    reach = jnp.exp2(rates * jnp.sum(stepd, axis=0)[None])
    state_in = carried(state_last, reach, "seq", 1)
    y_rows, marks = correct(alive, y_local, stepd, c_diag, rates, marks, state_in, tb=block)
    scan_out = y_rows + d_skip[None] * x_float
    gate_act = jax.nn.silu(z_gate)
    gated_output_rows = (scan_out * gate_act).astype(jnp.bfloat16)
    branch_share = lax.psum_scatter(
        jnp.dot(gated_output_rows, w_out, preferred_element_type=jnp.float32),
        "tensor",
        scatter_dimension=0,
        tiled=True,
    )
    share_rows = hidden_in.astype(jnp.float32)
    result = share_rows + branch_share
    output = result.astype(jnp.bfloat16)
    valid_share = lax.dynamic_slice_in_dim(valid_mask, row_start, row_share, 0)
    total_tokens = float(tok_rows * lax.axis_size(("dp", "seq")))
    grad_out = (
        total_tokens / total_count * valid_share[:, None] * (result - teacher.astype(jnp.float32))
    )
    grad_low = grad_out.astype(jnp.bfloat16)
    piece = lax.all_gather(grad_low, "tensor", axis=0, tiled=True)
    block_rows = jnp.einsum("tw,ew->te", piece, w_out, preferred_element_type=jnp.float32)
    d_gated = block_rows
    d_wout = jnp.einsum("te,tw->ew", gated_output_rows, piece, preferred_element_type=jnp.float32)
    d_gated, d_wout = (d_gated, d_wout)
    d_scan = d_gated * gate_act
    d_z = d_gated * scan_out * silu_slope(z_gate)
    d_skip_part = jnp.sum(d_scan * x_float, axis=0)
    adjoint_first = entry(alive, stepd, d_scan, col_pair, rates, tb=block)
    adjoint_in = carried(adjoint_first, reach, "seq", -1)
    ones = diagonal(jnp.ones((CH, N), F32))
    weighted_b, d_rate, d_b_part, d_c_part, a_log_part = bwd(
        stepd, inject, d_scan, col_pair, b_diag, ones, rates, marks, adjoint_in, tb=block, w=1024
    )
    d_step = LN2 * d_rate + x_float * weighted_b
    a_log_part = LN2 * a_log_part
    d_b_part = jnp.sum(d_b_part, axis=0).reshape(tok_rows, N)
    d_c_part = jnp.sum(d_c_part, axis=0).reshape(tok_rows, N)
    d_xlow = d_skip[None] * d_scan + step_size * weighted_b
    d_pre = d_step * jax.nn.sigmoid(pre_act)
    dt_bias_part = jnp.sum(d_pre, axis=0)
    d_pre_low = d_pre.astype(jnp.bfloat16)
    d_wdt = jnp.einsum("tr,te->re", step_low, d_pre_low, preferred_element_type=jnp.float32)
    d_rank = jnp.einsum("te,re->tr", d_pre_low, w_dt, preferred_element_type=jnp.float32)
    d_mixed = lax.psum(jnp.concatenate([d_rank, d_b_part, d_c_part], 1), "tensor")
    d_mixed_low = d_mixed.astype(jnp.bfloat16)
    d_wx = jnp.einsum("te,tj->ej", x_low, d_mixed_low, preferred_element_type=jnp.float32)
    d_wx_rank = d_wx[:, :rank_width]
    d_wx_state = d_wx[:, rank_width:]
    d_xlow = d_xlow + jnp.einsum("tj,ej->te", d_mixed_low, w_x, preferred_element_type=jnp.float32)
    d_conv = d_xlow * silu_slope(conv_sum)
    conv_bias_part = jnp.sum(d_conv, axis=0)
    conv_weight_rows = []
    for offset in range(conv_taps):
        conv_weight_rows.append(
            jnp.sum(d_conv * ext_x[offset : offset + tok_rows] * tap_keeps[offset], axis=0)
        )
    conv_weight_part = jnp.stack(conv_weight_rows, 0)
    conv_padded = jnp.concatenate([d_conv, jnp.zeros((back_rows, chan_lanes), jnp.float32)], 0)
    d_x = jnp.zeros((tok_rows, chan_lanes), jnp.float32)
    for offset in range(conv_taps):
        lead = back_rows - offset
        keep_padded = jnp.concatenate(
            [tap_keeps[offset], jnp.zeros((back_rows, 1), jnp.float32)], 0
        )
        d_x = (
            d_x
            + conv_weight[offset].astype(jnp.float32)[None]
            * conv_padded[lead : lead + tok_rows]
            * keep_padded[lead : lead + tok_rows]
        )
    front_rows = []
    for place in range(back_rows):
        front_total = jnp.zeros((chan_lanes,), jnp.float32)
        for offset in range(place + 1):
            front_total = (
                front_total
                + conv_weight[offset].astype(jnp.float32)
                * d_conv[place - offset]
                * tap_keeps[offset][place - offset, 0]
            )
        front_rows.append(front_total)
    front_grad = jnp.stack(front_rows, 0)
    carried_grad = passed_along(front_grad, "seq", -1)
    d_x = d_x.at[tok_rows - back_rows :].add(carried_grad)
    d_xz = jnp.stack([d_x, d_z], 1).astype(jnp.bfloat16)
    d_win = jnp.einsum("td,tke->dke", normalized_rows, d_xz, preferred_element_type=jnp.float32)
    d_norm_part = jnp.einsum("tke,dke->td", d_xz, w_in, preferred_element_type=jnp.float32)
    scaled_rows = full_rows * inv_rms
    gain_partial = jnp.sum(d_norm_part * scaled_rows, axis=0)
    d_norm_share, gain_part = (
        lax.psum_scatter(d_norm_part, "tensor", scatter_dimension=0, tiled=True),
        lax.psum_scatter(gain_partial, "tensor", scatter_dimension=0, tiled=True),
    )
    inv_share = lax.dynamic_slice_in_dim(inv_rms, row_start, row_share, 0)
    inner_sum = jnp.sum(d_norm_share * full_gain[None] * share_rows, axis=1, keepdims=True)
    inv_cube = inv_share * inv_share * inv_share
    input_grad = (
        grad_out
        + inv_share * full_gain[None] * d_norm_share
        - share_rows * inv_cube * inner_sum / model_width
    )
    g_in, g_x_rank, g_x_state, g_dt, g_out = (
        lax.psum_scatter(d_win, ("dp", "seq"), scatter_dimension=0, tiled=True),
        lax.psum_scatter(d_wx_rank, ("dp", "seq"), scatter_dimension=1, tiled=True),
        lax.psum_scatter(d_wx_state, ("dp", "seq"), scatter_dimension=1, tiled=True),
        lax.psum_scatter(d_wdt, ("dp", "seq"), scatter_dimension=0, tiled=True),
        lax.psum_scatter(d_wout, ("dp", "seq"), scatter_dimension=1, tiled=True),
    )
    g_gain, g_conv_w, g_conv_b, g_bias, g_alog, g_skip = lax.psum(
        (gain_part, conv_weight_part, conv_bias_part, dt_bias_part, a_log_part, d_skip_part),
        ("dp", "seq"),
    )
    return (
        output,
        input_grad,
        g_gain,
        g_in,
        g_conv_w,
        g_conv_b,
        g_x_rank,
        g_x_state,
        g_dt,
        g_bias,
        g_alog,
        g_skip,
        g_out,
    )


def solution(mesh):
    placed = (
        P(("dp", "seq", "tensor"), None),
        P(("dp", "seq", "tensor"), None),
        P(("dp", "seq")),
        P("tensor"),
        P(("dp", "seq"), None, "tensor"),
        P(None, "tensor"),
        P("tensor"),
        P("tensor", ("dp", "seq")),
        P(("dp", "seq"), "tensor"),
        P("tensor"),
        P(None, "tensor"),
        P("tensor"),
        P("tensor", ("dp", "seq")),
    )
    return jax.shard_map(
        on_device,
        mesh=mesh,
        in_specs=placed,
        out_specs=(
            P(("dp", "seq", "tensor"), None),
            P(("dp", "seq", "tensor"), None),
            P("tensor"),
            P(("dp", "seq"), None, "tensor"),
            P(None, "tensor"),
            P("tensor"),
            P("tensor", ("dp", "seq")),
            P("tensor", ("dp", "seq")),
            P(("dp", "seq"), "tensor"),
            P("tensor"),
            P(None, "tensor"),
            P("tensor"),
            P("tensor", ("dp", "seq")),
        ),
        check_vma=False,
    )
```

profile of v0, /device:TPU:0, one launch (start us, length us, event | category | flops | bytes accessed | tf_op | source)
XLA Modules:
  0.0 1195.3 jit_solution(2457990236915273386)
XLA Ops:
  8.0 2.5 copy.51
  11.9 4.9 collective-permute-start
  16.8 12.3 %all-gather = bf16[4,1,512]{2,1,0:T(2,128)(2,1)S(1)} all-gather(bf16[1,1,512]{2,1,0:T(2,128)(2,1)S(1)} %reshape.251), channel_id=1, replica_groups=mesh['dp'=4,'seq'=2,'tensor'=4] {'tensor'}, dimensions={0}, use_global_device_ids=true | all-gather | bytes 5120 | tf_op jit(solution)/shard_map/all_gather | solution.py:326
  29.1 16.2 %all-gather.1 = bf16[8,20,1024]{2,1,0:T(8,128)(2,1)S(1)} all-gather(bf16[1,20,1024]{2,1,0:T(8,128)(2,1)S(1)} %bitcast.116), channel_id=1, replica_groups=mesh['dp'=4,'seq'=2,'tensor'=4] {'dp','seq'}, dimensions={0}, use_global_device_ids=true | all-gather | bytes 368640 | tf_op jit(solution)/shard_map/all_gather | solution.py:317
  46.1 47.1 %all-gather.7.cloned.1.call-done = bf16[1024,2048]{1,0:T(8,128)(2,1)} async-done(((bf16[256,2048]{1,0:T(8,128)(2,1)}), bf16[1024,2048]{1,0:T(8,128)(2,1)}) %all-gather.7.cloned.1.call-update) | async-done | bytes 4194320 | tf_op jit(solution)/shard_map/all_gather | solution.py:325
  93.2 3.1 fusion.4
  96.3 52.3 %all-gather.9.cloned.1.call-done = bf16[2048,2,1024]{2,0,1:T(8,128)(2,1)} async-done(((bf16[256,2,1024]{2,0,1:T(8,128)(2,1)}), bf16[2048,2,1024]{2,0,1:T(8,128)(2,1)}) %all-gather.9.cloned.1.call-update) | async-done | bytes 8388624 | tf_op jit(solution)/shard_map/all_gather | solution.py:316
  148.6 12.6 %fusion.17 = f32[1024,2,1024]{2,0,1:T(8,128)S(1)} fusion(bf16[2048,2,1024]{2,0,1:T(8,128)(2,1)} %all-gather.9.cloned.1.call-done, bf16[1024,2048]{1,0:T(8,128)(2,1)} %all-gather.7.cloned.1.call-done, f32[2048]{0:T(1024)S(1)} %bitcast.100, f32[1024]{0:T(1024)S(1)} %add_rsqrt_fusion), kind=kOutput, calls=%fused_computation.46 | convolution fusion | flops 8598323200 | bytes 20983808 | tf_op jit(solution)/shard_map/td,dke->tke/dot_general | solution.py:332
  161.2 3.0 collective-permute-start.1
  165.7 5.2 multiply_convert_fusion.2
  173.3 18.0 %all_gather.28 = bf16[128,1024]{1,0:T(8,128)(2,1)S(1)} all-gather(bf16[16,1024]{1,0:T(8,128)(2,1)S(1)} %copy-done.43), channel_id=1, replica_groups=mesh['dp'=4,'seq'=2,'tensor'=4] {'dp','seq'}, dimensions={0}, use_global_device_ids=true | all-gather | bytes 294912 | tf_op jit(solution)/shard_map/all_gather | solution.py:318
  193.4 21.0 %all-reduce.13.cloned.1.call-done = f32[1024,160]{0,1:T(8,128)} async-done(((f32[1024,160]{0,1:T(8,128)}), f32[1024,160]{0,1:T(8,128)}) %all-reduce.13.cloned.1.call-update) | async-done | bytes 655376 | tf_op jit(solution)/shard_map/psum | solution.py:356
  223.9 8.7 fusion.61
  232.5 24.3 %scan_forward.1 = (f32[1024,1024]{1,0:T(8,128)S(1)}, f32[8,16,1024]{2,1,0:T(8,128)S(1)}, f32[16,1024]{1,0:T(8,128)S(1)}) custom-call(f32[1024,1024]{1,0:T(8,128)} %get-tuple-element.121.stepd_ref, f32[1024,1024]{1,0:T(8,128)} %get-tuple-element.130.u_ref, f32[64,16,32]{2,1,0:T(8,128)S(1)} %pad_maximum_fusion.5.bc_ref, ...), custom_call_target="tpu_custom_call" | custom-call | tf_op jit(solution)/shard_map/scan_forward/pallas_call | solution.py:57
  258.9 3.4 collective-permute-start.2
  264.2 12.9 %scan_correct.1 = (f32[1024,1024]{1,0:T(8,128)S(1)}, f32[8,16,1024]{2,1,0:T(8,128)S(1)}) custom-call(s32[8]{0:T(128)S(1)} %compare_convert_fusion.2.alive_ref, f32[1024,1024]{1,0:T(8,128)} %copy-done.1, f32[1024,1024]{1,0:T(8,128)} %get-tuple-element.121.stepd_ref, bf16[1024,256]{1,0:T(8,128)(2,1)S(1)} %get-tuple-element.142.cdiag_ref, ...), custom_call_target="tpu_custom_call" | custom-call | tf_op jit(solution)/shard_map/scan_correct/pallas_call | solution.py:211
  279.1 4.9 multiply_convert_fusion.1
  283.9 10.6 fusion.69
  298.8 20.8 %all-reduce.4 = bf16[16]{0:T(256)(128)(2,1)S(1)} all-reduce(bf16[16]{0:T(256)(128)(2,1)S(1)} %dynamic-update-slice.4), channel_id=1, replica_groups=mesh['dp'=4,'seq'=2,'tensor'=4] {'dp','seq'}, use_global_device_ids=true, to_apply=%add.4 | all-reduce | flops 16 | bytes 64
  321.8 124.3 %reduce-scatter.7.cloned.1.call-done = f32[256,2048]{1,0:T(8,128)} async-done(((f32[1024,2048]{1,0:T(8,128)}), f32[256,2048]{1,0:T(8,128)}) %reduce-scatter.7.cloned.1.call-update) | async-done | bytes 2097168 | tf_op jit(solution)/shard_map/reduce_scatter | solution.py:381
  446.0 3.4 fusion.25
  452.3 78.8 %all-gather.13.cloned.1.call-done = bf16[1024,2048]{1,0:T(8,128)(2,1)} async-done(((bf16[256,2048]{1,0:T(8,128)(2,1)}), bf16[1024,2048]{1,0:T(8,128)(2,1)}) %all-gather.13.cloned.1.call-update) | async-done | bytes 4194320 | tf_op jit(solution)/shard_map/all_gather | solution.py:396
  531.1 16.1 %fusion.10 = (f32[1024]{0:T(1024)}, f32[1024,1024]{1,0:T(8,128)}, bf16[1024,1,1024]{2,0,1:T(8,128)(2,1)}) fusion(bf16[1024,1024]{1,0:T(8,128)(2,1)} %copy-done.4, f32[1024,2,1024]{2,0,1:T(8,128)} %copy-done.11, f32[1024,1024]{1,0:T(8,128)} %copy-done.2, f32[1024]{0:T(1024)S(1)} %copy-done.53, bf16[1024,2048]{1,0:T(8,128)(2,1)} %all-gather.13.cloned.1.call-done, ...), kind=kOutput, calls=%fused_computation.20 | convolution fusion | flops 4312792064 | bytes 25174016 | tf_op jit(solution)/shard_map/tw,ew->te/dot_general | solution.py:397
  547.2 10.7 scan_entry.1
  559.3 7.4 collective-permute-done.3.gin_ref
  566.7 77.1 %scan_backward.1 = (f32[1024,1024]{1,0:T(8,128)S(1)}, f32[1024,1024]{1,0:T(8,128)}, f32[1,64,256]{2,1,0:T(8,128)S(1)}, f32[1,64,256]{2,1,0:T(8,128)S(1)}, f32[16,1024]{1,0:T(8,128)S(1)}) custom-call(f32[1024,1024]{1,0:T(8,128)} %get-tuple-element.121.stepd_ref, f32[1024,1024]{1,0:T(8,128)} %get-tuple-element.130.u_ref, ...), custom_call_target="tpu_custom_call" | custom-call | tf_op jit(solution)/shard_map/scan_backward/pallas_call | solution.py:141
  646.6 6.8 fusion.59
  655.7 28.3 %all-reduce.16 = bf16[1024,160]{0,1:T(8,128)(2,1)S(1)} all-reduce(f32[1024,160]{0,1:T(8,128)S(1)} %pad_maximum_fusion.4), channel_id=1, replica_groups=mesh['dp'=4,'seq'=2,'tensor'=4] {'tensor'}, use_global_device_ids=true, to_apply=%region_9.10 | all-reduce | flops 163840 | bytes 983040 | tf_op jit(solution)/shard_map/psum | solution.py:420
  684.1 15.8 %fusion.57 = (f32[1024]{0:T(1024)S(1)}, f32[1024]{0:T(1024)S(1)}, f32[1024]{0:T(1024)S(1)}, f32[1024]{0:T(1024)S(1)}, f32[1024]{0:T(1024)S(1)}, /*index=5*/f32[1024,1024]{1,0:T(8,128)S(1)}) fusion(f32[1024]{0:T(1024)S(1)} %copy-done.21, f32[1024,2,1024]{2,0,1:T(8,128)} %copy-done.11, f32[1024]{0:T(1024)S(1)} %copy-done.37, f32[1024,1024]{1,0:T(8,128)} %copy-done.9, ...), kind=kOutput, calls=%fused_computation.142 | convolution fusion | flops 372239360 | bytes 30072832 | tf_op jit(solution)/shard_map/tj,ej->te/dot_general | solution.py:425
  700.0 4.3 fusion.90
  704.3 4.2 multiply_add_fusion
  709.1 3.9 multiply_multiply_fusion.1
  715.7 3.0 collective-permute-done.4
  720.8 2.7 convert.14
  724.3 14.2 %fusion.3 = (f32[2048]{0:T(1024)S(1)}, f32[1024,2048]{1,0:T(8,128)}) fusion(bf16[1024,2048]{1,0:T(8,128)(2,1)S(1)} %copy-done.14, f32[1024]{0:T(1024)S(1)} %copy-done.52, bf16[2048,2,1024]{2,0,1:T(8,128)(2,1)} %all-gather.9.cloned.1.call-done, bf16[1024,1,1024]{2,0,1:T(8,128)(2,1)} %get-tuple-element.126, bf16[1024,1,1024]{2,0,1:T(8,128)(2,1)S(1)} %convert.14), kind=kOutput, calls=%fused_computation.6 | convolution fusion | flops 8600418304 | bytes 25178112 | tf_op jit(solution)/shard_map/tke,dke->td/dot_general | solution.py:463
  738.8 14.9 %fusion.15 = f32[2048,2,1024]{2,0,1:T(8,128)} fusion(bf16[1024,1,1024]{2,0,1:T(8,128)(2,1)} %get-tuple-element.126, bf16[1024,1,1024]{2,0,1:T(8,128)(2,1)S(1)} %convert.14, bf16[1024,2048]{1,0:T(8,128)(2,1)} %all-gather.7.cloned.1.call-done, f32[2048]{0:T(1024)S(1)} %bitcast.101, f32[1024]{0:T(1024)S(1)} %copy-done.52), kind=kOutput, calls=%fused_computation.45 | convolution fusion | flops 8606711808 | bytes 25178112 | tf_op jit(solution)/shard_map/td,tke->dke/dot_general | solution.py:462
  755.8 2.3 fusion.26
  758.3 10.7 fusion.70
  771.6 10.5 all-reduce.5
  782.2 24.1 %all-reduce.7 = (f32[512]{0:T(512)}, f32[4,1024]{1,0:T(4,128)}, f32[1024]{0:T(1024)}, f32[1024]{0:T(1024)}, f32[1024]{0:T(1024)}) all-reduce(f32[512]{0:T(512)S(1)} %dynamic-slice.14, f32[4,1024]{1,0:T(4,128)S(1)} %pad_maximum_fusion.7, f32[1024]{0:T(1024)S(1)} %get-tuple-element.100, ...), channel_id=1, replica_groups=mesh['dp'=4,'seq'=2,'tensor'=4] {'dp','seq'}, use_global_device_ids=true, to_apply=%region_14.15 | all-reduce | flops 7680 | bytes 61440 | tf_op jit(solution)/shard_map/psum | solution.py:485
  807.7 108.4 %reduce-scatter.9.cloned.1.call-done = f32[256,2048]{1,0:T(8,128)} async-done(((f32[1024,2048]{1,0:T(8,128)}), f32[256,2048]{1,0:T(8,128)}) %reduce-scatter.9.cloned.1.call-update) | async-done | bytes 2097168 | tf_op jit(solution)/shard_map/reduce_scatter | solution.py:467
  916.1 2.1 fusion.22
  918.3 4.0 fusion.21
  922.3 114.1 %reduce-scatter.11.cloned.1.call-done = f32[256,2,1024]{2,0,1:T(8,128)} async-done(((f32[2048,2,1024]{2,0,1:T(8,128)}), f32[256,2,1024]{2,0,1:T(8,128)}) %reduce-scatter.11.cloned.1.call-update) | async-done | bytes 2097168 | tf_op jit(solution)/shard_map/reduce_scatter | solution.py:479
  1036.4 4.5 copy.59
  1040.9 33.1 %reduce-scatter.13.cloned.1.call-done = f32[1024,16]{0,1:T(8,128)} async-done(((f32[1024,128]{0,1:T(8,128)}), f32[1024,16]{0,1:T(8,128)}) %reduce-scatter.13.cloned.1.call-update) | async-done | bytes 65552 | tf_op jit(solution)/shard_map/reduce_scatter | solution.py:480
  1074.0 38.1 %reduce-scatter.15.cloned.1.call-done = f32[16,1024]{1,0:T(8,128)} async-done(((f32[128,1024]{1,0:T(8,128)}), f32[16,1024]{1,0:T(8,128)}) %reduce-scatter.15.cloned.1.call-update) | async-done | bytes 65552 | tf_op jit(solution)/shard_map/reduce_scatter | solution.py:482
  1112.2 75.2 %reduce-scatter.17.cloned.1.call-done = f32[1024,256]{1,0:T(8,128)} async-done(((f32[1024,2048]{1,0:T(8,128)}), f32[1024,256]{1,0:T(8,128)}) %reduce-scatter.17.cloned.1.call-update) | async-done | bytes 1048592 | tf_op jit(solution)/shard_map/reduce_scatter | solution.py:483
  (229 shorter events, 47.4 us)
Async XLA Ops:
  7.2 38.1 %copy-start.19 = (bf16[4,1024]{1,0:T(4,128)(2,1)S(1)}, bf16[4,1024]{1,0:T(4,128)(2,1)}, u32[]{:S(2)}) copy-start(bf16[4,1024]{1,0:T(4,128)(2,1)} %param.20) | copy-start | bytes 24580
  7.2 86.0 %all-gather.7.cloned.1.call-start = ((), (), s32[]{:S(2)}) async-start(), calls=%async_computation.6 | async-start | bytes 5242880 | tf_op jit(solution)/shard_map/all_gather | solution.py:325
  8.0 140.6 %all-gather.9.cloned.1.call-start = ((), (), s32[]{:S(2)}) async-start(), calls=%async_computation.7 | async-start | bytes 9437184 | tf_op jit(solution)/shard_map/all_gather | solution.py:316
  10.5 203.9 %all-reduce.13.cloned.1.call-start = ((), (), s32[]{:S(2)}) async-start(), calls=%async_computation.8 | async-start | bytes 1310720 | tf_op jit(solution)/shard_map/psum | solution.py:356
  11.9 33.6 %collective-permute-start = (f32[3]{0:T(128)S(1)}, f32[3]{0:T(128)S(1)}, u32[]{:S(2)}, u32[]{:S(2)}) collective-permute-start(f32[3]{0:T(128)S(1)} %slice.155), channel_id=1, source_target_pairs={{0,4},{1,5},{2,6},{3,7},{8,12},{9,13},{10,14},{11,15},{16,20},{17,... | collective-permute-start | bytes 44 | tf_op jit(solution)/shard_map/ppermute | solution.py:19
  45.3 125.6 %copy-start.16 = (bf16[160,1024]{1,0:T(8,128)(2,1)}, bf16[160,1024]{1,0:T(8,128)(2,1)S(1)}, u32[]{:S(2)}) copy-start(bf16[160,1024]{1,0:T(8,128)(2,1)S(1)} %reshape.254) | copy-start | bytes 983044
  45.4 120.3 %copy-start.20 = (f32[1024]{0:T(1024)}, f32[1024]{0:T(1024)S(1)}, u32[]{:S(2)}) copy-start(f32[1024]{0:T(1024)S(1)} %compare_convert_fusion) | copy-start | bytes 12292
  45.4 120.3 %copy-start.22 = (f32[1,1024]{1,0:T(1,128)}, f32[1,1024]{1,0:T(1,128)S(1)}, u32[]{:S(2)}) copy-start(f32[1,1024]{1,0:T(1,128)S(1)} %get-tuple-element.137) | copy-start | bytes 12292
  45.4 120.2 %copy-start.24 = (f32[1,1024]{1,0:T(1,128)}, f32[1,1024]{1,0:T(1,128)S(1)}, u32[]{:S(2)}) copy-start(f32[1,1024]{1,0:T(1,128)S(1)} %get-tuple-element.138) | copy-start | bytes 12292
  45.4 120.2 %copy-start.26 = (f32[1,1024]{1,0:T(1,128)}, f32[1,1024]{1,0:T(1,128)S(1)}, u32[]{:S(2)}) copy-start(f32[1,1024]{1,0:T(1,128)S(1)} %get-tuple-element.139) | copy-start | bytes 12292
  45.4 120.2 %copy-start.28 = (f32[1,1024]{1,0:T(1,128)}, f32[1,1024]{1,0:T(1,128)S(1)}, u32[]{:S(2)}) copy-start(f32[1,1024]{1,0:T(1,128)S(1)} %get-tuple-element.140) | copy-start | bytes 12292
  46.1 119.6 %copy-start.32 = (f32[1024]{0:T(1024)}, f32[1024]{0:T(1024)S(1)}, u32[]{:S(2)}) copy-start(f32[1024]{0:T(1024)S(1)} %get-tuple-element.143) | copy-start | bytes 12292
  46.1 119.6 %copy-start.35 = (f32[1024]{0:T(1024)}, f32[1024]{0:T(1024)S(1)}, u32[]{:S(2)}) copy-start(f32[1024]{0:T(1024)S(1)} %get-tuple-element.144) | copy-start | bytes 12292
  46.1 119.6 %copy-start.40 = (f32[1024]{0:T(1024)}, f32[1024]{0:T(1024)S(1)}, u32[]{:S(2)}) copy-start(f32[1024]{0:T(1024)S(1)} %get-tuple-element.147) | copy-start | bytes 12292
  96.3 64.9 %copy-start.51 = (f32[1024]{0:T(1024)}, f32[1024]{0:T(1024)S(1)}, u32[]{:S(2)}) copy-start(f32[1024]{0:T(1024)S(1)} %add_rsqrt_fusion) | copy-start | bytes 12292
  161.2 4.5 collective-permute-start.1
  170.9 52.9 %copy-start.4 = (bf16[1024,1024]{1,0:T(8,128)(2,1)}, bf16[1024,1024]{1,0:T(8,128)(2,1)S(1)}, u32[]{:S(2)}) copy-start(bf16[1024,1024]{1,0:T(8,128)(2,1)S(1)} %get-tuple-element.122) | copy-start | bytes 6291460
  172.6 111.3 %all-gather.11.cloned.1.call-start = ((), (), s32[]{:S(2)}) async-start(), calls=%async_computation.9 | async-start | bytes 4718592 | tf_op jit(solution)/shard_map/all_gather | solution.py:319
  173.2 272.8 %reduce-scatter.7.cloned.1.call-start = ((), (), s32[]{:S(2)}) async-start(), calls=%async_computation.10 | async-start | bytes 10485760 | tf_op jit(solution)/shard_map/reduce_scatter | solution.py:381
  232.5 29.8 %copy-start.63 = (s32[8]{0:T(128)S(1)}, s32[8]{0:T(128)}, u32[]{:S(2)}) copy-start(s32[8]{0:T(128)} %copy-done.62) | copy-start | bytes 100
  232.5 29.8 %copy-start.64 = (s32[8,1]{0,1:T(1,128)S(1)}, s32[8,1]{0,1:T(1,128)}, u32[]{:S(2)}) copy-start(s32[8,1]{0,1:T(1,128)} %reduce-window.9) | copy-start | bytes 100
  258.9 5.3 collective-permute-start.2
  294.5 151.5 %copy-start.10 = (bf16[256,2048]{1,0:T(8,128)(2,1)S(1)}, bf16[256,2048]{1,0:T(8,128)(2,1)}, u32[]{:S(2)}) copy-start(bf16[256,2048]{1,0:T(8,128)(2,1)} %param.15) | copy-start | bytes 3145732
  294.6 155.1 %copy-start.55 = (s32[256]{0:T(256)S(1)}, s32[256]{0:T(256)}, u32[]{:S(2)}) copy-start(s32[256]{0:T(256)} %and_select_fusion.1) | copy-start | bytes 3076
  294.6 155.2 %copy-start.41 = (f32[1024]{0:T(1024)S(1)}, f32[1024]{0:T(1024)}, u32[]{:S(2)}) copy-start(f32[1024]{0:T(1024)} %copy-done.40) | copy-start | bytes 12292
  294.6 156.3 %copy-start.36 = (f32[1024]{0:T(1024)S(1)}, f32[1024]{0:T(1024)}, u32[]{:S(2)}) copy-start(f32[1024]{0:T(1024)} %copy-done.35) | copy-start | bytes 12292
  294.6 157.0 %copy-start.33 = (f32[1024]{0:T(1024)S(1)}, f32[1024]{0:T(1024)}, u32[]{:S(2)}) copy-start(f32[1024]{0:T(1024)} %copy-done.32) | copy-start | bytes 12292
  294.6 236.4 %all-gather.13.cloned.1.call-start = ((), (), s32[]{:S(2)}) async-start(), calls=%async_computation.11 | async-start | bytes 5242880 | tf_op jit(solution)/shard_map/all_gather | solution.py:396
  321.8 225.4 %copy-start.49 = (f32[256]{0:T(256)}, f32[256]{0:T(256)S(1)}, u32[]{:S(2)}) copy-start(f32[256]{0:T(256)S(1)} %dynamic-slice_multiply_fusion) | copy-start | bytes 3076
  449.4 356.9 %all-reduce.15.cloned.1.call-start = ((), (), s32[]{:S(2)}) async-start(), calls=%async_computation.17 | async-start | bytes 393216
  557.9 8.8 collective-permute-start.3
  566.7 79.9 %copy-start.47 = (f32[1024]{0:T(1024)S(1)}, f32[1024]{0:T(1024)}, u32[]{:S(2)}) copy-start(f32[1024]{0:T(1024)} %param.24) | copy-start | bytes 12292
  653.4 30.6 %copy-start.17 = (bf16[160,1024]{1,0:T(8,128)(2,1)S(1)}, bf16[160,1024]{1,0:T(8,128)(2,1)}, u32[]{:S(2)}) copy-start(bf16[160,1024]{1,0:T(8,128)(2,1)} %copy-done.16) | copy-start | bytes 983044
  653.4 30.6 %copy-start.21 = (f32[1024]{0:T(1024)S(1)}, f32[1024]{0:T(1024)}, u32[]{:S(2)}) copy-start(f32[1024]{0:T(1024)} %copy-done.20) | copy-start | bytes 12292
  653.4 30.6 %copy-start.34 = (f32[1024]{0:T(1024)S(1)}, f32[1024]{0:T(1024)}, u32[]{:S(2)}) copy-start(f32[1024]{0:T(1024)} %copy-done.32) | copy-start | bytes 12292
  653.4 30.6 %copy-start.37 = (f32[1024]{0:T(1024)S(1)}, f32[1024]{0:T(1024)}, u32[]{:S(2)}) copy-start(f32[1024]{0:T(1024)} %copy-done.35) | copy-start | bytes 12292
  653.4 30.6 %copy-start.42 = (f32[1024]{0:T(1024)S(1)}, f32[1024]{0:T(1024)}, u32[]{:S(2)}) copy-start(f32[1024]{0:T(1024)} %copy-done.40) | copy-start | bytes 12292
  653.4 30.6 %copy-start.45 = (f32[3,1024]{1,0:T(4,128)S(1)}, f32[3,1024]{1,0:T(4,128)}, u32[]{:S(2)}) copy-start(f32[3,1024]{1,0:T(4,128)} %copy-done.44) | copy-start | bytes 36868
  653.4 30.6 %copy-start.54 = (f32[1024]{0:T(1024)S(1)}, f32[1024]{0:T(1024)}, u32[]{:S(2)}) copy-start(f32[1024]{0:T(1024)} %param.26) | copy-start | bytes 12292
  713.0 5.6 collective-permute-start.4
  715.6 200.4 %reduce-scatter.9.cloned.1.call-start = ((), (), s32[]{:S(2)}) async-start(), calls=%async_computation.12 | async-start | bytes 10485760 | tf_op jit(solution)/shard_map/reduce_scatter | solution.py:467
  738.5 297.9 %reduce-scatter.11.cloned.1.call-start = ((), (), s32[]{:S(2)}) async-start(), calls=%async_computation.13 | async-start | bytes 18874368 | tf_op jit(solution)/shard_map/reduce_scatter | solution.py:479
  753.7 320.3 %reduce-scatter.13.cloned.1.call-start = ((), (), s32[]{:S(2)}) async-start(), calls=%async_computation.14 | async-start | bytes 589824 | tf_op jit(solution)/shard_map/reduce_scatter | solution.py:480
  755.8 356.4 %reduce-scatter.15.cloned.1.call-start = ((), (), s32[]{:S(2)}) async-start(), calls=%async_computation.15 | async-start | bytes 589824 | tf_op jit(solution)/shard_map/reduce_scatter | solution.py:482
  758.2 429.1 %reduce-scatter.17.cloned.1.call-start = ((), (), s32[]{:S(2)}) async-start(), calls=%async_computation.16 | async-start | bytes 9437184 | tf_op jit(solution)/shard_map/reduce_scatter | solution.py:483
  769.0 149.2 %copy-start.12 = (f32[256,2048]{1,0:T(8,128)S(1)}, f32[256,2048]{1,0:T(8,128)}, u32[]{:S(2)}) copy-start(f32[256,2048]{1,0:T(8,128)} %reduce-scatter.7.cloned.1.call-done) | copy-start | bytes 6291460
  769.0 149.2 %copy-start.50 = (f32[256]{0:T(256)S(1)}, f32[256]{0:T(256)}, u32[]{:S(2)}) copy-start(f32[256]{0:T(256)} %copy-done.49) | copy-start | bytes 3076
  922.3 265.1 %copy-start.30 = (f32[16,1024]{1,0:T(8,128)S(1)}, f32[16,1024]{1,0:T(8,128)}, u32[]{:S(2)}) copy-start(f32[16,1024]{1,0:T(8,128)} %get-tuple-element.176) | copy-start | bytes 196612
  (34 other events, 332.3 us)
Sparse Core Ops, SparseCore 0:
  9.6 83.5 all-gather.6
  95.7 52.8 all-gather.8
  172.8 41.5 all-reduce.12
  216.1 36.9 all-gather.10
  294.7 151.2 reduce-scatter.6
  449.5 81.4 all-gather.12
  715.8 54.0 all-reduce.14
  772.2 143.8 reduce-scatter.8
  919.6 116.6 reduce-scatter.10
  1039.9 34.1 reduce-scatter.12
  1078.0 34.1 reduce-scatter.14
  1116.0 71.2 reduce-scatter.16
where the time goes:
time: 1200 us
  waiting for transfers between devices  707 us (59%)
  blocking collectives  130 us (11%)
  Pallas kernels  125 us (10%)
  matrix products  109 us (9%)
  other arithmetic  52.7 us (4%)
  local copies, waits for them, and re-layouts  35.3 us (3%)
  between operations  21.5 us (2%)
  starting transfers between devices  14.8 us (1%)
    reduce_scatter x1, waiting for transfers between devices, on_device(): lax.psum_scatter(jnp.dot(gated_output_rows, w_out, preferred_element_type...  124 us
    reduce_scatter x1, waiting for transfers between devices, on_device(): lax.psum_scatter(d_win, ('dp', 'seq'), scatter_dimension=0, tiled=True)  114 us
    reduce_scatter x1, waiting for transfers between devices, on_device(): lax.psum_scatter(d_norm_part, 'tensor', scatter_dimension=0, tiled=True)  108 us
    all_gather x1, waiting for transfers between devices, on_device(): piece = lax.all_gather(grad_low, 'tensor', axis=0, tiled=True)  78.8 us
    pallas_call x1, Pallas kernels, bwd(): pl.pallas_call(functools.partial(bwd_kernel, unroll=unroll), grid=grid, i...  77.1 us
    reduce_scatter x1, waiting for transfers between devices, on_device(): lax.psum_scatter(d_wout, ('dp', 'seq'), scatter_dimension=1, tiled=True)  75.2 us
    all_gather x1, waiting for transfers between devices, on_device(): lax.all_gather(input_projection_weight, ('dp', 'seq'), axis=0, tiled=True)  52.3 us
    all_gather x1, waiting for transfers between devices, on_device(): lax.all_gather(hidden_in, 'tensor', axis=0, tiled=True)  47.1 us
  transfers between devices with their start and end apart: 17, of which 14 were waited for; matrix products, arithmetic and copies ran while one was open for 8% of the time, Pallas kernels for 3%

commit v1 on v0

--- a/solution.py
+++ b/solution.py
@@ -379,11 +379,11 @@
     gate_act = jax.nn.silu(z_gate)
     gated_output_rows = (scan_out * gate_act).astype(jnp.bfloat16)
     branch_share = lax.psum_scatter(
-        jnp.dot(gated_output_rows, w_out, preferred_element_type=jnp.float32),
+        jnp.dot(gated_output_rows, w_out, preferred_element_type=F32).astype(BF16),
         "tensor",
         scatter_dimension=0,
         tiled=True,
-    )
+    ).astype(F32)
     share_rows = hidden_in.astype(jnp.float32)
     result = share_rows + branch_share
     output = result.astype(jnp.bfloat16)
@@ -396,7 +396,7 @@
     piece = lax.all_gather(grad_low, "tensor", axis=0, tiled=True)
     block_rows = jnp.einsum("tw,ew->te", piece, w_out, preferred_element_type=jnp.float32)
     d_gated = block_rows
-    d_wout = jnp.einsum("te,tw->ew", gated_output_rows, piece, preferred_element_type=jnp.float32)
+    d_wout = jnp.einsum("te,tw->we", gated_output_rows, piece, preferred_element_type=jnp.float32)
     d_gated, d_wout = (d_gated, d_wout)
     d_scan = d_gated * gate_act
     d_z = d_gated * scan_out * silu_slope(z_gate)
@@ -461,13 +461,10 @@
     d_xz = jnp.stack([d_x, d_z], 1).astype(jnp.bfloat16)
     d_win = jnp.einsum("td,tke->dke", normalized_rows, d_xz, preferred_element_type=jnp.float32)
     d_norm_part = jnp.einsum("tke,dke->td", d_xz, w_in, preferred_element_type=jnp.float32)
-    scaled_rows = full_rows * inv_rms
-    gain_partial = jnp.sum(d_norm_part * scaled_rows, axis=0)
-    d_norm_share, gain_part = (
-        lax.psum_scatter(d_norm_part, "tensor", scatter_dimension=0, tiled=True),
-        lax.psum_scatter(gain_partial, "tensor", scatter_dimension=0, tiled=True),
-    )
     inv_share = lax.dynamic_slice_in_dim(inv_rms, row_start, row_share, 0)
+    d_norm_share = lax.psum_scatter(d_norm_part.astype(BF16), "tensor", scatter_dimension=0, tiled=True).astype(F32)
+    gain_partial = jnp.sum(d_norm_share * share_rows * inv_share, axis=0)
+    gain_part = lax.psum_scatter(gain_partial, "tensor", scatter_dimension=0, tiled=True)
     inner_sum = jnp.sum(d_norm_share * full_gain[None] * share_rows, axis=1, keepdims=True)
     inv_cube = inv_share * inv_share * inv_share
     input_grad = (
@@ -475,13 +472,19 @@
         + inv_share * full_gain[None] * d_norm_share
         - share_rows * inv_cube * inner_sum / model_width
     )
-    g_in, g_x_rank, g_x_state, g_dt, g_out = (
-        lax.psum_scatter(d_win, ("dp", "seq"), scatter_dimension=0, tiled=True),
-        lax.psum_scatter(d_wx_rank, ("dp", "seq"), scatter_dimension=1, tiled=True),
-        lax.psum_scatter(d_wx_state, ("dp", "seq"), scatter_dimension=1, tiled=True),
-        lax.psum_scatter(d_wdt, ("dp", "seq"), scatter_dimension=0, tiled=True),
-        lax.psum_scatter(d_wout, ("dp", "seq"), scatter_dimension=1, tiled=True),
-    )
+    parts = lax.axis_size(("dp", "seq"))
+    rows_x = jnp.concatenate([d_wx_rank.T.reshape(parts, -1, chan_lanes), d_wx_state.T.reshape(parts, -1, chan_lanes)], 1)
+    rows_dt = d_wdt.reshape(parts, -1, chan_lanes)
+    g_small = lax.psum_scatter(
+        jnp.concatenate([rows_x, rows_dt], 1), ("dp", "seq"), scatter_dimension=0, tiled=True
+    )[0]
+    rank_here = rank_width // parts
+    state_here = 2 * state_width // parts
+    g_x_rank = g_small[:rank_here].T
+    g_x_state = g_small[rank_here : rank_here + state_here].T
+    g_dt = g_small[rank_here + state_here :]
+    g_in = lax.psum_scatter(d_win.astype(BF16), ("dp", "seq"), scatter_dimension=0, tiled=True).astype(F32)
+    g_out = lax.psum_scatter(d_wout.astype(BF16), ("dp", "seq"), scatter_dimension=0, tiled=True).astype(F32).T
     g_gain, g_conv_w, g_conv_b, g_bias, g_alog, g_skip = lax.psum(
         (gain_part, conv_weight_part, conv_bias_part, dt_bias_part, a_log_part, d_skip_part),
         ("dp", "seq"),

time: 1200 us -> 936 us (0.78)
  waiting for transfers between devices: 707 us -> 437 us
    reduce_scatter x5 -> x4, waiting for transfers between devices: 369 us -> 115 us  [the longest x1 74.4 us: on_device(): lax.psum_scatter(d_norm_part.astype(BF16), 'tensor', scatter_dimension=0,...]
    reduce_scatter x1, waiting for transfers between devices: 124 us -> 56.4 us  [on_device(): lax.psum_scatter(jnp.dot(gated_output_rows, w_out, preferred_element_type...]
    psum x0 -> x1, waiting for transfers between devices: none -> 52.5 us  [on_device(): lax.psum((gain_part, conv_weight_part, conv_bias_part, dt_bias_part, a_lo...]
  transfers between devices with their start and end apart: 17 -> 16, of which waited for: 14 -> 12; matrix products, arithmetic and copies ran while one was open for 8% -> 13% of each run, Pallas kernels for 3% -> 4%
where the time goes in v1:
time: 936 us; the launch traced here: 928 us
  waiting for transfers between devices  437 us (47%)
  blocking collectives  133 us (14%)
  Pallas kernels  125 us (13%)
  matrix products  109 us (12%)
  other arithmetic  53.7 us (6%)
  local copies, waits for them, and re-layouts  34.6 us (4%)
  between operations  20.5 us (2%)
  starting transfers between devices  15.2 us (2%)
    all_gather x1, waiting for transfers between devices, on_device(): piece = lax.all_gather(grad_low, 'tensor', axis=0, tiled=True)  81.2 us
    pallas_call x1, Pallas kernels, bwd(): pl.pallas_call(functools.partial(bwd_kernel, unroll=unroll), grid=grid, i...  77.3 us
    reduce_scatter x1, waiting for transfers between devices, on_device(): lax.psum_scatter(d_norm_part.astype(BF16), 'tensor', scatter_dimension=0,...  74.4 us
    reduce_scatter x1, waiting for transfers between devices, on_device(): lax.psum_scatter(jnp.dot(gated_output_rows, w_out, preferred_element_type...  56.4 us
    psum x1, waiting for transfers between devices, on_device(): lax.psum((gain_part, conv_weight_part, conv_bias_part, dt_bias_part, a_lo...  52.5 us
    all_gather x1, waiting for transfers between devices, on_device(): lax.all_gather(input_projection_weight, ('dp', 'seq'), axis=0, tiled=True)  52.3 us
    all_gather x1, waiting for transfers between devices, on_device(): lax.all_gather(hidden_in, 'tensor', axis=0, tiled=True)  47 us
    reduce_scatter x1, waiting for transfers between devices, on_device(): lax.psum_scatter(d_win.astype(BF16), ('dp', 'seq'), scatter_dimension=0,...  33.3 us
  transfers between devices with their start and end apart: 16, of which 12 were waited for; matrix products, arithmetic and copies ran while one was open for 13% of the time, Pallas kernels for 4%

profile of v1, /device:TPU:0, one launch (start us, length us, event | category | flops | bytes accessed | tf_op | source)
XLA Modules:
  0.0 927.9 jit_solution(4018668899986248244)
XLA Ops:
  8.0 2.5 copy.54
  11.9 4.9 collective-permute-start
  16.8 12.3 %all-gather = bf16[4,1,512]{2,1,0:T(2,128)(2,1)S(1)} all-gather(bf16[1,1,512]{2,1,0:T(2,128)(2,1)S(1)} %reshape.266), channel_id=1, replica_groups=mesh['dp'=4,'seq'=2,'tensor'=4] {'tensor'}, dimensions={0}, use_global_device_ids=true | all-gather | bytes 5120 | tf_op jit(solution)/shard_map/all_gather | solution.py:326
  29.1 16.2 %all-gather.1 = bf16[8,20,1024]{2,1,0:T(8,128)(2,1)S(1)} all-gather(bf16[1,20,1024]{2,1,0:T(8,128)(2,1)S(1)} %bitcast.135), channel_id=1, replica_groups=mesh['dp'=4,'seq'=2,'tensor'=4] {'dp','seq'}, dimensions={0}, use_global_device_ids=true | all-gather | bytes 368640 | tf_op jit(solution)/shard_map/all_gather | solution.py:317
  46.1 47.0 %all-gather.7.cloned.1.call-done = bf16[1024,2048]{1,0:T(8,128)(2,1)} async-done(((bf16[256,2048]{1,0:T(8,128)(2,1)}), bf16[1024,2048]{1,0:T(8,128)(2,1)}) %all-gather.7.cloned.1.call-update) | async-done | bytes 4194320 | tf_op jit(solution)/shard_map/all_gather | solution.py:325
  93.2 3.1 fusion
  96.3 52.3 %all-gather.9.cloned.1.call-done = bf16[2048,2,1024]{2,0,1:T(8,128)(2,1)} async-done(((bf16[256,2,1024]{2,0,1:T(8,128)(2,1)}), bf16[2048,2,1024]{2,0,1:T(8,128)(2,1)}) %all-gather.9.cloned.1.call-update) | async-done | bytes 8388624 | tf_op jit(solution)/shard_map/all_gather | solution.py:316
  148.6 12.6 %fusion.14 = f32[1024,2,1024]{2,0,1:T(8,128)S(1)} fusion(bf16[2048,2,1024]{2,0,1:T(8,128)(2,1)} %all-gather.9.cloned.1.call-done, bf16[1024,2048]{1,0:T(8,128)(2,1)} %all-gather.7.cloned.1.call-done, f32[2048]{0:T(1024)S(1)} %bitcast.119, f32[1024]{0:T(1024)S(1)} %add_rsqrt_fusion), kind=kOutput, calls=%fused_computation.49 | convolution fusion | flops 8598323200 | bytes 20983808 | tf_op jit(solution)/shard_map/td,dke->tke/dot_general | solution.py:332
  161.2 3.0 collective-permute-start.1
  165.7 5.3 multiply_convert_fusion.2
  173.4 18.0 %all_gather.28 = bf16[128,1024]{1,0:T(8,128)(2,1)S(1)} all-gather(bf16[16,1024]{1,0:T(8,128)(2,1)S(1)} %copy-done.37), channel_id=1, replica_groups=mesh['dp'=4,'seq'=2,'tensor'=4] {'dp','seq'}, dimensions={0}, use_global_device_ids=true | all-gather | bytes 294912 | tf_op jit(solution)/shard_map/all_gather | solution.py:318
  193.5 21.1 %all-reduce.11.cloned.1.call-done = f32[1024,160]{0,1:T(8,128)} async-done(((f32[1024,160]{0,1:T(8,128)}), f32[1024,160]{0,1:T(8,128)}) %all-reduce.11.cloned.1.call-update) | async-done | bytes 655376 | tf_op jit(solution)/shard_map/psum | solution.py:356
  224.0 8.6 fusion.61
  232.7 24.3 %scan_forward.1 = (f32[1024,1024]{1,0:T(8,128)S(1)}, f32[8,16,1024]{2,1,0:T(8,128)S(1)}, f32[16,1024]{1,0:T(8,128)S(1)}) custom-call(f32[1024,1024]{1,0:T(8,128)} %get-tuple-element.121.stepd_ref, f32[1024,1024]{1,0:T(8,128)} %get-tuple-element.130.u_ref, f32[64,16,32]{2,1,0:T(8,128)S(1)} %pad_maximum_fusion.6.bc_ref, ...), custom_call_target="tpu_custom_call" | custom-call | tf_op jit(solution)/shard_map/scan_forward/pallas_call | solution.py:57
  259.1 3.4 collective-permute-start.2
  264.3 12.9 %scan_correct.1 = (f32[1024,1024]{1,0:T(8,128)S(1)}, f32[8,16,1024]{2,1,0:T(8,128)S(1)}) custom-call(s32[8]{0:T(128)S(1)} %compare_convert_fusion.2.alive_ref, f32[1024,1024]{1,0:T(8,128)} %copy-done.1, f32[1024,1024]{1,0:T(8,128)} %get-tuple-element.121.stepd_ref, bf16[1024,256]{1,0:T(8,128)(2,1)S(1)} %get-tuple-element.144.cdiag_ref, ...), custom_call_target="tpu_custom_call" | custom-call | tf_op jit(solution)/shard_map/scan_correct/pallas_call | solution.py:211
  279.2 4.9 multiply_convert_fusion.1
  284.1 9.3 %convolution_convert_fusion.2 = bf16[1024,2048]{1,0:T(8,128)(2,1)} fusion(bf16[1024,1024]{1,0:T(8,128)(2,1)} %multiply_convert_fusion.1, bf16[1024,2048]{1,0:T(8,128)(2,1)} %all-gather.11.cloned.1.call-done), kind=kOutput, calls=%fused_computation.42 | convolution fusion | flops 4297064448 | bytes 10485760 | tf_op jit(solution)/shard_map/dot_general | solution.py:382
  297.6 18.8 %all-reduce.4 = bf16[16]{0:T(256)(128)(2,1)S(1)} all-reduce(bf16[16]{0:T(256)(128)(2,1)S(1)} %dynamic-update-slice.4), channel_id=1, replica_groups=mesh['dp'=4,'seq'=2,'tensor'=4] {'dp','seq'}, use_global_device_ids=true, to_apply=%add.4 | all-reduce | flops 16 | bytes 64
  318.6 56.4 %reduce-scatter.6.cloned.1.call-done = bf16[256,2048]{1,0:T(8,128)(2,1)} async-done(((bf16[1024,2048]{1,0:T(8,128)(2,1)}), bf16[256,2048]{1,0:T(8,128)(2,1)}) %reduce-scatter.6.cloned.1.call-update) | async-done | bytes 1048592 | tf_op jit(solution)/shard_map/reduce_scatter | solution.py:381
  375.0 3.1 fusion.25
  378.4 81.2 %all-gather.13.cloned.1.call-done = bf16[1024,2048]{1,0:T(8,128)(2,1)} async-done(((bf16[256,2048]{1,0:T(8,128)(2,1)}), bf16[1024,2048]{1,0:T(8,128)(2,1)}) %all-gather.13.cloned.1.call-update) | async-done | bytes 4194320 | tf_op jit(solution)/shard_map/all_gather | solution.py:396
  459.6 16.1 %fusion.8 = (f32[1024]{0:T(1024)}, f32[1024,1024]{1,0:T(8,128)}, bf16[1024,1,1024]{2,0,1:T(8,128)(2,1)}) fusion(bf16[1024,1024]{1,0:T(8,128)(2,1)} %copy-done.4, f32[1024,2,1024]{2,0,1:T(8,128)} %copy-done.11, f32[1024,1024]{1,0:T(8,128)} %copy-done.2, f32[1024]{0:T(1024)S(1)} %copy-done.48, bf16[1024,2048]{1,0:T(8,128)(2,1)} %all-gather.13.cloned.1.call-done, ...), kind=kOutput, calls=%fused_computation.19 | convolution fusion | flops 4312792064 | bytes 25174016 | tf_op jit(solution)/shard_map/tw,ew->te/dot_general | solution.py:397
  475.7 10.7 %scan_entry.1 = f32[16,1024]{1,0:T(8,128)S(1)} custom-call(s32[8]{0:T(128)S(1)} %compare_convert_fusion.2.alive_ref, f32[1024,1024]{1,0:T(8,128)S(1)} %copy-done, f32[1024,1024]{1,0:T(8,128)} %get-tuple-element.115.ds_ref, f32[64,16,32]{2,1,0:T(8,128)S(1)} %pad_maximum_fusion.6.bc_ref, f32[16,1024]{1,0:T(8,128)S(1)} %fusion.38.rate_ref), custom_call_target="tpu_custom_call" | custom-call | tf_op jit(solution)/shard_map/scan_entry/pallas_call | solution.py:256
  487.8 6.5 collective-permute-done.3.gin_ref
  494.4 77.3 %scan_backward.1 = (f32[1024,1024]{1,0:T(8,128)S(1)}, f32[1024,1024]{1,0:T(8,128)}, f32[1,64,256]{2,1,0:T(8,128)S(1)}, f32[1,64,256]{2,1,0:T(8,128)S(1)}, f32[16,1024]{1,0:T(8,128)S(1)}) custom-call(f32[1024,1024]{1,0:T(8,128)} %get-tuple-element.121.stepd_ref, f32[1024,1024]{1,0:T(8,128)} %get-tuple-element.130.u_ref, ...), custom_call_target="tpu_custom_call" | custom-call | tf_op jit(solution)/shard_map/scan_backward/pallas_call | solution.py:141
  571.7 5.4 fusion.59
  581.9 31.8 %all-reduce.14 = bf16[1024,160]{0,1:T(8,128)(2,1)S(1)} all-reduce(f32[1024,160]{0,1:T(8,128)S(1)} %pad_maximum_fusion.5), channel_id=1, replica_groups=mesh['dp'=4,'seq'=2,'tensor'=4] {'tensor'}, use_global_device_ids=true, to_apply=%region_9.10 | all-reduce | flops 163840 | bytes 983040 | tf_op jit(solution)/shard_map/psum | solution.py:420
  613.7 2.1 fusion.68
  615.9 2.0 fusion.26
  620.2 9.7 %convolution_convert_fusion.1 = bf16[2048,1024]{1,0:T(8,128)(2,1)} fusion(bf16[1024,2048]{1,0:T(8,128)(2,1)} %all-gather.13.cloned.1.call-done, bf16[1024,1024]{1,0:T(8,128)(2,1)} %multiply_convert_fusion.1), kind=kOutput, calls=%fused_computation.41 | convolution fusion | flops 4297064448 | bytes 10485760 | tf_op jit(solution)/shard_map/te,tw->we/dot_general | solution.py:399
  631.3 16.4 %fusion.57 = (f32[1024]{0:T(1024)S(1)}, f32[1024]{0:T(1024)S(1)}, f32[1024]{0:T(1024)S(1)}, f32[1024]{0:T(1024)S(1)}, f32[1024]{0:T(1024)S(1)}, /*index=5*/f32[1024,1024]{1,0:T(8,128)S(1)}) fusion(f32[1024]{0:T(1024)S(1)} %copy-done.21, f32[1024,2,1024]{2,0,1:T(8,128)} %copy-done.11, f32[1024]{0:T(1024)S(1)} %copy-done.34, f32[1024,1024]{1,0:T(8,128)} %copy-done.9, ...), kind=kOutput, calls=%fused_computation.153 | convolution fusion | flops 372239360 | bytes 30072832 | tf_op jit(solution)/shard_map/tj,ej->te/dot_general | solution.py:425
  647.6 3.9 multiply_multiply_fusion.1
  653.2 4.3 fusion.87
  657.5 3.1 multiply_add_fusion
  662.0 2.6 convert.15
  665.9 13.9 %bitcast_convert_fusion = bf16[1024,2048]{1,0:T(8,128)(2,1)} fusion(bf16[2048,2,1024]{2,0,1:T(8,128)(2,1)} %all-gather.9.cloned.1.call-done, bf16[1024,1,1024]{2,0,1:T(8,128)(2,1)} %get-tuple-element.126, bf16[1024,1,1024]{2,0,1:T(8,128)(2,1)S(1)} %convert.15), kind=kOutput, calls=%fused_computation.6 | convolution fusion | flops 8594128896 | bytes 16777216 | tf_op jit(solution)/shard_map/tke,dke->td/dot_general | solution.py:463
  680.5 14.5 %convolution_convert_fusion = bf16[2048,2,1024]{2,0,1:T(8,128)(2,1)} fusion(bf16[1024,1,1024]{2,0,1:T(8,128)(2,1)} %get-tuple-element.126, bf16[1024,1,1024]{2,0,1:T(8,128)(2,1)} %copy-done.14, bf16[1024,2048]{1,0:T(8,128)(2,1)} %all-gather.7.cloned.1.call-done, f32[2048]{0:T(1024)S(1)} %bitcast.120, f32[1024]{0:T(1024)S(1)} %copy-done.47), kind=kOutput, calls=%fused_computation.13 | convolution fusion | flops 8610906112 | bytes 16789504 | tf_op jit(solution)/shard_map/td,tke->dke/dot_general | solution.py:462
  700.6 7.7 reduce-scatter.14.cloned.1.call-done
  708.3 2.1 convert_bitcast_fusion
  710.4 2.5 copy.63
  712.9 74.4 %reduce-scatter.8.cloned.1.call-done = bf16[256,2048]{1,0:T(8,128)(2,1)} async-done(((bf16[1024,2048]{1,0:T(8,128)(2,1)}), bf16[256,2048]{1,0:T(8,128)(2,1)}) %reduce-scatter.8.cloned.1.call-update) | async-done | bytes 1048592 | tf_op jit(solution)/shard_map/reduce_scatter | solution.py:465
  789.3 4.3 fusion.17
  793.6 11.0 %all-reduce.5 = f32[2048]{0:T(1024)S(1)} all-reduce(f32[2048]{0:T(1024)S(1)} %get-tuple-element.105), channel_id=4, replica_groups=mesh['dp'=4,'seq'=2,'tensor'=4] {'tensor'}, use_global_device_ids=true, to_apply=%region_13.14.clone | all-reduce | flops 2048 | bytes 16384
  804.8 25.2 %all-reduce.6 = (f32[512]{0:T(512)}, f32[4,1024]{1,0:T(4,128)}, f32[1024]{0:T(1024)}, f32[1024]{0:T(1024)}, f32[1024]{0:T(1024)}) all-reduce(f32[512]{0:T(512)S(1)} %dynamic-slice.14, f32[4,1024]{1,0:T(4,128)S(1)} %pad_maximum_fusion.8, f32[1024]{0:T(1024)S(1)} %get-tuple-element.100, ...), channel_id=1, replica_groups=mesh['dp'=4,'seq'=2,'tensor'=4] {'dp','seq'}, use_global_device_ids=true, to_apply=%region_14.15 | all-reduce | flops 7680 | bytes 61440 | tf_op jit(solution)/shard_map/psum | solution.py:488
  829.9 33.3 %reduce-scatter.10.cloned.1.call-done = bf16[256,2,1024]{2,0,1:T(8,128)(2,1)} async-done(((bf16[2048,2,1024]{2,0,1:T(8,128)(2,1)}), bf16[256,2,1024]{2,0,1:T(8,128)(2,1)}) %reduce-scatter.10.cloned.1.call-update) | async-done | bytes 1048592 | tf_op jit(solution)/shard_map/reduce_scatter | solution.py:486
  863.2 3.6 copy.62
  866.9 52.5 %all-reduce.13.cloned.1.call-done = f32[16,1024]{1,0:T(8,128)} async-done(((f32[16,1024]{1,0:T(8,128)}), f32[16,1024]{1,0:T(8,128)}) %all-reduce.13.cloned.1.call-update) | async-done | bytes 65552 | tf_op jit(solution)/shard_map/psum | solution.py:488
  (221 shorter events, 49.2 us)
Async XLA Ops:
  7.2 21.9 %copy-start.30 = (bf16[1024,20]{0,1:T(8,128)(2,1)S(1)}, bf16[1024,20]{0,1:T(8,128)(2,1)}, u32[]{:S(2)}) copy-start(bf16[1024,20]{0,1:T(8,128)(2,1)} %param.22) | copy-start | bytes 122884
  7.2 38.2 %copy-start.19 = (bf16[4,1024]{1,0:T(4,128)(2,1)S(1)}, bf16[4,1024]{1,0:T(4,128)(2,1)}, u32[]{:S(2)}) copy-start(bf16[4,1024]{1,0:T(4,128)(2,1)} %param.20) | copy-start | bytes 24580
  7.2 86.0 %all-gather.7.cloned.1.call-start = ((), (), s32[]{:S(2)}) async-start(), calls=%async_computation.5 | async-start | bytes 5242880 | tf_op jit(solution)/shard_map/all_gather | solution.py:325
  8.0 140.6 %all-gather.9.cloned.1.call-start = ((), (), s32[]{:S(2)}) async-start(), calls=%async_computation.6 | async-start | bytes 9437184 | tf_op jit(solution)/shard_map/all_gather | solution.py:316
  10.5 204.1 %all-reduce.11.cloned.1.call-start = ((), (), s32[]{:S(2)}) async-start(), calls=%async_computation.7 | async-start | bytes 1310720 | tf_op jit(solution)/shard_map/psum | solution.py:356
  11.9 33.6 %collective-permute-start = (f32[3]{0:T(128)S(1)}, f32[3]{0:T(128)S(1)}, u32[]{:S(2)}, u32[]{:S(2)}) collective-permute-start(f32[3]{0:T(128)S(1)} %slice.173), channel_id=1, source_target_pairs={{0,4},{1,5},{2,6},{3,7},{8,12},{9,13},{10,14},{11,15},{16,20},{17,... | collective-permute-start | bytes 44 | tf_op jit(solution)/shard_map/ppermute | solution.py:19
  45.4 125.7 %copy-start.15 = (bf16[160,1024]{1,0:T(8,128)(2,1)}, bf16[160,1024]{1,0:T(8,128)(2,1)S(1)}, u32[]{:S(2)}) copy-start(bf16[160,1024]{1,0:T(8,128)(2,1)S(1)} %reshape.269) | copy-start | bytes 983044
  45.4 120.3 %copy-start.20 = (f32[1024]{0:T(1024)}, f32[1024]{0:T(1024)S(1)}, u32[]{:S(2)}) copy-start(f32[1024]{0:T(1024)S(1)} %compare_convert_fusion) | copy-start | bytes 12292
  45.4 120.3 %copy-start.22 = (f32[1,1024]{1,0:T(1,128)}, f32[1,1024]{1,0:T(1,128)S(1)}, u32[]{:S(2)}) copy-start(f32[1,1024]{1,0:T(1,128)S(1)} %get-tuple-element.139) | copy-start | bytes 12292
  45.4 120.2 %copy-start.24 = (f32[1,1024]{1,0:T(1,128)}, f32[1,1024]{1,0:T(1,128)S(1)}, u32[]{:S(2)}) copy-start(f32[1,1024]{1,0:T(1,128)S(1)} %get-tuple-element.140) | copy-start | bytes 12292
  45.4 120.2 %copy-start.26 = (f32[1,1024]{1,0:T(1,128)}, f32[1,1024]{1,0:T(1,128)S(1)}, u32[]{:S(2)}) copy-start(f32[1,1024]{1,0:T(1,128)S(1)} %get-tuple-element.141) | copy-start | bytes 12292
  45.5 120.2 %copy-start.28 = (f32[1,1024]{1,0:T(1,128)}, f32[1,1024]{1,0:T(1,128)S(1)}, u32[]{:S(2)}) copy-start(f32[1,1024]{1,0:T(1,128)S(1)} %get-tuple-element.142) | copy-start | bytes 12292
  46.1 119.6 %copy-start.31 = (f32[1024]{0:T(1024)}, f32[1024]{0:T(1024)S(1)}, u32[]{:S(2)}) copy-start(f32[1024]{0:T(1024)S(1)} %get-tuple-element.145) | copy-start | bytes 12292
  46.1 119.6 %copy-start.33 = (f32[1024]{0:T(1024)}, f32[1024]{0:T(1024)S(1)}, u32[]{:S(2)}) copy-start(f32[1024]{0:T(1024)S(1)} %get-tuple-element.146) | copy-start | bytes 12292
  46.1 119.6 %copy-start.35 = (f32[1024]{0:T(1024)}, f32[1024]{0:T(1024)S(1)}, u32[]{:S(2)}) copy-start(f32[1024]{0:T(1024)S(1)} %get-tuple-element.149) | copy-start | bytes 12292
  96.3 64.9 %copy-start.46 = (f32[1024]{0:T(1024)}, f32[1024]{0:T(1024)S(1)}, u32[]{:S(2)}) copy-start(f32[1024]{0:T(1024)S(1)} %add_rsqrt_fusion) | copy-start | bytes 12292
  161.2 4.5 collective-permute-start.1
  171.0 53.0 %copy-start.4 = (bf16[1024,1024]{1,0:T(8,128)(2,1)}, bf16[1024,1024]{1,0:T(8,128)(2,1)S(1)}, u32[]{:S(2)}) copy-start(bf16[1024,1024]{1,0:T(8,128)(2,1)S(1)} %get-tuple-element.122) | copy-start | bytes 6291460
  171.0 21.6 %copy-start.17 = (f32[16,1024]{1,0:T(8,128)S(1)}, f32[16,1024]{1,0:T(8,128)}, u32[]{:S(2)}) copy-start(f32[16,1024]{1,0:T(8,128)} %param.25) | copy-start | bytes 196612
  172.7 111.4 %all-gather.11.cloned.1.call-start = ((), (), s32[]{:S(2)}) async-start(), calls=%async_computation.8 | async-start | bytes 4718592 | tf_op jit(solution)/shard_map/all_gather | solution.py:319
  173.3 201.7 %reduce-scatter.6.cloned.1.call-start = ((), (), s32[]{:S(2)}) async-start(), calls=%async_computation.9 | async-start | bytes 5242880 | tf_op jit(solution)/shard_map/reduce_scatter | solution.py:381
  232.7 26.4 %copy-start.18 = (f32[16,1024]{1,0:T(8,128)S(1)}, f32[16,1024]{1,0:T(8,128)}, u32[]{:S(2)}) copy-start(f32[16,1024]{1,0:T(8,128)} %param.25) | copy-start | bytes 196612
  232.7 29.8 %copy-start.58 = (s32[8]{0:T(128)S(1)}, s32[8]{0:T(128)}, u32[]{:S(2)}) copy-start(s32[8]{0:T(128)} %copy-done.57) | copy-start | bytes 100
  232.7 29.8 %copy-start.59 = (s32[8,1]{0,1:T(1,128)S(1)}, s32[8,1]{0,1:T(1,128)}, u32[]{:S(2)}) copy-start(s32[8,1]{0,1:T(1,128)} %reduce-window.9) | copy-start | bytes 100
  259.1 5.3 collective-permute-start.2
  293.4 23.0 %copy-start.52 = (pred[1024]{0:T(1024)(128)(4,1)S(1)}, pred[1024]{0:T(1024)(128)(4,1)}, u32[]{:S(2)}) copy-start(pred[1024]{0:T(1024)(128)(4,1)} %get-tuple-element.119) | copy-start | bytes 3076
  293.4 81.6 %copy-start.8 = (bf16[256,2048]{1,0:T(8,128)(2,1)S(1)}, bf16[256,2048]{1,0:T(8,128)(2,1)}, u32[]{:S(2)}) copy-start(bf16[256,2048]{1,0:T(8,128)(2,1)} %param.15) | copy-start | bytes 3145732
  293.5 166.1 %all-gather.13.cloned.1.call-start = ((), (), s32[]{:S(2)}) async-start(), calls=%async_computation.10 | async-start | bytes 5242880 | tf_op jit(solution)/shard_map/all_gather | solution.py:396
  318.6 157.1 %copy-start.44 = (f32[256]{0:T(256)}, f32[256]{0:T(256)S(1)}, u32[]{:S(2)}) copy-start(f32[256]{0:T(256)S(1)} %dynamic-slice_multiply_fusion) | copy-start | bytes 3076
  378.2 319.5 %reduce-scatter.12.cloned.1.call-start = ((), (), s32[]{:S(2)}) async-start(), calls=%async_computation.13 | async-start | bytes 1474560 | tf_op jit(solution)/shard_map/reduce_scatter | solution.py:478
  459.6 16.1 %copy-start = (f32[1024,1024]{1,0:T(8,128)S(1)}, f32[1024,1024]{1,0:T(8,128)}, u32[]{:S(2)}) copy-start(f32[1024,1024]{1,0:T(8,128)} %get-tuple-element.121.stepd_ref) | copy-start | bytes 12582916
  486.5 7.9 collective-permute-start.3
  494.4 77.3 %copy-start.6 = (bf16[1024,1024]{1,0:T(8,128)(2,1)S(1)}, bf16[1024,1024]{1,0:T(8,128)(2,1)}, u32[]{:S(2)}) copy-start(bf16[1024,1024]{1,0:T(8,128)(2,1)} %copy-done.4) | copy-start | bytes 6291460
  494.4 77.3 %copy-start.10 = (f32[1024,1024]{1,0:T(8,128)S(1)}, f32[1024,1024]{1,0:T(8,128)}, u32[]{:S(2)}) copy-start(f32[1024,1024]{1,0:T(8,128)} %get-tuple-element.156) | copy-start | bytes 12582916
  494.4 77.3 %copy-start.41 = (f32[1024]{0:T(1024)S(1)}, f32[1024]{0:T(1024)}, u32[]{:S(2)}) copy-start(f32[1024]{0:T(1024)} %param.24) | copy-start | bytes 12292
  580.4 35.5 %copy-start.13 = (f32[1024,160]{0,1:T(8,128)S(1)}, f32[1024,160]{0,1:T(8,128)}, u32[]{:S(2)}) copy-start(f32[1024,160]{0,1:T(8,128)} %all-reduce.11.cloned.1.call-done) | copy-start | bytes 1966084
  619.2 89.1 %reduce-scatter.14.cloned.1.call-start = ((), (), s32[]{:S(2)}) async-start(), calls=%async_computation.15 | async-start | bytes 4718592 | tf_op jit(solution)/shard_map/reduce_scatter | solution.py:487
  629.9 157.5 %reduce-scatter.8.cloned.1.call-start = ((), (), s32[]{:S(2)}) async-start(), calls=%async_computation.11 | async-start | bytes 5242880 | tf_op jit(solution)/shard_map/reduce_scatter | solution.py:465
  631.2 21.9 %copy-start.23 = (f32[1,1024]{1,0:T(1,128)S(1)}, f32[1,1024]{1,0:T(1,128)}, u32[]{:S(2)}) copy-start(f32[1,1024]{1,0:T(1,128)} %copy-done.22) | copy-start | bytes 12292
  631.2 21.9 %copy-start.25 = (f32[1,1024]{1,0:T(1,128)S(1)}, f32[1,1024]{1,0:T(1,128)}, u32[]{:S(2)}) copy-start(f32[1,1024]{1,0:T(1,128)} %copy-done.24) | copy-start | bytes 12292
  631.2 21.9 %copy-start.27 = (f32[1,1024]{1,0:T(1,128)S(1)}, f32[1,1024]{1,0:T(1,128)}, u32[]{:S(2)}) copy-start(f32[1,1024]{1,0:T(1,128)} %copy-done.26) | copy-start | bytes 12292
  631.2 21.9 %copy-start.29 = (f32[1,1024]{1,0:T(1,128)S(1)}, f32[1,1024]{1,0:T(1,128)}, u32[]{:S(2)}) copy-start(f32[1,1024]{1,0:T(1,128)} %copy-done.28) | copy-start | bytes 12292
  651.6 9.0 collective-permute-start.4
  679.9 183.4 %reduce-scatter.10.cloned.1.call-start = ((), (), s32[]{:S(2)}) async-start(), calls=%async_computation.12 | async-start | bytes 9437184 | tf_op jit(solution)/shard_map/reduce_scatter | solution.py:486
  695.0 94.3 %copy-start.12 = (bf16[256,2048]{1,0:T(8,128)(2,1)S(1)}, bf16[256,2048]{1,0:T(8,128)(2,1)}, u32[]{:S(2)}) copy-start(bf16[256,2048]{1,0:T(8,128)(2,1)} %param.16) | copy-start | bytes 3145732
  695.0 94.3 %copy-start.45 = (f32[256]{0:T(256)S(1)}, f32[256]{0:T(256)}, u32[]{:S(2)}) copy-start(f32[256]{0:T(256)} %copy-done.44) | copy-start | bytes 3076
  695.0 224.4 %all-reduce.13.cloned.1.call-start = ((), (), s32[]{:S(2)}) async-start(), calls=%async_computation.14 | async-start | bytes 131072 | tf_op jit(solution)/shard_map/psum | solution.py:488
  789.3 15.5 %copy-start.51 = (f32[1024]{0:T(1024)S(1)}, f32[1024]{0:T(1024)}, u32[]{:S(2)}) copy-start(f32[1024]{0:T(1024)} %get-tuple-element.114) | copy-start | bytes 12292
  (28 other events, 129.7 us)
Sparse Core Ops, SparseCore 0:
  9.6 83.5 all-gather.6
  95.7 52.8 all-gather.8
  172.9 41.6 all-reduce.10
  216.3 36.9 all-gather.10
  293.6 81.4 reduce-scatter.5
  378.3 81.2 all-gather.12
  619.4 33.9 reduce-scatter.11
  657.1 51.1 reduce-scatter.13
  710.6 76.7 reduce-scatter.7
  791.1 72.1 reduce-scatter.9
  866.9 52.4 all-reduce.12

commit v2 on v1

--- a/solution.py
+++ b/solution.py
@@ -11,6 +11,7 @@
 LOG2E = 1.4426950408889634
 LN2 = 0.6931471805599453
 FAR = 1e30
+MESH = pl.DeviceIdType.MESH
 
 
 def passed_along(x, axis, by):
@@ -283,6 +284,250 @@
     tokens = values.shape[0]
     mine = jnp.arange(CH * N)[None] // N == jnp.arange(tokens)[:, None] % CH
     return jnp.where(mine, jnp.tile(values.astype(BF16), (1, CH)), 0)
+
+
+def mesh_copy(src, dst, send, recv, **where):
+    return pltpu.make_async_remote_copy(
+        src_ref=src, dst_ref=dst, send_sem=send, recv_sem=recv, device_id=where, device_id_type=MESH
+    )
+
+
+def place():
+    dp, seq, mine = lax.axis_index("dp"), lax.axis_index("seq"), lax.axis_index("tensor")
+    return dp, seq, mine
+
+
+def tail_kernel(n, dps, seqs, subs, lag, dx_ref, dz_ref, w_ref, nrm_ref, sm_ref, all_ref,
+                dn_ref, gin_ref, gs_ref, ga_ref,
+                zr, zl, part_r, part_l, one_send, one_recv, two_recv, sm_one, sm_two, all_one, all_two,
+                r_send, r_recv, l_send, l_recv, w1s, w1r, w2s, w2r, s1s, s1r, s2s, s2r, a1s, a1r, a2s, a2r):
+    dp, seq, t = place()
+    core, hi = dp % 2, dp // 2
+    chips = dps // 2 * seqs
+    chip = hi * seqs + seq
+    rows = dn_ref.shape[0]
+    part = rows // subs
+    wide = dn_ref.shape[1]
+    wrows = gin_ref.shape[1]
+    tile = 512
+
+    def owner(q, c):
+        return (q // seqs * 2 + c) * seqs + q % seqs
+
+    def to_chip(q):
+        return dict(dp=q // seqs * 2 + core, seq=q % seqs)
+
+    barrier = pltpu.get_barrier_semaphore()
+    pl.semaphore_signal(barrier, inc=1, device_id=dict(dp=hi * 2 + 1 - core), device_id_type=MESH)
+    for step in range(1, chips):
+        q = lax.rem(chip + step, chips)
+        pl.semaphore_signal(barrier, inc=1, device_id=to_chip(q), device_id_type=MESH)
+
+    for peer in (lax.rem(t + 1, n), lax.rem(t + n - 1, n)):
+        pl.semaphore_signal(barrier, inc=1, device_id=dict(tensor=peer), device_id_type=MESH)
+    pl.semaphore_wait(barrier, chips + 2)
+
+    partner = dict(dp=hi * 2 + 1 - core)
+    right, left = dict(tensor=lax.rem(t + 1, n)), dict(tensor=lax.rem(t + n - 1, n))
+
+    def r_copy(i):
+        return mesh_copy(zr.at[i], zr.at[i], r_send.at[i], r_recv.at[i], **right)
+
+    def l_copy(i):
+        return mesh_copy(zl.at[i], zl.at[i], l_send.at[i], l_recv.at[i], **left)
+
+    def w1_copy(q):
+        return mesh_copy(one_send.at[q], one_recv.at[q], w1s.at[q], w1r.at[q], **partner)
+
+    def w2_copy(q, slot):
+        return mesh_copy(one_recv.at[q], two_recv.at[slot], w2s.at[q], w2r.at[slot], **to_chip(q))
+
+    def s1_copy(q):
+        return mesh_copy(sm_ref.at[owner(q, 1 - core)], sm_one.at[q], s1s.at[q], s1r.at[q], **partner)
+
+    def s2_copy(q, slot):
+        return mesh_copy(sm_one.at[q], sm_two.at[slot], s2s.at[q], s2r.at[slot], **to_chip(q))
+
+    def a1_copy():
+        return mesh_copy(all_ref, all_one, a1s, a1r, **partner)
+
+    def a2_copy(q, slot):
+        return mesh_copy(all_one, all_two.at[slot], a2s.at[q], a2r.at[slot], **to_chip(q))
+
+    def partial_rows(o, dst):
+        here = pl.ds(pl.multiple_of(o * rows, rows), rows)
+
+        @pl.loop(0, wide // tile)
+        def _(j):
+            cols = pl.ds(pl.multiple_of(j * tile, tile), tile)
+            nt = (((1,), (1,)), ((), ()))
+            dst[:, cols] = lax.dot_general(
+                dx_ref[here, :], w_ref[0, cols, :], nt, preferred_element_type=F32
+            ) + lax.dot_general(dz_ref[here, :], w_ref[1, cols, :], nt, preferred_element_type=F32)
+
+    def weight_rows(p, k):
+        cols = pl.ds(pl.multiple_of(p * wrows, wrows), wrows)
+        tn = (((0,), (0,)), ((), ()))
+        d_ref = dx_ref if k == 0 else dz_ref
+        return lax.dot_general(nrm_ref[:, cols], d_ref[...], tn, preferred_element_type=F32)
+
+    for q in range(chips):
+        s1_copy(q).start()
+    a1_copy().start()
+
+    def stream(i, limit, start, buf, copy, part_ref, owner_of):
+        @pl.when(jnp.logical_and(i >= 0, i < limit))
+        def _():
+            k, sub = i // subs, i % subs
+
+            @pl.when(sub == 0)
+            def _():
+                partial_rows(owner_of(k), part_ref)
+
+            here = part_ref[pl.ds(pl.multiple_of(sub * part, part), part), :]
+
+            @pl.when(start)
+            def _():
+                buf[i] = here.astype(BF16)
+
+            @pl.when(jnp.logical_not(start))
+            def _():
+                copy(i).wait_recv()
+                buf[i] = (here + buf[i].astype(F32)).astype(BF16)
+
+            copy(i).start()
+
+    def step(g, _):
+        stream(g - lag * t, (n - 1 - t) * subs, t == 0, zr, r_copy, part_r, lambda k: n - 1 - k)
+        stream(g - lag * (n - 1 - t), t * subs, t == n - 1, zl, l_copy, part_l, lambda k: k)
+
+        @pl.when(g < chips)
+        def _():
+            for k in range(2):
+                one_send[g, k] = weight_rows(owner(g, 1 - core), k).astype(BF16)
+            w1_copy(g).start()
+
+        @pl.when(jnp.logical_and(g >= chips, g < 2 * chips - 1))
+        def _():
+            q = lax.rem(chip + 1 + g - chips, chips)
+            w1_copy(q).wait_recv()
+            for k in range(2):
+                one_recv[q, k] = (weight_rows(owner(q, core), k) + one_recv[q, k].astype(F32)).astype(BF16)
+            w2_copy(q, chip).start()
+
+        @pl.when(g == 2 * chips - 1)
+        def _():
+            for q in range(chips):
+                s1_copy(q).wait_recv()
+                sm_one[q] = sm_one[q] + sm_ref[owner(q, core)]
+            a1_copy().wait_recv()
+            all_one[...] = all_one[...] + all_ref[...]
+            for ahead in range(1, chips):
+                q = lax.rem(chip + ahead, chips)
+                s2_copy(q, chip).start()
+                a2_copy(q, chip).start()
+            w1_copy(chip).wait_recv()
+            for k in range(2):
+                gin_ref[k] = weight_rows(owner(chip, core), k) + one_recv[chip, k].astype(F32)
+
+        @pl.when(g == 2 * chips)
+        def _():
+            partial_rows(t, dn_ref)
+
+        return 0
+
+    steps = max((n - 1) * max(subs, lag), 2 * chips + 1)
+    lax.fori_loop(0, steps, step, 0)
+
+    @pl.loop(0, subs)
+    def _(s):
+        here = pl.ds(pl.multiple_of(s * part, part), part)
+
+        @pl.when(t > 0)
+        def _():
+            i = (n - 1 - t) * subs + s
+            r_copy(i).wait_recv()
+            dn_ref[here, :] = dn_ref[here, :] + zr[i].astype(F32)
+
+        @pl.when(t < n - 1)
+        def _():
+            i = t * subs + s
+            l_copy(i).wait_recv()
+            dn_ref[here, :] = dn_ref[here, :] + zl[i].astype(F32)
+
+    gs_ref[...] = sm_one[chip]
+    ga_ref[...] = all_one[...]
+    for ahead in range(1, chips):
+        q = lax.rem(chip + ahead, chips)
+        s2_copy(q, q).wait_recv()
+        gs_ref[...] = gs_ref[...] + sm_two[q]
+        a2_copy(q, q).wait_recv()
+        ga_ref[...] = ga_ref[...] + all_two[q]
+        w2_copy(q, q).wait_recv()
+        gin_ref[...] = gin_ref[...] + two_recv[q].astype(F32)
+
+    for q in range(chips):
+        s1_copy(q).wait_send()
+        w1_copy(q).wait_send()
+    a1_copy().wait_send()
+    for ahead in range(1, chips):
+        q = lax.rem(chip + ahead, chips)
+        s2_copy(q, chip).wait_send()
+        a2_copy(q, chip).wait_send()
+        w2_copy(q, chip).wait_send()
+
+    @pl.loop(0, (n - 1) * subs)
+    def _(i):
+        @pl.when(i < (n - 1 - t) * subs)
+        def _():
+            r_copy(i).wait_send()
+
+        @pl.when(i < t * subs)
+        def _():
+            l_copy(i).wait_send()
+
+
+def tail(dx, dz, w_full, normed, small, whole):
+    n, dps, seqs = (lax.axis_size(axis) for axis in ("tensor", "dp", "seq"))
+    chips = dps // 2 * seqs
+    rows = dx.shape[0] // n
+    wide, lanes = w_full.shape[1], w_full.shape[2]
+    wrows = wide // (dps * seqs)
+    subs = max(1, rows // 64)
+    hops = (n - 1) * subs
+    vmem = pl.BlockSpec(memory_space=pltpu.VMEM)
+    dma = pltpu.SemaphoreType.DMA
+    few = dma((chips,))
+    return pl.pallas_call(
+        functools.partial(tail_kernel, n, dps, seqs, subs, 2),
+        out_shape=[
+            jax.ShapeDtypeStruct((rows, wide), F32),
+            jax.ShapeDtypeStruct((2, wrows, lanes), F32),
+            jax.ShapeDtypeStruct(small.shape[1:], F32),
+            jax.ShapeDtypeStruct(whole.shape, F32),
+        ],
+        in_specs=[vmem] * 6,
+        out_specs=[vmem] * 4,
+        scratch_shapes=[
+            pltpu.VMEM((hops, rows // subs, wide), BF16),
+            pltpu.VMEM((hops, rows // subs, wide), BF16),
+            pltpu.VMEM((rows, wide), F32),
+            pltpu.VMEM((rows, wide), F32),
+            pltpu.VMEM((chips, 2, wrows, lanes), BF16),
+            pltpu.VMEM((chips, 2, wrows, lanes), BF16),
+            pltpu.VMEM((chips, 2, wrows, lanes), BF16),
+            pltpu.VMEM((chips,) + small.shape[1:], F32),
+            pltpu.VMEM((chips,) + small.shape[1:], F32),
+            pltpu.VMEM(whole.shape, F32),
+            pltpu.VMEM((chips,) + whole.shape, F32),
+            dma((hops,)), dma((hops,)), dma((hops,)), dma((hops,)),
+            few, few, few, few, few, few, few, few, dma, dma, few, few,
+        ],
+        compiler_params=pltpu.CompilerParams(
+            collective_id=2, has_side_effects=True, vmem_limit_bytes=60 << 20
+        ),
+        name="tail_sums",
+    )(dx, dz, w_full, normed, small, whole)
 
 
 def on_device(
@@ -313,7 +558,7 @@
         jnp.stack([count_here // 32, count_here % 32]).astype(jnp.float32).astype(jnp.bfloat16)
     )
     w_in, w_x, w_dt, w_out, count_pairs = (
-        lax.all_gather(input_projection_weight, ("dp", "seq"), axis=0, tiled=True),
+        lax.all_gather(jnp.swapaxes(input_projection_weight, 0, 1), ("dp", "seq"), axis=1, tiled=True),
         lax.all_gather(xproj_weight, ("dp", "seq"), axis=1, tiled=True),
         lax.all_gather(dtproj_weight, ("dp", "seq"), axis=0, tiled=True),
         lax.all_gather(output_projection_weight, ("dp", "seq"), axis=1, tiled=True),
@@ -329,11 +574,8 @@
     full_gain = full_gain_b.astype(jnp.float32)
     inv_rms = lax.rsqrt(jnp.mean(full_rows * full_rows, axis=1, keepdims=True) + EPS)
     normalized_rows = (full_rows * inv_rms * full_gain[None]).astype(jnp.bfloat16)
-    projected_input_gate = jnp.einsum(
-        "td,dke->tke", normalized_rows, w_in, preferred_element_type=jnp.float32
-    )
-    x_inner = projected_input_gate[:, 0]
-    z_gate = projected_input_gate[:, 1]
+    x_inner = jnp.dot(normalized_rows, w_in[0], preferred_element_type=F32)
+    z_gate = jnp.dot(normalized_rows, w_in[1], preferred_element_type=F32)
     seg_float = segment_ids.astype(jnp.float32)
     prev_x, prev_seg = passed_along(
         (x_inner[tok_rows - back_rows :], seg_float[tok_rows - back_rows :]), "seq", 1
@@ -458,11 +700,22 @@
     front_grad = jnp.stack(front_rows, 0)
     carried_grad = passed_along(front_grad, "seq", -1)
     d_x = d_x.at[tok_rows - back_rows :].add(carried_grad)
-    d_xz = jnp.stack([d_x, d_z], 1).astype(jnp.bfloat16)
-    d_win = jnp.einsum("td,tke->dke", normalized_rows, d_xz, preferred_element_type=jnp.float32)
-    d_norm_part = jnp.einsum("tke,dke->td", d_xz, w_in, preferred_element_type=jnp.float32)
+    parts = lax.axis_size(("dp", "seq"))
+    small = jnp.concatenate(
+        [
+            d_wx_rank.T.reshape(parts, -1, chan_lanes),
+            d_wx_state.T.reshape(parts, -1, chan_lanes),
+            d_wdt.reshape(parts, -1, chan_lanes),
+            jnp.zeros((parts, 4, chan_lanes), F32),
+        ],
+        1,
+    )
+    whole = jnp.concatenate(
+        [a_log_part, conv_weight_part, jnp.stack([conv_bias_part, dt_bias_part, d_skip_part, d_skip_part], 0)], 0
+    )
+    d_norm_share, g_in, g_small, g_whole = tail(d_x.astype(BF16), d_z.astype(BF16), w_in, normalized_rows, small, whole)
+    g_in = jnp.swapaxes(g_in, 0, 1)
     inv_share = lax.dynamic_slice_in_dim(inv_rms, row_start, row_share, 0)
-    d_norm_share = lax.psum_scatter(d_norm_part.astype(BF16), "tensor", scatter_dimension=0, tiled=True).astype(F32)
     gain_partial = jnp.sum(d_norm_share * share_rows * inv_share, axis=0)
     gain_part = lax.psum_scatter(gain_partial, "tensor", scatter_dimension=0, tiled=True)
     inner_sum = jnp.sum(d_norm_share * full_gain[None] * share_rows, axis=1, keepdims=True)
@@ -472,23 +725,15 @@
         + inv_share * full_gain[None] * d_norm_share
         - share_rows * inv_cube * inner_sum / model_width
     )
-    parts = lax.axis_size(("dp", "seq"))
-    rows_x = jnp.concatenate([d_wx_rank.T.reshape(parts, -1, chan_lanes), d_wx_state.T.reshape(parts, -1, chan_lanes)], 1)
-    rows_dt = d_wdt.reshape(parts, -1, chan_lanes)
-    g_small = lax.psum_scatter(
-        jnp.concatenate([rows_x, rows_dt], 1), ("dp", "seq"), scatter_dimension=0, tiled=True
-    )[0]
     rank_here = rank_width // parts
     state_here = 2 * state_width // parts
     g_x_rank = g_small[:rank_here].T
     g_x_state = g_small[rank_here : rank_here + state_here].T
-    g_dt = g_small[rank_here + state_here :]
-    g_in = lax.psum_scatter(d_win.astype(BF16), ("dp", "seq"), scatter_dimension=0, tiled=True).astype(F32)
+    g_dt = g_small[rank_here + state_here : rank_here + state_here + rank_here]
     g_out = lax.psum_scatter(d_wout.astype(BF16), ("dp", "seq"), scatter_dimension=0, tiled=True).astype(F32).T
-    g_gain, g_conv_w, g_conv_b, g_bias, g_alog, g_skip = lax.psum(
-        (gain_part, conv_weight_part, conv_bias_part, dt_bias_part, a_log_part, d_skip_part),
-        ("dp", "seq"),
-    )
+    g_gain = lax.psum(gain_part, ("dp", "seq"))
+    g_alog, g_conv_w = g_whole[:N], g_whole[N : N + conv_taps]
+    g_conv_b, g_bias, g_skip = g_whole[N + conv_taps], g_whole[N + conv_taps + 1], g_whole[N + conv_taps + 2]
     return (
         output,
         input_grad,

time: 936 us -> 802 us (0.86)
  waiting for transfers between devices: 437 us -> 256 us
  Pallas kernels: 125 us -> 211 us
  matrix products: 109 us -> 78.3 us
    reduce_scatter x3 -> x0, waiting for transfers between devices: 108 us -> none  [the longest x1 74.4 us: on_device(): lax.psum_scatter(d_norm_part.astype(BF16), 'tensor', scatter_dimension=0,...]
    pallas_call x0 -> x1, Pallas kernels: none -> 85.5 us  [tail(): pl.pallas_call(functools.partial(tail_kernel, n, dps, seqs, subs, 2), out...]
    psum x1 -> x0, waiting for transfers between devices: 52.5 us -> none  [on_device(): lax.psum((gain_part, conv_weight_part, conv_bias_part, dt_bias_part, a_lo...]
    dot_general x3 -> x2, matrix products: 41 us -> 16.7 us  [the longest x1 9.23 us: on_device(): z_gate = jnp.dot(normalized_rows, w_in[1], preferred_element_type=F32)]
    unnamed x2, blocking collectives: 29.8 us -> 43.3 us
    psum x1, blocking collectives: 25.2 us -> 12.9 us  [on_device(): g_gain = lax.psum(gain_part, ('dp', 'seq'))]
    unnamed x131 -> x124, local copies, waits for them, and re-layouts: 19.9 us -> 15.5 us
  transfers between devices with their start and end apart: 16 -> 12, of which waited for: 12 -> 8; matrix products, arithmetic and copies ran while one was open for 13% -> 15% of each run, Pallas kernels for 4% -> 25%
where the time goes in v2:
time: 802 us; the launch traced here: 797 us
  waiting for transfers between devices  256 us (32%)
  Pallas kernels  211 us (26%)
  blocking collectives  134 us (17%)
  matrix products  78.3 us (10%)
  other arithmetic  46.7 us (6%)
  local copies, waits for them, and re-layouts  34.8 us (4%)
  between operations  20.7 us (3%)
  starting transfers between devices  14.3 us (2%)
    pallas_call x1, Pallas kernels, tail(): pl.pallas_call(functools.partial(tail_kernel, n, dps, seqs, subs, 2), out...  85.5 us
    all_gather x1, waiting for transfers between devices, on_device(): piece = lax.all_gather(grad_low, 'tensor', axis=0, tiled=True)  77.9 us
    pallas_call x1, Pallas kernels, bwd(): pl.pallas_call(functools.partial(bwd_kernel, unroll=unroll), grid=grid, i...  77.3 us
    reduce_scatter x1, waiting for transfers between devices, on_device(): lax.psum_scatter(jnp.dot(gated_output_rows, w_out, preferred_element_type...  56.2 us
    all_gather x1, waiting for transfers between devices, on_device(): lax.all_gather(jnp.swapaxes(input_projection_weight, 0, 1), ('dp', 'seq')...  48.9 us
    all_gather x1, waiting for transfers between devices, on_device(): lax.all_gather(hidden_in, 'tensor', axis=0, tiled=True)  47.7 us
    unnamed x2, blocking collectives  43.3 us
    psum x1, blocking collectives, on_device(): lax.psum(jnp.concatenate([d_rank, d_b_part, d_c_part], 1), 'tensor')  31.8 us
  transfers between devices with their start and end apart: 12, of which 8 were waited for; matrix products, arithmetic and copies ran while one was open for 15% of the time, Pallas kernels for 25%

profile of v2, /device:TPU:0, one launch (start us, length us, event | category | flops | bytes accessed | tf_op | source)
XLA Modules:
  0.0 796.5 jit_solution(12732822627626786847)
XLA Ops:
  8.0 2.5 copy.63
  11.9 4.9 collective-permute-start
  16.8 12.3 %all-gather = bf16[4,1,512]{2,1,0:T(2,128)(2,1)S(1)} all-gather(bf16[1,1,512]{2,1,0:T(2,128)(2,1)S(1)} %reshape.260), channel_id=1, replica_groups=mesh['dp'=4,'seq'=2,'tensor'=4] {'tensor'}, dimensions={0}, use_global_device_ids=true | all-gather | bytes 5120 | tf_op jit(solution)/shard_map/all_gather | solution.py:571
  29.1 16.2 %all-gather.1 = bf16[8,20,1024]{2,1,0:T(8,128)(2,1)S(1)} all-gather(bf16[1,20,1024]{2,1,0:T(8,128)(2,1)S(1)} %bitcast.104), channel_id=1, replica_groups=mesh['dp'=4,'seq'=2,'tensor'=4] {'dp','seq'}, dimensions={0}, use_global_device_ids=true | all-gather | bytes 368640 | tf_op jit(solution)/shard_map/all_gather | solution.py:562
  45.5 47.7 %all-gather.7.cloned.1.call-done = bf16[1024,2048]{1,0:T(8,128)(2,1)} async-done(((bf16[256,2048]{1,0:T(8,128)(2,1)}), bf16[1024,2048]{1,0:T(8,128)(2,1)}) %all-gather.7.cloned.1.call-update) | async-done | bytes 4194320 | tf_op jit(solution)/shard_map/all_gather | solution.py:570
  93.2 3.2 fusion
  96.6 3.0 fusion.2.nrm_ref
  99.7 48.9 %all-gather.9.cloned.1.call-done.w_ref = bf16[2,2048,1024]{2,1,0:T(8,128)(2,1)} async-done(((bf16[2,256,1024]{2,1,0:T(8,128)(2,1)}), bf16[2,2048,1024]{2,1,0:T(8,128)(2,1)}) %all-gather.9.cloned.1.call-update) | async-done | bytes 8388624 | tf_op jit(solution)/shard_map/all_gather | solution.py:561
  148.6 7.5 fusion.10
  156.1 3.0 collective-permute-start.1
  160.6 5.2 multiply_convert_fusion.2
  165.8 1.7 fusion.61
  168.2 17.7 %all_gather.28 = bf16[128,1024]{1,0:T(8,128)(2,1)S(1)} all-gather(bf16[16,1024]{1,0:T(8,128)(2,1)S(1)} %copy-done.39), channel_id=1, replica_groups=mesh['dp'=4,'seq'=2,'tensor'=4] {'dp','seq'}, dimensions={0}, use_global_device_ids=true | all-gather | bytes 294912 | tf_op jit(solution)/shard_map/all_gather | solution.py:563
  187.9 21.4 %all-reduce.9.cloned.1.call-done = f32[1024,160]{0,1:T(8,128)} async-done(((f32[1024,160]{0,1:T(8,128)}), f32[1024,160]{0,1:T(8,128)}) %all-reduce.9.cloned.1.call-update) | async-done | bytes 655376 | tf_op jit(solution)/shard_map/psum | solution.py:598
  215.3 1.8 copy_bitcast_fusion.1
  217.3 1.5 compare_select_fusion.1
  218.8 8.7 %fusion.53 = (f32[1024]{0:T(1024)S(1)}, f32[1024,1024]{1,0:T(8,128)}, f32[1024,1024]{1,0:T(8,128)}, f32[1024,1024]{1,0:T(8,128)}) fusion(f32[1024]{0:T(1024)} %param.24, pred[1024]{0:T(1024)(128)(4,1)} %get-tuple-element.150, bf16[1024,1024]{1,0:T(8,128)(2,1)S(1)} %get-tuple-element.122, bf16[128,1024]{1,0:T(8,128)(2,1)S(1)} %all_gather.28, ...), kind=kOutput, calls=%fused_computation.142 | convolution fusion | flops 279968768 | bytes 15213568 | tf_op jit(solution)/shard_map/dot_general | solution.py:604
  227.6 24.3 %scan_forward.1 = (f32[1024,1024]{1,0:T(8,128)S(1)}, f32[8,16,1024]{2,1,0:T(8,128)S(1)}, f32[16,1024]{1,0:T(8,128)S(1)}) custom-call(f32[1024,1024]{1,0:T(8,128)} %get-tuple-element.121.stepd_ref, f32[1024,1024]{1,0:T(8,128)} %get-tuple-element.130.u_ref, f32[64,16,32]{2,1,0:T(8,128)S(1)} %pad_maximum_fusion.2.bc_ref, ...), custom_call_target="tpu_custom_call" | custom-call | tf_op jit(solution)/shard_map/scan_forward/pallas_call | solution.py:58
  251.9 2.0 copy-done.1
  253.9 3.4 collective-permute-start.2
  257.3 1.9 collective-permute-done.2.sin_ref
  259.2 13.0 %scan_correct.1 = (f32[1024,1024]{1,0:T(8,128)S(1)}, f32[8,16,1024]{2,1,0:T(8,128)S(1)}) custom-call(s32[8]{0:T(128)S(1)} %compare_convert_fusion.2.alive_ref, f32[1024,1024]{1,0:T(8,128)} %copy-done.1, f32[1024,1024]{1,0:T(8,128)} %get-tuple-element.121.stepd_ref, bf16[1024,256]{1,0:T(8,128)(2,1)S(1)} %get-tuple-element.147.cdiag_ref, ...), custom_call_target="tpu_custom_call" | custom-call | tf_op jit(solution)/shard_map/scan_correct/pallas_call | solution.py:212
  272.3 2.0 copy-done.3
  274.2 9.2 %multiply_convert_fusion.1 = (bf16[1024,1024]{1,0:T(8,128)(2,1)}, f32[1024,1024]{1,0:T(8,128)}) fusion(f32[1024,1024]{1,0:T(8,128)S(1)} %get-tuple-element.42, bf16[1024,1024]{1,0:T(8,128)(2,1)S(1)} %copy-done.5, f32[1024]{0:T(1024)S(1)} %copy-done.50, bf16[1024,2048]{1,0:T(8,128)(2,1)S(1)} %copy-done.9, ...), kind=kOutput, calls=%fused_computation.33 | convolution fusion | flops 4304404480 | bytes 20975616 | tf_op jit(solution)/shard_map/dot_general | solution.py:578
  283.5 9.3 %convolution_convert_fusion.1 = bf16[1024,2048]{1,0:T(8,128)(2,1)} fusion(bf16[1024,1024]{1,0:T(8,128)(2,1)} %get-tuple-element.160, bf16[1024,2048]{1,0:T(8,128)(2,1)} %all-gather.11.cloned.1.call-done), kind=kOutput, calls=%fused_computation.40 | convolution fusion | flops 4297064448 | bytes 10485760 | tf_op jit(solution)/shard_map/dot_general | solution.py:624
  297.3 21.0 %all-reduce.4 = bf16[16]{0:T(256)(128)(2,1)S(1)} all-reduce(bf16[16]{0:T(256)(128)(2,1)S(1)} %dynamic-update-slice.3), channel_id=1, replica_groups=mesh['dp'=4,'seq'=2,'tensor'=4] {'dp','seq'}, use_global_device_ids=true, to_apply=%add.4 | all-reduce | flops 16 | bytes 64
  320.4 56.2 %reduce-scatter.3.cloned.1.call-done = bf16[256,2048]{1,0:T(8,128)(2,1)} async-done(((bf16[1024,2048]{1,0:T(8,128)(2,1)}), bf16[256,2048]{1,0:T(8,128)(2,1)}) %reduce-scatter.3.cloned.1.call-update) | async-done | bytes 1048592 | tf_op jit(solution)/shard_map/reduce_scatter | solution.py:623
  376.6 3.1 fusion.21
  383.3 77.9 %all-gather.13.cloned.1.call-done = bf16[1024,2048]{1,0:T(8,128)(2,1)} async-done(((bf16[256,2048]{1,0:T(8,128)(2,1)}), bf16[1024,2048]{1,0:T(8,128)(2,1)}) %all-gather.13.cloned.1.call-update) | async-done | bytes 4194320 | tf_op jit(solution)/shard_map/all_gather | solution.py:638
  461.2 15.5 %fusion.8 = (f32[1024]{0:T(1024)S(1)}, f32[1024,1024]{1,0:T(8,128)}, bf16[1024,1024]{1,0:T(8,128)(2,1)}) fusion(bf16[1024,1024]{1,0:T(8,128)(2,1)} %copy-done.4, f32[1024,1024]{1,0:T(8,128)} %get-tuple-element.161, f32[1024,1024]{1,0:T(8,128)} %copy-done.3, f32[1024]{0:T(1024)S(1)} %copy-done.50, bf16[1024,2048]{1,0:T(8,128)(2,1)} %all-gather.13.cloned.1.call-done, ...), kind=kOutput, calls=%fused_computation.17 | convolution fusion | flops 4312792064 | bytes 25174016 | tf_op jit(solution)/shard_map/tw,ew->te/dot_general | solution.py:639
  476.7 11.1 %scan_entry.1 = f32[16,1024]{1,0:T(8,128)S(1)} custom-call(s32[8]{0:T(128)S(1)} %compare_convert_fusion.2.alive_ref, f32[1024,1024]{1,0:T(8,128)S(1)} %copy-done, f32[1024,1024]{1,0:T(8,128)} %get-tuple-element.115.ds_ref, f32[64,16,32]{2,1,0:T(8,128)S(1)} %pad_maximum_fusion.2.bc_ref, f32[16,1024]{1,0:T(8,128)S(1)} %fusion.34.rate_ref), custom_call_target="tpu_custom_call" | custom-call | tf_op jit(solution)/shard_map/scan_entry/pallas_call | solution.py:257
  489.2 6.2 convolution_convert_fusion
  495.8 77.3 %scan_backward.1 = (f32[1024,1024]{1,0:T(8,128)S(1)}, f32[1024,1024]{1,0:T(8,128)}, f32[1,64,256]{2,1,0:T(8,128)S(1)}, f32[1,64,256]{2,1,0:T(8,128)S(1)}, f32[16,1024]{1,0:T(8,128)S(1)}) custom-call(f32[1024,1024]{1,0:T(8,128)} %get-tuple-element.121.stepd_ref, f32[1024,1024]{1,0:T(8,128)} %get-tuple-element.130.u_ref, ...), custom_call_target="tpu_custom_call" | custom-call | tf_op jit(solution)/shard_map/scan_backward/pallas_call | solution.py:142
  573.1 5.0 fusion.51
  581.1 31.8 %all-reduce.10 = bf16[1024,160]{0,1:T(8,128)(2,1)S(1)} all-reduce(f32[1024,160]{0,1:T(8,128)S(1)} %pad_maximum_fusion.1), channel_id=1, replica_groups=mesh['dp'=4,'seq'=2,'tensor'=4] {'tensor'}, use_global_device_ids=true, to_apply=%region_9.10 | all-reduce | flops 163840 | bytes 983040 | tf_op jit(solution)/shard_map/psum | solution.py:662
  612.9 2.1 fusion.62
  615.2 16.7 %multiply_reduce_fusion.1 = (f32[1024]{0:T(1024)S(1)}, f32[1024]{0:T(1024)S(1)}, f32[1024]{0:T(1024)S(1)}, f32[1024]{0:T(1024)S(1)}, f32[1024]{0:T(1024)S(1)}, /*index=5*/f32[1024,1024]{1,0:T(8,128)S(1)}) fusion(f32[1024,1024]{1,0:T(8,128)} %copy-done.14, f32[3,1024]{1,0:T(4,128)S(1)} %copy-done.42, f32[1024]{0:T(1024)S(1)} %copy-done.38, ...), kind=kOutput, calls=%fused_computation.24 | convolution fusion | flops 372239360 | bytes 25878528 | tf_op jit(solution)/shard_map/tj,ej->te/dot_general | solution.py:667
  632.0 3.9 multiply_multiply_fusion.1
  635.9 1.5 collective-permute-start.4
  639.2 4.2 multiply_add_fusion
  646.8 3.8 convert_element_type.163.dx_ref
  650.7 85.5 %tail_sums.1 = (f32[256,2048]{1,0:T(8,128)}, f32[2,256,1024]{2,1,0:T(8,128)}, f32[40,1024]{1,0:T(8,128)}, f32[24,1024]{1,0:T(8,128)}) custom-call(bf16[1024,1024]{1,0:T(8,128)(2,1)} %convert_element_type.163.dx_ref, bf16[1024,1024]{1,0:T(8,128)(2,1)} %get-tuple-element.126.dz_ref, bf16[2,2048,1024]{2,1,0:T(8,128)(2,1)} %all-gather.9.cloned.1.call-done.w_ref, ...), custom_call_target="tpu_custom_call" | custom-call | tf_op jit(solution)/shard_map/tail_sums/pallas_call | solution.py:501
  736.2 1.6 slice.218
  739.2 4.5 copy.58
  744.4 22.3 %all-reduce.5 = f32[2048]{0:T(1024)S(1)} all-reduce(f32[2048]{0:T(1024)S(1)} %get-tuple-element.110), channel_id=3, replica_groups=mesh['dp'=4,'seq'=2,'tensor'=4] {'tensor'}, use_global_device_ids=true, to_apply=%region_19.20.clone | all-reduce | flops 2048 | bytes 16384
  766.8 12.9 %psum.23 = f32[512]{0:T(512)} all-reduce(f32[512]{0:T(512)S(1)} %dynamic-slice.14), channel_id=1, replica_groups=mesh['dp'=4,'seq'=2,'tensor'=4] {'dp','seq'}, use_global_device_ids=true, to_apply=%region_20.21 | all-reduce | flops 512 | bytes 4096 | tf_op jit(solution)/shard_map/psum | solution.py:734
  779.6 1.5 fusion.58
  782.4 4.6 fusion.16
  (205 shorter events, 33.3 us)
Async XLA Ops:
  7.2 21.9 %copy-start.47 = (bf16[1024]{0:T(1024)(128)(2,1)S(1)}, bf16[1024]{0:T(1024)(128)(2,1)}, u32[]{:S(2)}) copy-start(bf16[1024]{0:T(1024)(128)(2,1)} %param.21) | copy-start | bytes 6148
  7.2 21.9 %copy-start.22 = (bf16[1024,20]{0,1:T(8,128)(2,1)S(1)}, bf16[1024,20]{0,1:T(8,128)(2,1)}, u32[]{:S(2)}) copy-start(bf16[1024,20]{0,1:T(8,128)(2,1)} %param.22) | copy-start | bytes 122884
  7.2 38.2 %copy-start.21 = (bf16[4,1024]{1,0:T(4,128)(2,1)S(1)}, bf16[4,1024]{1,0:T(4,128)(2,1)}, u32[]{:S(2)}) copy-start(bf16[4,1024]{1,0:T(4,128)(2,1)} %param.20) | copy-start | bytes 24580
  7.2 86.0 %all-gather.7.cloned.1.call-start = ((), (), s32[]{:S(2)}) async-start(), calls=%async_computation.2 | async-start | bytes 5242880 | tf_op jit(solution)/shard_map/all_gather | solution.py:570
  8.0 140.6 %all-gather.9.cloned.1.call-start = ((), (), s32[]{:S(2)}) async-start(), calls=%async_computation.3 | async-start | bytes 9437184 | tf_op jit(solution)/shard_map/all_gather | solution.py:561
  10.5 198.9 %all-reduce.9.cloned.1.call-start = ((), (), s32[]{:S(2)}) async-start(), calls=%async_computation.4 | async-start | bytes 1310720 | tf_op jit(solution)/shard_map/psum | solution.py:598
  11.9 147.3 %collective-permute-start = (f32[3]{0:T(128)S(1)}, f32[3]{0:T(128)S(1)}, u32[]{:S(2)}, u32[]{:S(2)}) collective-permute-start(f32[3]{0:T(128)S(1)} %slice.175), channel_id=1, source_target_pairs={{0,4},{1,5},{2,6},{3,7},{8,12},{9,13},{10,14},{11,15},{16,20},{17,... | collective-permute-start | bytes 44 | tf_op jit(solution)/shard_map/ppermute | solution.py:20
  45.4 120.5 %copy-start.17 = (bf16[160,1024]{1,0:T(8,128)(2,1)}, bf16[160,1024]{1,0:T(8,128)(2,1)S(1)}, u32[]{:S(2)}) copy-start(bf16[160,1024]{1,0:T(8,128)(2,1)S(1)} %reshape.263) | copy-start | bytes 983044
  45.4 115.2 %copy-start.27 = (f32[1024]{0:T(1024)}, f32[1024]{0:T(1024)S(1)}, u32[]{:S(2)}) copy-start(f32[1024]{0:T(1024)S(1)} %compare_convert_fusion) | copy-start | bytes 12292
  45.4 115.1 %copy-start.29 = (f32[1,1024]{1,0:T(1,128)}, f32[1,1024]{1,0:T(1,128)S(1)}, u32[]{:S(2)}) copy-start(f32[1,1024]{1,0:T(1,128)S(1)} %get-tuple-element.142) | copy-start | bytes 12292
  45.4 115.1 %copy-start.31 = (f32[1,1024]{1,0:T(1,128)}, f32[1,1024]{1,0:T(1,128)S(1)}, u32[]{:S(2)}) copy-start(f32[1,1024]{1,0:T(1,128)S(1)} %get-tuple-element.143) | copy-start | bytes 12292
  45.5 115.1 %copy-start.33 = (f32[1,1024]{1,0:T(1,128)}, f32[1,1024]{1,0:T(1,128)S(1)}, u32[]{:S(2)}) copy-start(f32[1,1024]{1,0:T(1,128)S(1)} %get-tuple-element.144) | copy-start | bytes 12292
  45.5 115.1 %copy-start.35 = (f32[1,1024]{1,0:T(1,128)}, f32[1,1024]{1,0:T(1,128)S(1)}, u32[]{:S(2)}) copy-start(f32[1,1024]{1,0:T(1,128)S(1)} %get-tuple-element.145) | copy-start | bytes 12292
  156.1 4.5 collective-permute-start.1
  165.8 53.0 %copy-start.4 = (bf16[1024,1024]{1,0:T(8,128)(2,1)}, bf16[1024,1024]{1,0:T(8,128)(2,1)S(1)}, u32[]{:S(2)}) copy-start(bf16[1024,1024]{1,0:T(8,128)(2,1)S(1)} %get-tuple-element.122) | copy-start | bytes 6291460
  165.8 21.2 %copy-start.19 = (f32[16,1024]{1,0:T(8,128)S(1)}, f32[16,1024]{1,0:T(8,128)}, u32[]{:S(2)}) copy-start(f32[16,1024]{1,0:T(8,128)} %param.25) | copy-start | bytes 196612
  167.5 115.9 %all-gather.11.cloned.1.call-start = ((), (), s32[]{:S(2)}) async-start(), calls=%async_computation.5 | async-start | bytes 4718592 | tf_op jit(solution)/shard_map/all_gather | solution.py:564
  168.1 208.5 %reduce-scatter.3.cloned.1.call-start = ((), (), s32[]{:S(2)}) async-start(), calls=%async_computation.6 | async-start | bytes 5242880 | tf_op jit(solution)/shard_map/reduce_scatter | solution.py:623
  227.6 29.7 %copy-start.54 = (s32[8]{0:T(128)S(1)}, s32[8]{0:T(128)}, u32[]{:S(2)}) copy-start(s32[8]{0:T(128)} %copy-done.53) | copy-start | bytes 100
  227.6 29.7 %copy-start.55 = (s32[8,1]{0,1:T(1,128)S(1)}, s32[8,1]{0,1:T(1,128)}, u32[]{:S(2)}) copy-start(s32[8,1]{0,1:T(1,128)} %reduce-window.9) | copy-start | bytes 100
  253.9 5.3 collective-permute-start.2
  259.2 15.0 %copy-start.5 = (bf16[1024,1024]{1,0:T(8,128)(2,1)S(1)}, bf16[1024,1024]{1,0:T(8,128)(2,1)}, u32[]{:S(2)}) copy-start(bf16[1024,1024]{1,0:T(8,128)(2,1)} %copy-done.4) | copy-start | bytes 6291460
  259.2 15.0 %copy-start.9 = (bf16[1024,2048]{1,0:T(8,128)(2,1)S(1)}, bf16[1024,2048]{1,0:T(8,128)(2,1)}, u32[]{:S(2)}) copy-start(bf16[1024,2048]{1,0:T(8,128)(2,1)} %fusion.2.nrm_ref) | copy-start | bytes 12582916
  259.2 15.0 %copy-start.50 = (f32[1024]{0:T(1024)S(1)}, f32[1024]{0:T(1024)}, u32[]{:S(2)}) copy-start(f32[1024]{0:T(1024)} %param.26) | copy-start | bytes 12292
  292.8 25.5 %copy-start.46 = (pred[1024]{0:T(1024)(128)(4,1)S(1)}, pred[1024]{0:T(1024)(128)(4,1)}, u32[]{:S(2)}) copy-start(pred[1024]{0:T(1024)(128)(4,1)} %get-tuple-element.119) | copy-start | bytes 3076
  292.8 83.8 %copy-start.10 = (bf16[256,2048]{1,0:T(8,128)(2,1)S(1)}, bf16[256,2048]{1,0:T(8,128)(2,1)}, u32[]{:S(2)}) copy-start(bf16[256,2048]{1,0:T(8,128)(2,1)} %param.15) | copy-start | bytes 3145732
  292.8 87.1 %copy-start.51 = (u32[32]{0:T(128)S(1)}, u32[32]{0:T(128)}, u32[]{:S(2)}) copy-start(u32[32]{0:T(128)} %constant.166) | copy-start | bytes 388
  292.8 88.3 %copy-start.45 = (s32[256]{0:T(256)S(1)}, s32[256]{0:T(256)}, u32[]{:S(2)}) copy-start(s32[256]{0:T(256)} %and_select_fusion.1) | copy-start | bytes 3076
  292.8 88.4 %copy-start.38 = (f32[1024]{0:T(1024)S(1)}, f32[1024]{0:T(1024)}, u32[]{:S(2)}) copy-start(f32[1024]{0:T(1024)} %copy-done.37) | copy-start | bytes 12292
  292.8 88.9 %copy-start.24 = (f32[1024]{0:T(1024)S(1)}, f32[1024]{0:T(1024)}, u32[]{:S(2)}) copy-start(f32[1024]{0:T(1024)} %copy-done.23) | copy-start | bytes 12292
  292.8 89.0 %copy-start.26 = (f32[1024]{0:T(1024)S(1)}, f32[1024]{0:T(1024)}, u32[]{:S(2)}) copy-start(f32[1024]{0:T(1024)} %copy-done.25) | copy-start | bytes 12292
  292.9 168.3 %all-gather.13.cloned.1.call-start = ((), (), s32[]{:S(2)}) async-start(), calls=%async_computation.7 | async-start | bytes 5242880 | tf_op jit(solution)/shard_map/all_gather | solution.py:638
  379.7 407.3 %reduce-scatter.5.cloned.1.call-start = ((), (), s32[]{:S(2)}) async-start(), calls=%async_computation.8 | async-start | bytes 4718592 | tf_op jit(solution)/shard_map/reduce_scatter | solution.py:733
  461.2 15.5 %copy-start = (f32[1024,1024]{1,0:T(8,128)S(1)}, f32[1024,1024]{1,0:T(8,128)}, u32[]{:S(2)}) copy-start(f32[1024,1024]{1,0:T(8,128)} %get-tuple-element.121.stepd_ref) | copy-start | bytes 12582916
  476.7 12.5 %copy-start.49 = (bf16[1024,2048]{1,0:T(8,128)(2,1)S(1)}, bf16[1024,2048]{1,0:T(8,128)(2,1)}, u32[]{:S(2)}) copy-start(bf16[1024,2048]{1,0:T(8,128)(2,1)} %all-gather.13.cloned.1.call-done) | copy-start | bytes 12582916
  476.7 12.5 %copy-start.56 = (bf16[1024,1024]{1,0:T(8,128)(2,1)S(1)}, bf16[1024,1024]{1,0:T(8,128)(2,1)}, u32[]{:S(2)}) copy-start(bf16[1024,1024]{1,0:T(8,128)(2,1)} %get-tuple-element.160) | copy-start | bytes 6291460
  487.9 7.9 collective-permute-start.3
  495.8 77.3 %copy-start.6 = (bf16[1024,1024]{1,0:T(8,128)(2,1)S(1)}, bf16[1024,1024]{1,0:T(8,128)(2,1)}, u32[]{:S(2)}) copy-start(bf16[1024,1024]{1,0:T(8,128)(2,1)} %copy-done.4) | copy-start | bytes 6291460
  495.8 77.3 %copy-start.11 = (f32[1024,1024]{1,0:T(8,128)S(1)}, f32[1024,1024]{1,0:T(8,128)}, u32[]{:S(2)}) copy-start(f32[1024,1024]{1,0:T(8,128)} %get-tuple-element.159) | copy-start | bytes 12582916
  495.8 77.3 %copy-start.44 = (f32[1024]{0:T(1024)S(1)}, f32[1024]{0:T(1024)}, u32[]{:S(2)}) copy-start(f32[1024]{0:T(1024)} %param.24) | copy-start | bytes 12292
  580.7 34.5 %copy-start.18 = (bf16[160,1024]{1,0:T(8,128)(2,1)S(1)}, bf16[160,1024]{1,0:T(8,128)(2,1)}, u32[]{:S(2)}) copy-start(bf16[160,1024]{1,0:T(8,128)(2,1)} %copy-done.17) | copy-start | bytes 983044
  580.7 34.5 %copy-start.28 = (f32[1024]{0:T(1024)S(1)}, f32[1024]{0:T(1024)}, u32[]{:S(2)}) copy-start(f32[1024]{0:T(1024)} %copy-done.27) | copy-start | bytes 12292
  580.7 34.5 %copy-start.42 = (f32[3,1024]{1,0:T(4,128)S(1)}, f32[3,1024]{1,0:T(4,128)}, u32[]{:S(2)}) copy-start(f32[3,1024]{1,0:T(4,128)} %copy-done.41) | copy-start | bytes 36868
  615.2 22.2 %copy-start.8 = (bf16[1024,1024]{1,0:T(8,128)(2,1)S(1)}, bf16[1024,1024]{1,0:T(8,128)(2,1)}, u32[]{:S(2)}) copy-start(bf16[1024,1024]{1,0:T(8,128)(2,1)} %copy-done.7) | copy-start | bytes 6291460
  615.2 22.2 %copy-start.16 = (f32[1024,160]{0,1:T(8,128)S(1)}, f32[1024,160]{0,1:T(8,128)}, u32[]{:S(2)}) copy-start(f32[1024,160]{0,1:T(8,128)} %all-reduce.9.cloned.1.call-done) | copy-start | bytes 1966084
  635.9 8.8 %collective-permute-start.4 = (f32[3,1024]{1,0:T(4,128)S(1)}, f32[3,1024]{1,0:T(4,128)S(1)}, u32[]{:S(2)}, u32[]{:S(2)}) collective-permute-start(f32[3,1024]{1,0:T(4,128)S(1)} %pad_maximum_fusion.3), channel_id=1, source_target_pairs={{4,0},{5,1},{6,2},{7,3},{12,8},{13,9},{14,10},{15,11},{20,16},{21,... | collective-permute-start | bytes 36872 | tf_op jit(solution)/shard_map/ppermute | solution.py:20
  736.2 44.9 %copy-start.20 = (f32[40,1024]{1,0:T(8,128)S(1)}, f32[40,1024]{1,0:T(8,128)}, u32[]{:S(2)}) copy-start(f32[40,1024]{1,0:T(8,128)} %get-tuple-element.52) | copy-start | bytes 491524
  736.2 46.2 %copy-start.15 = (bf16[256,2048]{1,0:T(8,128)(2,1)S(1)}, bf16[256,2048]{1,0:T(8,128)(2,1)}, u32[]{:S(2)}) copy-start(bf16[256,2048]{1,0:T(8,128)(2,1)} %param.16) | copy-start | bytes 3145732
  (21 other events, 105.2 us)
Sparse Core Ops, SparseCore 0:
  9.6 83.5 all-gather.6
  95.7 52.8 all-gather.8
  167.7 41.6 all-reduce.8
  211.1 37.0 all-gather.10
  293.0 83.5 reduce-scatter.2
  379.9 81.3 all-gather.12
  495.6 53.7 reduce-scatter.4

commit v3 on v2

--- a/solution.py
+++ b/solution.py
@@ -299,8 +299,9 @@
 
 def tail_kernel(n, dps, seqs, subs, lag, dx_ref, dz_ref, w_ref, nrm_ref, sm_ref, all_ref,
                 dn_ref, gin_ref, gs_ref, ga_ref,
+                gacc, gsend, grecv, all_mine,
                 zr, zl, part_r, part_l, one_send, one_recv, two_recv, sm_one, sm_two, all_one, all_two,
-                r_send, r_recv, l_send, l_recv, w1s, w1r, w2s, w2r, s1s, s1r, s2s, s2r, a1s, a1r, a2s, a2r):
+                r_send, r_recv, l_send, l_recv, w1s, w1r, w2s, w2r, s1s, s1r, s2s, s2r, a1s, a1r, a2s, a2r, gs, gr):
     dp, seq, t = place()
     core, hi = dp % 2, dp // 2
     chips = dps // 2 * seqs
@@ -323,9 +324,10 @@
         q = lax.rem(chip + step, chips)
         pl.semaphore_signal(barrier, inc=1, device_id=to_chip(q), device_id_type=MESH)
 
-    for peer in (lax.rem(t + 1, n), lax.rem(t + n - 1, n)):
-        pl.semaphore_signal(barrier, inc=1, device_id=dict(tensor=peer), device_id_type=MESH)
-    pl.semaphore_wait(barrier, chips + 2)
+    for ahead in range(1, n):
+        pl.semaphore_signal(barrier, inc=1, device_id=dict(tensor=lax.rem(t + ahead, n)), device_id_type=MESH)
+    pl.semaphore_wait(barrier, chips + n - 1)
+    gacc[...] = jnp.zeros_like(gacc)
 
     partner = dict(dp=hi * 2 + 1 - core)
     right, left = dict(tensor=lax.rem(t + 1, n)), dict(tensor=lax.rem(t + n - 1, n))
@@ -349,10 +351,13 @@
         return mesh_copy(sm_one.at[q], sm_two.at[slot], s2s.at[q], s2r.at[slot], **to_chip(q))
 
     def a1_copy():
-        return mesh_copy(all_ref, all_one, a1s, a1r, **partner)
+        return mesh_copy(all_mine, all_one, a1s, a1r, **partner)
 
     def a2_copy(q, slot):
         return mesh_copy(all_one, all_two.at[slot], a2s.at[q], a2r.at[slot], **to_chip(q))
+
+    def g_copy(p, slot):
+        return mesh_copy(gsend.at[p], grecv.at[slot], gs.at[p], gr.at[slot], tensor=p)
 
     def partial_rows(o, dst):
         here = pl.ds(pl.multiple_of(o * rows, rows), rows)
@@ -361,9 +366,12 @@
         def _(j):
             cols = pl.ds(pl.multiple_of(j * tile, tile), tile)
             nt = (((1,), (1,)), ((), ()))
-            dst[:, cols] = lax.dot_general(
+            block = lax.dot_general(
                 dx_ref[here, :], w_ref[0, cols, :], nt, preferred_element_type=F32
             ) + lax.dot_general(dz_ref[here, :], w_ref[1, cols, :], nt, preferred_element_type=F32)
+            dst[:, cols] = block
+            scaled = block * nrm_ref[here, cols].astype(F32)
+            gacc[:, cols] = gacc[:, cols] + jnp.sum(scaled.reshape(rows // 8, 8, tile), axis=0)
 
     def weight_rows(p, k):
         cols = pl.ds(pl.multiple_of(p * wrows, wrows), wrows)
@@ -373,7 +381,6 @@
 
     for q in range(chips):
         s1_copy(q).start()
-    a1_copy().start()
 
     def stream(i, limit, start, buf, copy, part_ref, owner_of):
         @pl.when(jnp.logical_and(i >= 0, i < limit))
@@ -384,18 +391,20 @@
             def _():
                 partial_rows(owner_of(k), part_ref)
 
-            here = part_ref[pl.ds(pl.multiple_of(sub * part, part), part), :]
-
-            @pl.when(start)
+            @pl.when(jnp.logical_and(start, sub == 0))
             def _():
-                buf[i] = here.astype(BF16)
+                @pl.loop(0, subs)
+                def _(j):
+                    here = part_ref[pl.ds(pl.multiple_of(j * part, part), part), :]
+                    buf[k * subs + j] = here.astype(BF16)
+                    copy(k * subs + j).start()
 
             @pl.when(jnp.logical_not(start))
             def _():
+                here = part_ref[pl.ds(pl.multiple_of(sub * part, part), part), :]
                 copy(i).wait_recv()
                 buf[i] = (here + buf[i].astype(F32)).astype(BF16)
-
-            copy(i).start()
+                copy(i).start()
 
     def step(g, _):
         stream(g - lag * t, (n - 1 - t) * subs, t == 0, zr, r_copy, part_r, lambda k: n - 1 - k)
@@ -420,12 +429,9 @@
             for q in range(chips):
                 s1_copy(q).wait_recv()
                 sm_one[q] = sm_one[q] + sm_ref[owner(q, core)]
-            a1_copy().wait_recv()
-            all_one[...] = all_one[...] + all_ref[...]
             for ahead in range(1, chips):
                 q = lax.rem(chip + ahead, chips)
                 s2_copy(q, chip).start()
-                a2_copy(q, chip).start()
             w1_copy(chip).wait_recv()
             for k in range(2):
                 gin_ref[k] = weight_rows(owner(chip, core), k) + one_recv[chip, k].astype(F32)
@@ -439,6 +445,12 @@
     steps = max((n - 1) * max(subs, lag), 2 * chips + 1)
     lax.fori_loop(0, steps, step, 0)
 
+    share = wide // n
+    for p in range(n):
+        gsend[p] = gacc[:, p * share:(p + 1) * share]
+    for ahead in range(1, n):
+        g_copy(lax.rem(t + ahead, n), t).start()
+
     @pl.loop(0, subs)
     def _(s):
         here = pl.ds(pl.multiple_of(s * part, part), part)
@@ -455,21 +467,40 @@
             l_copy(i).wait_recv()
             dn_ref[here, :] = dn_ref[here, :] + zl[i].astype(F32)
 
+    plain = all_ref.shape[0]
+    all_mine[0:plain, :] = all_ref[...]
+    all_mine[plain:, :] = jnp.zeros((8, all_mine.shape[1]), F32)
+    all_mine[plain:, 0:share] = gsend[t]
+    for ahead in range(1, n):
+        p = lax.rem(t + ahead, n)
+        g_copy(p, p).wait_recv()
+        all_mine[plain:, 0:share] = all_mine[plain:, 0:share] + grecv[p]
+    a1_copy().start()
     gs_ref[...] = sm_one[chip]
-    ga_ref[...] = all_one[...]
     for ahead in range(1, chips):
         q = lax.rem(chip + ahead, chips)
         s2_copy(q, q).wait_recv()
         gs_ref[...] = gs_ref[...] + sm_two[q]
+    a1_copy().wait_recv()
+    all_one[...] = all_one[...] + all_mine[...]
+    for ahead in range(1, chips):
+        a2_copy(lax.rem(chip + ahead, chips), chip).start()
+    ga_ref[...] = all_one[...]
+    for ahead in range(1, chips):
+        q = lax.rem(chip + ahead, chips)
+        w2_copy(q, q).wait_recv()
+        gin_ref[...] = gin_ref[...] + two_recv[q].astype(F32)
+    for ahead in range(1, chips):
+        q = lax.rem(chip + ahead, chips)
         a2_copy(q, q).wait_recv()
         ga_ref[...] = ga_ref[...] + all_two[q]
-        w2_copy(q, q).wait_recv()
-        gin_ref[...] = gin_ref[...] + two_recv[q].astype(F32)
 
     for q in range(chips):
         s1_copy(q).wait_send()
         w1_copy(q).wait_send()
     a1_copy().wait_send()
+    for ahead in range(1, n):
+        g_copy(lax.rem(t + ahead, n), t).wait_send()
     for ahead in range(1, chips):
         q = lax.rem(chip + ahead, chips)
         s2_copy(q, chip).wait_send()
@@ -493,7 +524,7 @@
     rows = dx.shape[0] // n
     wide, lanes = w_full.shape[1], w_full.shape[2]
     wrows = wide // (dps * seqs)
-    subs = max(1, rows // 64)
+    subs = max(1, rows // 32)
     hops = (n - 1) * subs
     vmem = pl.BlockSpec(memory_space=pltpu.VMEM)
     dma = pltpu.SemaphoreType.DMA
@@ -504,11 +535,15 @@
             jax.ShapeDtypeStruct((rows, wide), F32),
             jax.ShapeDtypeStruct((2, wrows, lanes), F32),
             jax.ShapeDtypeStruct(small.shape[1:], F32),
-            jax.ShapeDtypeStruct(whole.shape, F32),
+            jax.ShapeDtypeStruct((whole.shape[0] + 8, lanes), F32),
         ],
         in_specs=[vmem] * 6,
         out_specs=[vmem] * 4,
         scratch_shapes=[
+            pltpu.VMEM((8, wide), F32),
+            pltpu.VMEM((n, 8, wide // n), F32),
+            pltpu.VMEM((n, 8, wide // n), F32),
+            pltpu.VMEM((whole.shape[0] + 8, lanes), F32),
             pltpu.VMEM((hops, rows // subs, wide), BF16),
             pltpu.VMEM((hops, rows // subs, wide), BF16),
             pltpu.VMEM((rows, wide), F32),
@@ -518,16 +553,228 @@
             pltpu.VMEM((chips, 2, wrows, lanes), BF16),
             pltpu.VMEM((chips,) + small.shape[1:], F32),
             pltpu.VMEM((chips,) + small.shape[1:], F32),
-            pltpu.VMEM(whole.shape, F32),
-            pltpu.VMEM((chips,) + whole.shape, F32),
+            pltpu.VMEM((whole.shape[0] + 8, lanes), F32),
+            pltpu.VMEM((chips, whole.shape[0] + 8, lanes), F32),
             dma((hops,)), dma((hops,)), dma((hops,)), dma((hops,)),
-            few, few, few, few, few, few, few, few, dma, dma, few, few,
+            few, few, few, few, few, few, few, few, dma, dma, few, few, dma((n,)), dma((n,)),
         ],
         compiler_params=pltpu.CompilerParams(
             collective_id=2, has_side_effects=True, vmem_limit_bytes=60 << 20
         ),
         name="tail_sums",
     )(dx, dz, w_full, normed, small, whole)
+
+
+def mid_kernel(n, subs, lag, gated_ref, w_ref, hid_ref, tea_ref, scale_ref, z_ref, scan_ref,
+               out_ref, go_ref, piece_ref, dscan_ref, dz_ref,
+               zr, zl, part_r, part_l, r_send, r_recv, l_send, l_recv, ar_send, ar_recv, al_send, al_recv):
+    t = lax.axis_index("tensor")
+    rows, wide = hid_ref.shape
+    part = rows // subs
+    tile = 512
+    right, left = dict(tensor=lax.rem(t + 1, n)), dict(tensor=lax.rem(t + n - 1, n))
+
+    barrier = pltpu.get_barrier_semaphore()
+    for peer in (right, left):
+        pl.semaphore_signal(barrier, inc=1, device_id=peer, device_id_type=MESH)
+    pl.semaphore_wait(barrier, 2)
+
+    def r_copy(i):
+        return mesh_copy(zr.at[i], zr.at[i], r_send.at[i], r_recv.at[i], **right)
+
+    def l_copy(i):
+        return mesh_copy(zl.at[i], zl.at[i], l_send.at[i], l_recv.at[i], **left)
+
+    def at(o, s):
+        return pl.ds(pl.multiple_of(o * rows + s * part, part), part)
+
+    def ar_copy(o, s):
+        ref = piece_ref.at[at(o, s), :]
+        return mesh_copy(ref, ref, ar_send.at[o * subs + s], ar_recv.at[o * subs + s], **right)
+
+    def al_copy(o, s):
+        ref = piece_ref.at[at(o, s), :]
+        return mesh_copy(ref, ref, al_send.at[o * subs + s], al_recv.at[o * subs + s], **left)
+
+    def partial_rows(o, dst):
+        here = pl.ds(pl.multiple_of(o * rows, rows), rows)
+
+        @pl.loop(0, wide // tile)
+        def _(j):
+            cols = pl.ds(pl.multiple_of(j * tile, tile), tile)
+            nt = (((1,), (1,)), ((), ()))
+            dst[:, cols] = lax.dot_general(gated_ref[here, :], w_ref[cols, :], nt, preferred_element_type=F32)
+
+    def backward_rows(o):
+        here = pl.ds(pl.multiple_of(o * rows, rows), rows)
+        d_gated = jnp.dot(piece_ref[here, :], w_ref[...], preferred_element_type=F32)
+        z = z_ref[here, :]
+        s = 1.0 / (1.0 + jnp.exp(-z))
+        dscan_ref[here, :] = d_gated * (z * s)
+        dz_ref[here, :] = (d_gated * scan_ref[here, :] * (s * (1.0 + z * (1.0 - s)))).astype(BF16)
+
+    def stream(i, limit, start, buf, copy, part_ref, owner_of):
+        @pl.when(jnp.logical_and(i >= 0, i < limit))
+        def _():
+            k, sub = i // subs, i % subs
+
+            @pl.when(sub == 0)
+            def _():
+                partial_rows(owner_of(k), part_ref)
+
+            @pl.when(jnp.logical_and(start, sub == 0))
+            def _():
+                @pl.loop(0, subs)
+                def _(j):
+                    here = part_ref[pl.ds(pl.multiple_of(j * part, part), part), :]
+                    buf[k * subs + j] = here.astype(BF16)
+                    copy(k * subs + j).start()
+
+            @pl.when(jnp.logical_not(start))
+            def _():
+                here = part_ref[pl.ds(pl.multiple_of(sub * part, part), part), :]
+                copy(i).wait_recv()
+                buf[i] = (here + buf[i].astype(F32)).astype(BF16)
+                copy(i).start()
+
+    def ready(o):
+        from_left = jnp.where(o > 0, lag * o + (n - 1 - o) * subs, 0)
+        from_right = jnp.where(o < n - 1, lag * (n - 1 - o) + o * subs, 0)
+        return jnp.maximum(from_left, from_right)
+
+    gap = max(subs, lag)
+    base = lag + (n - 2) * subs if subs >= lag else (n - 1) * lag
+
+    def turn(d, o):
+        inner = base + (d - o) * gap
+        inner = jnp.where(d == 0, (n - 1) * gap, inner)
+        return jnp.where(d == n - 1, base + (n - 2 - o) * gap + lag, inner)
+
+    def finish(s):
+        here = pl.ds(pl.multiple_of(s * part, part), part)
+
+        @pl.when(s == 0)
+        def _():
+            partial_rows(t, go_ref)
+
+        @pl.when(t > 0)
+        def _():
+            i = (n - 1 - t) * subs + s
+            r_copy(i).wait_recv()
+            go_ref[here, :] = go_ref[here, :] + zr[i].astype(F32)
+
+        @pl.when(t < n - 1)
+        def _():
+            i = t * subs + s
+            l_copy(i).wait_recv()
+            go_ref[here, :] = go_ref[here, :] + zl[i].astype(F32)
+
+        result = hid_ref[here, :].astype(F32) + go_ref[here, :]
+        out_ref[here, :] = result.astype(BF16)
+        grad = scale_ref[here, :] * (result - tea_ref[here, :].astype(F32))
+        go_ref[here, :] = grad
+        piece_ref[at(t, s), :] = grad.astype(BF16)
+
+    def step(g, _):
+        stream(g - lag * t, (n - 1 - t) * subs, t == 0, zr, r_copy, part_r, lambda k: n - 1 - k)
+        stream(g - lag * (n - 1 - t), t * subs, t == n - 1, zl, l_copy, part_l, lambda k: k)
+
+        @pl.loop(0, n)
+        def _(o):
+            s_own = g - ready(t)
+            s_right = g - turn(t, o)
+            s_left = g - turn(n - 1 - t, n - 1 - o)
+
+            @pl.when(jnp.logical_and(o == t, jnp.logical_and(s_own >= 0, s_own < subs)))
+            def _():
+                finish(s_own)
+
+            @pl.when(jnp.logical_and(o <= t, jnp.logical_and(s_right >= 0, s_right < subs)))
+            def _():
+                @pl.when(o < t)
+                def _():
+                    ar_copy(o, s_right).wait_recv()
+
+                @pl.when(t < n - 1)
+                def _():
+                    ar_copy(o, s_right).start()
+
+            @pl.when(jnp.logical_and(o >= t, jnp.logical_and(s_left >= 0, s_left < subs)))
+            def _():
+                @pl.when(o > t)
+                def _():
+                    al_copy(o, s_left).wait_recv()
+
+                @pl.when(t > 0)
+                def _():
+                    al_copy(o, s_left).start()
+
+            s_done = jnp.where(o == t, s_own, jnp.where(o < t, s_right, s_left))
+
+            @pl.when(s_done == subs - 1)
+            def _():
+                backward_rows(o)
+
+        return 0
+
+    steps = base + (n - 1) * gap + subs + lag
+    lax.fori_loop(0, steps, step, 0)
+
+    @pl.loop(0, (n - 1) * subs)
+    def _(i):
+        @pl.when(i < (n - 1 - t) * subs)
+        def _():
+            r_copy(i).wait_send()
+
+        @pl.when(i < t * subs)
+        def _():
+            l_copy(i).wait_send()
+
+    @pl.loop(0, n * subs)
+    def _(i):
+        o, s = i // subs, i % subs
+
+        @pl.when(jnp.logical_and(o <= t, t < n - 1))
+        def _():
+            ar_copy(o, s).wait_send()
+
+        @pl.when(jnp.logical_and(o >= t, t > 0))
+        def _():
+            al_copy(o, s).wait_send()
+
+
+def middle(gated, w_out, hidden, teacher, scale, z_gate, scan_out):
+    n = lax.axis_size("tensor")
+    rows, wide = hidden.shape
+    tokens, lanes = gated.shape
+    subs = max(1, rows // 32)
+    hops = (n - 1) * subs
+    vmem = pl.BlockSpec(memory_space=pltpu.VMEM)
+    dma = pltpu.SemaphoreType.DMA
+    return pl.pallas_call(
+        functools.partial(mid_kernel, n, subs, 2),
+        out_shape=[
+            jax.ShapeDtypeStruct((rows, wide), BF16),
+            jax.ShapeDtypeStruct((rows, wide), F32),
+            jax.ShapeDtypeStruct((tokens, wide), BF16),
+            jax.ShapeDtypeStruct((tokens, lanes), F32),
+            jax.ShapeDtypeStruct((tokens, lanes), BF16),
+        ],
+        in_specs=[vmem] * 7,
+        out_specs=[vmem] * 5,
+        scratch_shapes=[
+            pltpu.VMEM((hops, rows // subs, wide), BF16),
+            pltpu.VMEM((hops, rows // subs, wide), BF16),
+            pltpu.VMEM((rows, wide), F32),
+            pltpu.VMEM((rows, wide), F32),
+            dma((hops,)), dma((hops,)), dma((hops,)), dma((hops,)),
+            dma((n * subs,)), dma((n * subs,)), dma((n * subs,)), dma((n * subs,)),
+        ],
+        compiler_params=pltpu.CompilerParams(
+            collective_id=1, has_side_effects=True, vmem_limit_bytes=60 << 20
+        ),
+        name="middle",
+    )(gated, w_out, hidden, teacher, scale, z_gate, scan_out)
 
 
 def on_device(
@@ -561,7 +808,7 @@
         lax.all_gather(jnp.swapaxes(input_projection_weight, 0, 1), ("dp", "seq"), axis=1, tiled=True),
         lax.all_gather(xproj_weight, ("dp", "seq"), axis=1, tiled=True),
         lax.all_gather(dtproj_weight, ("dp", "seq"), axis=0, tiled=True),
-        lax.all_gather(output_projection_weight, ("dp", "seq"), axis=1, tiled=True),
+        lax.all_gather(output_projection_weight.T, ("dp", "seq"), axis=0, tiled=True),
         lax.all_gather(count_pair, ("dp", "seq"), axis=0, tiled=True),
     )
     count_pairs = count_pairs.astype(jnp.float32).reshape(-1, 2)
@@ -620,28 +867,14 @@
     scan_out = y_rows + d_skip[None] * x_float
     gate_act = jax.nn.silu(z_gate)
     gated_output_rows = (scan_out * gate_act).astype(jnp.bfloat16)
-    branch_share = lax.psum_scatter(
-        jnp.dot(gated_output_rows, w_out, preferred_element_type=F32).astype(BF16),
-        "tensor",
-        scatter_dimension=0,
-        tiled=True,
-    ).astype(F32)
-    share_rows = hidden_in.astype(jnp.float32)
-    result = share_rows + branch_share
-    output = result.astype(jnp.bfloat16)
+    share_rows = hidden_in.astype(F32)
     valid_share = lax.dynamic_slice_in_dim(valid_mask, row_start, row_share, 0)
     total_tokens = float(tok_rows * lax.axis_size(("dp", "seq")))
-    grad_out = (
-        total_tokens / total_count * valid_share[:, None] * (result - teacher.astype(jnp.float32))
-    )
-    grad_low = grad_out.astype(jnp.bfloat16)
-    piece = lax.all_gather(grad_low, "tensor", axis=0, tiled=True)
-    block_rows = jnp.einsum("tw,ew->te", piece, w_out, preferred_element_type=jnp.float32)
-    d_gated = block_rows
+    scale = (total_tokens / total_count * valid_share)[:, None]
+    output, grad_out, piece, d_scan, d_z = middle(
+        gated_output_rows, w_out, hidden_in, teacher, scale, z_gate, scan_out
+    )
     d_wout = jnp.einsum("te,tw->we", gated_output_rows, piece, preferred_element_type=jnp.float32)
-    d_gated, d_wout = (d_gated, d_wout)
-    d_scan = d_gated * gate_act
-    d_z = d_gated * scan_out * silu_slope(z_gate)
     d_skip_part = jnp.sum(d_scan * x_float, axis=0)
     adjoint_first = entry(alive, stepd, d_scan, col_pair, rates, tb=block)
     adjoint_in = carried(adjoint_first, reach, "seq", -1)
@@ -713,11 +946,9 @@
     whole = jnp.concatenate(
         [a_log_part, conv_weight_part, jnp.stack([conv_bias_part, dt_bias_part, d_skip_part, d_skip_part], 0)], 0
     )
-    d_norm_share, g_in, g_small, g_whole = tail(d_x.astype(BF16), d_z.astype(BF16), w_in, normalized_rows, small, whole)
+    d_norm_share, g_in, g_small, g_whole = tail(d_x.astype(BF16), d_z, w_in, normalized_rows, small, whole)
     g_in = jnp.swapaxes(g_in, 0, 1)
     inv_share = lax.dynamic_slice_in_dim(inv_rms, row_start, row_share, 0)
-    gain_partial = jnp.sum(d_norm_share * share_rows * inv_share, axis=0)
-    gain_part = lax.psum_scatter(gain_partial, "tensor", scatter_dimension=0, tiled=True)
     inner_sum = jnp.sum(d_norm_share * full_gain[None] * share_rows, axis=1, keepdims=True)
     inv_cube = inv_share * inv_share * inv_share
     input_grad = (
@@ -731,7 +962,7 @@
     g_x_state = g_small[rank_here : rank_here + state_here].T
     g_dt = g_small[rank_here + state_here : rank_here + state_here + rank_here]
     g_out = lax.psum_scatter(d_wout.astype(BF16), ("dp", "seq"), scatter_dimension=0, tiled=True).astype(F32).T
-    g_gain = lax.psum(gain_part, ("dp", "seq"))
+    g_gain = jnp.sum(g_whole[N + conv_taps + 4 :, : norm_gain.shape[0]], axis=0) / norm_gain.astype(F32)
     g_alog, g_conv_w = g_whole[:N], g_whole[N : N + conv_taps]
     g_conv_b, g_bias, g_skip = g_whole[N + conv_taps], g_whole[N + conv_taps + 1], g_whole[N + conv_taps + 2]
     return (

time: 802 us -> 732 us (0.913)
  Pallas kernels: 211 us -> 365 us
  waiting for transfers between devices: 256 us -> 102 us
  blocking collectives: 134 us -> 87 us
  matrix products: 78.3 us -> 50.2 us
    pallas_call x0 -> x1, Pallas kernels: none -> 141 us  [middle(): pl.pallas_call(functools.partial(mid_kernel, n, subs, 2), out_shape=[jax....]
    all_gather x2 -> x1, waiting for transfers between devices: 77.9 us -> 0.01 us  [on_device(): lax.all_gather(output_projection_weight.T, ('dp', 'seq'), axis=0, tiled=T...]
    reduce_scatter x1 -> x0, waiting for transfers between devices: 56.2 us -> none  [on_device(): lax.psum_scatter(jnp.dot(gated_output_rows, w_out, preferred_element_type...]
    unnamed x2 -> x1, blocking collectives: 43.3 us -> 14.9 us
    dot_general x2 -> x0, matrix products: 24.8 us -> none  [the longest x1 15.5 us: on_device(): jnp.einsum('tw,ew->te', piece, w_out, preferred_element_type=jnp.float32)]
    psum x1, waiting for transfers between devices: 21.4 us -> 0.01 us  [on_device(): lax.psum(jnp.dot(x_low, w_x, preferred_element_type=jnp.float32), 'tensor')]
    psum x1 -> x0, blocking collectives: 12.9 us -> none  [on_device(): g_gain = lax.psum(gain_part, ('dp', 'seq'))]
    pallas_call x1, Pallas kernels: 85.5 us -> 96.8 us  [tail(): pl.pallas_call(functools.partial(tail_kernel, n, dps, seqs, subs, 2), out...]
  transfers between devices with their start and end apart: 12 -> 10, of which waited for: 8 -> 4; matrix products, arithmetic and copies ran while one was open for 15% -> 17% of each run, Pallas kernels for 25% -> 29%
where the time goes in v3:
time: 732 us; the launch traced here: 725 us
  Pallas kernels  365 us (50%)
  waiting for transfers between devices  102 us (14%)
  blocking collectives  87 us (12%)
  matrix products  50.2 us (7%)
  other arithmetic  46.3 us (6%)
  local copies, waits for them, and re-layouts  39.2 us (5%)
  between operations  19.7 us (3%)
  starting transfers between devices  14.7 us (2%)
    pallas_call x1, Pallas kernels, middle(): pl.pallas_call(functools.partial(mid_kernel, n, subs, 2), out_shape=[jax....  141 us
    pallas_call x1, Pallas kernels, tail(): pl.pallas_call(functools.partial(tail_kernel, n, dps, seqs, subs, 2), out...  96.8 us
    pallas_call x1, Pallas kernels, bwd(): pl.pallas_call(functools.partial(bwd_kernel, unroll=unroll), grid=grid, i...  77.3 us
    all_gather x1, waiting for transfers between devices, on_device(): lax.all_gather(jnp.swapaxes(input_projection_weight, 0, 1), ('dp', 'seq')...  48.9 us
    all_gather x1, waiting for transfers between devices, on_device(): lax.all_gather(hidden_in, 'tensor', axis=0, tiled=True)  48.4 us
    psum x1, blocking collectives, on_device(): lax.psum(jnp.concatenate([d_rank, d_b_part, d_c_part], 1), 'tensor')  27.3 us
    pallas_call x1, Pallas kernels, fwd(): pl.pallas_call(functools.partial(fwd_kernel, unroll=unroll), grid=grid, i...  24.5 us
    all_gather x1, blocking collectives, on_device(): lax.all_gather(dtproj_weight, ('dp', 'seq'), axis=0, tiled=True)  16.4 us
  transfers between devices with their start and end apart: 10, of which 4 were waited for; matrix products, arithmetic and copies ran while one was open for 17% of the time, Pallas kernels for 29%

profile of v3, /device:TPU:0, one launch (start us, length us, event | category | flops | bytes accessed | tf_op | source)
XLA Modules:
  0.0 724.5 jit_solution(9683995918900969388)
XLA Ops:
  8.0 2.5 copy.70
  11.3 4.9 collective-permute-start
  16.2 12.2 %all-gather = bf16[4,1,512]{2,1,0:T(2,128)(2,1)S(1)} all-gather(bf16[1,1,512]{2,1,0:T(2,128)(2,1)S(1)} %reshape.258), channel_id=1, replica_groups=mesh['dp'=4,'seq'=2,'tensor'=4] {'tensor'}, dimensions={0}, use_global_device_ids=true | all-gather | bytes 5120 | tf_op jit(solution)/shard_map/all_gather | solution.py:818
  28.5 16.2 %all-gather.1 = bf16[8,20,1024]{2,1,0:T(8,128)(2,1)S(1)} all-gather(bf16[1,20,1024]{2,1,0:T(8,128)(2,1)S(1)} %bitcast.100), channel_id=1, replica_groups=mesh['dp'=4,'seq'=2,'tensor'=4] {'dp','seq'}, dimensions={0}, use_global_device_ids=true | all-gather | bytes 368640 | tf_op jit(solution)/shard_map/all_gather | solution.py:809
  44.8 48.4 %all-gather.6.cloned.1.call-done = bf16[1024,2048]{1,0:T(8,128)(2,1)} async-done(((bf16[256,2048]{1,0:T(8,128)(2,1)}), bf16[1024,2048]{1,0:T(8,128)(2,1)}) %all-gather.6.cloned.1.call-update) | async-done | bytes 4194320 | tf_op jit(solution)/shard_map/all_gather | solution.py:817
  93.2 3.2 fusion
  96.6 3.1 fusion.2.nrm_ref
  99.7 48.9 %all-gather.8.cloned.1.call-done.w_ref = bf16[2,2048,1024]{2,1,0:T(8,128)(2,1)} async-done(((bf16[2,256,1024]{2,1,0:T(8,128)(2,1)}), bf16[2,2048,1024]{2,1,0:T(8,128)(2,1)}) %all-gather.8.cloned.1.call-update) | async-done | bytes 8388624 | tf_op jit(solution)/shard_map/all_gather | solution.py:808
  148.6 7.5 %fusion.10 = f32[1024,1024]{1,0:T(8,128)S(1)} fusion(bf16[1024,2048]{1,0:T(8,128)(2,1)} %fusion.2.nrm_ref, bf16[2,2048,1024]{2,1,0:T(8,128)(2,1)} %all-gather.8.cloned.1.call-done.w_ref), kind=kOutput, calls=%fused_computation.22 | convolution fusion | flops 4294967296 | bytes 12582912 | tf_op jit(solution)/shard_map/dot_general | solution.py:824
  156.1 3.0 collective-permute-start.1
  161.2 5.1 multiply_convert_fusion.1
  166.4 1.7 fusion.55
  173.4 14.9 %all-reduce.4 = bf16[16]{0:T(256)(128)(2,1)S(1)} all-reduce(bf16[16]{0:T(256)(128)(2,1)S(1)} %dynamic-update-slice.3), channel_id=1, replica_groups=mesh['dp'=4,'seq'=2,'tensor'=4] {'dp','seq'}, use_global_device_ids=true, to_apply=%add.4 | all-reduce | flops 16 | bytes 64
  191.9 16.4 %all_gather.25 = bf16[128,1024]{1,0:T(8,128)(2,1)S(1)} all-gather(bf16[16,1024]{1,0:T(8,128)(2,1)S(1)} %copy-done.42), channel_id=1, replica_groups=mesh['dp'=4,'seq'=2,'tensor'=4] {'dp','seq'}, dimensions={0}, use_global_device_ids=true | all-gather | bytes 294912 | tf_op jit(solution)/shard_map/all_gather | solution.py:810
  219.1 1.9 copy_bitcast_fusion.1
  221.3 1.4 compare_select_fusion.1
  222.7 8.7 %fusion.47 = (f32[1024]{0:T(1024)S(1)}, f32[1024,1024]{1,0:T(8,128)}, f32[1024,1024]{1,0:T(8,128)}, f32[1024,1024]{1,0:T(8,128)}) fusion(f32[1024]{0:T(1024)} %param.24, pred[1024]{0:T(1024)(128)(4,1)} %get-tuple-element.156, bf16[1024,1024]{1,0:T(8,128)(2,1)S(1)} %get-tuple-element.130, bf16[128,1024]{1,0:T(8,128)(2,1)S(1)} %all_gather.25, ...), kind=kOutput, calls=%fused_computation.132 | convolution fusion | flops 279968768 | bytes 15213568 | tf_op jit(solution)/shard_map/dot_general | solution.py:851
  231.4 24.5 %scan_forward.1 = (f32[1024,1024]{1,0:T(8,128)S(1)}, f32[8,16,1024]{2,1,0:T(8,128)S(1)}, f32[16,1024]{1,0:T(8,128)S(1)}) custom-call(f32[1024,1024]{1,0:T(8,128)} %get-tuple-element.129.stepd_ref, f32[1024,1024]{1,0:T(8,128)} %get-tuple-element.137.u_ref, f32[64,16,32]{2,1,0:T(8,128)S(1)} %pad_maximum_fusion.2.bc_ref, ...), custom_call_target="tpu_custom_call" | custom-call | tf_op jit(solution)/shard_map/scan_forward/pallas_call | solution.py:58
  256.0 3.5 collective-permute-start.2
  259.6 6.3 fusion.9.z_ref
  265.9 14.4 %scan_correct.1 = (f32[1024,1024]{1,0:T(8,128)S(1)}, f32[8,16,1024]{2,1,0:T(8,128)S(1)}) custom-call(s32[8]{0:T(128)S(1)} %compare_convert_fusion.2.alive_ref, f32[1024,1024]{1,0:T(8,128)} %copy-done.1, f32[1024,1024]{1,0:T(8,128)} %get-tuple-element.129.stepd_ref, bf16[1024,256]{1,0:T(8,128)(2,1)S(1)} %get-tuple-element.153.cdiag_ref, ...), custom_call_target="tpu_custom_call" | custom-call | tf_op jit(solution)/shard_map/scan_correct/pallas_call | solution.py:212
  280.3 4.4 multiply_convert_fusion
  284.7 141.1 %middle.1 = (bf16[256,2048]{1,0:T(8,128)(2,1)}, f32[256,2048]{1,0:T(8,128)}, bf16[1024,2048]{1,0:T(8,128)(2,1)}, f32[1024,1024]{1,0:T(8,128)}, bf16[1024,1024]{1,0:T(8,128)(2,1)}) custom-call(bf16[1024,1024]{1,0:T(8,128)(2,1)} %get-tuple-element.126.gated_ref, bf16[2048,1024]{1,0:T(8,128)(2,1)} %all-gather.10.cloned.1.call-done.w_ref, ...), custom_call_target="tpu_custom_call" | custom-call | tf_op jit(solution)/shard_map/middle/pallas_call | solution.py:754
  425.9 2.2 copy-done
  428.0 11.1 %scan_entry.1 = f32[16,1024]{1,0:T(8,128)S(1)} custom-call(s32[8]{0:T(128)S(1)} %compare_convert_fusion.2.alive_ref, f32[1024,1024]{1,0:T(8,128)S(1)} %copy-done, f32[1024,1024]{1,0:T(8,128)} %get-tuple-element.50.ds_ref, f32[64,16,32]{2,1,0:T(8,128)S(1)} %pad_maximum_fusion.2.bc_ref, f32[16,1024]{1,0:T(8,128)S(1)} %fusion.28.rate_ref), custom_call_target="tpu_custom_call" | custom-call | tf_op jit(solution)/shard_map/scan_entry/pallas_call | solution.py:257
  439.2 1.5 collective-permute-start.3
  440.7 6.2 convolution_convert_fusion
  447.0 3.5 collective-permute-done.3.gin_ref
  450.5 77.3 %scan_backward.1 = (f32[1024,1024]{1,0:T(8,128)S(1)}, f32[1024,1024]{1,0:T(8,128)}, f32[1,64,256]{2,1,0:T(8,128)S(1)}, f32[1,64,256]{2,1,0:T(8,128)S(1)}, f32[16,1024]{1,0:T(8,128)S(1)}) custom-call(f32[1024,1024]{1,0:T(8,128)} %get-tuple-element.129.stepd_ref, f32[1024,1024]{1,0:T(8,128)} %get-tuple-element.137.u_ref, ...), custom_call_target="tpu_custom_call" | custom-call | tf_op jit(solution)/shard_map/scan_backward/pallas_call | solution.py:142
  527.8 6.2 fusion.44
  534.1 1.3 copy-done.7
  537.1 27.3 %all-reduce.9 = bf16[1024,160]{0,1:T(8,128)(2,1)S(1)} all-reduce(f32[1024,160]{0,1:T(8,128)S(1)} %pad_maximum_fusion.1), channel_id=1, replica_groups=mesh['dp'=4,'seq'=2,'tensor'=4] {'tensor'}, use_global_device_ids=true, to_apply=%region_8.9 | all-reduce | flops 163840 | bytes 983040 | tf_op jit(solution)/shard_map/psum | solution.py:895
  564.4 2.1 fusion.56
  566.7 16.4 %multiply_reduce_fusion.1 = (f32[1024]{0:T(1024)S(1)}, f32[1024]{0:T(1024)S(1)}, f32[1024]{0:T(1024)S(1)}, f32[1024]{0:T(1024)S(1)}, f32[1024]{0:T(1024)S(1)}, /*index=5*/f32[1024,1024]{1,0:T(8,128)S(1)}) fusion(f32[1024,1024]{1,0:T(8,128)} %copy-done.15, f32[3,1024]{1,0:T(4,128)S(1)} %copy-done.44, f32[1024]{0:T(1024)S(1)} %copy-done.41, ...), kind=kOutput, calls=%fused_computation.24 | convolution fusion | flops 372239360 | bytes 25878528 | tf_op jit(solution)/shard_map/tj,ej->te/dot_general | solution.py:900
  583.2 3.7 multiply_multiply_fusion.1
  586.9 1.5 collective-permute-start.4
  590.3 4.2 multiply_add_fusion
  596.6 1.4 scatter-add.4
  598.0 3.8 convert_element_type.142.dx_ref
  601.8 96.8 %tail_sums.1 = (f32[256,2048]{1,0:T(8,128)}, f32[2,256,1024]{2,1,0:T(8,128)}, f32[40,1024]{1,0:T(8,128)}, f32[32,1024]{1,0:T(8,128)}) custom-call(bf16[1024,1024]{1,0:T(8,128)(2,1)} %convert_element_type.142.dx_ref, bf16[1024,1024]{1,0:T(8,128)(2,1)} %get-tuple-element.56.dz_ref, bf16[2,2048,1024]{2,1,0:T(8,128)(2,1)} %all-gather.8.cloned.1.call-done.w_ref, ...), custom_call_target="tpu_custom_call" | custom-call | tf_op jit(solution)/shard_map/tail_sums/pallas_call | solution.py:532
  698.7 1.6 slice.222
  700.3 1.4 slice.216
  701.6 4.5 copy.65
  707.5 1.5 fusion.52
  709.0 1.4 slice_bitcast_fusion.6
  710.3 1.6 fusion.51
  712.3 2.0 fusion.15
  715.4 1.3 copy.66
  (207 shorter events, 28.7 us)
Async XLA Ops:
  7.2 21.2 %copy-start.57 = (bf16[1024]{0:T(1024)(128)(2,1)S(1)}, bf16[1024]{0:T(1024)(128)(2,1)}, u32[]{:S(2)}) copy-start(bf16[1024]{0:T(1024)(128)(2,1)} %param.21) | copy-start | bytes 6148
  7.2 21.2 %copy-start.27 = (bf16[1024,20]{0,1:T(8,128)(2,1)S(1)}, bf16[1024,20]{0,1:T(8,128)(2,1)}, u32[]{:S(2)}) copy-start(bf16[1024,20]{0,1:T(8,128)(2,1)} %param.22) | copy-start | bytes 122884
  7.2 37.5 %copy-start.25 = (bf16[4,1024]{1,0:T(4,128)(2,1)S(1)}, bf16[4,1024]{1,0:T(4,128)(2,1)}, u32[]{:S(2)}) copy-start(bf16[4,1024]{1,0:T(4,128)(2,1)} %param.20) | copy-start | bytes 24580
  7.2 85.9 %all-gather.6.cloned.1.call-start = ((), (), s32[]{:S(2)}) async-start(), calls=%async_computation.1 | async-start | bytes 5242880 | tf_op jit(solution)/shard_map/all_gather | solution.py:817
  8.0 140.6 %all-gather.8.cloned.1.call-start = ((), (), s32[]{:S(2)}) async-start(), calls=%async_computation.2 | async-start | bytes 9437184 | tf_op jit(solution)/shard_map/all_gather | solution.py:808
  10.5 202.7 %all-reduce.8.cloned.1.call-start = ((), (), s32[]{:S(2)}) async-start(), calls=%async_computation.3 | async-start | bytes 1310720 | tf_op jit(solution)/shard_map/psum | solution.py:845
  11.3 147.9 %collective-permute-start = (f32[3]{0:T(128)S(1)}, f32[3]{0:T(128)S(1)}, u32[]{:S(2)}, u32[]{:S(2)}) collective-permute-start(f32[3]{0:T(128)S(1)} %slice.178), channel_id=1, source_target_pairs={{0,4},{1,5},{2,6},{3,7},{8,12},{9,13},{10,14},{11,15},{16,20},{17,... | collective-permute-start | bytes 44 | tf_op jit(solution)/shard_map/ppermute | solution.py:20
  28.4 71.2 %copy-start.23 = (f32[4,1,512]{2,1,0:T(1,128)}, f32[4,1,512]{2,1,0:T(1,128)S(1)}, u32[]{:S(2)}) copy-start(f32[4,1,512]{2,1,0:T(1,128)S(1)} %convert_element_type.146) | copy-start | bytes 24580
  44.7 121.7 %copy-start.18 = (bf16[160,1024]{1,0:T(8,128)(2,1)}, bf16[160,1024]{1,0:T(8,128)(2,1)S(1)}, u32[]{:S(2)}) copy-start(bf16[160,1024]{1,0:T(8,128)(2,1)S(1)} %reshape.261) | copy-start | bytes 983044
  44.7 115.9 %copy-start.30 = (f32[1024]{0:T(1024)}, f32[1024]{0:T(1024)S(1)}, u32[]{:S(2)}) copy-start(f32[1024]{0:T(1024)S(1)} %compare_convert_fusion) | copy-start | bytes 12292
  44.7 115.8 %copy-start.32 = (f32[1,1024]{1,0:T(1,128)}, f32[1,1024]{1,0:T(1,128)S(1)}, u32[]{:S(2)}) copy-start(f32[1,1024]{1,0:T(1,128)S(1)} %get-tuple-element.148) | copy-start | bytes 12292
  44.8 115.8 %copy-start.34 = (f32[1,1024]{1,0:T(1,128)}, f32[1,1024]{1,0:T(1,128)S(1)}, u32[]{:S(2)}) copy-start(f32[1,1024]{1,0:T(1,128)S(1)} %get-tuple-element.149) | copy-start | bytes 12292
  44.8 115.8 %copy-start.36 = (f32[1,1024]{1,0:T(1,128)}, f32[1,1024]{1,0:T(1,128)S(1)}, u32[]{:S(2)}) copy-start(f32[1,1024]{1,0:T(1,128)S(1)} %get-tuple-element.150) | copy-start | bytes 12292
  44.8 115.8 %copy-start.38 = (f32[1,1024]{1,0:T(1,128)}, f32[1,1024]{1,0:T(1,128)S(1)}, u32[]{:S(2)}) copy-start(f32[1,1024]{1,0:T(1,128)S(1)} %get-tuple-element.151) | copy-start | bytes 12292
  156.1 4.5 collective-permute-start.1
  159.8 51.4 %copy-start.40 = (f32[1024]{0:T(1024)}, f32[1024]{0:T(1024)S(1)}, u32[]{:S(2)}) copy-start(f32[1024]{0:T(1024)S(1)} %get-tuple-element.158) | copy-start | bytes 12292
  159.8 52.1 %copy-start.28 = (f32[1024]{0:T(1024)}, f32[1024]{0:T(1024)S(1)}, u32[]{:S(2)}) copy-start(f32[1024]{0:T(1024)S(1)} %get-tuple-element.155) | copy-start | bytes 12292
  166.3 65.1 %copy-start.3 = (bf16[1024,1024]{1,0:T(8,128)(2,1)}, bf16[1024,1024]{1,0:T(8,128)(2,1)S(1)}, u32[]{:S(2)}) copy-start(bf16[1024,1024]{1,0:T(8,128)(2,1)S(1)} %get-tuple-element.130) | copy-start | bytes 6291460
  166.3 25.5 %copy-start.42 = (bf16[16,1024]{1,0:T(8,128)(2,1)S(1)}, bf16[16,1024]{1,0:T(8,128)(2,1)}, u32[]{:S(2)}) copy-start(bf16[16,1024]{1,0:T(8,128)(2,1)} %param.23) | copy-start | bytes 98308
  166.3 42.6 %copy-start.21 = (f32[16,1024]{1,0:T(8,128)S(1)}, f32[16,1024]{1,0:T(8,128)}, u32[]{:S(2)}) copy-start(f32[16,1024]{1,0:T(8,128)} %param.25) | copy-start | bytes 196612
  168.1 116.7 %all-gather.10.cloned.1.call-start = ((), (), s32[]{:S(2)}) async-start(), calls=%async_computation.4 | async-start | bytes 4718592 | tf_op jit(solution)/shard_map/all_gather | solution.py:811
  169.2 545.1 %reduce-scatter.2.cloned.1.call-start = ((), (), s32[]{:S(2)}) async-start(), calls=%async_computation.5 | async-start | bytes 4718592 | tf_op jit(solution)/shard_map/reduce_scatter | solution.py:964
  231.4 28.1 %copy-start.9 = (bf16[1024,2048]{1,0:T(8,128)(2,1)S(1)}, bf16[1024,2048]{1,0:T(8,128)(2,1)}, u32[]{:S(2)}) copy-start(bf16[1024,2048]{1,0:T(8,128)(2,1)} %fusion.2.nrm_ref) | copy-start | bytes 12582916
  256.0 9.9 %collective-permute-start.2 = (f32[16,1024]{1,0:T(8,128)S(1)}, f32[16,1024]{1,0:T(8,128)S(1)}, u32[]{:S(2)}, u32[]{:S(2)}) collective-permute-start(f32[16,1024]{1,0:T(8,128)S(1)} %fusion.30), channel_id=1, source_target_pairs={{0,4},{1,5},{2,6},{3,7},{8,12},{9,13},{10,14},{11,15},{16,20},{17,... | collective-permute-start | bytes 196616 | tf_op jit(solution)/shard_map/ppermute | solution.py:20
  265.8 14.4 %copy-start.12 = (f32[1024,1024]{1,0:T(8,128)}, f32[1024,1024]{1,0:T(8,128)S(1)}, u32[]{:S(2)}) copy-start(f32[1024,1024]{1,0:T(8,128)S(1)} %fusion.9.z_ref) | copy-start | bytes 12582916
  265.9 14.4 %copy-start.4 = (bf16[1024,1024]{1,0:T(8,128)(2,1)S(1)}, bf16[1024,1024]{1,0:T(8,128)(2,1)}, u32[]{:S(2)}) copy-start(bf16[1024,1024]{1,0:T(8,128)(2,1)} %copy-done.3) | copy-start | bytes 6291460
  265.9 14.4 %copy-start.52 = (f32[1024]{0:T(1024)S(1)}, f32[1024]{0:T(1024)}, u32[]{:S(2)}) copy-start(f32[1024]{0:T(1024)} %param.26) | copy-start | bytes 12292
  439.2 11.3 %collective-permute-start.3 = (f32[16,1024]{1,0:T(8,128)S(1)}, f32[16,1024]{1,0:T(8,128)S(1)}, u32[]{:S(2)}, u32[]{:S(2)}) collective-permute-start(f32[16,1024]{1,0:T(8,128)S(1)} %fusion.29), channel_id=1, source_target_pairs={{4,0},{5,1},{6,2},{7,3},{12,8},{13,9},{14,10},{15,11},{20,16},{21,... | collective-permute-start | bytes 196616 | tf_op jit(solution)/shard_map/ppermute | solution.py:20
  450.5 77.3 %copy-start.5 = (bf16[1024,1024]{1,0:T(8,128)(2,1)S(1)}, bf16[1024,1024]{1,0:T(8,128)(2,1)}, u32[]{:S(2)}) copy-start(bf16[1024,1024]{1,0:T(8,128)(2,1)} %copy-done.3) | copy-start | bytes 6291460
  450.5 77.3 %copy-start.6 = (f32[1024,1024]{1,0:T(8,128)S(1)}, f32[1024,1024]{1,0:T(8,128)}, u32[]{:S(2)}) copy-start(f32[1024,1024]{1,0:T(8,128)} %get-tuple-element.50.ds_ref) | copy-start | bytes 12582916
  450.5 77.3 %copy-start.49 = (f32[1024]{0:T(1024)S(1)}, f32[1024]{0:T(1024)}, u32[]{:S(2)}) copy-start(f32[1024]{0:T(1024)} %param.24) | copy-start | bytes 12292
  536.6 30.0 %copy-start.19 = (bf16[160,1024]{1,0:T(8,128)(2,1)S(1)}, bf16[160,1024]{1,0:T(8,128)(2,1)}, u32[]{:S(2)}) copy-start(bf16[160,1024]{1,0:T(8,128)(2,1)} %copy-done.18) | copy-start | bytes 983044
  536.6 30.0 %copy-start.29 = (f32[1024]{0:T(1024)S(1)}, f32[1024]{0:T(1024)}, u32[]{:S(2)}) copy-start(f32[1024]{0:T(1024)} %copy-done.28) | copy-start | bytes 12292
  536.6 30.0 %copy-start.31 = (f32[1024]{0:T(1024)S(1)}, f32[1024]{0:T(1024)}, u32[]{:S(2)}) copy-start(f32[1024]{0:T(1024)} %copy-done.30) | copy-start | bytes 12292
  536.6 30.0 %copy-start.41 = (f32[1024]{0:T(1024)S(1)}, f32[1024]{0:T(1024)}, u32[]{:S(2)}) copy-start(f32[1024]{0:T(1024)} %copy-done.40) | copy-start | bytes 12292
  536.6 30.0 %copy-start.44 = (f32[3,1024]{1,0:T(4,128)S(1)}, f32[3,1024]{1,0:T(4,128)}, u32[]{:S(2)}) copy-start(f32[3,1024]{1,0:T(4,128)} %copy-done.43) | copy-start | bytes 36868
  566.7 16.5 %copy-start.26 = (bf16[4,1024]{1,0:T(4,128)(2,1)S(1)}, bf16[4,1024]{1,0:T(4,128)(2,1)}, u32[]{:S(2)}) copy-start(bf16[4,1024]{1,0:T(4,128)(2,1)} %param.20) | copy-start | bytes 24580
  566.7 21.8 %copy-start.8 = (bf16[1024,1024]{1,0:T(8,128)(2,1)S(1)}, bf16[1024,1024]{1,0:T(8,128)(2,1)}, u32[]{:S(2)}) copy-start(bf16[1024,1024]{1,0:T(8,128)(2,1)} %copy-done.7) | copy-start | bytes 6291460
  566.7 21.8 %copy-start.16 = (f32[1024,160]{0,1:T(8,128)S(1)}, f32[1024,160]{0,1:T(8,128)}, u32[]{:S(2)}) copy-start(f32[1024,160]{0,1:T(8,128)} %all-reduce.8.cloned.1.call-done) | copy-start | bytes 1966084
  566.7 22.3 %copy-start.58 = (f32[40]{0:T(128)S(1)}, f32[40]{0:T(128)}, u32[]{:S(2)}) copy-start(f32[40]{0:T(128)} %pad.9.clone) | copy-start | bytes 484
  586.9 8.9 %collective-permute-start.4 = (f32[3,1024]{1,0:T(4,128)S(1)}, f32[3,1024]{1,0:T(4,128)S(1)}, u32[]{:S(2)}, u32[]{:S(2)}) collective-permute-start(f32[3,1024]{1,0:T(4,128)S(1)} %pad_maximum_fusion.3), channel_id=1, source_target_pairs={{4,0},{5,1},{6,2},{7,3},{12,8},{13,9},{14,10},{15,11},{20,16},{21,... | collective-permute-start | bytes 36872 | tf_op jit(solution)/shard_map/ppermute | solution.py:20
  601.8 105.1 %copy-start.56 = (bf16[512]{0:T(512)(128)(2,1)S(1)}, bf16[512]{0:T(512)(128)(2,1)}, u32[]{:S(2)}) copy-start(bf16[512]{0:T(512)(128)(2,1)} %param.18) | copy-start | bytes 3076
  601.8 110.1 %copy-start.24 = (f32[4,1,512]{2,1,0:T(1,128)S(1)}, f32[4,1,512]{2,1,0:T(1,128)}, u32[]{:S(2)}) copy-start(f32[4,1,512]{2,1,0:T(1,128)} %copy-done.23) | copy-start | bytes 24580
  698.6 13.3 %copy-start.10 = (bf16[256,2048]{1,0:T(8,128)(2,1)S(1)}, bf16[256,2048]{1,0:T(8,128)(2,1)}, u32[]{:S(2)}) copy-start(bf16[256,2048]{1,0:T(8,128)(2,1)} %hid_ref.1) | copy-start | bytes 3145732
  698.6 13.3 %copy-start.13 = (f32[256,2048]{1,0:T(8,128)S(1)}, f32[256,2048]{1,0:T(8,128)}, u32[]{:S(2)}) copy-start(f32[256,2048]{1,0:T(8,128)} %get-tuple-element.58) | copy-start | bytes 6291460
  698.6 13.6 %copy-start.17 = (f32[256,2048]{1,0:T(8,128)S(1)}, f32[256,2048]{1,0:T(8,128)}, u32[]{:S(2)}) copy-start(f32[256,2048]{1,0:T(8,128)} %get-tuple-element.49) | copy-start | bytes 6291460
  698.6 13.6 %copy-start.51 = (f32[256]{0:T(256)S(1)}, f32[256]{0:T(256)}, u32[]{:S(2)}) copy-start(f32[256]{0:T(256)} %copy-done.50) | copy-start | bytes 3076
  698.6 13.6 %copy-start.54 = (f32[256,1]{0,1:T(1,128)S(1)}, f32[256,1]{0,1:T(1,128)}, u32[]{:S(2)}) copy-start(f32[256,1]{0,1:T(1,128)} %multiply_multiply_fusion.2) | copy-start | bytes 3076
  (23 other events, 154.2 us)
Sparse Core Ops, SparseCore 0:
  9.6 83.4 all-gather.5
  95.6 52.9 all-gather.7
  168.2 41.6 all-reduce.7
  211.7 36.2 all-gather.9
  447.1 55.3 reduce-scatter.1

commit v4 on v3

--- a/solution.py
+++ b/solution.py
@@ -777,6 +777,285 @@
     )(gated, w_out, hidden, teacher, scale, z_gate, scan_out)
 
 
+def front_kernel(n, dps, seqs, subs, lag, hid_ref, gain_ref, cnt_ref, win_ref, wsm_ref,
+                 x_ref, z_ref, nrm_ref, w_ref, prev_ref, total_ref, gfull, ws_ref,
+                 rows_ref, grecv, cnt_one, cnt_two,
+                 ar_send, ar_recv, al_send, al_recv, gs, gr, c1s, c1r, c2s, c2r, hs, hr, ls,
+                 chip_send, chip_recv, core_send, core_recv):
+    dp, seq, t = place()
+    core, hi = dp % 2, dp // 2
+    chips = dps // 2 * seqs
+    chip = hi * seqs + seq
+    rows, wide = hid_ref.shape
+    part = rows // subs
+    share = wide // n
+    wrows = win_ref.shape[1]
+    tile = 512
+    gap = max(subs, lag)
+    partner = dict(dp=hi * 2 + 1 - core)
+    right, left = dict(tensor=lax.rem(t + 1, n)), dict(tensor=lax.rem(t + n - 1, n))
+
+    def owner(q, c):
+        return (q // seqs * 2 + c) * seqs + q % seqs
+
+    def to_chip(q):
+        return dict(dp=q // seqs * 2 + core, seq=q % seqs)
+
+    barrier = pltpu.get_barrier_semaphore()
+    pl.semaphore_signal(barrier, inc=1, device_id=partner, device_id_type=MESH)
+    for ahead in range(1, chips):
+        pl.semaphore_signal(barrier, inc=1, device_id=to_chip(lax.rem(chip + ahead, chips)), device_id_type=MESH)
+    for ahead in range(1, n):
+        pl.semaphore_signal(barrier, inc=1, device_id=dict(tensor=lax.rem(t + ahead, n)), device_id_type=MESH)
+    pl.semaphore_wait(barrier, chips + n - 1)
+
+    def at(o, s):
+        return pl.ds(pl.multiple_of(o * rows + s * part, part), part)
+
+    def ar_copy(o, s):
+        ref = rows_ref.at[at(o, s), :]
+        return mesh_copy(ref, ref, ar_send.at[o * subs + s], ar_recv.at[o * subs + s], **right)
+
+    def al_copy(o, s):
+        ref = rows_ref.at[at(o, s), :]
+        return mesh_copy(ref, ref, al_send.at[o * subs + s], al_recv.at[o * subs + s], **left)
+
+    def g_copy(p, slot):
+        return mesh_copy(gain_ref, grecv.at[slot], gs.at[p], gr.at[slot], tensor=p)
+
+    def block(kind, p):
+        if kind == 0:
+            return w_ref.at[:, pl.ds(pl.multiple_of(p * wrows, wrows), wrows), :]
+        return ws_ref.at[p]
+
+    stored = (win_ref, wsm_ref)
+
+    def chip_copy(kind, q, p):
+        return mesh_copy(stored[kind], block(kind, p), chip_send.at[kind, q], chip_recv.at[kind, p], **to_chip(q))
+
+    def core_copy(kind, p, own):
+        src = stored[kind] if own else block(kind, p)
+        return mesh_copy(src, block(kind, p), core_send.at[kind, p], core_recv.at[kind, p], **partner)
+
+    mine = owner(chip, core)
+
+    def count_one():
+        return mesh_copy(cnt_ref, cnt_one, c1s, c1r, **partner)
+
+    def count_two(q, slot):
+        return mesh_copy(cnt_one, cnt_two.at[slot], c2s.at[q], c2r.at[slot], **to_chip(q))
+
+    def edge_copy():
+        last = x_ref.at[pl.ds(x_ref.shape[0] - 8, 8), :]
+        return mesh_copy(last, prev_ref, hs, hr, seq=lax.rem(seq + 1, seqs))
+
+    def local_copy():
+        return pltpu.make_async_copy(wsm_ref, block(1, mine), ls)
+
+    for ahead in range(1, n):
+        g_copy(lax.rem(t + ahead, n), t).start()
+    count_one().start()
+    rows_ref[pl.ds(pl.multiple_of(t * rows, rows), rows), :] = hid_ref[...]
+
+    @pl.loop(0, subs)
+    def _(s):
+        @pl.when(t < n - 1)
+        def _():
+            ar_copy(t, s).start()
+
+        @pl.when(t > 0)
+        def _():
+            al_copy(t, s).start()
+
+    def share_out(kind):
+        for ahead in range(1, chips):
+            chip_copy(kind, lax.rem(chip + ahead, chips), mine).start()
+        core_copy(kind, mine, True).start()
+
+    share_out(1)
+    share_out(0)
+    local_copy().start()
+    w_ref[:, pl.ds(pl.multiple_of(mine * wrows, wrows), wrows), :] = win_ref[...]
+
+    gfull[...] = jnp.zeros_like(gfull)
+    for ahead in range(1, n):
+        p = lax.rem(t + ahead, n)
+        g_copy(p, p).wait_recv()
+    grecv[t] = gain_ref[...]
+    for p in range(n):
+        gfull[:, p * share:(p + 1) * share] = grecv[p]
+    count_one().wait_recv()
+    count_one().wait_send()
+    cnt_one[...] = cnt_one[...] + cnt_ref[...]
+    for ahead in range(1, chips):
+        count_two(lax.rem(chip + ahead, chips), chip).start()
+
+    def normalize(o):
+        @pl.loop(0, subs)
+        def _(s):
+            here = at(o, s)
+            values = rows_ref[here, :].astype(F32)
+            inv = lax.rsqrt(jnp.mean(values * values, axis=1, keepdims=True) + EPS)
+            nrm_ref[here, :] = (values * inv * gfull[0:1, :]).astype(BF16)
+
+    def project(o):
+        here = pl.ds(pl.multiple_of(o * rows, rows), rows)
+        for k, dst in enumerate((x_ref, z_ref)):
+            lanes = dst.shape[1]
+            width = min(tile, lanes)
+
+            @pl.loop(0, lanes // width)
+            def _(j):
+                cols = pl.ds(pl.multiple_of(j * width, width), width)
+                dst[here, cols] = jnp.dot(nrm_ref[here, :], w_ref[k, :, cols], preferred_element_type=F32)
+
+    def turn(d, o):
+        final = jnp.where(o == 0, (n - 1) * gap + 1, (n - 2 - o) * gap + lag)
+        return jnp.where(d == n - 1, final, (d - o) * gap)
+
+    weights_at = (n - 1) * gap
+
+    def step(g, _):
+        @pl.when(g == 0)
+        def _():
+            normalize(t)
+
+        @pl.when(g == weights_at)
+        def _():
+            for kind in (1, 0):
+                for ahead in range(1, chips):
+                    q = lax.rem(chip + ahead, chips)
+                    chip_copy(kind, q, owner(q, core)).wait_recv()
+                    core_copy(kind, owner(q, core), False).start()
+            for kind in (1, 0):
+                for q in range(chips):
+                    core_copy(kind, owner(q, 1 - core), True).wait_recv()
+            project(t)
+
+        @pl.loop(0, n)
+        def _(o):
+            s_right = g - turn(t, o)
+            s_left = g - turn(n - 1 - t, n - 1 - o)
+
+            @pl.when(jnp.logical_and(o < t, jnp.logical_and(s_right >= 0, s_right < subs)))
+            def _():
+                ar_copy(o, s_right).wait_recv()
+
+                @pl.when(t < n - 1)
+                def _():
+                    ar_copy(o, s_right).start()
+
+            @pl.when(jnp.logical_and(o > t, jnp.logical_and(s_left >= 0, s_left < subs)))
+            def _():
+                al_copy(o, s_left).wait_recv()
+
+                @pl.when(t > 0)
+                def _():
+                    al_copy(o, s_left).start()
+
+            landed = jnp.where(o < t, s_right, s_left) - subs + 1
+
+            @pl.when(jnp.logical_and(o != t, landed == 0))
+            def _():
+                normalize(o)
+
+            ripe = jnp.where(g == weights_at, landed >= 0, jnp.logical_and(g > weights_at, landed == 0))
+
+            @pl.when(jnp.logical_and(o != t, ripe))
+            def _():
+                project(o)
+
+        return 0
+
+    steps = weights_at + 1 + subs
+    lax.fori_loop(0, steps, step, 0)
+
+    @pl.when(seq < seqs - 1)
+    def _():
+        edge_copy().start()
+
+    total_ref[...] = cnt_one[...]
+    for ahead in range(1, chips):
+        q = lax.rem(chip + ahead, chips)
+        count_two(q, q).wait_recv()
+        total_ref[...] = total_ref[...] + cnt_two[q]
+
+    @pl.when(seq == 0)
+    def _():
+        prev_ref[...] = jnp.zeros_like(prev_ref)
+
+    @pl.when(seq > 0)
+    def _():
+        edge_copy().wait_recv()
+
+    @pl.when(seq < seqs - 1)
+    def _():
+        edge_copy().wait_send()
+
+    local_copy().wait()
+    for kind in range(2):
+        for ahead in range(1, chips):
+            chip_copy(kind, lax.rem(chip + ahead, chips), mine).wait_send()
+        for q in range(chips):
+            core_copy(kind, owner(q, core), False).wait_send()
+    for ahead in range(1, chips):
+        count_two(lax.rem(chip + ahead, chips), chip).wait_send()
+    for ahead in range(1, n):
+        g_copy(lax.rem(t + ahead, n), t).wait_send()
+
+    @pl.loop(0, n * subs)
+    def _(i):
+        o, s = i // subs, i % subs
+
+        @pl.when(jnp.logical_and(o <= t, t < n - 1))
+        def _():
+            ar_copy(o, s).wait_send()
+
+        @pl.when(jnp.logical_and(o >= t, t > 0))
+        def _():
+            al_copy(o, s).wait_send()
+
+
+def front(hidden, gain, count, w_in, w_small):
+    n, dps, seqs = (lax.axis_size(axis) for axis in ("tensor", "dp", "seq"))
+    parts = dps * seqs
+    chips = parts // 2
+    rows, wide = hidden.shape
+    lanes = w_in.shape[2]
+    tokens = rows * n
+    subs = max(1, rows // 32)
+    vmem, hbm = pl.BlockSpec(memory_space=pltpu.VMEM), pl.BlockSpec(memory_space=pl.ANY)
+    dma = pltpu.SemaphoreType.DMA
+    many, few, peers = dma((n * subs,)), dma((chips,)), dma((n,))
+    return pl.pallas_call(
+        functools.partial(front_kernel, n, dps, seqs, subs, 2),
+        out_shape=[
+            jax.ShapeDtypeStruct((tokens, lanes), F32),
+            jax.ShapeDtypeStruct((tokens, lanes), F32),
+            jax.ShapeDtypeStruct((tokens, wide), BF16),
+            jax.ShapeDtypeStruct((2, wide, lanes), BF16),
+            jax.ShapeDtypeStruct((8, lanes), F32),
+            jax.ShapeDtypeStruct(count.shape, F32),
+            jax.ShapeDtypeStruct((gain.shape[0], wide), F32),
+            jax.ShapeDtypeStruct((parts,) + w_small.shape, BF16),
+        ],
+        in_specs=[vmem] * 5,
+        out_specs=[vmem] * 7 + [hbm],
+        scratch_shapes=[
+            pltpu.VMEM((tokens, wide), BF16),
+            pltpu.VMEM((n,) + gain.shape, F32),
+            pltpu.VMEM(count.shape, F32),
+            pltpu.VMEM((chips,) + count.shape, F32),
+            many, many, many, many, peers, peers, dma, dma, few, few, dma, dma, dma,
+            dma((2, chips)), dma((2, parts)), dma((2, parts)), dma((2, parts)),
+        ],
+        compiler_params=pltpu.CompilerParams(
+            collective_id=3, has_side_effects=True, vmem_limit_bytes=60 << 20
+        ),
+        name="front",
+    )(hidden, gain, count, w_in, w_small)
+
+
 def on_device(
     hidden_in,
     teacher,
@@ -800,33 +1079,30 @@
     back_rows = conv_taps - 1
     row_start = lax.axis_index("tensor") * row_share
     valid_mask = (segment_ids != 0).astype(jnp.float32)
-    count_here = jnp.sum((segment_ids != 0).astype(jnp.int32))
-    count_pair = (
-        jnp.stack([count_here // 32, count_here % 32]).astype(jnp.float32).astype(jnp.bfloat16)
+    count_here = jnp.full((8, 128), jnp.sum(valid_mask))
+    parts = lax.axis_size(("dp", "seq"))
+    gain_tile = jnp.broadcast_to(norm_gain.astype(F32)[None], (8, norm_gain.shape[0]))
+    x_cols, dt_rows = xproj_weight.shape[1], dtproj_weight.shape[0]
+    pad = -(x_cols + dt_rows) % 16
+    w_small = jnp.concatenate([xproj_weight.T, dtproj_weight, jnp.zeros((pad, chan_lanes), BF16)], 0)
+    x_inner, z_gate, normalized_rows, w_in, prev_rows, total, gain_rows, w_small = front(
+        hidden_in,
+        gain_tile,
+        count_here,
+        jnp.swapaxes(input_projection_weight, 0, 1),
+        w_small,
     )
-    w_in, w_x, w_dt, w_out, count_pairs = (
-        lax.all_gather(jnp.swapaxes(input_projection_weight, 0, 1), ("dp", "seq"), axis=1, tiled=True),
-        lax.all_gather(xproj_weight, ("dp", "seq"), axis=1, tiled=True),
-        lax.all_gather(dtproj_weight, ("dp", "seq"), axis=0, tiled=True),
-        lax.all_gather(output_projection_weight.T, ("dp", "seq"), axis=0, tiled=True),
-        lax.all_gather(count_pair, ("dp", "seq"), axis=0, tiled=True),
-    )
-    count_pairs = count_pairs.astype(jnp.float32).reshape(-1, 2)
-    total_count = 32.0 * jnp.sum(count_pairs[:, 0]) + jnp.sum(count_pairs[:, 1])
-    full_rows_b, full_gain_b = (
-        lax.all_gather(hidden_in, "tensor", axis=0, tiled=True),
-        lax.all_gather(norm_gain, "tensor", axis=0, tiled=True),
-    )
-    full_rows = full_rows_b.astype(jnp.float32)
-    full_gain = full_gain_b.astype(jnp.float32)
-    inv_rms = lax.rsqrt(jnp.mean(full_rows * full_rows, axis=1, keepdims=True) + EPS)
-    normalized_rows = (full_rows * inv_rms * full_gain[None]).astype(jnp.bfloat16)
-    x_inner = jnp.dot(normalized_rows, w_in[0], preferred_element_type=F32)
-    z_gate = jnp.dot(normalized_rows, w_in[1], preferred_element_type=F32)
-    seg_float = segment_ids.astype(jnp.float32)
-    prev_x, prev_seg = passed_along(
-        (x_inner[tok_rows - back_rows :], seg_float[tok_rows - back_rows :]), "seq", 1
-    )
+    w_out_rows, z_gate = lax.optimization_barrier((output_projection_weight.T, z_gate))
+    w_out = lax.all_gather(w_out_rows, ("dp", "seq"), axis=0, tiled=True)
+    total_count = total[0, 0]
+    w_x = w_small[:, :x_cols].reshape(parts * x_cols, chan_lanes)
+    w_dt = w_small[:, x_cols : x_cols + dt_rows].reshape(parts * dt_rows, chan_lanes)
+    share_rows = hidden_in.astype(F32)
+    full_gain = gain_rows[0]
+    inv_share = lax.rsqrt(jnp.mean(share_rows * share_rows, axis=1, keepdims=True) + EPS)
+    seg_float = segment_ids.astype(F32)
+    prev_x = prev_rows[8 - back_rows :]
+    prev_seg = jnp.where(lax.axis_index("seq") > 0, seg_float[:1], jnp.zeros((back_rows,), F32))
     ext_x = jnp.concatenate([prev_x, x_inner], 0)
     ext_seg = jnp.concatenate([prev_seg, seg_float], 0)
     tap_keeps = []
@@ -842,7 +1118,7 @@
         )
     x_low = jax.nn.silu(conv_sum).astype(jnp.bfloat16)
     x_float = x_low.astype(jnp.float32)
-    mixed_rows = lax.psum(jnp.dot(x_low, w_x, preferred_element_type=jnp.float32), "tensor")
+    mixed_rows = lax.psum(jnp.einsum("te,je->tj", x_low, w_x, preferred_element_type=F32), "tensor")
     rank_width = w_dt.shape[0]
     state_width = (mixed_rows.shape[1] - rank_width) // 2
     step_low = mixed_rows[:, :rank_width].astype(jnp.bfloat16)
@@ -867,7 +1143,6 @@
     scan_out = y_rows + d_skip[None] * x_float
     gate_act = jax.nn.silu(z_gate)
     gated_output_rows = (scan_out * gate_act).astype(jnp.bfloat16)
-    share_rows = hidden_in.astype(F32)
     valid_share = lax.dynamic_slice_in_dim(valid_mask, row_start, row_share, 0)
     total_tokens = float(tok_rows * lax.axis_size(("dp", "seq")))
     scale = (total_tokens / total_count * valid_share)[:, None]
@@ -897,7 +1172,7 @@
     d_wx = jnp.einsum("te,tj->ej", x_low, d_mixed_low, preferred_element_type=jnp.float32)
     d_wx_rank = d_wx[:, :rank_width]
     d_wx_state = d_wx[:, rank_width:]
-    d_xlow = d_xlow + jnp.einsum("tj,ej->te", d_mixed_low, w_x, preferred_element_type=jnp.float32)
+    d_xlow = d_xlow + jnp.dot(d_mixed_low, w_x, preferred_element_type=F32)
     d_conv = d_xlow * silu_slope(conv_sum)
     conv_bias_part = jnp.sum(d_conv, axis=0)
     conv_weight_rows = []
@@ -933,7 +1208,6 @@
     front_grad = jnp.stack(front_rows, 0)
     carried_grad = passed_along(front_grad, "seq", -1)
     d_x = d_x.at[tok_rows - back_rows :].add(carried_grad)
-    parts = lax.axis_size(("dp", "seq"))
     small = jnp.concatenate(
         [
             d_wx_rank.T.reshape(parts, -1, chan_lanes),
@@ -948,7 +1222,6 @@
     )
     d_norm_share, g_in, g_small, g_whole = tail(d_x.astype(BF16), d_z, w_in, normalized_rows, small, whole)
     g_in = jnp.swapaxes(g_in, 0, 1)
-    inv_share = lax.dynamic_slice_in_dim(inv_rms, row_start, row_share, 0)
     inner_sum = jnp.sum(d_norm_share * full_gain[None] * share_rows, axis=1, keepdims=True)
     inv_cube = inv_share * inv_share * inv_share
     input_grad = (

time: 732 us -> 684 us (0.934)
  Pallas kernels: 365 us -> 453 us
  waiting for transfers between devices: 102 us -> 37.2 us
  blocking collectives: 87 us -> 28.2 us
  matrix products: 50.2 us -> 36.6 us
  starting transfers between devices: 14.7 us -> 6.48 us
  other arithmetic: 46.3 us -> 54.3 us
    all_gather x3 -> x1, waiting for transfers between devices: 97.3 us -> 0.01 us  [on_device(): w_out = lax.all_gather(w_out_rows, ('dp', 'seq'), axis=0, tiled=True)]
    pallas_call x0 -> x1, Pallas kernels: none -> 91 us  [front(): pl.pallas_call(functools.partial(front_kernel, n, dps, seqs, subs, 2), ou...]
    all_gather x3 -> x0, blocking collectives: 44.8 us -> none  [the longest x1 16.4 us: on_device(): lax.all_gather(dtproj_weight, ('dp', 'seq'), axis=0, tiled=True)]
    psum x1, waiting for transfers between devices: 0.01 us -> 30 us  [on_device(): lax.psum(jnp.einsum('te,je->tj', x_low, w_x, preferred_element_type=F32),...]
    unnamed x1 -> x0, blocking collectives: 14.9 us -> none
    dot_general x4 -> x2, matrix products: 31.8 us -> 19.1 us  [the longest x1 17.4 us: on_device(): d_xlow = d_xlow + jnp.dot(d_mixed_low, w_x, preferred_element_type=F32)]
    ppermute x5 -> x3, starting transfers between devices: 14.5 us -> 6.18 us  [passed_along(): return lax.ppermute(x, axis, pairs)]
    convert_element_type x1, other arithmetic: 5.15 us -> 12.9 us  [on_device(): x_low = jax.nn.silu(conv_sum).astype(jnp.bfloat16)]
  transfers between devices with their start and end apart: 10 -> 6, of which waited for: 4 -> 3; matrix products, arithmetic and copies ran while one was open for 17% -> 15% of each run, Pallas kernels for 29% -> 31%
where the time goes in v4:
time: 684 us; the launch traced here: 679 us
  Pallas kernels  453 us (66%)
  other arithmetic  54.3 us (8%)
  local copies, waits for them, and re-layouts  45.7 us (7%)
  waiting for transfers between devices  37.2 us (5%)
  matrix products  36.6 us (5%)
  blocking collectives  28.2 us (4%)
  between operations  18.2 us (3%)
    pallas_call x1, Pallas kernels, middle(): pl.pallas_call(functools.partial(mid_kernel, n, subs, 2), out_shape=[jax....  138 us
    pallas_call x1, Pallas kernels, tail(): pl.pallas_call(functools.partial(tail_kernel, n, dps, seqs, subs, 2), out...  97.7 us
    pallas_call x1, Pallas kernels, front(): pl.pallas_call(functools.partial(front_kernel, n, dps, seqs, subs, 2), ou...  91 us
    pallas_call x1, Pallas kernels, bwd(): pl.pallas_call(functools.partial(bwd_kernel, unroll=unroll), grid=grid, i...  77.3 us
    psum x1, waiting for transfers between devices, on_device(): lax.psum(jnp.einsum('te,je->tj', x_low, w_x, preferred_element_type=F32),...  30 us
    psum x1, blocking collectives, on_device(): lax.psum(jnp.concatenate([d_rank, d_b_part, d_c_part], 1), 'tensor')  28.2 us
    pallas_call x1, Pallas kernels, fwd(): pl.pallas_call(functools.partial(fwd_kernel, unroll=unroll), grid=grid, i...  24.3 us
    dot_general x1, matrix products, on_device(): d_xlow = d_xlow + jnp.dot(d_mixed_low, w_x, preferred_element_type=F32)  17.4 us
  transfers between devices with their start and end apart: 6, of which 3 were waited for; matrix products, arithmetic and copies ran while one was open for 15% of the time, Pallas kernels for 31%

profile of v4, /device:TPU:0, one launch (start us, length us, event | category | flops | bytes accessed | tf_op | source)
XLA Modules:
  0.0 679.4 jit_solution(14126490510539009942)
XLA Ops:
  8.1 1.3 fusion.37
  14.2 2.5 copy.59
  16.8 1.5 maximum_maximum_fusion.1.wsm_ref
  18.3 1.2 broadcast_in_dim.51.cnt_ref
  19.5 1.3 broadcast_in_dim.50.gain_ref
  20.8 91.0 %front.1 = (f32[1024,1024]{1,0:T(8,128)}, f32[1024,1024]{1,0:T(8,128)}, bf16[1024,2048]{1,0:T(8,128)(2,1)}, bf16[2,2048,1024]{2,1,0:T(8,128)(2,1)}, f32[8,1024]{...) custom-call(bf16[256,2048]{1,0:T(8,128)(2,1)} %hid_ref.3, ...), custom_call_target="tpu_custom_call" | custom-call | tf_op jit(solution)/shard_map/front/pallas_call | solution.py:1030
  113.7 12.9 %multiply_convert_fusion.1 = (bf16[1024,1024]{1,0:T(8,128)(2,1)S(1)}, f32[1024,1024]{1,0:T(8,128)}) fusion(f32[1024]{0:T(1024)S(1)} %get-tuple-element.165, f32[1024,1024]{1,0:T(8,128)} %get-tuple-element.55, f32[1024]{0:T(1024)S(1)} %bitcast.96, f32[1024]{0:T(1024)S(1)} %get-tuple-element.170, f32[3,1024]{1,0:T(4,128)S(1)} %slice.181, ...), kind=kLoop, calls=%fused_computation.24 | loop fusion | flops 20971520 | bytes 10534912 | tf_op jit(solution)/shard_map/convert_element_type | solution.py:1119
  126.7 1.7 fusion.49
  130.3 1.1 slice.192
  131.7 1.2 slice.195
  132.9 1.4 slice.196
  139.2 30.0 %all-reduce.8.cloned.1.call-done = f32[1024,160]{0,1:T(8,128)} async-done(((f32[1024,160]{0,1:T(8,128)}), f32[1024,160]{0,1:T(8,128)}) %all-reduce.8.cloned.1.call-update) | async-done | bytes 655376 | tf_op jit(solution)/shard_map/psum | solution.py:1121
  175.0 1.8 copy_bitcast_fusion.1
  177.1 1.4 compare_select_fusion.1
  178.5 8.7 %fusion.41 = (f32[1024]{0:T(1024)S(1)}, f32[1024,1024]{1,0:T(8,128)}, f32[1024,1024]{1,0:T(8,128)}, f32[1024,1024]{1,0:T(8,128)}) fusion(f32[1024]{0:T(1024)} %param.24, pred[1024]{0:T(1024)(128)(4,1)} %get-tuple-element.168, bf16[1024,1024]{1,0:T(8,128)(2,1)S(1)} %get-tuple-element.135, bf16[128,1024]{1,0:T(8,128)(2,1)S(1)} %bitcast.79, ...), kind=kOutput, calls=%fused_computation.118 | convolution fusion | flops 279968768 | bytes 15213568 | tf_op jit(solution)/shard_map/dot_general | solution.py:1127
  187.2 24.3 %scan_forward.1 = (f32[1024,1024]{1,0:T(8,128)S(1)}, f32[8,16,1024]{2,1,0:T(8,128)S(1)}, f32[16,1024]{1,0:T(8,128)S(1)}) custom-call(f32[1024,1024]{1,0:T(8,128)} %get-tuple-element.134.stepd_ref, f32[1024,1024]{1,0:T(8,128)} %get-tuple-element.142.u_ref, f32[64,16,32]{2,1,0:T(8,128)S(1)} %pad_maximum_fusion.2.bc_ref, ...), custom_call_target="tpu_custom_call" | custom-call | tf_op jit(solution)/shard_map/scan_forward/pallas_call | solution.py:58
  211.6 2.0 copy-done.1
  213.6 3.4 collective-permute-start
  217.7 1.2 collective-permute-done.sin_ref
  218.9 13.0 %scan_correct.1 = (f32[1024,1024]{1,0:T(8,128)S(1)}, f32[8,16,1024]{2,1,0:T(8,128)S(1)}) custom-call(s32[8]{0:T(128)S(1)} %compare_convert_fusion.3.alive_ref, f32[1024,1024]{1,0:T(8,128)} %copy-done.1, f32[1024,1024]{1,0:T(8,128)} %get-tuple-element.134.stepd_ref, bf16[1024,256]{1,0:T(8,128)(2,1)S(1)} %get-tuple-element.158.cdiag_ref, ...), custom_call_target="tpu_custom_call" | custom-call | tf_op jit(solution)/shard_map/scan_correct/pallas_call | solution.py:212
  232.0 4.4 multiply_convert_fusion
  236.4 138.3 %middle.1 = (bf16[256,2048]{1,0:T(8,128)(2,1)}, f32[256,2048]{1,0:T(8,128)}, bf16[1024,2048]{1,0:T(8,128)(2,1)}, f32[1024,1024]{1,0:T(8,128)}, bf16[1024,1024]{1,0:T(8,128)(2,1)}) custom-call(bf16[1024,1024]{1,0:T(8,128)(2,1)} %get-tuple-element.131.gated_ref, bf16[2048,1024]{1,0:T(8,128)(2,1)} %all-gather.2.cloned.1.call-done.w_ref, ...), custom_call_target="tpu_custom_call" | custom-call | tf_op jit(solution)/shard_map/middle/pallas_call | solution.py:754
  374.8 2.2 copy-done
  376.9 11.1 %scan_entry.1 = f32[16,1024]{1,0:T(8,128)S(1)} custom-call(s32[8]{0:T(128)S(1)} %compare_convert_fusion.3.alive_ref, f32[1024,1024]{1,0:T(8,128)S(1)} %copy-done, f32[1024,1024]{1,0:T(8,128)} %get-tuple-element.68.ds_ref, f32[64,16,32]{2,1,0:T(8,128)S(1)} %pad_maximum_fusion.2.bc_ref, f32[16,1024]{1,0:T(8,128)S(1)} %fusion.24.rate_ref), custom_call_target="tpu_custom_call" | custom-call | tf_op jit(solution)/shard_map/scan_entry/pallas_call | solution.py:257
  388.1 1.5 collective-permute-start.1
  389.6 6.2 convolution_convert_fusion
  395.9 6.0 collective-permute-done.1.gin_ref
  401.8 77.3 %scan_backward.1 = (f32[1024,1024]{1,0:T(8,128)S(1)}, f32[1024,1024]{1,0:T(8,128)}, f32[1,64,256]{2,1,0:T(8,128)S(1)}, f32[1,64,256]{2,1,0:T(8,128)S(1)}, f32[16,1024]{1,0:T(8,128)S(1)}) custom-call(f32[1024,1024]{1,0:T(8,128)} %get-tuple-element.134.stepd_ref, f32[1024,1024]{1,0:T(8,128)} %get-tuple-element.142.u_ref, ...), custom_call_target="tpu_custom_call" | custom-call | tf_op jit(solution)/shard_map/scan_backward/pallas_call | solution.py:142
  479.2 6.3 fusion.38
  485.5 1.6 fusion.15
  487.9 1.1 pad_maximum_fusion.1
  489.0 28.2 %all-reduce.9 = bf16[1024,160]{0,1:T(8,128)(2,1)S(1)} all-reduce(f32[1024,160]{0,1:T(8,128)S(1)} %pad_maximum_fusion.1), channel_id=1, replica_groups=mesh['dp'=4,'seq'=2,'tensor'=4] {'tensor'}, use_global_device_ids=true, to_apply=%region_6.7 | all-reduce | flops 163840 | bytes 983040 | tf_op jit(solution)/shard_map/psum | solution.py:1170
  517.2 17.4 %multiply_reduce_fusion.1 = (f32[1024]{0:T(1024)}, f32[1024]{0:T(1024)}, f32[1024]{0:T(1024)}, f32[1024]{0:T(1024)}, f32[1024]{0:T(1024)}, /*index=5*/f32[1024,1024]{1,0:T(8,128)S(1)}) fusion(f32[1024,1024]{1,0:T(8,128)} %get-tuple-element.55, f32[3,1024]{1,0:T(4,128)S(1)} %copy-done.27, f32[1024]{0:T(1024)S(1)} %copy-done.41, f32[1024]{0:T(1024)S(1)} %copy-done.29, ...), kind=kOutput, calls=%fused_computation.15 | convolution fusion | flops 372239360 | bytes 25878528 | tf_op jit(solution)/shard_map/dot_general | solution.py:1175
  534.7 3.9 multiply_multiply_fusion.1
  538.6 1.3 collective-permute-start.2
  541.7 2.4 maximum_maximum_fusion.sm_ref
  544.3 4.5 multiply_add_fusion
  548.8 1.3 concatenate.45.all_ref
  550.9 1.4 scatter-add.4
  552.3 3.8 convert_element_type.120.dx_ref
  556.1 97.7 %tail_sums.1 = (f32[256,2048]{1,0:T(8,128)}, f32[2,256,1024]{2,1,0:T(8,128)}, f32[40,1024]{1,0:T(8,128)}, f32[32,1024]{1,0:T(8,128)}) custom-call(bf16[1024,1024]{1,0:T(8,128)(2,1)} %convert_element_type.120.dx_ref, bf16[1024,1024]{1,0:T(8,128)(2,1)} %get-tuple-element.74.dz_ref, bf16[2,2048,1024]{2,1,0:T(8,128)(2,1)} %get-tuple-element.75.w_ref, ...), custom_call_target="tpu_custom_call" | custom-call | tf_op jit(solution)/shard_map/tail_sums/pallas_call | solution.py:532
  653.9 1.5 slice.216
  655.4 1.6 slice.222
  656.9 4.5 copy.54
  663.3 1.5 fusion.46
  666.1 2.0 fusion.11
  668.1 1.1 convert_bitcast_fusion
  669.2 1.3 copy.55
  (181 shorter events, 26.8 us)
Async XLA Ops:
  8.0 161.1 %all-reduce.8.cloned.1.call-start = ((), (), s32[]{:S(2)}) async-start(), calls=%async_computation.1 | async-start | bytes 1310720 | tf_op jit(solution)/shard_map/psum | solution.py:1121
  10.8 115.8 %copy-start.30 = (f32[1024]{0:T(1024)}, f32[1024]{0:T(1024)S(1)}, u32[]{:S(2)}) copy-start(f32[1024]{0:T(1024)S(1)} %get-tuple-element.165) | copy-start | bytes 12292
  13.3 123.8 %copy-start.40 = (f32[1024]{0:T(1024)}, f32[1024]{0:T(1024)S(1)}, u32[]{:S(2)}) copy-start(f32[1024]{0:T(1024)S(1)} %get-tuple-element.170) | copy-start | bytes 12292
  13.3 125.1 %copy-start.28 = (f32[1024]{0:T(1024)}, f32[1024]{0:T(1024)S(1)}, u32[]{:S(2)}) copy-start(f32[1024]{0:T(1024)S(1)} %get-tuple-element.167) | copy-start | bytes 12292
  14.2 112.5 %copy-start.32 = (f32[1,1024]{1,0:T(1,128)}, f32[1,1024]{1,0:T(1,128)S(1)}, u32[]{:S(2)}) copy-start(f32[1,1024]{1,0:T(1,128)S(1)} %get-tuple-element.153) | copy-start | bytes 12292
  14.2 112.5 %copy-start.34 = (f32[1,1024]{1,0:T(1,128)}, f32[1,1024]{1,0:T(1,128)S(1)}, u32[]{:S(2)}) copy-start(f32[1,1024]{1,0:T(1,128)S(1)} %get-tuple-element.154) | copy-start | bytes 12292
  14.2 112.5 %copy-start.36 = (f32[1,1024]{1,0:T(1,128)}, f32[1,1024]{1,0:T(1,128)S(1)}, u32[]{:S(2)}) copy-start(f32[1,1024]{1,0:T(1,128)S(1)} %get-tuple-element.155) | copy-start | bytes 12292
  14.2 112.5 %copy-start.38 = (f32[1,1024]{1,0:T(1,128)}, f32[1,1024]{1,0:T(1,128)S(1)}, u32[]{:S(2)}) copy-start(f32[1,1024]{1,0:T(1,128)S(1)} %get-tuple-element.156) | copy-start | bytes 12292
  112.6 14.1 %copy-start.26 = (f32[3,1024]{1,0:T(4,128)}, f32[3,1024]{1,0:T(4,128)S(1)}, u32[]{:S(2)}) copy-start(f32[3,1024]{1,0:T(4,128)S(1)} %slice.181) | copy-start | bytes 36868
  113.7 13.0 %copy-start.18 = (bf16[160,1024]{1,0:T(8,128)(2,1)}, bf16[160,1024]{1,0:T(8,128)(2,1)S(1)}, u32[]{:S(2)}) copy-start(bf16[160,1024]{1,0:T(8,128)(2,1)S(1)} %reshape.234) | copy-start | bytes 983044
  113.7 14.7 %copy-start.22 = (bf16[1024,256]{1,0:T(8,128)(2,1)S(1)}, bf16[1024,256]{1,0:T(8,128)(2,1)}, u32[]{:S(2)}) copy-start(bf16[1024,256]{1,0:T(8,128)(2,1)} %param.27) | copy-start | bytes 1572868
  126.7 60.6 %copy-start.3 = (bf16[1024,1024]{1,0:T(8,128)(2,1)}, bf16[1024,1024]{1,0:T(8,128)(2,1)S(1)}, u32[]{:S(2)}) copy-start(bf16[1024,1024]{1,0:T(8,128)(2,1)S(1)} %get-tuple-element.135) | copy-start | bytes 6291460
  126.7 12.4 %copy-start.21 = (f32[16,1024]{1,0:T(8,128)S(1)}, f32[16,1024]{1,0:T(8,128)}, u32[]{:S(2)}) copy-start(f32[16,1024]{1,0:T(8,128)} %param.25) | copy-start | bytes 196612
  128.4 108.0 %all-gather.2.cloned.1.call-start = ((), (), s32[]{:S(2)}) async-start(), calls=%async_computation.2 | async-start | bytes 4718592 | tf_op jit(solution)/shard_map/all_gather | solution.py:1096
  129.5 538.5 %reduce-scatter.2.cloned.1.call-start = ((), (), s32[]{:S(2)}) async-start(), calls=%async_computation.3 | async-start | bytes 4718592 | tf_op jit(solution)/shard_map/reduce_scatter | solution.py:1237
  131.4 47.1 %copy-start.15 = (bf16[8,16,1024]{2,1,0:T(8,128)(2,1)}, bf16[8,16,1024]{2,1,0:T(8,128)(2,1)S(1)}, u32[]{:S(2)}) copy-start(bf16[8,16,1024]{2,1,0:T(8,128)(2,1)S(1)} %slice.192) | copy-start | bytes 786436
  136.4 37.6 %copy-start.48 = (s32[256]{0:T(256)}, s32[256]{0:T(256)S(1)}, u32[]{:S(2)}) copy-start(s32[256]{0:T(256)S(1)} %and_select_fusion.1) | copy-start | bytes 3076
  213.6 5.3 collective-permute-start
  218.9 13.1 %copy-start.4 = (bf16[1024,1024]{1,0:T(8,128)(2,1)S(1)}, bf16[1024,1024]{1,0:T(8,128)(2,1)}, u32[]{:S(2)}) copy-start(bf16[1024,1024]{1,0:T(8,128)(2,1)} %copy-done.3) | copy-start | bytes 6291460
  218.9 13.1 %copy-start.9 = (f32[1024,1024]{1,0:T(8,128)S(1)}, f32[1024,1024]{1,0:T(8,128)}, u32[]{:S(2)}) copy-start(f32[1024,1024]{1,0:T(8,128)} %get-tuple-element.62.z_ref) | copy-start | bytes 12582916
  218.9 13.1 %copy-start.46 = (f32[1024]{0:T(1024)S(1)}, f32[1024]{0:T(1024)}, u32[]{:S(2)}) copy-start(f32[1024]{0:T(1024)} %param.26) | copy-start | bytes 12292
  376.9 12.7 %copy-start.11 = (bf16[1024,1024]{1,0:T(8,128)(2,1)S(1)}, bf16[1024,1024]{1,0:T(8,128)(2,1)}, u32[]{:S(2)}) copy-start(bf16[1024,1024]{1,0:T(8,128)(2,1)} %get-tuple-element.131.gated_ref) | copy-start | bytes 6291460
  376.9 12.7 %copy-start.56 = (bf16[1024,2048]{1,0:T(8,128)(2,1)S(1)}, bf16[1024,2048]{1,0:T(8,128)(2,1)}, u32[]{:S(2)}) copy-start(bf16[1024,2048]{1,0:T(8,128)(2,1)} %get-tuple-element.82) | copy-start | bytes 12582916
  388.1 13.7 %collective-permute-start.1 = (f32[16,1024]{1,0:T(8,128)S(1)}, f32[16,1024]{1,0:T(8,128)S(1)}, u32[]{:S(2)}, u32[]{:S(2)}) collective-permute-start(f32[16,1024]{1,0:T(8,128)S(1)} %fusion.25), channel_id=1, source_target_pairs={{4,0},{5,1},{6,2},{7,3},{12,8},{13,9},{14,10},{15,11},{20,16},{21,... | collective-permute-start | bytes 196616 | tf_op jit(solution)/shard_map/ppermute | solution.py:20
  401.8 77.3 %copy-start.5 = (bf16[1024,1024]{1,0:T(8,128)(2,1)S(1)}, bf16[1024,1024]{1,0:T(8,128)(2,1)}, u32[]{:S(2)}) copy-start(bf16[1024,1024]{1,0:T(8,128)(2,1)} %copy-done.3) | copy-start | bytes 6291460
  401.8 77.3 %copy-start.7 = (f32[1024,1024]{1,0:T(8,128)S(1)}, f32[1024,1024]{1,0:T(8,128)}, u32[]{:S(2)}) copy-start(f32[1024,1024]{1,0:T(8,128)} %get-tuple-element.68.ds_ref) | copy-start | bytes 12582916
  401.8 77.3 %copy-start.45 = (f32[1024]{0:T(1024)S(1)}, f32[1024]{0:T(1024)}, u32[]{:S(2)}) copy-start(f32[1024]{0:T(1024)} %param.24) | copy-start | bytes 12292
  479.1 6.3 copy-start.2
  479.2 6.4 copy-start.16
  485.4 31.7 %copy-start.19 = (bf16[160,1024]{1,0:T(8,128)(2,1)S(1)}, bf16[160,1024]{1,0:T(8,128)(2,1)}, u32[]{:S(2)}) copy-start(bf16[160,1024]{1,0:T(8,128)(2,1)} %copy-done.18) | copy-start | bytes 983044
  485.5 31.7 %copy-start.27 = (f32[3,1024]{1,0:T(4,128)S(1)}, f32[3,1024]{1,0:T(4,128)}, u32[]{:S(2)}) copy-start(f32[3,1024]{1,0:T(4,128)} %copy-done.26) | copy-start | bytes 36868
  485.5 31.7 %copy-start.29 = (f32[1024]{0:T(1024)S(1)}, f32[1024]{0:T(1024)}, u32[]{:S(2)}) copy-start(f32[1024]{0:T(1024)} %copy-done.28) | copy-start | bytes 12292
  485.5 31.7 %copy-start.31 = (f32[1024]{0:T(1024)S(1)}, f32[1024]{0:T(1024)}, u32[]{:S(2)}) copy-start(f32[1024]{0:T(1024)} %copy-done.30) | copy-start | bytes 12292
  485.5 31.7 %copy-start.41 = (f32[1024]{0:T(1024)S(1)}, f32[1024]{0:T(1024)}, u32[]{:S(2)}) copy-start(f32[1024]{0:T(1024)} %copy-done.40) | copy-start | bytes 12292
  485.5 31.7 %copy-start.47 = (f32[1024]{0:T(1024)S(1)}, f32[1024]{0:T(1024)}, u32[]{:S(2)}) copy-start(f32[1024]{0:T(1024)} %param.26) | copy-start | bytes 12292
  517.2 17.4 %copy-start.24 = (bf16[4,1024]{1,0:T(4,128)(2,1)S(1)}, bf16[4,1024]{1,0:T(4,128)(2,1)}, u32[]{:S(2)}) copy-start(bf16[4,1024]{1,0:T(4,128)(2,1)} %param.20) | copy-start | bytes 24580
  517.2 22.7 %copy-start.6 = (bf16[1024,1024]{1,0:T(8,128)(2,1)S(1)}, bf16[1024,1024]{1,0:T(8,128)(2,1)}, u32[]{:S(2)}) copy-start(bf16[1024,1024]{1,0:T(8,128)(2,1)} %copy-done.3) | copy-start | bytes 6291460
  534.6 5.8 copy-start.12
  534.6 6.6 copy-start.14
  534.6 7.1 %copy-start.55 = (f32[40]{0:T(128)S(1)}, f32[40]{0:T(128)}, u32[]{:S(2)}) copy-start(f32[40]{0:T(128)} %pad.10.clone) | copy-start | bytes 484
  538.6 11.5 %collective-permute-start.2 = (f32[3,1024]{1,0:T(4,128)S(1)}, f32[3,1024]{1,0:T(4,128)S(1)}, u32[]{:S(2)}, u32[]{:S(2)}) collective-permute-start(f32[3,1024]{1,0:T(4,128)S(1)} %pad_maximum_fusion.3), channel_id=1, source_target_pairs={{4,0},{5,1},{6,2},{7,3},{12,8},{13,9},{14,10},{15,11},{20,16},{21,... | collective-permute-start | bytes 36872 | tf_op jit(solution)/shard_map/ppermute | solution.py:20
  544.2 4.5 copy-start.49
  556.1 106.1 %copy-start.25 = (f32[1,2048]{1,0:T(1,128)S(1)}, f32[1,2048]{1,0:T(1,128)}, u32[]{:S(2)}) copy-start(f32[1,2048]{1,0:T(1,128)} %slice.196) | copy-start | bytes 24580
  653.8 8.4 %copy-start.8 = (bf16[256,2048]{1,0:T(8,128)(2,1)S(1)}, bf16[256,2048]{1,0:T(8,128)(2,1)}, u32[]{:S(2)}) copy-start(bf16[256,2048]{1,0:T(8,128)(2,1)} %hid_ref.3) | copy-start | bytes 3145732
  653.8 8.4 %copy-start.10 = (f32[256,2048]{1,0:T(8,128)S(1)}, f32[256,2048]{1,0:T(8,128)}, u32[]{:S(2)}) copy-start(f32[256,2048]{1,0:T(8,128)} %get-tuple-element.78) | copy-start | bytes 6291460
  653.8 8.9 %copy-start.54 = (bf16[512]{0:T(512)(128)(2,1)S(1)}, bf16[512]{0:T(512)(128)(2,1)}, u32[]{:S(2)}) copy-start(bf16[512]{0:T(512)(128)(2,1)} %param.18) | copy-start | bytes 3076
  653.8 11.0 %copy-start.23 = (f32[40,1024]{1,0:T(8,128)S(1)}, f32[40,1024]{1,0:T(8,128)}, u32[]{:S(2)}) copy-start(f32[40,1024]{1,0:T(8,128)} %get-tuple-element.81) | copy-start | bytes 491524
  653.8 12.2 %copy-start.17 = (f32[256,2048]{1,0:T(8,128)S(1)}, f32[256,2048]{1,0:T(8,128)}, u32[]{:S(2)}) copy-start(f32[256,2048]{1,0:T(8,128)} %get-tuple-element.66) | copy-start | bytes 6291460
  (15 other events, 55.8 us)
Sparse Core Ops, SparseCore 0:
  128.5 40.5 all-reduce.7
Sparse Core Ops, SparseCore 1:
  130.8 36.6 all-gather.1
  396.0 60.5 reduce-scatter.1

commit v5 on v4

--- a/solution.py
+++ b/solution.py
@@ -11,6 +11,7 @@
 LOG2E = 1.4426950408889634
 LN2 = 0.6931471805599453
 FAR = 1e30
+SMALL_ROWS = 24
 MESH = pl.DeviceIdType.MESH
 
 
@@ -81,7 +82,7 @@
     )(stepd, u, bc, cdiag, rate)
 
 def bwd_kernel(stepd_ref, u_ref, ds_ref, bc_ref, bdiag_ref, ones_ref, rate_ref, ckpt_ref, gin_ref,
-               wb_ref, dn_ref, db_ref, dc_ref, acc_ref, g_ref, sbf_ref, abf_ref, rbf_ref, *, unroll):
+               wb_ref, dn_ref, db_ref, dc_ref, acc_ref, g_ref, sbf_ref, abf_ref, rbf_ref, pb_ref, pc_ref, *, unroll):
     @pl.when(pl.program_id(1) == 0)
     def _():
         g_ref[...] = gin_ref[...]
@@ -89,10 +90,17 @@
     rate = rate_ref[...]
     tb = stepd_ref.shape[0]
     nc = tb // CH
+    def fold(v):
+        p = v[:, 0:128]
+        for q in range(1, v.shape[1] // 128):
+            p = p + v[:, q * 128:(q + 1) * 128]
+        return p
     row = lax.broadcasted_iota(jnp.int32, (CH, CH * N), 0)
     lane = lax.broadcasted_iota(jnp.int32, (CH, CH * N), 1)
     diag = (row == lane // N).astype(F32)
     sbf_ref[0:N, :] = ckpt_ref[0].astype(BF16)
+    nt = (((1,), (1,)), ((), ()))
+    lanes = jnp.ones((8, 128), BF16)
 
     def forward(c, s):
         base = pl.multiple_of(c * CH, CH)
@@ -101,9 +109,12 @@
             dec = jnp.exp2(rate * stepd_ref[pl.ds(base + k, 1), :])
             s = dec * s + bc[:, k:k + 1] * u_ref[pl.ds(base + k, 1), :]
             sbf_ref[pl.ds(pl.multiple_of((base + k + 1) * N, N), N), :] = s.astype(BF16)
+            pc_ref[k * N:(k + 1) * N, :] = fold(s * ds_ref[pl.ds(base + k, 1), :])
+        dc = lax.dot_general(lanes, pc_ref[...].astype(BF16), nt, preferred_element_type=F32)
+        dc_ref[0, pl.ds(c, 1), :] = dc[0:1]
         return s
 
-    lax.fori_loop(0, nc, forward, ckpt_ref[0])
+    lax.fori_loop(0, nc, forward, ckpt_ref[0], unroll=unroll)
 
     def backward(c, carry):
         g, acc = carry
@@ -114,6 +125,7 @@
             sd = stepd_ref[pl.ds(base + k, 1), :]
             adj = g + bc[:, CH + k:CH + k + 1] * ds_ref[pl.ds(base + k, 1), :]
             abf_ref[k * N:(k + 1) * N, :] = adj.astype(BF16)
+            pb_ref[k * N:(k + 1) * N, :] = fold(adj * u_ref[pl.ds(base + k, 1), :])
             g = jnp.exp2(rate * sd) * adj
             before = sbf_ref[pl.ds(pl.multiple_of((base + k) * N, N), N), :].astype(F32)
             r = g * before * rate
@@ -121,12 +133,8 @@
             acc = acc + r * sd
         wb_ref[pl.ds(base, CH), :] = jnp.dot(bdiag_ref[pl.ds(base, CH), :], abf_ref[...], preferred_element_type=F32)
         dn_ref[pl.ds(base, CH), :] = jnp.dot(ones_ref[...], rbf_ref[...], preferred_element_type=F32)
-        nt = (((1,), (1,)), ((), ()))
-        now = sbf_ref[pl.ds(pl.multiple_of((base + 1) * N, N), CH * N), :]
-        db = lax.dot_general(u_ref[pl.ds(base, CH), :].astype(BF16), abf_ref[...], nt, preferred_element_type=F32)
-        dc = lax.dot_general(ds_ref[pl.ds(base, CH), :].astype(BF16), now, nt, preferred_element_type=F32)
-        db_ref[0, pl.ds(c, 1), :] = jnp.sum(db * diag, axis=0, keepdims=True)
-        dc_ref[0, pl.ds(c, 1), :] = jnp.sum(dc * diag, axis=0, keepdims=True)
+        db = lax.dot_general(lanes, pb_ref[...].astype(BF16), nt, preferred_element_type=F32)
+        db_ref[0, pl.ds(c, 1), :] = db[0:1]
         return g, acc
 
     g, acc = lax.fori_loop(0, nc, backward, (g_ref[...], acc_ref[...]), unroll=unroll)
@@ -165,7 +173,7 @@
             jax.ShapeDtypeStruct((N, c), F32),
         ],
         scratch_shapes=[pltpu.VMEM((N, w), F32), pltpu.VMEM(((tb + 1) * N, w), BF16),
-                        pltpu.VMEM((CH * N, w), BF16), pltpu.VMEM((CH * N, w), BF16)],
+                        pltpu.VMEM((CH * N, w), BF16), pltpu.VMEM((CH * N, w), BF16), pltpu.VMEM((CH * N, 128), F32), pltpu.VMEM((CH * N, 128), F32)],
         compiler_params=pltpu.CompilerParams(vmem_limit_bytes=48 << 20),
         name="scan_backward",
     )(stepd, u, ds, bc, bdiag, ones, rate, ckpt, gin)
@@ -195,7 +203,7 @@
             )
             return s
 
-        state_ref[...] = lax.fori_loop(0, y_ref.shape[0] // CH, chunk, state_ref[...])
+        state_ref[...] = lax.fori_loop(0, y_ref.shape[0] // CH, chunk, state_ref[...], unroll=8)
 
     @pl.when(jnp.logical_not(alive))
     def _():
@@ -245,7 +253,7 @@
                 g = jnp.exp2(rate * stepd_ref[pl.ds(base + k, 1), :]) * adj
             return g
 
-        g_ref[...] = lax.fori_loop(0, nc, chunk, g_ref[...])
+        g_ref[...] = lax.fori_loop(0, nc, chunk, g_ref[...], unroll=8)
 
 
 def entry(alive, stepd, ds, bc, rate, tb=128, w=512):
@@ -777,9 +785,10 @@
     )(gated, w_out, hidden, teacher, scale, z_gate, scan_out)
 
 
-def front_kernel(n, dps, seqs, subs, lag, hid_ref, gain_ref, cnt_ref, win_ref, wsm_ref,
-                 x_ref, z_ref, nrm_ref, w_ref, prev_ref, total_ref, gfull, ws_ref,
-                 rows_ref, grecv, cnt_one, cnt_two,
+def front_kernel(n, dps, seqs, subs, lag, hid_ref, gain_ref, cnt_ref, win_ref, wsm_ref, taps_ref, keep_ref,
+                 x_out, z_out, nrm_out, w_out, conv_out, low_out, total_ref, gfull, ws_ref, mixed_ref,
+                 rows_ref, grecv, cnt_one, cnt_two, x_ref, z_ref, nrm_ref, w_ref, conv_ref, low_ref,
+                 mix_send, mix_recv, mix_own, outs, ms, mr, ns, nr,
                  ar_send, ar_recv, al_send, al_recv, gs, gr, c1s, c1r, c2s, c2r, hs, hr, ls,
                  chip_send, chip_recv, core_send, core_recv):
     dp, seq, t = place()
@@ -847,7 +856,17 @@
 
     def edge_copy():
         last = x_ref.at[pl.ds(x_ref.shape[0] - 8, 8), :]
-        return mesh_copy(last, prev_ref, hs, hr, seq=lax.rem(seq + 1, seqs))
+        return mesh_copy(last, x_ref.at[pl.ds(0, 8), :], hs, hr, seq=lax.rem(seq + 1, seqs))
+
+    def mix_copy(p, slot):
+        return mesh_copy(mix_send.at[p], mix_recv.at[slot], ms.at[p], mr.at[slot], tensor=p)
+
+    def sum_copy(p, slot):
+        return mesh_copy(mixed_ref.at[slot], mixed_ref.at[slot], ns.at[p], nr.at[slot], tensor=p)
+
+    def written(i):
+        src = (w_ref, nrm_ref, z_ref, x_ref, conv_ref, low_ref)[i]
+        return pltpu.make_async_copy(src, (w_out, nrm_out, z_out, x_out, conv_out, low_out)[i], outs.at[i])
 
     def local_copy():
         return pltpu.make_async_copy(wsm_ref, block(1, mine), ls)
@@ -903,11 +922,12 @@
         for k, dst in enumerate((x_ref, z_ref)):
             lanes = dst.shape[1]
             width = min(tile, lanes)
+            there = pl.ds(pl.multiple_of(o * rows + 8 - 8 * k, 8), rows)
 
             @pl.loop(0, lanes // width)
             def _(j):
                 cols = pl.ds(pl.multiple_of(j * width, width), width)
-                dst[here, cols] = jnp.dot(nrm_ref[here, :], w_ref[k, :, cols], preferred_element_type=F32)
+                dst[there, cols] = jnp.dot(nrm_ref[here, :], w_ref[k, :, cols], preferred_element_type=F32)
 
     def turn(d, o):
         final = jnp.where(o == 0, (n - 1) * gap + 1, (n - 2 - o) * gap + lag)
@@ -974,25 +994,88 @@
     def _():
         edge_copy().start()
 
+    @pl.when(seq == 0)
+    def _():
+        x_ref[0:8, :] = jnp.zeros((8, x_ref.shape[1]), F32)
+
+    for i in range(3):
+        written(i).start()
+
+    @pl.when(seq > 0)
+    def _():
+        edge_copy().wait_recv()
+
+    @pl.when(seq < seqs - 1)
+    def _():
+        edge_copy().wait_send()
+
+    written(3).start()
+    local_copy().wait()
+    lanes = low_ref.shape[1]
+    width = min(tile, lanes)
+    piece = min(64, rows)
+    taps = keep_ref.shape[1]
+
+    def convolve(o):
+        @pl.loop(0, rows // piece * (lanes // width))
+        def _(i):
+            base = o * rows + i // (lanes // width) * piece
+            here = pl.ds(pl.multiple_of(base, piece), piece)
+            cols = pl.ds(pl.multiple_of(i % (lanes // width) * width, width), width)
+            span = x_ref[pl.ds(pl.multiple_of(base, piece), piece + 8), cols]
+            keep = keep_ref[here, :]
+            total = jnp.broadcast_to(taps_ref[taps:taps + 1, cols], (piece, width))
+            for j in range(taps):
+                first = 8 - (taps - 1) + j
+                total = total + taps_ref[j:j + 1, cols] * span[first:first + piece] * keep[:, j:j + 1]
+            conv_ref[here, cols] = total
+            low_ref[here, cols] = (total / (1.0 + jnp.exp(-total))).astype(BF16)
+
+    groups, depth = ws_ref.shape[0], ws_ref.shape[1]
+    used = mix_own.shape[0] // groups
+
+    @pl.loop(0, n)
+    def _(i):
+        o = lax.rem(t + 1 + i, n)
+        convolve(o)
+        nt = (((1,), (1,)), ((), ()))
+        low = low_ref[pl.ds(pl.multiple_of(o * rows, rows), rows), :]
+        weights = ws_ref[...].reshape(groups * depth, lanes)
+        mix = lax.dot_general(weights, low, nt, preferred_element_type=F32)
+        mix = jnp.concatenate([mix[p * depth:p * depth + used] for p in range(groups)], 0)
+
+        @pl.when(o != t)
+        def _():
+            mix_send[o] = mix.astype(BF16)
+            mix_copy(o, t).start()
+
+        @pl.when(o == t)
+        def _():
+            mix_own[...] = mix
+
+    for i in range(4, 6):
+        written(i).start()
+    for ahead in range(1, n):
+        p = lax.rem(t + ahead, n)
+        mix_copy(p, p).wait_recv()
+        mix_own[...] = mix_own[...] + mix_recv[p].astype(F32)
+    mixed_ref[t] = mix_own[...].astype(BF16)
+    for ahead in range(1, n):
+        sum_copy(lax.rem(t + ahead, n), t).start()
     total_ref[...] = cnt_one[...]
     for ahead in range(1, chips):
         q = lax.rem(chip + ahead, chips)
         count_two(q, q).wait_recv()
         total_ref[...] = total_ref[...] + cnt_two[q]
-
-    @pl.when(seq == 0)
-    def _():
-        prev_ref[...] = jnp.zeros_like(prev_ref)
-
-    @pl.when(seq > 0)
-    def _():
-        edge_copy().wait_recv()
-
-    @pl.when(seq < seqs - 1)
-    def _():
-        edge_copy().wait_send()
-
-    local_copy().wait()
+    for ahead in range(1, n):
+        p = lax.rem(t + ahead, n)
+        sum_copy(p, p).wait_recv()
+    for ahead in range(1, n):
+        p = lax.rem(t + ahead, n)
+        mix_copy(p, t).wait_send()
+        sum_copy(p, t).wait_send()
+    for i in range(6):
+        written(i).wait()
     for kind in range(2):
         for ahead in range(1, chips):
             chip_copy(kind, lax.rem(chip + ahead, chips), mine).wait_send()
@@ -1016,13 +1099,14 @@
             al_copy(o, s).wait_send()
 
 
-def front(hidden, gain, count, w_in, w_small):
+def front(hidden, gain, count, w_in, w_small, taps, keeps):
     n, dps, seqs = (lax.axis_size(axis) for axis in ("tensor", "dp", "seq"))
     parts = dps * seqs
     chips = parts // 2
     rows, wide = hidden.shape
     lanes = w_in.shape[2]
     tokens = rows * n
+    mixed = parts * SMALL_ROWS
     subs = max(1, rows // 32)
     vmem, hbm = pl.BlockSpec(memory_space=pltpu.VMEM), pl.BlockSpec(memory_space=pl.ANY)
     dma = pltpu.SemaphoreType.DMA
@@ -1030,22 +1114,34 @@
     return pl.pallas_call(
         functools.partial(front_kernel, n, dps, seqs, subs, 2),
         out_shape=[
-            jax.ShapeDtypeStruct((tokens, lanes), F32),
+            jax.ShapeDtypeStruct((tokens + 8, lanes), F32),
             jax.ShapeDtypeStruct((tokens, lanes), F32),
             jax.ShapeDtypeStruct((tokens, wide), BF16),
             jax.ShapeDtypeStruct((2, wide, lanes), BF16),
-            jax.ShapeDtypeStruct((8, lanes), F32),
+            jax.ShapeDtypeStruct((tokens, lanes), F32),
+            jax.ShapeDtypeStruct((tokens, lanes), BF16),
             jax.ShapeDtypeStruct(count.shape, F32),
             jax.ShapeDtypeStruct((gain.shape[0], wide), F32),
             jax.ShapeDtypeStruct((parts,) + w_small.shape, BF16),
+            jax.ShapeDtypeStruct((n, mixed, rows), BF16),
         ],
-        in_specs=[vmem] * 5,
-        out_specs=[vmem] * 7 + [hbm],
+        in_specs=[vmem] * 7,
+        out_specs=[hbm] * 6 + [vmem] * 4,
         scratch_shapes=[
             pltpu.VMEM((tokens, wide), BF16),
             pltpu.VMEM((n,) + gain.shape, F32),
             pltpu.VMEM(count.shape, F32),
             pltpu.VMEM((chips,) + count.shape, F32),
+            pltpu.VMEM((tokens + 8, lanes), F32),
+            pltpu.VMEM((tokens, lanes), F32),
+            pltpu.VMEM((tokens, wide), BF16),
+            pltpu.VMEM((2, wide, lanes), BF16),
+            pltpu.VMEM((tokens, lanes), F32),
+            pltpu.VMEM((tokens, lanes), BF16),
+            pltpu.VMEM((n, mixed, rows), BF16),
+            pltpu.VMEM((n, mixed, rows), BF16),
+            pltpu.VMEM((mixed, rows), F32),
+            dma((6,)), peers, peers, peers, peers,
             many, many, many, many, peers, peers, dma, dma, few, few, dma, dma, dma,
             dma((2, chips)), dma((2, parts)), dma((2, parts)), dma((2, parts)),
         ],
@@ -1053,7 +1149,7 @@
             collective_id=3, has_side_effects=True, vmem_limit_bytes=60 << 20
         ),
         name="front",
-    )(hidden, gain, count, w_in, w_small)
+    )(hidden, gain, count, w_in, w_small, taps, keeps)
 
 
 def on_device(
@@ -1083,42 +1179,45 @@
     parts = lax.axis_size(("dp", "seq"))
     gain_tile = jnp.broadcast_to(norm_gain.astype(F32)[None], (8, norm_gain.shape[0]))
     x_cols, dt_rows = xproj_weight.shape[1], dtproj_weight.shape[0]
-    pad = -(x_cols + dt_rows) % 16
-    w_small = jnp.concatenate([xproj_weight.T, dtproj_weight, jnp.zeros((pad, chan_lanes), BF16)], 0)
-    x_inner, z_gate, normalized_rows, w_in, prev_rows, total, gain_rows, w_small = front(
+    w_small = jnp.concatenate(
+        [
+            xproj_weight.T,
+            jnp.zeros((SMALL_ROWS - x_cols, chan_lanes), BF16),
+            dtproj_weight,
+            jnp.zeros((-(SMALL_ROWS + dt_rows) % 16, chan_lanes), BF16),
+        ],
+        0,
+    )
+    seg_float = segment_ids.astype(F32)
+    prev_seg = jnp.where(lax.axis_index("seq") > 0, seg_float[:1], jnp.zeros((back_rows,), F32))
+    ext_seg = jnp.concatenate([prev_seg, seg_float], 0)
+    tap_keeps = []
+    for offset in range(conv_taps):
+        tap_keeps.append((ext_seg[offset : offset + tok_rows] == seg_float).astype(F32)[:, None])
+    taps = jnp.concatenate(
+        [conv_weight.astype(F32), conv_bias.astype(F32)[None], jnp.zeros((7 - conv_taps, chan_lanes), F32)], 0
+    )
+    x_rows, z_gate, normalized_rows, w_in, conv_sum, x_low, total, gain_rows, w_small, mixed = front(
         hidden_in,
         gain_tile,
         count_here,
         jnp.swapaxes(input_projection_weight, 0, 1),
         w_small,
+        taps,
+        jnp.concatenate(tap_keeps, 1),
     )
     w_out_rows, z_gate = lax.optimization_barrier((output_projection_weight.T, z_gate))
     w_out = lax.all_gather(w_out_rows, ("dp", "seq"), axis=0, tiled=True)
     total_count = total[0, 0]
     w_x = w_small[:, :x_cols].reshape(parts * x_cols, chan_lanes)
-    w_dt = w_small[:, x_cols : x_cols + dt_rows].reshape(parts * dt_rows, chan_lanes)
+    w_dt = w_small[:, SMALL_ROWS : SMALL_ROWS + dt_rows].reshape(parts * dt_rows, chan_lanes)
     share_rows = hidden_in.astype(F32)
     full_gain = gain_rows[0]
     inv_share = lax.rsqrt(jnp.mean(share_rows * share_rows, axis=1, keepdims=True) + EPS)
-    seg_float = segment_ids.astype(F32)
-    prev_x = prev_rows[8 - back_rows :]
-    prev_seg = jnp.where(lax.axis_index("seq") > 0, seg_float[:1], jnp.zeros((back_rows,), F32))
-    ext_x = jnp.concatenate([prev_x, x_inner], 0)
-    ext_seg = jnp.concatenate([prev_seg, seg_float], 0)
-    tap_keeps = []
-    conv_sum = jnp.broadcast_to(conv_bias.astype(jnp.float32)[None], (tok_rows, chan_lanes))
-    for offset in range(conv_taps):
-        keep_tap = (ext_seg[offset : offset + tok_rows] == seg_float).astype(jnp.float32)[:, None]
-        tap_keeps.append(keep_tap)
-        conv_sum = (
-            conv_sum
-            + conv_weight[offset].astype(jnp.float32)[None]
-            * ext_x[offset : offset + tok_rows]
-            * keep_tap
-        )
-    x_low = jax.nn.silu(conv_sum).astype(jnp.bfloat16)
-    x_float = x_low.astype(jnp.float32)
-    mixed_rows = lax.psum(jnp.einsum("te,je->tj", x_low, w_x, preferred_element_type=F32), "tensor")
+    ext_x = x_rows[8 - back_rows :]
+    x_float = x_low.astype(F32)
+    mixed = mixed.reshape(-1, parts, SMALL_ROWS, row_share)[:, :, :x_cols]
+    mixed_rows = mixed.transpose(0, 3, 1, 2).reshape(tok_rows, parts * x_cols).astype(F32)
     rank_width = w_dt.shape[0]
     state_width = (mixed_rows.shape[1] - rank_width) // 2
     step_low = mixed_rows[:, :rank_width].astype(jnp.bfloat16)
@@ -1136,7 +1235,7 @@
     b_diag, c_diag = diagonal(b_in), diagonal(c_out)
     resets = jnp.sum((same_doc == 0).astype(jnp.int32).reshape(-1, block), axis=1)
     alive = (jnp.cumsum(resets) - resets == 0).astype(jnp.int32)
-    y_local, marks, state_last = fwd(stepd, inject, col_pair, c_diag, rates, tb=block, unroll=2)
+    y_local, marks, state_last = fwd(stepd, inject, col_pair, c_diag, rates, tb=block, unroll=8)
     reach = jnp.exp2(rates * jnp.sum(stepd, axis=0)[None])
     state_in = carried(state_last, reach, "seq", 1)
     y_rows, marks = correct(alive, y_local, stepd, c_diag, rates, marks, state_in, tb=block)
@@ -1155,7 +1254,7 @@
     adjoint_in = carried(adjoint_first, reach, "seq", -1)
     ones = diagonal(jnp.ones((CH, N), F32))
     weighted_b, d_rate, d_b_part, d_c_part, a_log_part = bwd(
-        stepd, inject, d_scan, col_pair, b_diag, ones, rates, marks, adjoint_in, tb=block, w=1024
+        stepd, inject, d_scan, col_pair, b_diag, ones, rates, marks, adjoint_in, tb=block, unroll=8
     )
     d_step = LN2 * d_rate + x_float * weighted_b
     a_log_part = LN2 * a_log_part

time: 684 us -> 610 us (0.89)
  waiting for transfers between devices: 37.2 us -> 0.18 us
  Pallas kernels: 453 us -> 432 us
  matrix products: 36.6 us -> 26 us
    psum x1 -> x0, waiting for transfers between devices: 30 us -> none  [on_device(): lax.psum(jnp.einsum('te,je->tj', x_low, w_x, preferred_element_type=F32),...]
    pallas_call x1, Pallas kernels: 77.3 us -> 51.6 us  [bwd(): pl.pallas_call(functools.partial(bwd_kernel, unroll=unroll), grid=grid, i...]
    reduce_sum x0 -> x3, other arithmetic: none -> 13.7 us  [the longest x1 13.6 us: on_device(): jnp.sum(d_conv * ext_x[offset:offset + tok_rows] * tap_keeps[offset], axi...]
    pallas_call x1, Pallas kernels: 91 us -> 105 us  [front(): pl.pallas_call(functools.partial(front_kernel, n, dps, seqs, subs, 2), ou...]
    convert_element_type x3 -> x1, other arithmetic: 14.2 us -> 0.71 us  [on_device(): conv_weight.astype(F32)]
    dot_general x1, matrix products: 17.4 us -> 8.61 us  [on_device(): d_xlow = d_xlow + jnp.dot(d_mixed_low, w_x, preferred_element_type=F32)]
    pallas_call x1, Pallas kernels: 24.3 us -> 17 us  [fwd(): pl.pallas_call(functools.partial(fwd_kernel, unroll=unroll), grid=grid, i...]
    ppermute x3, waiting for transfers between devices: 7.18 us -> 0.14 us  [passed_along(): return lax.ppermute(x, axis, pairs)]
  transfers between devices with their start and end apart: 6 -> 5, of which waited for: 3 -> 1; matrix products, arithmetic and copies ran while one was open for 15% -> 16% of each run, Pallas kernels for 31% -> 29%
where the time goes in v5:
time: 610 us; the launch traced here: 602 us
  Pallas kernels  432 us (71%)
  other arithmetic  49.7 us (8%)
  local copies, waits for them, and re-layouts  41.3 us (7%)
  blocking collectives  28.8 us (5%)
  matrix products  26 us (4%)
  between operations  16.6 us (3%)
  starting transfers between devices  7.14 us (1%)
    pallas_call x1, Pallas kernels, middle(): pl.pallas_call(functools.partial(mid_kernel, n, subs, 2), out_shape=[jax....  141 us
    pallas_call x1, Pallas kernels, front(): pl.pallas_call(functools.partial(front_kernel, n, dps, seqs, subs, 2), ou...  105 us
    pallas_call x1, Pallas kernels, tail(): pl.pallas_call(functools.partial(tail_kernel, n, dps, seqs, subs, 2), out...  95.8 us
    pallas_call x1, Pallas kernels, bwd(): pl.pallas_call(functools.partial(bwd_kernel, unroll=unroll), grid=grid, i...  51.6 us
    psum x1, blocking collectives, on_device(): lax.psum(jnp.concatenate([d_rank, d_b_part, d_c_part], 1), 'tensor')  28.8 us
    pallas_call x1, Pallas kernels, fwd(): pl.pallas_call(functools.partial(fwd_kernel, unroll=unroll), grid=grid, i...  17 us
    unnamed x79, local copies, waits for them, and re-layouts  16.9 us
    reduce_sum x1, other arithmetic, on_device(): jnp.sum(d_conv * ext_x[offset:offset + tok_rows] * tap_keeps[offset], axi...  13.6 us
  transfers between devices with their start and end apart: 5, of which 1 were waited for; matrix products, arithmetic and copies ran while one was open for 16% of the time, Pallas kernels for 29%

profile of v5, /device:TPU:0, one launch (start us, length us, event | category | flops | bytes accessed | tf_op | source)
XLA Modules:
  0.0 601.8 jit_solution(4954034142332132384)
XLA Ops:
  7.2 1.3 fusion.37
  12.8 1.0 copy.60.keep_ref
  13.8 2.0 copy.65
  15.9 2.5 copy.77
  19.1 1.5 maximum_maximum_fusion.1.wsm_ref
  20.6 1.2 broadcast_in_dim.88.cnt_ref
  21.9 1.3 broadcast_in_dim.87.gain_ref
  23.2 104.7 %front.1 = (f32[1032,1024]{1,0:T(8,128)}, f32[1024,1024]{1,0:T(8,128)}, bf16[1024,2048]{1,0:T(8,128)(2,1)}, bf16[2,2048,1024]{2,1,0:T(8,128)(2,1)}, f32[1024,102...) custom-call(bf16[256,2048]{1,0:T(8,128)(2,1)} %hid_ref.3, ...), custom_call_target="tpu_custom_call" | custom-call | tf_op jit(solution)/shard_map/front/pallas_call | solution.py:1114
  127.9 1.3 copy.72
  129.2 1.1 slice.185
  132.5 7.5 %fusion.41 = (f32[1024]{0:T(1024)S(1)}, f32[1024,1024]{1,0:T(8,128)}, f32[1024,1024]{1,0:T(8,128)}, f32[1024,1024]{1,0:T(8,128)}) fusion(f32[1024]{0:T(1024)S(1)} %copy-done.32, pred[1024]{0:T(1024)(128)(4,1)S(1)} %get-tuple-element.152, bf16[1024,1024]{1,0:T(8,128)(2,1)} %get-tuple-element.58, bf16[128,1024]{1,0:T(8,128)(2,1)S(1)} %bitcast.98, ...), kind=kOutput, calls=%fused_computation.113 | convolution fusion | flops 279968768 | bytes 15213568 | tf_op jit(solution)/shard_map/dot_general | solution.py:1226
  140.0 17.0 %scan_forward.1 = (f32[1024,1024]{1,0:T(8,128)S(1)}, f32[8,16,1024]{2,1,0:T(8,128)S(1)}, f32[16,1024]{1,0:T(8,128)S(1)}) custom-call(f32[1024,1024]{1,0:T(8,128)} %get-tuple-element.151.stepd_ref, f32[1024,1024]{1,0:T(8,128)} %get-tuple-element.158.u_ref, f32[64,16,32]{2,1,0:T(8,128)S(1)} %pad_maximum_fusion.1.bc_ref, ...), custom_call_target="tpu_custom_call" | custom-call | tf_op jit(solution)/shard_map/scan_forward/pallas_call | solution.py:59
  156.9 1.9 copy-done.1
  158.9 4.3 collective-permute-start
  164.8 1.2 slice.188
  166.0 1.4 slice.189
  168.2 0.8 copy.66.scale_ref
  169.0 0.8 reshape.241
  173.2 11.5 %scan_correct.1 = (f32[1024,1024]{1,0:T(8,128)S(1)}, f32[8,16,1024]{2,1,0:T(8,128)S(1)}) custom-call(s32[8]{0:T(128)S(1)} %compare_convert_fusion.3.alive_ref, f32[1024,1024]{1,0:T(8,128)} %copy-done.1, f32[1024,1024]{1,0:T(8,128)} %get-tuple-element.151.stepd_ref, bf16[1024,256]{1,0:T(8,128)(2,1)S(1)} %get-tuple-element.174.cdiag_ref, ...), custom_call_target="tpu_custom_call" | custom-call | tf_op jit(solution)/shard_map/scan_correct/pallas_call | solution.py:220
  184.7 4.4 multiply_convert_fusion
  189.2 141.0 %middle.1 = (bf16[256,2048]{1,0:T(8,128)(2,1)}, f32[256,2048]{1,0:T(8,128)}, bf16[1024,2048]{1,0:T(8,128)(2,1)}, f32[1024,1024]{1,0:T(8,128)}, bf16[1024,1024]{1,0:T(8,128)(2,1)}) custom-call(bf16[1024,1024]{1,0:T(8,128)(2,1)} %get-tuple-element.148.gated_ref, bf16[2048,1024]{1,0:T(8,128)(2,1)} %all-gather.2.cloned.1.call-done.w_ref, ...), custom_call_target="tpu_custom_call" | custom-call | tf_op jit(solution)/shard_map/middle/pallas_call | solution.py:762
  330.2 2.2 copy-done
  332.4 10.5 %scan_entry.1 = f32[16,1024]{1,0:T(8,128)S(1)} custom-call(s32[8]{0:T(128)S(1)} %compare_convert_fusion.3.alive_ref, f32[1024,1024]{1,0:T(8,128)S(1)} %copy-done, f32[1024,1024]{1,0:T(8,128)} %get-tuple-element.70.ds_ref, f32[64,16,32]{2,1,0:T(8,128)S(1)} %pad_maximum_fusion.1.bc_ref, f32[16,1024]{1,0:T(8,128)S(1)} %fusion.24.rate_ref), custom_call_target="tpu_custom_call" | custom-call | tf_op jit(solution)/shard_map/scan_entry/pallas_call | solution.py:265
  342.9 1.5 collective-permute-start.1
  344.4 6.2 %convolution_convert_fusion = bf16[2048,1024]{1,0:T(8,128)(2,1)} fusion(bf16[1024,2048]{1,0:T(8,128)(2,1)S(1)} %copy-done.35, bf16[1024,1024]{1,0:T(8,128)(2,1)S(1)} %copy-done.7), kind=kOutput, calls=%fused_computation.19 | convolution fusion | flops 4297064448 | bytes 10485760 | tf_op jit(solution)/shard_map/te,tw->we/dot_general | solution.py:1251
  350.8 51.6 %scan_backward.1 = (f32[1024,1024]{1,0:T(8,128)}, f32[1024,1024]{1,0:T(8,128)}, f32[2,64,256]{2,1,0:T(8,128)S(1)}, f32[2,64,256]{2,1,0:T(8,128)S(1)}, f32[16,1024]{1,0:T(8,128)S(1)}) custom-call(f32[1024,1024]{1,0:T(8,128)} %get-tuple-element.151.stepd_ref, f32[1024,1024]{1,0:T(8,128)} %get-tuple-element.158.u_ref, f32[1024,1024]{1,0:T(8,128)} %get-tuple-element.70.ds_ref, ...), custom_call_target="tpu_custom_call" | custom-call | tf_op jit(solution)/shard_map/scan_backward/pallas_call | solution.py:150
  402.4 7.7 %fusion.38 = (f32[1024]{0:T(1024)S(1)}, bf16[1024,1024]{1,0:T(8,128)(2,1)S(1)}, f32[1024]{0:T(1024)S(1)}) fusion(f32[1024,1024]{1,0:T(8,128)} %get-tuple-element.187, f32[1024]{0:T(1024)} %param.24, f32[1024,1024]{1,0:T(8,128)} %get-tuple-element.72, bf16[1024,1024]{1,0:T(8,128)(2,1)} %get-tuple-element.58, f32[1024,1024]{1,0:T(8,128)} %get-tuple-element.73, ...), kind=kLoop, calls=%fused_computation.112 | loop fusion | flops 13629440 | bytes 20983808 | tf_op jit(solution)/shard_map/reduce_sum | solution.py:1265
  410.2 1.6 fusion.13
  412.5 1.1 pad_maximum_fusion
  413.6 28.8 %all-reduce.6 = bf16[1024,160]{0,1:T(8,128)(2,1)S(1)} all-reduce(f32[1024,160]{0,1:T(8,128)S(1)} %pad_maximum_fusion), channel_id=1, replica_groups=mesh['dp'=4,'seq'=2,'tensor'=4] {'tensor'}, use_global_device_ids=true, to_apply=%region_7.8 | all-reduce | flops 163840 | bytes 983040 | tf_op jit(solution)/shard_map/psum | solution.py:1269
  442.5 8.6 %multiply_multiply_fusion = f32[1024,1024]{1,0:T(8,128)S(1)} fusion(f32[1024,1024]{1,0:T(8,128)} %get-tuple-element.76, f32[1024,1024]{1,0:T(8,128)} %get-tuple-element.72, f32[1024,1024]{1,0:T(8,128)} %get-tuple-element.70.ds_ref, f32[1024]{0:T(1024)S(1)} %copy-done.30, bf16[160,1024]{1,0:T(8,128)(2,1)} %reshape.241, bf16[1024,160]{0,1:T(8,128)(2,1)S(1)} %all-reduce.6, ...), kind=kOutput, calls=%fused_computation.17 | convolution fusion | flops 355467264 | bytes 21635072 | tf_op jit(solution)/shard_map/dot_general | solution.py:1274
  451.2 3.8 multiply_multiply_fusion.1
  455.0 1.3 collective-permute-start.2
  457.1 1.5 fusion.11
  458.7 1.3 maximum_maximum_fusion.sm_ref
  460.0 13.6 %multiply_reduce_fusion = (f32[1024]{0:T(1024)S(1)}, f32[1024]{0:T(1024)S(1)}, f32[1024]{0:T(1024)S(1)}, f32[1024]{0:T(1024)S(1)}, f32[1024]{0:T(1024)S(1)}, /*index=5*/f32[1024,1024]{1,0:T(8,128)}) fusion(f32[1024,1024]{1,0:T(8,128)S(1)} %copy-done.9, f32[1032,1024]{1,0:T(8,128)} %get-tuple-element.81, f32[1024]{0:T(1024)S(1)} %copy-done.21, ...), kind=kLoop, calls=%fused_computation.9 | loop fusion | flops 25160704 | bytes 25231360 | tf_op jit(solution)/shard_map/reduce_sum | solution.py:1280
  473.7 1.3 concatenate.49.all_ref
  475.8 1.4 scatter-add.4
  477.1 3.8 convert_element_type.125.dx_ref
  481.0 95.8 %tail_sums.1 = (f32[256,2048]{1,0:T(8,128)}, f32[2,256,1024]{2,1,0:T(8,128)}, f32[40,1024]{1,0:T(8,128)}, f32[32,1024]{1,0:T(8,128)}) custom-call(bf16[1024,1024]{1,0:T(8,128)(2,1)} %convert_element_type.125.dx_ref, bf16[1024,1024]{1,0:T(8,128)(2,1)} %get-tuple-element.77.dz_ref, bf16[2,2048,1024]{2,1,0:T(8,128)(2,1)} %get-tuple-element.78.w_ref, ...), custom_call_target="tpu_custom_call" | custom-call | tf_op jit(solution)/shard_map/tail_sums/pallas_call | solution.py:540
  576.9 1.5 slice.218
  578.4 1.6 slice.224
  579.9 4.5 copy.70
  586.3 1.5 fusion.46
  589.1 2.0 fusion.9
  591.1 1.1 convert_bitcast_fusion
  592.2 1.3 copy.71
  593.5 1.0 copy.82
  (145 shorter events, 17.1 us)
Async XLA Ops:
  7.2 182.0 %all-gather.2.cloned.1.call-start = ((), (), s32[]{:S(2)}) async-start(), calls=%async_computation.1 | async-start | bytes 4718592 | tf_op jit(solution)/shard_map/all_gather | solution.py:1210
  10.0 119.2 %copy-start.20 = (f32[1024]{0:T(1024)}, f32[1024]{0:T(1024)S(1)}, u32[]{:S(2)}) copy-start(f32[1024]{0:T(1024)S(1)} %get-tuple-element.181) | copy-start | bytes 12292
  12.1 157.7 %copy-start.18 = (f32[1024]{0:T(1024)}, f32[1024]{0:T(1024)S(1)}, u32[]{:S(2)}) copy-start(f32[1024]{0:T(1024)S(1)} %get-tuple-element.184) | copy-start | bytes 12292
  127.9 463.2 %reduce-scatter.2.cloned.1.call-start = ((), (), s32[]{:S(2)}) async-start(), calls=%async_computation.2 | async-start | bytes 4718592 | tf_op jit(solution)/shard_map/reduce_scatter | solution.py:1336
  129.2 3.2 copy-start.11
  130.3 1.9 copy-start.13
  130.9 1.6 copy-start.32
  140.0 23.8 %copy-start.14 = (bf16[8,48,1024]{2,1,0:T(8,128)(2,1)S(1)}, bf16[8,48,1024]{2,1,0:T(8,128)(2,1)}, u32[]{:S(2)}) copy-start(bf16[8,48,1024]{2,1,0:T(8,128)(2,1)} %get-tuple-element.57) | copy-start | bytes 2359300
  140.0 31.9 %copy-start.15 = (bf16[4,1024]{1,0:T(4,128)(2,1)S(1)}, bf16[4,1024]{1,0:T(4,128)(2,1)}, u32[]{:S(2)}) copy-start(bf16[4,1024]{1,0:T(4,128)(2,1)} %param.20) | copy-start | bytes 24580
  156.9 1.9 copy-start.1
  158.9 14.2 %collective-permute-start = (f32[16,1024]{1,0:T(8,128)S(1)}, f32[16,1024]{1,0:T(8,128)S(1)}, u32[]{:S(2)}, u32[]{:S(2)}) collective-permute-start(f32[16,1024]{1,0:T(8,128)S(1)} %fusion.26), channel_id=1, source_target_pairs={{0,4},{1,5},{2,6},{3,7},{8,12},{9,13},{10,14},{11,15},{16,20},{17,... | collective-permute-start | bytes 196616 | tf_op jit(solution)/shard_map/ppermute | solution.py:21
  173.1 11.5 %copy-start.2 = (bf16[1024,1024]{1,0:T(8,128)(2,1)S(1)}, bf16[1024,1024]{1,0:T(8,128)(2,1)}, u32[]{:S(2)}) copy-start(bf16[1024,1024]{1,0:T(8,128)(2,1)} %get-tuple-element.58) | copy-start | bytes 6291460
  173.1 11.6 %copy-start.5 = (f32[1024,1024]{1,0:T(8,128)S(1)}, f32[1024,1024]{1,0:T(8,128)}, u32[]{:S(2)}) copy-start(f32[1024,1024]{1,0:T(8,128)} %get-tuple-element.64.z_ref) | copy-start | bytes 12582916
  173.1 11.6 %copy-start.29 = (f32[1024]{0:T(1024)S(1)}, f32[1024]{0:T(1024)}, u32[]{:S(2)}) copy-start(f32[1024]{0:T(1024)} %param.26) | copy-start | bytes 12292
  330.2 2.2 copy-start
  332.4 12.0 %copy-start.7 = (bf16[1024,1024]{1,0:T(8,128)(2,1)S(1)}, bf16[1024,1024]{1,0:T(8,128)(2,1)}, u32[]{:S(2)}) copy-start(bf16[1024,1024]{1,0:T(8,128)(2,1)} %get-tuple-element.148.gated_ref) | copy-start | bytes 6291460
  332.4 12.0 %copy-start.35 = (bf16[1024,2048]{1,0:T(8,128)(2,1)S(1)}, bf16[1024,2048]{1,0:T(8,128)(2,1)}, u32[]{:S(2)}) copy-start(bf16[1024,2048]{1,0:T(8,128)(2,1)} %get-tuple-element.86) | copy-start | bytes 12582916
  342.9 7.9 %collective-permute-start.1 = (f32[16,1024]{1,0:T(8,128)S(1)}, f32[16,1024]{1,0:T(8,128)S(1)}, u32[]{:S(2)}, u32[]{:S(2)}) collective-permute-start(f32[16,1024]{1,0:T(8,128)S(1)} %fusion.25), channel_id=1, source_target_pairs={{4,0},{5,1},{6,2},{7,3},{12,8},{13,9},{14,10},{15,11},{20,16},{21,... | collective-permute-start | bytes 196616 | tf_op jit(solution)/shard_map/ppermute | solution.py:21
  410.2 32.3 %copy-start.30 = (f32[1024]{0:T(1024)S(1)}, f32[1024]{0:T(1024)}, u32[]{:S(2)}) copy-start(f32[1024]{0:T(1024)} %param.26) | copy-start | bytes 12292
  410.2 32.3 %copy-start.33 = (f32[1024]{0:T(1024)S(1)}, f32[1024]{0:T(1024)}, u32[]{:S(2)}) copy-start(f32[1024]{0:T(1024)} %param.24) | copy-start | bytes 12292
  442.5 13.8 %copy-start.3 = (bf16[1024,1024]{1,0:T(8,128)(2,1)S(1)}, bf16[1024,1024]{1,0:T(8,128)(2,1)}, u32[]{:S(2)}) copy-start(bf16[1024,1024]{1,0:T(8,128)(2,1)} %get-tuple-element.58) | copy-start | bytes 6291460
  451.1 5.7 copy-start.8
  451.2 7.5 %copy-start.34 = (f32[40]{0:T(128)S(1)}, f32[40]{0:T(128)}, u32[]{:S(2)}) copy-start(f32[40]{0:T(128)} %pad.10.clone) | copy-start | bytes 484
  455.0 20.0 %collective-permute-start.2 = (f32[3,1024]{1,0:T(4,128)S(1)}, f32[3,1024]{1,0:T(4,128)S(1)}, u32[]{:S(2)}, u32[]{:S(2)}) collective-permute-start(f32[3,1024]{1,0:T(4,128)S(1)} %pad_maximum_fusion.3), channel_id=1, source_target_pairs={{4,0},{5,1},{6,2},{7,3},{12,8},{13,9},{14,10},{15,11},{20,16},{21,... | collective-permute-start | bytes 36872 | tf_op jit(solution)/shard_map/ppermute | solution.py:21
  456.9 3.1 copy-start.19
  456.9 3.1 copy-start.21
  456.9 3.1 copy-start.22
  456.9 3.0 copy-start.23
  456.9 3.0 copy-start.24
  456.9 3.0 copy-start.25
  457.0 3.0 copy-start.26
  457.0 3.0 copy-start.27
  457.0 3.0 copy-start.28
  457.1 2.9 copy-start.9
  481.0 104.2 %copy-start.17 = (f32[1,2048]{1,0:T(1,128)S(1)}, f32[1,2048]{1,0:T(1,128)}, u32[]{:S(2)}) copy-start(f32[1,2048]{1,0:T(1,128)} %slice.189) | copy-start | bytes 24580
  576.8 8.4 %copy-start.4 = (bf16[256,2048]{1,0:T(8,128)(2,1)S(1)}, bf16[256,2048]{1,0:T(8,128)(2,1)}, u32[]{:S(2)}) copy-start(bf16[256,2048]{1,0:T(8,128)(2,1)} %hid_ref.3) | copy-start | bytes 3145732
  576.8 8.4 %copy-start.6 = (f32[256,2048]{1,0:T(8,128)S(1)}, f32[256,2048]{1,0:T(8,128)}, u32[]{:S(2)}) copy-start(f32[256,2048]{1,0:T(8,128)} %get-tuple-element.82) | copy-start | bytes 6291460
  576.8 8.9 %copy-start.31 = (bf16[512]{0:T(512)(128)(2,1)S(1)}, bf16[512]{0:T(512)(128)(2,1)}, u32[]{:S(2)}) copy-start(bf16[512]{0:T(512)(128)(2,1)} %param.18) | copy-start | bytes 3076
  576.8 11.0 %copy-start.16 = (f32[40,1024]{1,0:T(8,128)S(1)}, f32[40,1024]{1,0:T(8,128)}, u32[]{:S(2)}) copy-start(f32[40,1024]{1,0:T(8,128)} %get-tuple-element.85) | copy-start | bytes 491524
  576.9 12.2 %copy-start.10 = (f32[256,2048]{1,0:T(8,128)S(1)}, f32[256,2048]{1,0:T(8,128)}, u32[]{:S(2)}) copy-start(f32[256,2048]{1,0:T(8,128)} %get-tuple-element.68) | copy-start | bytes 6291460
  589.1 4.5 copy-start.12
Sparse Core Ops, SparseCore 0:
  128.0 38.7 all-gather.1
  350.8 52.2 reduce-scatter.1

commit v6 on v5

--- a/solution.py
+++ b/solution.py
@@ -82,22 +82,26 @@
     )(stepd, u, bc, cdiag, rate)
 
 def bwd_kernel(stepd_ref, u_ref, ds_ref, bc_ref, bdiag_ref, ones_ref, rate_ref, ckpt_ref, gin_ref,
-               wb_ref, dn_ref, db_ref, dc_ref, acc_ref, g_ref, sbf_ref, abf_ref, rbf_ref, pb_ref, pc_ref, *, unroll):
+               step_ref, sig_ref, low_ref, skip_ref, wdt_ref,
+               dpl_ref, e_ref, rank_ref, db_ref, dc_ref, acc_ref, bias_ref, dskip_ref,
+               g_ref, sbf_ref, abf_ref, rbf_ref, pb_ref, pc_ref, wb_ref, dn_ref, *, unroll):
     @pl.when(pl.program_id(1) == 0)
     def _():
         g_ref[...] = gin_ref[...]
         acc_ref[...] = jnp.zeros_like(acc_ref)
+        bias_ref[...] = jnp.zeros_like(bias_ref)
+        dskip_ref[...] = jnp.zeros_like(dskip_ref)
+
     rate = rate_ref[...]
     tb = stepd_ref.shape[0]
     nc = tb // CH
+
     def fold(v):
         p = v[:, 0:128]
         for q in range(1, v.shape[1] // 128):
             p = p + v[:, q * 128:(q + 1) * 128]
         return p
-    row = lax.broadcasted_iota(jnp.int32, (CH, CH * N), 0)
-    lane = lax.broadcasted_iota(jnp.int32, (CH, CH * N), 1)
-    diag = (row == lane // N).astype(F32)
+
     sbf_ref[0:N, :] = ckpt_ref[0].astype(BF16)
     nt = (((1,), (1,)), ((), ()))
     lanes = jnp.ones((8, 128), BF16)
@@ -141,11 +145,22 @@
     g_ref[...] = g
     acc_ref[...] = acc
 
-def bwd(stepd, u, ds, bc, bdiag, ones, rate, ckpt, gin, tb=128, w=512, unroll=1):
+    low, ds, weighted = low_ref[...].astype(F32), ds_ref[...], wb_ref[...]
+    d_pre = (LN2 * dn_ref[...] + low * weighted) * sig_ref[...]
+    d_pre_low = d_pre.astype(BF16)
+    dpl_ref[...] = d_pre_low
+    e_ref[...] = skip_ref[...] * ds + step_ref[...] * weighted
+    bias_ref[...] = bias_ref[...] + jnp.sum(d_pre, axis=0, keepdims=True)
+    dskip_ref[...] = dskip_ref[...] + jnp.sum(ds * low, axis=0, keepdims=True)
+    rank_ref[0] = lax.dot_general(wdt_ref[...], d_pre_low, nt, preferred_element_type=F32)
+
+
+def bwd(stepd, u, ds, bc, bdiag, ones, rate, ckpt, gin, step, sig, low, skip, w_dt, tb=128, w=512, unroll=1):
     t, c = stepd.shape
     w = min(w, c)
     nb = t // tb
     grid = (c // w, nb)
+    rank = w_dt.shape[0]
     rows = pl.BlockSpec((tb, w), lambda j, i: (nb - 1 - i, j))
     return pl.pallas_call(
         functools.partial(bwd_kernel, unroll=unroll),
@@ -158,25 +173,35 @@
             pl.BlockSpec((N, w), lambda j, i: (0, j)),
             pl.BlockSpec((1, N, w), lambda j, i: (nb - 1 - i, 0, j)),
             pl.BlockSpec((N, w), lambda j, i: (0, j)),
+            rows, rows, rows,
+            pl.BlockSpec((1, w), lambda j, i: (0, j)),
+            pl.BlockSpec((rank, w), lambda j, i: (0, j)),
         ],
         out_specs=[
             rows, rows,
+            pl.BlockSpec((1, rank, tb), lambda j, i: (j, 0, nb - 1 - i)),
             pl.BlockSpec((1, tb // CH, CH * N), lambda j, i: (j, nb - 1 - i, 0)),
             pl.BlockSpec((1, tb // CH, CH * N), lambda j, i: (j, nb - 1 - i, 0)),
             pl.BlockSpec((N, w), lambda j, i: (0, j)),
+            pl.BlockSpec((1, w), lambda j, i: (0, j)),
+            pl.BlockSpec((1, w), lambda j, i: (0, j)),
         ],
         out_shape=[
+            jax.ShapeDtypeStruct((t, c), BF16),
             jax.ShapeDtypeStruct((t, c), F32),
-            jax.ShapeDtypeStruct((t, c), F32),
+            jax.ShapeDtypeStruct((c // w, rank, t), F32),
             jax.ShapeDtypeStruct((c // w, t // CH, CH * N), F32),
             jax.ShapeDtypeStruct((c // w, t // CH, CH * N), F32),
             jax.ShapeDtypeStruct((N, c), F32),
+            jax.ShapeDtypeStruct((1, c), F32),
+            jax.ShapeDtypeStruct((1, c), F32),
         ],
         scratch_shapes=[pltpu.VMEM((N, w), F32), pltpu.VMEM(((tb + 1) * N, w), BF16),
-                        pltpu.VMEM((CH * N, w), BF16), pltpu.VMEM((CH * N, w), BF16), pltpu.VMEM((CH * N, 128), F32), pltpu.VMEM((CH * N, 128), F32)],
+                        pltpu.VMEM((CH * N, w), BF16), pltpu.VMEM((CH * N, w), BF16), pltpu.VMEM((CH * N, 128), F32), pltpu.VMEM((CH * N, 128), F32),
+                        pltpu.VMEM((tb, w), F32), pltpu.VMEM((tb, w), F32)],
         compiler_params=pltpu.CompilerParams(vmem_limit_bytes=48 << 20),
         name="scan_backward",
-    )(stepd, u, ds, bc, bdiag, ones, rate, ckpt, gin)
+    )(stepd, u, ds, bc, bdiag, ones, rate, ckpt, gin, step, sig, low, skip, w_dt)
 
 
 def correct_kernel(alive_ref, y_ref, stepd_ref, cdiag_ref, rate_ref, ckpt_ref, sin_ref, yo_ref, ckpto_ref, state_ref, sbf_ref):
@@ -1150,6 +1175,185 @@
         ),
         name="front",
     )(hidden, gain, count, w_in, w_small, taps, keeps)
+
+
+def mixback_kernel(n, seqs, part_ref, e_hbm, conv_hbm, x_hbm, low_hbm, dpl_hbm, step_ref, wx_ref, taps_ref, keep_ref,
+                   dx_hbm, dwx_ref, dwdt_ref, dconvw_ref,
+                   e_ref, conv_ref, x_ref, low_ref, dpl_ref, dx_ref, dcv_ref, got, own, done, edge_out, edge_in,
+                   loads, store, ms, mr, ns, nr, es, er):
+    seq, t = lax.axis_index("seq"), lax.axis_index("tensor")
+    rows = part_ref.shape[2]
+    tokens, lanes = low_ref.shape
+    taps = keep_ref.shape[1]
+    width = min(512, lanes)
+    piece = min(64, rows)
+    across = lanes // width
+    pieces = tokens // piece * across
+    ahead_seq, behind_seq = lax.rem(seq + 1, seqs), lax.rem(seq + seqs - 1, seqs)
+
+    barrier = pltpu.get_barrier_semaphore()
+    for ahead in range(1, n):
+        pl.semaphore_signal(barrier, inc=1, device_id=dict(tensor=lax.rem(t + ahead, n)), device_id_type=MESH)
+    if seqs > 1:
+        for peer in (ahead_seq, behind_seq):
+            pl.semaphore_signal(barrier, inc=1, device_id=dict(seq=peer), device_id_type=MESH)
+    pl.semaphore_wait(barrier, n - 1 + (2 if seqs > 1 else 0))
+
+    def load(i):
+        src = (conv_hbm, dpl_hbm, e_hbm, low_hbm, x_hbm)[i]
+        return pltpu.make_async_copy(src, (conv_ref, dpl_ref, e_ref, low_ref, x_ref)[i], loads.at[i])
+
+    def mix_copy(p, slot):
+        return mesh_copy(part_ref.at[p], got.at[slot], ms.at[p], mr.at[slot], tensor=p)
+
+    def sum_copy(p, slot):
+        return mesh_copy(done.at[slot], done.at[slot], ns.at[p], nr.at[slot], tensor=p)
+
+    def edge_copy():
+        return mesh_copy(edge_out, edge_in, es, er, seq=behind_seq)
+
+    for ahead in range(1, n):
+        mix_copy(lax.rem(t + ahead, n), t).start()
+    for i in range(5):
+        load(i).start()
+
+    dcv_ref[0:8, :] = jnp.zeros((8, lanes), F32)
+    dcv_ref[tokens + 8:, :] = jnp.zeros((8, lanes), F32)
+    load(1).wait()
+    tn = (((0,), (0,)), ((), ()))
+
+    @pl.loop(0, across)
+    def _(j):
+        cols = pl.ds(pl.multiple_of(j * width, width), width)
+        dwdt_ref[:, cols] = jnp.dot(step_ref[...], dpl_ref[:, cols], preferred_element_type=F32)
+
+    own[...] = part_ref[t].astype(F32)
+    for ahead in range(1, n):
+        p = lax.rem(t + ahead, n)
+        mix_copy(p, p).wait_recv()
+        own[...] = own[...] + got[p].astype(F32)
+    done[t] = own[...].astype(BF16)
+    for ahead in range(1, n):
+        sum_copy(lax.rem(t + ahead, n), t).start()
+
+    load(0).wait()
+
+    @pl.loop(0, pieces)
+    def _(i):
+        here = pl.ds(pl.multiple_of(i // across * piece, piece), piece)
+        cols = pl.ds(pl.multiple_of(i % across * width, width), width)
+        v = conv_ref[here, cols]
+        s = 1.0 / (1.0 + jnp.exp(-v))
+        conv_ref[here, cols] = s * (1.0 + v * (1.0 - s))
+
+    for i in range(2, 5):
+        load(i).wait()
+    for ahead in range(1, n):
+        p = lax.rem(t + ahead, n)
+        sum_copy(p, p).wait_recv()
+
+    dwx_ref[...] = jnp.zeros_like(dwx_ref)
+    dconvw_ref[...] = jnp.zeros_like(dconvw_ref)
+
+    @pl.loop(0, n)
+    def _(o):
+        @pl.loop(0, across)
+        def _(j):
+            cols = pl.ds(pl.multiple_of(j * width, width), width)
+            here = pl.ds(pl.multiple_of(o * rows, rows), rows)
+            mixed = lax.dot_general(done[o], wx_ref[:, cols], tn, preferred_element_type=F32)
+            dcv = (e_ref[here, cols] + mixed) * conv_ref[here, cols]
+            dcv_ref[pl.ds(pl.multiple_of(o * rows + 8, 8), rows), cols] = dcv
+            dwx_ref[:, cols] = dwx_ref[:, cols] + jnp.dot(done[o], low_ref[here, cols], preferred_element_type=F32)
+
+    def shifted(base, size, cols):
+        span = dcv_ref[pl.ds(base, size + 8), cols]
+        keep = keep_ref[pl.ds(base, size + 8), :]
+        total = jnp.zeros((size, span.shape[1]), F32)
+        for j in range(taps):
+            late = taps - 1 - j
+            total = total + taps_ref[j:j + 1, cols] * (span * keep[:, j:j + 1])[late:late + size]
+        return total
+
+    if seqs > 1:
+        edge_out[...] = shifted(0, 8, slice(None))
+
+        @pl.when(seq > 0)
+        def _():
+            edge_copy().start()
+
+    @pl.loop(0, pieces)
+    def _(i):
+        base = pl.multiple_of(i // across * piece, piece)
+        cols = pl.ds(pl.multiple_of(i % across * width, width), width)
+        dx_ref[pl.ds(base, piece), cols] = shifted(pl.multiple_of(base + 8, 8), piece, cols).astype(BF16)
+        here = dcv_ref[pl.ds(pl.multiple_of(base + 8, 8), piece), cols]
+        keep = keep_ref[pl.ds(pl.multiple_of(base + 8, 8), piece), :]
+        span = x_ref[pl.ds(base, piece + 8), cols]
+        for j in range(taps):
+            first = 8 - (taps - 1) + j
+            tap = jnp.sum(here * keep[:, j:j + 1] * span[first:first + piece], axis=0, keepdims=True)
+            dconvw_ref[j:j + 1, cols] = dconvw_ref[j:j + 1, cols] + tap
+        dconvw_ref[taps:taps + 1, cols] = dconvw_ref[taps:taps + 1, cols] + jnp.sum(here, axis=0, keepdims=True)
+
+    if seqs > 1:
+        @pl.when(seq < seqs - 1)
+        def _():
+            edge_copy().wait_recv()
+            last = shifted(tokens - 16 + 8, 16, slice(None))
+            dx_ref[tokens - 16:, :] = (last + jnp.concatenate([jnp.zeros_like(edge_in), edge_in[...]], 0)).astype(BF16)
+
+        @pl.when(seq > 0)
+        def _():
+            edge_copy().wait_send()
+
+    out = pltpu.make_async_copy(dx_ref, dx_hbm, store)
+    out.start()
+    for ahead in range(1, n):
+        p = lax.rem(t + ahead, n)
+        mix_copy(p, t).wait_send()
+        sum_copy(p, t).wait_send()
+    out.wait()
+
+
+def mixback(part, e, conv_sum, x_rows, x_low, d_pre_low, step_t, w_x, taps, keeps):
+    n, seqs = lax.axis_size("tensor"), lax.axis_size("seq")
+    tokens, lanes = x_low.shape
+    mixed, rows = part.shape[1:]
+    rank = step_t.shape[0]
+    vmem, hbm = pl.BlockSpec(memory_space=pltpu.VMEM), pl.BlockSpec(memory_space=pl.ANY)
+    dma = pltpu.SemaphoreType.DMA
+    peers = dma((n,))
+    return pl.pallas_call(
+        functools.partial(mixback_kernel, n, seqs),
+        out_shape=[
+            jax.ShapeDtypeStruct((tokens, lanes), BF16),
+            jax.ShapeDtypeStruct((mixed, lanes), F32),
+            jax.ShapeDtypeStruct((rank, lanes), F32),
+            jax.ShapeDtypeStruct((8, lanes), F32),
+        ],
+        in_specs=[vmem] + [hbm] * 5 + [vmem] * 4,
+        out_specs=[hbm] + [vmem] * 3,
+        scratch_shapes=[
+            pltpu.VMEM((tokens, lanes), F32),
+            pltpu.VMEM((tokens, lanes), F32),
+            pltpu.VMEM((tokens + 8, lanes), F32),
+            pltpu.VMEM((tokens, lanes), BF16),
+            pltpu.VMEM((tokens, lanes), BF16),
+            pltpu.VMEM((tokens, lanes), BF16),
+            pltpu.VMEM((tokens + 16, lanes), F32),
+            pltpu.VMEM((n, mixed, rows), BF16),
+            pltpu.VMEM((mixed, rows), F32),
+            pltpu.VMEM((n, mixed, rows), BF16),
+            pltpu.VMEM((8, lanes), F32),
+            pltpu.VMEM((8, lanes), F32),
+            dma((5,)), dma, peers, peers, peers, peers, dma, dma,
+        ],
+        compiler_params=pltpu.CompilerParams(
+            collective_id=4, has_side_effects=True, vmem_limit_bytes=60 << 20
+        ),
+        name="mix_backward",
+    )(part, e, conv_sum, x_rows, x_low, d_pre_low, step_t, w_x, taps, keeps)
 
 
 def on_device(
@@ -1249,77 +1453,43 @@
         gated_output_rows, w_out, hidden_in, teacher, scale, z_gate, scan_out
     )
     d_wout = jnp.einsum("te,tw->we", gated_output_rows, piece, preferred_element_type=jnp.float32)
-    d_skip_part = jnp.sum(d_scan * x_float, axis=0)
     adjoint_first = entry(alive, stepd, d_scan, col_pair, rates, tb=block)
     adjoint_in = carried(adjoint_first, reach, "seq", -1)
     ones = diagonal(jnp.ones((CH, N), F32))
-    weighted_b, d_rate, d_b_part, d_c_part, a_log_part = bwd(
-        stepd, inject, d_scan, col_pair, b_diag, ones, rates, marks, adjoint_in, tb=block, unroll=8
+    d_pre_low, d_direct, d_rank_t, d_b_part, d_c_part, a_log_part, dt_bias_part, d_skip_part = bwd(
+        stepd, inject, d_scan, col_pair, b_diag, ones, rates, marks, adjoint_in,
+        step_size, jax.nn.sigmoid(pre_act), x_low, d_skip[None], w_dt, tb=block, unroll=8
     )
-    d_step = LN2 * d_rate + x_float * weighted_b
     a_log_part = LN2 * a_log_part
-    d_b_part = jnp.sum(d_b_part, axis=0).reshape(tok_rows, N)
-    d_c_part = jnp.sum(d_c_part, axis=0).reshape(tok_rows, N)
-    d_xlow = d_skip[None] * d_scan + step_size * weighted_b
-    d_pre = d_step * jax.nn.sigmoid(pre_act)
-    dt_bias_part = jnp.sum(d_pre, axis=0)
-    d_pre_low = d_pre.astype(jnp.bfloat16)
-    d_wdt = jnp.einsum("tr,te->re", step_low, d_pre_low, preferred_element_type=jnp.float32)
-    d_rank = jnp.einsum("te,re->tr", d_pre_low, w_dt, preferred_element_type=jnp.float32)
-    d_mixed = lax.psum(jnp.concatenate([d_rank, d_b_part, d_c_part], 1), "tensor")
-    d_mixed_low = d_mixed.astype(jnp.bfloat16)
-    d_wx = jnp.einsum("te,tj->ej", x_low, d_mixed_low, preferred_element_type=jnp.float32)
-    d_wx_rank = d_wx[:, :rank_width]
-    d_wx_state = d_wx[:, rank_width:]
-    d_xlow = d_xlow + jnp.dot(d_mixed_low, w_x, preferred_element_type=F32)
-    d_conv = d_xlow * silu_slope(conv_sum)
-    conv_bias_part = jnp.sum(d_conv, axis=0)
-    conv_weight_rows = []
-    for offset in range(conv_taps):
-        conv_weight_rows.append(
-            jnp.sum(d_conv * ext_x[offset : offset + tok_rows] * tap_keeps[offset], axis=0)
-        )
-    conv_weight_part = jnp.stack(conv_weight_rows, 0)
-    conv_padded = jnp.concatenate([d_conv, jnp.zeros((back_rows, chan_lanes), jnp.float32)], 0)
-    d_x = jnp.zeros((tok_rows, chan_lanes), jnp.float32)
-    for offset in range(conv_taps):
-        lead = back_rows - offset
-        keep_padded = jnp.concatenate(
-            [tap_keeps[offset], jnp.zeros((back_rows, 1), jnp.float32)], 0
-        )
-        d_x = (
-            d_x
-            + conv_weight[offset].astype(jnp.float32)[None]
-            * conv_padded[lead : lead + tok_rows]
-            * keep_padded[lead : lead + tok_rows]
-        )
-    front_rows = []
-    for place in range(back_rows):
-        front_total = jnp.zeros((chan_lanes,), jnp.float32)
-        for offset in range(place + 1):
-            front_total = (
-                front_total
-                + conv_weight[offset].astype(jnp.float32)
-                * d_conv[place - offset]
-                * tap_keeps[offset][place - offset, 0]
-            )
-        front_rows.append(front_total)
-    front_grad = jnp.stack(front_rows, 0)
-    carried_grad = passed_along(front_grad, "seq", -1)
-    d_x = d_x.at[tok_rows - back_rows :].add(carried_grad)
+    part = jnp.concatenate(
+        [
+            jnp.sum(d_rank_t, axis=0),
+            jnp.sum(d_b_part, axis=0).reshape(tok_rows, N).T,
+            jnp.sum(d_c_part, axis=0).reshape(tok_rows, N).T,
+        ],
+        0,
+    )
+    part = part.astype(BF16).reshape(part.shape[0], -1, row_share).transpose(1, 0, 2)
+    edge = jnp.zeros((8, conv_taps), F32)
+    d_x, d_wx, d_wdt, conv_parts = mixback(
+        part, d_direct, conv_sum, x_rows, x_low, d_pre_low, step_low.T, w_x, taps,
+        jnp.concatenate([edge] + [jnp.concatenate(tap_keeps, 1)] + [edge], 0),
+    )
+    d_wx_rank, d_wx_state = d_wx[:rank_width], d_wx[rank_width:]
+    conv_weight_part, conv_bias_part = conv_parts[:conv_taps], conv_parts[conv_taps]
     small = jnp.concatenate(
         [
-            d_wx_rank.T.reshape(parts, -1, chan_lanes),
-            d_wx_state.T.reshape(parts, -1, chan_lanes),
+            d_wx_rank.reshape(parts, -1, chan_lanes),
+            d_wx_state.reshape(parts, -1, chan_lanes),
             d_wdt.reshape(parts, -1, chan_lanes),
             jnp.zeros((parts, 4, chan_lanes), F32),
         ],
         1,
     )
     whole = jnp.concatenate(
-        [a_log_part, conv_weight_part, jnp.stack([conv_bias_part, dt_bias_part, d_skip_part, d_skip_part], 0)], 0
+        [a_log_part, conv_weight_part, conv_bias_part[None], dt_bias_part, d_skip_part, d_skip_part], 0
     )
-    d_norm_share, g_in, g_small, g_whole = tail(d_x.astype(BF16), d_z, w_in, normalized_rows, small, whole)
+    d_norm_share, g_in, g_small, g_whole = tail(d_x, d_z, w_in, normalized_rows, small, whole)
     g_in = jnp.swapaxes(g_in, 0, 1)
     inner_sum = jnp.sum(d_norm_share * full_gain[None] * share_rows, axis=1, keepdims=True)
     inv_cube = inv_share * inv_share * inv_share

time: 610 us -> 587 us (0.962)
  Pallas kernels: 432 us -> 469 us
  blocking collectives: 28.8 us -> 0 us
  other arithmetic: 49.7 us -> 24.9 us
  matrix products: 26 us -> 15 us
  starting transfers between devices: 7.14 us -> 16.7 us
    pallas_call x0 -> x1, Pallas kernels: none -> 32.4 us  [mixback(): pl.pallas_call(functools.partial(mixback_kernel, n, seqs), out_shape=[jax...]
    psum x1 -> x0, blocking collectives: 28.8 us -> none  [on_device(): lax.psum(jnp.concatenate([d_rank, d_b_part, d_c_part], 1), 'tensor')]
    reduce_sum x4 -> x3, other arithmetic: 21.4 us -> 0.09 us  [the longest x1 0.06 us: on_device(): jnp.sum(d_rank_t, axis=0)]
    dot_general x4 -> x0, matrix products: 12.3 us -> none  [the longest x1 8.61 us: on_device(): d_xlow = d_xlow + jnp.dot(d_mixed_low, w_x, preferred_element_type=F32)]
    ppermute x3 -> x2, starting transfers between devices: 7.06 us -> 16.6 us  [passed_along(): return lax.ppermute(x, axis, pairs)]
    pallas_call x1, Pallas kernels: 51.6 us -> 58 us  [bwd(): pl.pallas_call(functools.partial(bwd_kernel, unroll=unroll), grid=grid, i...]
    unnamed x79 -> x43, local copies, waits for them, and re-layouts: 16.9 us -> 18.9 us
  transfers between devices with their start and end apart: 5 -> 4, of which waited for: 1 -> 0; matrix products, arithmetic and copies ran while one was open for 16% -> 8% of each run, Pallas kernels for 29% -> 38%
where the time goes in v6:
time: 587 us; the launch traced here: 582 us
  Pallas kernels  469 us (80%)
  local copies, waits for them, and re-layouts  39.6 us (7%)
  other arithmetic  24.9 us (4%)
  starting transfers between devices  16.7 us (3%)
  between operations  16.1 us (3%)
  matrix products  15 us (3%)
    pallas_call x1, Pallas kernels, middle(): pl.pallas_call(functools.partial(mid_kernel, n, subs, 2), out_shape=[jax....  141 us
    pallas_call x1, Pallas kernels, front(): pl.pallas_call(functools.partial(front_kernel, n, dps, seqs, subs, 2), ou...  105 us
    pallas_call x1, Pallas kernels, tail(): pl.pallas_call(functools.partial(tail_kernel, n, dps, seqs, subs, 2), out...  94.5 us
    pallas_call x1, Pallas kernels, bwd(): pl.pallas_call(functools.partial(bwd_kernel, unroll=unroll), grid=grid, i...  58 us
    pallas_call x1, Pallas kernels, mixback(): pl.pallas_call(functools.partial(mixback_kernel, n, seqs), out_shape=[jax...  32.4 us
    unnamed x43, local copies, waits for them, and re-layouts  18.9 us
    pallas_call x1, Pallas kernels, fwd(): pl.pallas_call(functools.partial(fwd_kernel, unroll=unroll), grid=grid, i...  17 us
    ppermute x2, starting transfers between devices, passed_along(): return lax.ppermute(x, axis, pairs)  16.6 us
  transfers between devices with their start and end apart: 4, of which 0 were waited for; matrix products, arithmetic and copies ran while one was open for 8% of the time, Pallas kernels for 38%

profile of v6, /device:TPU:0, one launch (start us, length us, event | category | flops | bytes accessed | tf_op | source)
XLA Modules:
  0.0 581.8 jit_solution(15429570480905638060)
XLA Ops:
  7.2 1.3 fusion.18
  8.5 0.7 convert_element_type.61
  9.2 0.8 compare_convert_fusion
  12.1 0.7 convert_element_type.66
  13.2 0.8 concatenate.42.keep_ref
  14.0 2.0 copy.79
  16.0 2.5 copy.99
  19.3 1.5 maximum_maximum_fusion.1.wsm_ref
  20.8 1.2 broadcast_in_dim.96.cnt_ref
  22.7 104.7 %front.1 = (f32[1032,1024]{1,0:T(8,128)}, f32[1024,1024]{1,0:T(8,128)}, bf16[1024,2048]{1,0:T(8,128)(2,1)}, bf16[2,2048,1024]{2,1,0:T(8,128)(2,1)}, f32[1024,102...) custom-call(bf16[256,2048]{1,0:T(8,128)(2,1)} %hid_ref.3, ...), custom_call_target="tpu_custom_call" | custom-call | tf_op jit(solution)/shard_map/front/pallas_call | solution.py:1139
  127.4 1.3 copy.94
  128.7 1.0 slice.82
  131.9 5.6 fusion.20
  137.5 3.2 convert_multiply_fusion.1.u_ref
  140.8 17.0 %scan_forward.1 = (f32[1024,1024]{1,0:T(8,128)S(1)}, f32[8,16,1024]{2,1,0:T(8,128)S(1)}, f32[16,1024]{1,0:T(8,128)S(1)}) custom-call(f32[1024,1024]{1,0:T(8,128)} %get-tuple-element.146.stepd_ref, f32[1024,1024]{1,0:T(8,128)} %convert_multiply_fusion.1.u_ref, f32[64,16,32]{2,1,0:T(8,128)S(1)} %pad_maximum_fusion.1.bc_ref, ...), custom_call_target="tpu_custom_call" | custom-call | tf_op jit(solution)/shard_map/scan_forward/pallas_call | solution.py:59
  157.7 1.9 copy-done.1
  159.7 4.3 collective-permute-start
  164.3 1.2 slice.85
  166.3 0.8 copy.80.scale_ref
  167.1 11.5 %scan_correct.1 = (f32[1024,1024]{1,0:T(8,128)S(1)}, f32[8,16,1024]{2,1,0:T(8,128)S(1)}) custom-call(s32[8]{0:T(128)S(1)} %compare_convert_fusion.1.alive_ref, f32[1024,1024]{1,0:T(8,128)} %copy-done.1, f32[1024,1024]{1,0:T(8,128)} %get-tuple-element.146.stepd_ref, bf16[1024,256]{1,0:T(8,128)(2,1)S(1)} %get-tuple-element.161.cdiag_ref, ...), custom_call_target="tpu_custom_call" | custom-call | tf_op jit(solution)/shard_map/scan_correct/pallas_call | solution.py:245
  178.7 4.4 multiply_convert_fusion
  183.1 141.1 %middle.1 = (bf16[256,2048]{1,0:T(8,128)(2,1)}, f32[256,2048]{1,0:T(8,128)}, bf16[1024,2048]{1,0:T(8,128)(2,1)}, f32[1024,1024]{1,0:T(8,128)}, bf16[1024,1024]{1,0:T(8,128)(2,1)}) custom-call(bf16[1024,1024]{1,0:T(8,128)(2,1)} %get-tuple-element.143.gated_ref, bf16[2048,1024]{1,0:T(8,128)(2,1)} %all-gather.2.cloned.1.call-done.w_ref, ...), custom_call_target="tpu_custom_call" | custom-call | tf_op jit(solution)/shard_map/middle/pallas_call | solution.py:787
  324.2 9.4 %convolution_convert_fusion = bf16[2048,1024]{1,0:T(8,128)(2,1)} fusion(bf16[1024,2048]{1,0:T(8,128)(2,1)} %get-tuple-element.88, bf16[1024,1024]{1,0:T(8,128)(2,1)} %get-tuple-element.143.gated_ref), kind=kOutput, calls=%fused_computation.6 | convolution fusion | flops 4297064448 | bytes 10485760 | tf_op jit(solution)/shard_map/te,tw->we/dot_general | solution.py:1455
  333.6 0.7 slice_bitcast_fusion.step_ref
  334.7 0.8 pad_maximum_fusion.keep_ref
  335.6 2.5 copy-done
  338.1 10.1 %scan_entry.1 = f32[16,1024]{1,0:T(8,128)S(1)} custom-call(s32[8]{0:T(128)S(1)} %compare_convert_fusion.1.alive_ref, f32[1024,1024]{1,0:T(8,128)S(1)} %copy-done, f32[1024,1024]{1,0:T(8,128)} %get-tuple-element.65.ds_ref, f32[64,16,32]{2,1,0:T(8,128)S(1)} %pad_maximum_fusion.1.bc_ref, f32[16,1024]{1,0:T(8,128)S(1)} %fusion.8.rate_ref), custom_call_target="tpu_custom_call" | custom-call | tf_op jit(solution)/shard_map/scan_entry/pallas_call | solution.py:290
  348.3 12.4 %collective-permute-start.1 = (f32[16,1024]{1,0:T(8,128)S(1)}, f32[16,1024]{1,0:T(8,128)S(1)}, u32[]{:S(2)}, u32[]{:S(2)}) collective-permute-start(f32[16,1024]{1,0:T(8,128)S(1)} %fusion.9), channel_id=1, source_target_pairs={{4,0},{5,1},{6,2},{7,3},{12,8},{13,9},{14,10},{15,11},{20,16},{21,... | collective-permute-start | bytes 196616 | tf_op jit(solution)/shard_map/ppermute | solution.py:21
  360.9 0.8 slice.86
  361.7 0.8 reshape.208.wx_ref
  362.5 58.0 %scan_backward.1 = (bf16[1024,1024]{1,0:T(8,128)(2,1)S(1)}, f32[1024,1024]{1,0:T(8,128)}, f32[2,128,1024]{2,1,0:T(8,128)S(1)}, f32[2,64,256]{2,1,0:T(8,128)S(1)}...) custom-call(f32[1024,1024]{1,0:T(8,128)} %get-tuple-element.146.stepd_ref, ...), custom_call_target="tpu_custom_call" | custom-call | tf_op jit(solution)/shard_map/scan_backward/pallas_call | solution.py:165
  420.5 1.3 copy-done.2
  423.0 0.8 maximum_bitcast_fusion.part_ref
  423.7 32.4 %mix_backward.1 = (bf16[1024,1024]{1,0:T(8,128)(2,1)}, f32[160,1024]{1,0:T(8,128)}, f32[128,1024]{1,0:T(8,128)}, f32[8,1024]{1,0:T(8,128)}) custom-call(bf16[4,160,256]{2,1,0:T(8,128)(2,1)} %maximum_bitcast_fusion.part_ref, f32[1024,1024]{1,0:T(8,128)} %get-tuple-element.70.e_hbm, f32[1024,1024]{1,0:T(8,128)} %get-tuple-element.71.conv_hbm, ...), custom_call_target="tpu_custom_call" | custom-call | tf_op jit(solution)/shard_map/mix_backward/pallas_call | solution.py:1327
  456.2 0.9 slice.89
  457.1 1.1 slice.88
  458.2 2.0 concatenate.50.all_ref
  460.2 2.3 maximum_maximum_fusion.sm_ref
  462.6 94.5 %tail_sums.1 = (f32[256,2048]{1,0:T(8,128)}, f32[2,256,1024]{2,1,0:T(8,128)}, f32[40,1024]{1,0:T(8,128)}, f32[32,1024]{1,0:T(8,128)}) custom-call(bf16[1024,1024]{1,0:T(8,128)(2,1)} %get-tuple-element.74.dx_ref, bf16[1024,1024]{1,0:T(8,128)(2,1)} %get-tuple-element.75.dz_ref, bf16[2,2048,1024]{2,1,0:T(8,128)(2,1)} %get-tuple-element.76.w_ref, ...), custom_call_target="tpu_custom_call" | custom-call | tf_op jit(solution)/shard_map/tail_sums/pallas_call | solution.py:565
  557.1 1.5 slice.92
  558.7 1.6 slice.98
  560.2 4.5 copy.88
  564.7 0.7 slice_reduce_fusion
  566.6 1.5 fusion.25
  569.4 2.0 fusion.4
  571.4 1.1 convert_bitcast_fusion
  572.5 1.3 copy.89
  573.8 1.0 copy.101
  (102 shorter events, 10.0 us)
Async XLA Ops:
  7.2 14.9 %copy-start.16 = (bf16[512]{0:T(512)(128)(2,1)S(1)}, bf16[512]{0:T(512)(128)(2,1)}, u32[]{:S(2)}) copy-start(bf16[512]{0:T(512)(128)(2,1)} %param.16) | copy-start | bytes 3076
  7.2 175.9 %all-gather.2.cloned.1.call-start = ((), (), s32[]{:S(2)}) async-start(), calls=%async_computation.1 | async-start | bytes 4718592 | tf_op jit(solution)/shard_map/all_gather | solution.py:1414
  127.4 444.0 %reduce-scatter.2.cloned.1.call-start = ((), (), s32[]{:S(2)}) async-start(), calls=%async_computation.2 | async-start | bytes 4718592 | tf_op jit(solution)/shard_map/reduce_scatter | solution.py:1506
  129.7 1.9 copy-start.13
  130.2 1.6 copy-start.17
  131.9 5.6 copy-start.4
  137.5 3.3 copy-start.6
  157.7 1.9 copy-start.1
  159.7 7.4 %collective-permute-start = (f32[16,1024]{1,0:T(8,128)S(1)}, f32[16,1024]{1,0:T(8,128)S(1)}, u32[]{:S(2)}, u32[]{:S(2)}) collective-permute-start(f32[16,1024]{1,0:T(8,128)S(1)} %fusion.10), channel_id=1, source_target_pairs={{0,4},{1,5},{2,6},{3,7},{8,12},{9,13},{10,14},{11,15},{16,20},{17,... | collective-permute-start | bytes 196616 | tf_op jit(solution)/shard_map/ppermute | solution.py:21
  167.1 11.6 %copy-start.3 = (f32[1024]{0:T(1024)S(1)}, f32[1024]{0:T(1024)}, u32[]{:S(2)}) copy-start(f32[1024]{0:T(1024)} %param.24) | copy-start | bytes 12292
  167.1 11.6 %copy-start.5 = (bf16[1024,1024]{1,0:T(8,128)(2,1)S(1)}, bf16[1024,1024]{1,0:T(8,128)(2,1)}, u32[]{:S(2)}) copy-start(bf16[1024,1024]{1,0:T(8,128)(2,1)} %get-tuple-element.53.low_ref.low_hbm) | copy-start | bytes 6291460
  167.1 11.6 %copy-start.8 = (f32[1024,1024]{1,0:T(8,128)S(1)}, f32[1024,1024]{1,0:T(8,128)}, u32[]{:S(2)}) copy-start(f32[1024,1024]{1,0:T(8,128)} %get-tuple-element.59.z_ref) | copy-start | bytes 12582916
  333.6 1.1 copy-start.10
  335.6 2.5 copy-start
  338.1 22.6 %copy-start.14 = (bf16[8,48,1024]{2,1,0:T(8,128)(2,1)S(1)}, bf16[8,48,1024]{2,1,0:T(8,128)(2,1)}, u32[]{:S(2)}) copy-start(bf16[8,48,1024]{2,1,0:T(8,128)(2,1)} %get-tuple-element.52) | copy-start | bytes 2359300
  348.3 14.2 %collective-permute-start.1 = (f32[16,1024]{1,0:T(8,128)S(1)}, f32[16,1024]{1,0:T(8,128)S(1)}, u32[]{:S(2)}, u32[]{:S(2)}) collective-permute-start(f32[16,1024]{1,0:T(8,128)S(1)} %fusion.9), channel_id=1, source_target_pairs={{4,0},{5,1},{6,2},{7,3},{12,8},{13,9},{14,10},{15,11},{20,16},{21,... | collective-permute-start | bytes 196616 | tf_op jit(solution)/shard_map/ppermute | solution.py:21
  420.5 1.3 copy-start.2
  557.1 8.4 %copy-start.7 = (bf16[256,2048]{1,0:T(8,128)(2,1)S(1)}, bf16[256,2048]{1,0:T(8,128)(2,1)}, u32[]{:S(2)}) copy-start(bf16[256,2048]{1,0:T(8,128)(2,1)} %hid_ref.3) | copy-start | bytes 3145732
  557.1 8.4 %copy-start.9 = (f32[256,2048]{1,0:T(8,128)S(1)}, f32[256,2048]{1,0:T(8,128)}, u32[]{:S(2)}) copy-start(f32[256,2048]{1,0:T(8,128)} %get-tuple-element.84) | copy-start | bytes 6291460
  557.1 11.0 %copy-start.15 = (f32[40,1024]{1,0:T(8,128)S(1)}, f32[40,1024]{1,0:T(8,128)}, u32[]{:S(2)}) copy-start(f32[40,1024]{1,0:T(8,128)} %get-tuple-element.87) | copy-start | bytes 491524
  557.1 12.2 %copy-start.11 = (f32[256,2048]{1,0:T(8,128)S(1)}, f32[256,2048]{1,0:T(8,128)}, u32[]{:S(2)}) copy-start(f32[256,2048]{1,0:T(8,128)} %get-tuple-element.63) | copy-start | bytes 6291460
  569.4 4.5 copy-start.12
Sparse Core Ops, SparseCore 0:
  127.5 38.8 all-gather.1
  333.8 49.4 reduce-scatter.1

commit v7 on v6

--- a/solution.py
+++ b/solution.py
@@ -30,11 +30,19 @@
 N = 16
 CH = 16
 
-def fwd_kernel(stepd_ref, u_ref, bc_ref, cdiag_ref, rate_ref, y_ref, ckpt_ref, last_ref, state_ref, sbf_ref, *, unroll):
+def fwd_kernel(rank_ref, wdt_ref, bias_ref, low_ref, keep_ref, bc_ref, cdiag_ref, rate_ref,
+               y_ref, ckpt_ref, last_ref, stepd_ref, u_ref, step_ref, sig_ref, state_ref, sbf_ref, *, unroll):
     @pl.when(pl.program_id(1) == 0)
     def _():
         state_ref[...] = jnp.zeros_like(state_ref)
     ckpt_ref[0] = state_ref[...]
+    pre = jnp.dot(rank_ref[...], wdt_ref[...], preferred_element_type=F32) + bias_ref[...]
+    small = jnp.exp(-jnp.abs(pre))
+    step = jnp.maximum(pre, 0.0) + jnp.log1p(small)
+    step_ref[...] = step
+    sig_ref[...] = jnp.where(pre >= 0, 1.0, small) / (1.0 + small)
+    stepd_ref[...] = jnp.where(keep_ref[...] > 0, step, FAR)
+    u_ref[...] = step * low_ref[...].astype(F32)
     rate = rate_ref[...]
     tb = stepd_ref.shape[0]
 
@@ -52,34 +60,43 @@
     state_ref[...] = s
     last_ref[...] = s
 
-def fwd(stepd, u, bc, cdiag, rate, tb=128, w=512, unroll=1):
-    t, c = stepd.shape
+def fwd(rank, w_dt, bias, low, keep, bc, cdiag, rate, tb=128, w=512, unroll=1):
+    t, c = low.shape
     w = min(w, c)
     grid = (c // w, t // tb)
+    width = rank.shape[1]
+    rows = pl.BlockSpec((tb, w), lambda j, i: (i, j))
+    whole = jax.ShapeDtypeStruct((t, c), F32)
     return pl.pallas_call(
         functools.partial(fwd_kernel, unroll=unroll),
         grid=grid,
         in_specs=[
-            pl.BlockSpec((tb, w), lambda j, i: (i, j)),
-            pl.BlockSpec((tb, w), lambda j, i: (i, j)),
+            pl.BlockSpec((tb, width), lambda j, i: (i, 0)),
+            pl.BlockSpec((width, w), lambda j, i: (0, j)),
+            pl.BlockSpec((1, w), lambda j, i: (0, j)),
+            rows,
+            pl.BlockSpec((tb, 1), lambda j, i: (i, 0)),
             pl.BlockSpec((tb // CH, N, 2 * CH), lambda j, i: (i, 0, 0)),
             pl.BlockSpec((tb, CH * N), lambda j, i: (i, 0)),
             pl.BlockSpec((N, w), lambda j, i: (0, j)),
         ],
         out_specs=[
-            pl.BlockSpec((tb, w), lambda j, i: (i, j)),
+            rows,
             pl.BlockSpec((1, N, w), lambda j, i: (i, 0, j)),
             pl.BlockSpec((N, w), lambda j, i: (0, j)),
+            rows, rows, rows, rows,
         ],
         out_shape=[
-            jax.ShapeDtypeStruct((t, c), F32),
+            whole,
             jax.ShapeDtypeStruct((t // tb, N, c), F32),
             jax.ShapeDtypeStruct((N, c), F32),
+            whole, whole, whole, whole,
         ],
         scratch_shapes=[pltpu.VMEM((N, w), F32), pltpu.VMEM((CH * N, w), BF16)],
         compiler_params=pltpu.CompilerParams(vmem_limit_bytes=48 << 20),
         name="scan_forward",
-    )(stepd, u, bc, cdiag, rate)
+    )(rank, w_dt, bias, low, keep, bc, cdiag, rate)
+
 
 def bwd_kernel(stepd_ref, u_ref, ds_ref, bc_ref, bdiag_ref, ones_ref, rate_ref, ckpt_ref, gin_ref,
                step_ref, sig_ref, low_ref, skip_ref, wdt_ref,
@@ -204,7 +221,8 @@
     )(stepd, u, ds, bc, bdiag, ones, rate, ckpt, gin, step, sig, low, skip, w_dt)
 
 
-def correct_kernel(alive_ref, y_ref, stepd_ref, cdiag_ref, rate_ref, ckpt_ref, sin_ref, yo_ref, ckpto_ref, state_ref, sbf_ref):
+def correct_kernel(alive_ref, y_ref, stepd_ref, cdiag_ref, rate_ref, ckpt_ref, sin_ref, low_ref, skip_ref, z_ref,
+                   yo_ref, ckpto_ref, gated_ref, state_ref, sbf_ref):
     i = pl.program_id(1)
 
     @pl.when(i == 0)
@@ -235,8 +253,13 @@
         yo_ref[...] = y_ref[...]
         ckpto_ref[...] = ckpt_ref[...]
 
-
-def correct(alive, y, stepd, cdiag, rate, ckpt, state_in, tb=128, w=512):
+    total = yo_ref[...] + skip_ref[...] * low_ref[...].astype(F32)
+    z = z_ref[...]
+    yo_ref[...] = total
+    gated_ref[...] = (total * (z / (1.0 + jnp.exp(-z)))).astype(BF16)
+
+
+def correct(alive, y, stepd, cdiag, rate, ckpt, state_in, low, skip, z, tb=128, w=512):
     t, c = stepd.shape
     w = min(w, c)
     rows = pl.BlockSpec((tb, w), lambda j, i, _: (i, j))
@@ -247,14 +270,16 @@
         grid_spec=pltpu.PrefetchScalarGridSpec(
             num_scalar_prefetch=1,
             grid=(c // w, t // tb),
-            in_specs=[rows, rows, pl.BlockSpec((tb, CH * N), lambda j, i, _: (i, 0)), lanes, marks, lanes],
-            out_specs=[rows, marks],
+            in_specs=[rows, rows, pl.BlockSpec((tb, CH * N), lambda j, i, _: (i, 0)), lanes, marks, lanes,
+                      rows, pl.BlockSpec((1, w), lambda j, i, _: (0, j)), rows],
+            out_specs=[rows, marks, rows],
             scratch_shapes=[pltpu.VMEM((N, w), F32), pltpu.VMEM((CH * N, w), BF16)],
         ),
-        out_shape=[jax.ShapeDtypeStruct((t, c), F32), jax.ShapeDtypeStruct(ckpt.shape, F32)],
+        out_shape=[jax.ShapeDtypeStruct((t, c), F32), jax.ShapeDtypeStruct(ckpt.shape, F32),
+                   jax.ShapeDtypeStruct((t, c), BF16)],
         compiler_params=pltpu.CompilerParams(vmem_limit_bytes=48 << 20),
         name="scan_correct",
-    )(alive, y, stepd, cdiag, rate, ckpt, state_in)
+    )(alive, y, stepd, cdiag, rate, ckpt, state_in, low, skip, z)
 
 
 def entry_kernel(alive_ref, stepd_ref, ds_ref, bc_ref, rate_ref, g_ref):
@@ -303,8 +328,8 @@
 
 def carried(local, reach, axis, by):
     found = jnp.zeros_like(local)
-    for _ in range(lax.axis_size(axis) - 1):
-        found = passed_along(local + reach * found, axis, by)
+    for turn in range(lax.axis_size(axis) - 1):
+        found = passed_along(local if turn == 0 else local + reach() * found, axis, by)
     return found
 
 
@@ -330,20 +355,19 @@
     return dp, seq, mine
 
 
-def tail_kernel(n, dps, seqs, subs, lag, dx_ref, dz_ref, w_ref, nrm_ref, sm_ref, all_ref,
+def tail_kernel(n, dps, seqs, tile, lag, dx_ref, dz_ref, w_hbm, nrm_ref, sm_ref, all_ref,
                 dn_ref, gin_ref, gs_ref, ga_ref,
                 gacc, gsend, grecv, all_mine,
-                zr, zl, part_r, part_l, one_send, one_recv, two_recv, sm_one, sm_two, all_one, all_two,
+                zr, zl, w_ref, loads, one_send, one_recv, two_recv, sm_one, sm_two, all_one, all_two,
                 r_send, r_recv, l_send, l_recv, w1s, w1r, w2s, w2r, s1s, s1r, s2s, s2r, a1s, a1r, a2s, a2r, gs, gr):
     dp, seq, t = place()
     core, hi = dp % 2, dp // 2
     chips = dps // 2 * seqs
     chip = hi * seqs + seq
     rows = dn_ref.shape[0]
-    part = rows // subs
     wide = dn_ref.shape[1]
     wrows = gin_ref.shape[1]
-    tile = 512
+    subs = wide // tile
 
     def owner(q, c):
         return (q // seqs * 2 + c) * seqs + q % seqs
@@ -392,19 +416,23 @@
     def g_copy(p, slot):
         return mesh_copy(gsend.at[p], grecv.at[slot], gs.at[p], gr.at[slot], tensor=p)
 
-    def partial_rows(o, dst):
+    def cols_of(sub):
+        return pl.ds(pl.multiple_of(sub * tile, tile), tile)
+
+    def load(sub):
+        ref = w_ref.at[:, cols_of(sub), :]
+        return pltpu.make_async_copy(w_hbm.at[:, cols_of(sub), :], ref, loads.at[sub])
+
+    def partial_tile(o, sub):
         here = pl.ds(pl.multiple_of(o * rows, rows), rows)
-
-        @pl.loop(0, wide // tile)
-        def _(j):
-            cols = pl.ds(pl.multiple_of(j * tile, tile), tile)
-            nt = (((1,), (1,)), ((), ()))
-            block = lax.dot_general(
-                dx_ref[here, :], w_ref[0, cols, :], nt, preferred_element_type=F32
-            ) + lax.dot_general(dz_ref[here, :], w_ref[1, cols, :], nt, preferred_element_type=F32)
-            dst[:, cols] = block
-            scaled = block * nrm_ref[here, cols].astype(F32)
-            gacc[:, cols] = gacc[:, cols] + jnp.sum(scaled.reshape(rows // 8, 8, tile), axis=0)
+        cols = cols_of(sub)
+        nt = (((1,), (1,)), ((), ()))
+        block = lax.dot_general(
+            dx_ref[here, :], w_ref[0, cols, :], nt, preferred_element_type=F32
+        ) + lax.dot_general(dz_ref[here, :], w_ref[1, cols, :], nt, preferred_element_type=F32)
+        scaled = block * nrm_ref[here, cols].astype(F32)
+        gacc[:, cols] = gacc[:, cols] + jnp.sum(scaled.reshape(rows // 8, 8, tile), axis=0)
+        return block
 
     def weight_rows(p, k):
         cols = pl.ds(pl.multiple_of(p * wrows, wrows), wrows)
@@ -412,36 +440,36 @@
         d_ref = dx_ref if k == 0 else dz_ref
         return lax.dot_general(nrm_ref[:, cols], d_ref[...], tn, preferred_element_type=F32)
 
+    @pl.loop(0, subs)
+    def _(sub):
+        load(sub).start()
+
     for q in range(chips):
         s1_copy(q).start()
 
-    def stream(i, limit, start, buf, copy, part_ref, owner_of):
+    def stream(i, limit, start, buf, copy, owner_of):
         @pl.when(jnp.logical_and(i >= 0, i < limit))
         def _():
-            k, sub = i // subs, i % subs
-
-            @pl.when(sub == 0)
+            block = partial_tile(owner_of(i // subs), i % subs)
+
+            @pl.when(start)
             def _():
-                partial_rows(owner_of(k), part_ref)
-
-            @pl.when(jnp.logical_and(start, sub == 0))
-            def _():
-                @pl.loop(0, subs)
-                def _(j):
-                    here = part_ref[pl.ds(pl.multiple_of(j * part, part), part), :]
-                    buf[k * subs + j] = here.astype(BF16)
-                    copy(k * subs + j).start()
+                buf[i] = block.astype(BF16)
 
             @pl.when(jnp.logical_not(start))
             def _():
-                here = part_ref[pl.ds(pl.multiple_of(sub * part, part), part), :]
                 copy(i).wait_recv()
-                buf[i] = (here + buf[i].astype(F32)).astype(BF16)
-                copy(i).start()
+                buf[i] = (block + buf[i].astype(F32)).astype(BF16)
+
+            copy(i).start()
 
     def step(g, _):
-        stream(g - lag * t, (n - 1 - t) * subs, t == 0, zr, r_copy, part_r, lambda k: n - 1 - k)
-        stream(g - lag * (n - 1 - t), t * subs, t == n - 1, zl, l_copy, part_l, lambda k: k)
+        @pl.when(g < subs)
+        def _():
+            load(g).wait()
+
+        stream(g - lag * t, (n - 1 - t) * subs, t == 0, zr, r_copy, lambda k: n - 1 - k)
+        stream(g - lag * (n - 1 - t), t * subs, t == n - 1, zl, l_copy, lambda k: k)
 
         @pl.when(g < chips)
         def _():
@@ -469,13 +497,13 @@
             for k in range(2):
                 gin_ref[k] = weight_rows(owner(chip, core), k) + one_recv[chip, k].astype(F32)
 
-        @pl.when(g == 2 * chips)
-        def _():
-            partial_rows(t, dn_ref)
+        @pl.when(jnp.logical_and(g >= 2 * chips, g < 2 * chips + subs))
+        def _():
+            dn_ref[:, cols_of(g - 2 * chips)] = partial_tile(t, g - 2 * chips)
 
         return 0
 
-    steps = max((n - 1) * max(subs, lag), 2 * chips + 1)
+    steps = max((n - 1) * max(subs, lag), 2 * chips + subs)
     lax.fori_loop(0, steps, step, 0)
 
     share = wide // n
@@ -486,19 +514,19 @@
 
     @pl.loop(0, subs)
     def _(s):
-        here = pl.ds(pl.multiple_of(s * part, part), part)
+        cols = cols_of(s)
 
         @pl.when(t > 0)
         def _():
             i = (n - 1 - t) * subs + s
             r_copy(i).wait_recv()
-            dn_ref[here, :] = dn_ref[here, :] + zr[i].astype(F32)
+            dn_ref[:, cols] = dn_ref[:, cols] + zr[i].astype(F32)
 
         @pl.when(t < n - 1)
         def _():
             i = t * subs + s
             l_copy(i).wait_recv()
-            dn_ref[here, :] = dn_ref[here, :] + zl[i].astype(F32)
+            dn_ref[:, cols] = dn_ref[:, cols] + zl[i].astype(F32)
 
     plain = all_ref.shape[0]
     all_mine[0:plain, :] = all_ref[...]
@@ -557,30 +585,31 @@
     rows = dx.shape[0] // n
     wide, lanes = w_full.shape[1], w_full.shape[2]
     wrows = wide // (dps * seqs)
-    subs = max(1, rows // 32)
+    tile = 256
+    subs = wide // tile
     hops = (n - 1) * subs
-    vmem = pl.BlockSpec(memory_space=pltpu.VMEM)
+    vmem, hbm = pl.BlockSpec(memory_space=pltpu.VMEM), pl.BlockSpec(memory_space=pl.ANY)
     dma = pltpu.SemaphoreType.DMA
     few = dma((chips,))
     return pl.pallas_call(
-        functools.partial(tail_kernel, n, dps, seqs, subs, 2),
+        functools.partial(tail_kernel, n, dps, seqs, tile, 2),
         out_shape=[
             jax.ShapeDtypeStruct((rows, wide), F32),
             jax.ShapeDtypeStruct((2, wrows, lanes), F32),
             jax.ShapeDtypeStruct(small.shape[1:], F32),
             jax.ShapeDtypeStruct((whole.shape[0] + 8, lanes), F32),
         ],
-        in_specs=[vmem] * 6,
+        in_specs=[vmem] * 2 + [hbm] + [vmem] * 3,
         out_specs=[vmem] * 4,
         scratch_shapes=[
             pltpu.VMEM((8, wide), F32),
             pltpu.VMEM((n, 8, wide // n), F32),
             pltpu.VMEM((n, 8, wide // n), F32),
             pltpu.VMEM((whole.shape[0] + 8, lanes), F32),
-            pltpu.VMEM((hops, rows // subs, wide), BF16),
-            pltpu.VMEM((hops, rows // subs, wide), BF16),
-            pltpu.VMEM((rows, wide), F32),
-            pltpu.VMEM((rows, wide), F32),
+            pltpu.VMEM((hops, rows, tile), BF16),
+            pltpu.VMEM((hops, rows, tile), BF16),
+            pltpu.VMEM((2, wide, lanes), BF16),
+            dma((subs,)),
             pltpu.VMEM((chips, 2, wrows, lanes), BF16),
             pltpu.VMEM((chips, 2, wrows, lanes), BF16),
             pltpu.VMEM((chips, 2, wrows, lanes), BF16),
@@ -598,13 +627,14 @@
     )(dx, dz, w_full, normed, small, whole)
 
 
-def mid_kernel(n, subs, lag, gated_ref, w_ref, hid_ref, tea_ref, scale_ref, z_ref, scan_ref,
-               out_ref, go_ref, piece_ref, dscan_ref, dz_ref,
-               zr, zl, part_r, part_l, r_send, r_recv, l_send, l_recv, ar_send, ar_recv, al_send, al_recv):
+def mid_kernel(n, tile, lag, gated_ref, w_ref, hid_ref, tea_ref, scale_ref, z_hbm, scan_hbm,
+               out_ref, go_ref, dwo_hbm, dscan_hbm, dz_hbm,
+               zr, zl, dwo_ref, part_ref, piece_ref, z_ref, scan_ref, acc_ref, dz_ref, loads, stores, wstores,
+               r_send, r_recv, l_send, l_recv, ar_send, ar_recv, al_send, al_recv):
     t = lax.axis_index("tensor")
     rows, wide = hid_ref.shape
-    part = rows // subs
-    tile = 512
+    tokens, lanes = acc_ref.shape
+    waves = wide // tile
     right, left = dict(tensor=lax.rem(t + 1, n)), dict(tensor=lax.rem(t + n - 1, n))
 
     barrier = pltpu.get_barrier_semaphore()
@@ -612,196 +642,264 @@
         pl.semaphore_signal(barrier, inc=1, device_id=peer, device_id_type=MESH)
     pl.semaphore_wait(barrier, 2)
 
+    def load(i):
+        return pltpu.make_async_copy((z_hbm, scan_hbm)[i], (z_ref, scan_ref)[i], loads.at[i])
+
+    for i in range(2):
+        load(i).start()
+
     def r_copy(i):
         return mesh_copy(zr.at[i], zr.at[i], r_send.at[i], r_recv.at[i], **right)
 
     def l_copy(i):
         return mesh_copy(zl.at[i], zl.at[i], l_send.at[i], l_recv.at[i], **left)
 
-    def at(o, s):
-        return pl.ds(pl.multiple_of(o * rows + s * part, part), part)
-
-    def ar_copy(o, s):
-        ref = piece_ref.at[at(o, s), :]
-        return mesh_copy(ref, ref, ar_send.at[o * subs + s], ar_recv.at[o * subs + s], **right)
-
-    def al_copy(o, s):
-        ref = piece_ref.at[at(o, s), :]
-        return mesh_copy(ref, ref, al_send.at[o * subs + s], al_recv.at[o * subs + s], **left)
-
-    def partial_rows(o, dst):
-        here = pl.ds(pl.multiple_of(o * rows, rows), rows)
-
-        @pl.loop(0, wide // tile)
-        def _(j):
-            cols = pl.ds(pl.multiple_of(j * tile, tile), tile)
-            nt = (((1,), (1,)), ((), ()))
-            dst[:, cols] = lax.dot_general(gated_ref[here, :], w_ref[cols, :], nt, preferred_element_type=F32)
-
-    def backward_rows(o):
-        here = pl.ds(pl.multiple_of(o * rows, rows), rows)
-        d_gated = jnp.dot(piece_ref[here, :], w_ref[...], preferred_element_type=F32)
-        z = z_ref[here, :]
-        s = 1.0 / (1.0 + jnp.exp(-z))
-        dscan_ref[here, :] = d_gated * (z * s)
-        dz_ref[here, :] = (d_gated * scan_ref[here, :] * (s * (1.0 + z * (1.0 - s)))).astype(BF16)
-
-    def stream(i, limit, start, buf, copy, part_ref, owner_of):
-        @pl.when(jnp.logical_and(i >= 0, i < limit))
-        def _():
-            k, sub = i // subs, i % subs
-
-            @pl.when(sub == 0)
+    def rows_of(o):
+        return pl.ds(pl.multiple_of(o * rows, rows), rows)
+
+    def cols_of(w):
+        return pl.ds(pl.multiple_of(w * tile, tile), tile)
+
+    def ar_copy(o, w):
+        ref = piece_ref.at[rows_of(o), cols_of(w)]
+        return mesh_copy(ref, ref, ar_send.at[o * waves + w], ar_recv.at[o * waves + w], **right)
+
+    def al_copy(o, w):
+        ref = piece_ref.at[rows_of(o), cols_of(w)]
+        return mesh_copy(ref, ref, al_send.at[o * waves + w], al_recv.at[o * waves + w], **left)
+
+    def stream(i, hops, start, buf, copy, owner_of):
+        w, k = i // n, i % n
+
+        @pl.when(jnp.logical_and(jnp.logical_and(i >= 0, w < waves), k < hops))
+        def _():
+            slot = w * (n - 1) + k
+            here = part_ref[rows_of(owner_of(k)), cols_of(w)]
+
+            @pl.when(start)
             def _():
-                partial_rows(owner_of(k), part_ref)
-
-            @pl.when(jnp.logical_and(start, sub == 0))
-            def _():
-                @pl.loop(0, subs)
-                def _(j):
-                    here = part_ref[pl.ds(pl.multiple_of(j * part, part), part), :]
-                    buf[k * subs + j] = here.astype(BF16)
-                    copy(k * subs + j).start()
+                buf[slot] = here.astype(BF16)
 
             @pl.when(jnp.logical_not(start))
             def _():
-                here = part_ref[pl.ds(pl.multiple_of(sub * part, part), part), :]
-                copy(i).wait_recv()
-                buf[i] = (here + buf[i].astype(F32)).astype(BF16)
-                copy(i).start()
+                copy(slot).wait_recv()
+                buf[slot] = (here + buf[slot].astype(F32)).astype(BF16)
+
+            copy(slot).start()
 
     def ready(o):
-        from_left = jnp.where(o > 0, lag * o + (n - 1 - o) * subs, 0)
-        from_right = jnp.where(o < n - 1, lag * (n - 1 - o) + o * subs, 0)
+        from_left = jnp.where(o > 0, n - 1 - o + lag * o, 0)
+        from_right = jnp.where(o < n - 1, o + lag * (n - 1 - o), 0)
         return jnp.maximum(from_left, from_right)
 
-    gap = max(subs, lag)
-    base = lag + (n - 2) * subs if subs >= lag else (n - 1) * lag
-
-    def turn(d, o):
-        inner = base + (d - o) * gap
-        inner = jnp.where(d == 0, (n - 1) * gap, inner)
-        return jnp.where(d == n - 1, base + (n - 2 - o) * gap + lag, inner)
-
-    def finish(s):
-        here = pl.ds(pl.multiple_of(s * part, part), part)
-
-        @pl.when(s == 0)
-        def _():
-            partial_rows(t, go_ref)
+    def host_ready(o):
+        return max((n - 1 - o + lag * o) * (o > 0), (o + lag * (n - 1 - o)) * (o < n - 1))
+
+    def finish(w):
+        cols = cols_of(w)
+        go_ref[:, cols] = part_ref[rows_of(t), cols]
 
         @pl.when(t > 0)
         def _():
-            i = (n - 1 - t) * subs + s
-            r_copy(i).wait_recv()
-            go_ref[here, :] = go_ref[here, :] + zr[i].astype(F32)
+            slot = w * (n - 1) + n - 1 - t
+            r_copy(slot).wait_recv()
+            go_ref[:, cols] = go_ref[:, cols] + zr[slot].astype(F32)
 
         @pl.when(t < n - 1)
         def _():
-            i = t * subs + s
-            l_copy(i).wait_recv()
-            go_ref[here, :] = go_ref[here, :] + zl[i].astype(F32)
-
-        result = hid_ref[here, :].astype(F32) + go_ref[here, :]
-        out_ref[here, :] = result.astype(BF16)
-        grad = scale_ref[here, :] * (result - tea_ref[here, :].astype(F32))
-        go_ref[here, :] = grad
-        piece_ref[at(t, s), :] = grad.astype(BF16)
-
-    def step(g, _):
-        stream(g - lag * t, (n - 1 - t) * subs, t == 0, zr, r_copy, part_r, lambda k: n - 1 - k)
-        stream(g - lag * (n - 1 - t), t * subs, t == n - 1, zl, l_copy, part_l, lambda k: k)
+            slot = w * (n - 1) + t
+            l_copy(slot).wait_recv()
+            go_ref[:, cols] = go_ref[:, cols] + zl[slot].astype(F32)
+
+        result = hid_ref[:, cols].astype(F32) + go_ref[:, cols]
+        out_ref[:, cols] = result.astype(BF16)
+        grad = scale_ref[...] * (result - tea_ref[:, cols].astype(F32))
+        go_ref[:, cols] = grad
+        piece_ref[rows_of(t), cols] = grad.astype(BF16)
+
+        @pl.when(t < n - 1)
+        def _():
+            ar_copy(t, w).start()
+
+        @pl.when(t > 0)
+        def _():
+            al_copy(t, w).start()
+
+    def stored(i, o):
+        src = (acc_ref, dz_ref)[i].at[rows_of(o), :]
+        return pltpu.make_async_copy(src, (dscan_hbm, dz_hbm)[i].at[rows_of(o), :], stores.at[i, o])
+
+    def stored_weight(w):
+        here = pl.ds(pl.multiple_of(w * tile, tile), tile)
+        return pltpu.make_async_copy(dwo_ref.at[w], dwo_hbm.at[here, :], wstores.at[w])
+
+    def gate(o):
+        z = z_ref[rows_of(o), :]
+        s = 1.0 / (1.0 + jnp.exp(-z))
+        z_ref[rows_of(o), :] = z * s
+        scan_ref[rows_of(o), :] = scan_ref[rows_of(o), :] * (s * (1.0 + z * (1.0 - s)))
+
+    def backward(w):
+        tn = (((0,), (0,)), ((), ()))
+        dwo_ref[w] = lax.dot_general(
+            piece_ref[:, cols_of(w)], gated_ref[...], tn, preferred_element_type=F32
+        ).astype(BF16)
+        stored_weight(w).start()
 
         @pl.loop(0, n)
         def _(o):
-            s_own = g - ready(t)
-            s_right = g - turn(t, o)
-            s_left = g - turn(n - 1 - t, n - 1 - o)
-
-            @pl.when(jnp.logical_and(o == t, jnp.logical_and(s_own >= 0, s_own < subs)))
+            here = rows_of(o)
+            d_gated = jnp.dot(piece_ref[here, cols_of(w)], w_ref[cols_of(w), :], preferred_element_type=F32)
+
+            @pl.when(w == 0)
             def _():
-                finish(s_own)
-
-            @pl.when(jnp.logical_and(o <= t, jnp.logical_and(s_right >= 0, s_right < subs)))
+                acc_ref[here, :] = d_gated
+
+            @pl.when(jnp.logical_and(w > 0, w < waves - 1))
+            def _():
+                acc_ref[here, :] = acc_ref[here, :] + d_gated
+
+            @pl.when(w == waves - 1)
+            def _():
+                total = acc_ref[here, :] + d_gated
+                acc_ref[here, :] = total * z_ref[here, :]
+                dz_ref[here, :] = (total * scan_ref[here, :]).astype(BF16)
+                stored(0, o).start()
+                stored(1, o).start()
+
+    arrived = jnp.int32(0)
+    for o in range(n):
+        arrived = jnp.maximum(arrived, host_ready(o) + lag * jnp.abs(t - o))
+
+    def step(g, _):
+        @pl.when(jnp.logical_and(g % n == 0, g < n * waves))
+        def _():
+            cols = cols_of(g // n)
+            nt = (((1,), (1,)), ((), ()))
+
+            @pl.loop(0, n)
+            def _(o):
+                part_ref[rows_of(o), cols] = lax.dot_general(
+                    gated_ref[rows_of(o), :], w_ref[cols, :], nt, preferred_element_type=F32
+                )
+
+        stream(g - lag * t, n - 1 - t, t == 0, zr, r_copy, lambda k: n - 1 - k)
+        stream(g - lag * (n - 1 - t), t, t == n - 1, zl, l_copy, lambda k: k)
+
+        own = g - ready(t)
+
+        @pl.when(jnp.logical_and(own >= 0, jnp.logical_and(own % n == 0, own // n < waves)))
+        def _():
+            finish(own // n)
+
+        @pl.loop(0, n)
+        def _(o):
+            i = g - ready(o) - lag * jnp.abs(t - o)
+            w = i // n
+
+            @pl.when(jnp.logical_and(o != t, jnp.logical_and(i >= 0, jnp.logical_and(i % n == 0, w < waves))))
             def _():
                 @pl.when(o < t)
                 def _():
-                    ar_copy(o, s_right).wait_recv()
-
-                @pl.when(t < n - 1)
-                def _():
-                    ar_copy(o, s_right).start()
-
-            @pl.when(jnp.logical_and(o >= t, jnp.logical_and(s_left >= 0, s_left < subs)))
-            def _():
+                    ar_copy(o, w).wait_recv()
+
+                    @pl.when(t < n - 1)
+                    def _():
+                        ar_copy(o, w).start()
+
                 @pl.when(o > t)
                 def _():
-                    al_copy(o, s_left).wait_recv()
-
-                @pl.when(t > 0)
-                def _():
-                    al_copy(o, s_left).start()
-
-            s_done = jnp.where(o == t, s_own, jnp.where(o < t, s_right, s_left))
-
-            @pl.when(s_done == subs - 1)
-            def _():
-                backward_rows(o)
+                    al_copy(o, w).wait_recv()
+
+                    @pl.when(t > 0)
+                    def _():
+                        al_copy(o, w).start()
+
+        @pl.when(g == 1)
+        def _():
+            for i in range(2):
+                load(i).wait()
+
+        @pl.when(jnp.logical_and(g >= 1, g <= n))
+        def _():
+            gate(g - 1)
+
+        done = g - arrived
+
+        @pl.when(jnp.logical_and(done >= 0, jnp.logical_and(done % n == 0, done // n < waves)))
+        def _():
+            backward(done // n)
 
         return 0
 
-    steps = base + (n - 1) * gap + subs + lag
-    lax.fori_loop(0, steps, step, 0)
-
-    @pl.loop(0, (n - 1) * subs)
+    steps = max(host_ready(o) + lag * abs(o - d) for o in range(n) for d in range(n)) + n * (waves - 1) + 1
+    lax.fori_loop(0, max(steps, n + 1), step, 0)
+
+    @pl.loop(0, (n - 1) * waves)
     def _(i):
-        @pl.when(i < (n - 1 - t) * subs)
+        @pl.when(i % (n - 1) < n - 1 - t)
         def _():
             r_copy(i).wait_send()
 
-        @pl.when(i < t * subs)
+        @pl.when(i % (n - 1) < t)
         def _():
             l_copy(i).wait_send()
 
-    @pl.loop(0, n * subs)
+    @pl.loop(0, n * waves)
     def _(i):
-        o, s = i // subs, i % subs
+        o, w = i // waves, i % waves
 
         @pl.when(jnp.logical_and(o <= t, t < n - 1))
         def _():
-            ar_copy(o, s).wait_send()
+            ar_copy(o, w).wait_send()
 
         @pl.when(jnp.logical_and(o >= t, t > 0))
         def _():
-            al_copy(o, s).wait_send()
+            al_copy(o, w).wait_send()
+
+    @pl.loop(0, waves)
+    def _(w):
+        stored_weight(w).wait()
+
+    @pl.loop(0, n)
+    def _(o):
+        stored(0, o).wait()
+        stored(1, o).wait()
 
 
 def middle(gated, w_out, hidden, teacher, scale, z_gate, scan_out):
     n = lax.axis_size("tensor")
     rows, wide = hidden.shape
     tokens, lanes = gated.shape
-    subs = max(1, rows // 32)
-    hops = (n - 1) * subs
-    vmem = pl.BlockSpec(memory_space=pltpu.VMEM)
+    tile = 256
+    waves = wide // tile
+    hops = (n - 1) * waves
+    vmem, hbm = pl.BlockSpec(memory_space=pltpu.VMEM), pl.BlockSpec(memory_space=pl.ANY)
     dma = pltpu.SemaphoreType.DMA
     return pl.pallas_call(
-        functools.partial(mid_kernel, n, subs, 2),
+        functools.partial(mid_kernel, n, tile, 2),
         out_shape=[
             jax.ShapeDtypeStruct((rows, wide), BF16),
             jax.ShapeDtypeStruct((rows, wide), F32),
-            jax.ShapeDtypeStruct((tokens, wide), BF16),
+            jax.ShapeDtypeStruct((wide, lanes), BF16),
             jax.ShapeDtypeStruct((tokens, lanes), F32),
             jax.ShapeDtypeStruct((tokens, lanes), BF16),
         ],
-        in_specs=[vmem] * 7,
-        out_specs=[vmem] * 5,
+        in_specs=[vmem] * 5 + [hbm] * 2,
+        out_specs=[vmem] * 2 + [hbm] * 3,
         scratch_shapes=[
-            pltpu.VMEM((hops, rows // subs, wide), BF16),
-            pltpu.VMEM((hops, rows // subs, wide), BF16),
-            pltpu.VMEM((rows, wide), F32),
-            pltpu.VMEM((rows, wide), F32),
+            pltpu.VMEM((hops, rows, tile), BF16),
+            pltpu.VMEM((hops, rows, tile), BF16),
+            pltpu.VMEM((waves, tile, lanes), BF16),
+            pltpu.VMEM((tokens, wide), F32),
+            pltpu.VMEM((tokens, wide), BF16),
+            pltpu.VMEM((tokens, lanes), F32),
+            pltpu.VMEM((tokens, lanes), F32),
+            pltpu.VMEM((tokens, lanes), F32),
+            pltpu.VMEM((tokens, lanes), BF16),
+            dma((2,)), dma((2, n)), dma((waves,)),
             dma((hops,)), dma((hops,)), dma((hops,)), dma((hops,)),
-            dma((n * subs,)), dma((n * subs,)), dma((n * subs,)), dma((n * subs,)),
+            dma((n * waves,)), dma((n * waves,)), dma((n * waves,)), dma((n * waves,)),
         ],
         compiler_params=pltpu.CompilerParams(
             collective_id=1, has_side_effects=True, vmem_limit_bytes=60 << 20
@@ -810,9 +908,9 @@
     )(gated, w_out, hidden, teacher, scale, z_gate, scan_out)
 
 
-def front_kernel(n, dps, seqs, subs, lag, hid_ref, gain_ref, cnt_ref, win_ref, wsm_ref, taps_ref, keep_ref,
+def front_kernel(n, dps, seqs, subs, lag, hid_ref, gain_ref, seg_ref, win_ref, wsm_ref, taps_ref, keep_ref,
                  x_out, z_out, nrm_out, w_out, conv_out, low_out, total_ref, gfull, ws_ref, mixed_ref,
-                 rows_ref, grecv, cnt_one, cnt_two, x_ref, z_ref, nrm_ref, w_ref, conv_ref, low_ref,
+                 rows_ref, gain_tile, cnt_tile, grecv, cnt_one, cnt_two, x_ref, z_ref, nrm_ref, w_ref, conv_ref, low_ref,
                  mix_send, mix_recv, mix_own, outs, ms, mr, ns, nr,
                  ar_send, ar_recv, al_send, al_recv, gs, gr, c1s, c1r, c2s, c2r, hs, hr, ls,
                  chip_send, chip_recv, core_send, core_recv):
@@ -855,7 +953,7 @@
         return mesh_copy(ref, ref, al_send.at[o * subs + s], al_recv.at[o * subs + s], **left)
 
     def g_copy(p, slot):
-        return mesh_copy(gain_ref, grecv.at[slot], gs.at[p], gr.at[slot], tensor=p)
+        return mesh_copy(gain_tile, grecv.at[slot], gs.at[p], gr.at[slot], tensor=p)
 
     def block(kind, p):
         if kind == 0:
@@ -874,7 +972,7 @@
     mine = owner(chip, core)
 
     def count_one():
-        return mesh_copy(cnt_ref, cnt_one, c1s, c1r, **partner)
+        return mesh_copy(cnt_tile, cnt_one, c1s, c1r, **partner)
 
     def count_two(q, slot):
         return mesh_copy(cnt_one, cnt_two.at[slot], c2s.at[q], c2r.at[slot], **to_chip(q))
@@ -896,6 +994,8 @@
     def local_copy():
         return pltpu.make_async_copy(wsm_ref, block(1, mine), ls)
 
+    gain_tile[...] = jnp.broadcast_to(gain_ref[...].astype(F32), gain_tile.shape)
+    cnt_tile[...] = jnp.full(cnt_tile.shape, jnp.sum((seg_ref[...] != 0).astype(F32)))
     for ahead in range(1, n):
         g_copy(lax.rem(t + ahead, n), t).start()
     count_one().start()
@@ -925,12 +1025,12 @@
     for ahead in range(1, n):
         p = lax.rem(t + ahead, n)
         g_copy(p, p).wait_recv()
-    grecv[t] = gain_ref[...]
+    grecv[t] = gain_tile[...]
     for p in range(n):
         gfull[:, p * share:(p + 1) * share] = grecv[p]
     count_one().wait_recv()
     count_one().wait_send()
-    cnt_one[...] = cnt_one[...] + cnt_ref[...]
+    cnt_one[...] = cnt_one[...] + cnt_tile[...]
     for ahead in range(1, chips):
         count_two(lax.rem(chip + ahead, chips), chip).start()
 
@@ -1124,7 +1224,7 @@
             al_copy(o, s).wait_send()
 
 
-def front(hidden, gain, count, w_in, w_small, taps, keeps):
+def front(hidden, gain, segments, w_in, w_small, taps, keeps):
     n, dps, seqs = (lax.axis_size(axis) for axis in ("tensor", "dp", "seq"))
     parts = dps * seqs
     chips = parts // 2
@@ -1145,8 +1245,8 @@
             jax.ShapeDtypeStruct((2, wide, lanes), BF16),
             jax.ShapeDtypeStruct((tokens, lanes), F32),
             jax.ShapeDtypeStruct((tokens, lanes), BF16),
-            jax.ShapeDtypeStruct(count.shape, F32),
-            jax.ShapeDtypeStruct((gain.shape[0], wide), F32),
+            jax.ShapeDtypeStruct((8, 128), F32),
+            jax.ShapeDtypeStruct((8, wide), F32),
             jax.ShapeDtypeStruct((parts,) + w_small.shape, BF16),
             jax.ShapeDtypeStruct((n, mixed, rows), BF16),
         ],
@@ -1154,9 +1254,11 @@
         out_specs=[hbm] * 6 + [vmem] * 4,
         scratch_shapes=[
             pltpu.VMEM((tokens, wide), BF16),
-            pltpu.VMEM((n,) + gain.shape, F32),
-            pltpu.VMEM(count.shape, F32),
-            pltpu.VMEM((chips,) + count.shape, F32),
+            pltpu.VMEM((8, gain.shape[1]), F32),
+            pltpu.VMEM((8, 128), F32),
+            pltpu.VMEM((n, 8, gain.shape[1]), F32),
+            pltpu.VMEM((8, 128), F32),
+            pltpu.VMEM((chips, 8, 128), F32),
             pltpu.VMEM((tokens + 8, lanes), F32),
             pltpu.VMEM((tokens, lanes), F32),
             pltpu.VMEM((tokens, wide), BF16),
@@ -1174,7 +1276,7 @@
             collective_id=3, has_side_effects=True, vmem_limit_bytes=60 << 20
         ),
         name="front",
-    )(hidden, gain, count, w_in, w_small, taps, keeps)
+    )(hidden, gain, segments, w_in, w_small, taps, keeps)
 
 
 def mixback_kernel(n, seqs, part_ref, e_hbm, conv_hbm, x_hbm, low_hbm, dpl_hbm, step_ref, wx_ref, taps_ref, keep_ref,
@@ -1379,9 +1481,7 @@
     back_rows = conv_taps - 1
     row_start = lax.axis_index("tensor") * row_share
     valid_mask = (segment_ids != 0).astype(jnp.float32)
-    count_here = jnp.full((8, 128), jnp.sum(valid_mask))
     parts = lax.axis_size(("dp", "seq"))
-    gain_tile = jnp.broadcast_to(norm_gain.astype(F32)[None], (8, norm_gain.shape[0]))
     x_cols, dt_rows = xproj_weight.shape[1], dtproj_weight.shape[0]
     w_small = jnp.concatenate(
         [
@@ -1403,8 +1503,8 @@
     )
     x_rows, z_gate, normalized_rows, w_in, conv_sum, x_low, total, gain_rows, w_small, mixed = front(
         hidden_in,
-        gain_tile,
-        count_here,
+        norm_gain[None],
+        segment_ids.reshape(8, -1),
         jnp.swapaxes(input_projection_weight, 0, 1),
         w_small,
         taps,
@@ -1418,8 +1518,6 @@
     share_rows = hidden_in.astype(F32)
     full_gain = gain_rows[0]
     inv_share = lax.rsqrt(jnp.mean(share_rows * share_rows, axis=1, keepdims=True) + EPS)
-    ext_x = x_rows[8 - back_rows :]
-    x_float = x_low.astype(F32)
     mixed = mixed.reshape(-1, parts, SMALL_ROWS, row_share)[:, :, :x_cols]
     mixed_rows = mixed.transpose(0, 3, 1, 2).reshape(tok_rows, parts * x_cols).astype(F32)
     rank_width = w_dt.shape[0]
@@ -1427,38 +1525,36 @@
     step_low = mixed_rows[:, :rank_width].astype(jnp.bfloat16)
     b_in = mixed_rows[:, rank_width : rank_width + state_width]
     c_out = mixed_rows[:, rank_width + state_width :]
-    pre_act = jnp.dot(step_low, w_dt, preferred_element_type=jnp.float32) + dt_bias[None]
-    step_size = jax.nn.softplus(pre_act)
-    decay_rates = -jnp.exp(a_log)
     same_doc = (seg_float == ext_seg[back_rows - 1 : back_rows - 1 + tok_rows]).astype(jnp.float32)
-    rates = decay_rates * LOG2E
+    rates = -jnp.exp(a_log) * LOG2E
     block = 128
-    stepd = jnp.where(same_doc[:, None] != 0, step_size, FAR)
-    inject = step_size * x_float
     col_pair = jnp.concatenate([columns(b_in), columns(c_out)], -1)
     b_diag, c_diag = diagonal(b_in), diagonal(c_out)
     resets = jnp.sum((same_doc == 0).astype(jnp.int32).reshape(-1, block), axis=1)
     alive = (jnp.cumsum(resets) - resets == 0).astype(jnp.int32)
-    y_local, marks, state_last = fwd(stepd, inject, col_pair, c_diag, rates, tb=block, unroll=8)
-    reach = jnp.exp2(rates * jnp.sum(stepd, axis=0)[None])
+    y_local, marks, state_last, stepd, inject, step_size, step_slope = fwd(
+        step_low, w_dt, dt_bias[None], x_low, same_doc[:, None], col_pair, c_diag, rates, tb=block, unroll=8
+    )
+
+    def reach():
+        return jnp.exp2(rates * jnp.sum(stepd, axis=0)[None])
+
     state_in = carried(state_last, reach, "seq", 1)
-    y_rows, marks = correct(alive, y_local, stepd, c_diag, rates, marks, state_in, tb=block)
-    scan_out = y_rows + d_skip[None] * x_float
-    gate_act = jax.nn.silu(z_gate)
-    gated_output_rows = (scan_out * gate_act).astype(jnp.bfloat16)
+    scan_out, marks, gated_output_rows = correct(
+        alive, y_local, stepd, c_diag, rates, marks, state_in, x_low, d_skip[None], z_gate, tb=block
+    )
     valid_share = lax.dynamic_slice_in_dim(valid_mask, row_start, row_share, 0)
     total_tokens = float(tok_rows * lax.axis_size(("dp", "seq")))
     scale = (total_tokens / total_count * valid_share)[:, None]
-    output, grad_out, piece, d_scan, d_z = middle(
+    output, grad_out, d_wout, d_scan, d_z = middle(
         gated_output_rows, w_out, hidden_in, teacher, scale, z_gate, scan_out
     )
-    d_wout = jnp.einsum("te,tw->we", gated_output_rows, piece, preferred_element_type=jnp.float32)
     adjoint_first = entry(alive, stepd, d_scan, col_pair, rates, tb=block)
     adjoint_in = carried(adjoint_first, reach, "seq", -1)
     ones = diagonal(jnp.ones((CH, N), F32))
     d_pre_low, d_direct, d_rank_t, d_b_part, d_c_part, a_log_part, dt_bias_part, d_skip_part = bwd(
         stepd, inject, d_scan, col_pair, b_diag, ones, rates, marks, adjoint_in,
-        step_size, jax.nn.sigmoid(pre_act), x_low, d_skip[None], w_dt, tb=block, unroll=8
+        step_size, step_slope, x_low, d_skip[None], w_dt, tb=block, unroll=8
     )
     a_log_part = LN2 * a_log_part
     part = jnp.concatenate(
@@ -1503,7 +1599,7 @@
     g_x_rank = g_small[:rank_here].T
     g_x_state = g_small[rank_here : rank_here + state_here].T
     g_dt = g_small[rank_here + state_here : rank_here + state_here + rank_here]
-    g_out = lax.psum_scatter(d_wout.astype(BF16), ("dp", "seq"), scatter_dimension=0, tiled=True).astype(F32).T
+    g_out = lax.psum_scatter(d_wout, ("dp", "seq"), scatter_dimension=0, tiled=True).astype(F32).T
     g_gain = jnp.sum(g_whole[N + conv_taps + 4 :, : norm_gain.shape[0]], axis=0) / norm_gain.astype(F32)
     g_alog, g_conv_w = g_whole[:N], g_whole[N : N + conv_taps]
     g_conv_b, g_bias, g_skip = g_whole[N + conv_taps], g_whole[N + conv_taps + 1], g_whole[N + conv_taps + 2]

time: 587 us -> 542 us (0.923)
  Pallas kernels: 469 us -> 451 us
  matrix products: 15 us -> 0 us
  starting transfers between devices: 16.7 us -> 5.46 us
  other arithmetic: 24.9 us -> 18.1 us
    pallas_call x2, Pallas kernels: 236 us -> 211 us  [the longest x1 121 us: middle(): pl.pallas_call(functools.partial(mid_kernel, n, tile, 2), out_shape=[jax....]
    dot_general x2 -> x0, matrix products: 15 us -> none  [the longest x1 9.41 us: on_device(): jnp.einsum('te,tw->we', gated_output_rows, piece, preferred_element_type=...]
    ppermute x2, starting transfers between devices: 16.6 us -> 5.38 us  [passed_along(): return lax.ppermute(x, axis, pairs)]
    unnamed x43 -> x63, local copies, waits for them, and re-layouts: 18.9 us -> 21 us
  transfers between devices with their start and end apart: 4 -> 4, of which waited for: 0 -> 1; matrix products, arithmetic and copies ran while one was open for 8% -> 7% of each run, Pallas kernels for 38% -> 42%
where the time goes in v7:
time: 542 us; the launch traced here: 539 us
  Pallas kernels  451 us (83%)
  local copies, waits for them, and re-layouts  45.2 us (8%)
  other arithmetic  18.1 us (3%)
  between operations  15.8 us (3%)
  starting transfers between devices  5.46 us (1%)
    pallas_call x1, Pallas kernels, middle(): pl.pallas_call(functools.partial(mid_kernel, n, tile, 2), out_shape=[jax....  121 us
    pallas_call x1, Pallas kernels, front(): pl.pallas_call(functools.partial(front_kernel, n, dps, seqs, subs, 2), ou...  105 us
    pallas_call x1, Pallas kernels, tail(): pl.pallas_call(functools.partial(tail_kernel, n, dps, seqs, tile, 2), out...  90 us
    pallas_call x1, Pallas kernels, bwd(): pl.pallas_call(functools.partial(bwd_kernel, unroll=unroll), grid=grid, i...  58.4 us
    pallas_call x1, Pallas kernels, mixback(): pl.pallas_call(functools.partial(mixback_kernel, n, seqs), out_shape=[jax...  31 us
    pallas_call x1, Pallas kernels, fwd(): pl.pallas_call(functools.partial(fwd_kernel, unroll=unroll), grid=grid, i...  22 us
    unnamed x63, local copies, waits for them, and re-layouts  21 us
    pallas_call x1, Pallas kernels, correct(): pl.pallas_call(correct_kernel, grid_spec=pltpu.PrefetchScalarGridSpec(num...  14 us
  transfers between devices with their start and end apart: 4, of which 1 were waited for; matrix products, arithmetic and copies ran while one was open for 7% of the time, Pallas kernels for 42%

profile of v7, /device:TPU:0, one launch (start us, length us, event | category | flops | bytes accessed | tf_op | source)
XLA Modules:
  0.0 539.4 jit_solution(6125688283683918211)
XLA Ops:
  9.0 1.3 broadcast_in_dim.79.gain_ref
  13.2 0.8 concatenate.42.keep_ref
  14.1 2.1 copy.86
  16.1 1.2 copy.106
  18.9 104.8 %front.1 = (f32[1032,1024]{1,0:T(8,128)}, f32[1024,1024]{1,0:T(8,128)}, bf16[1024,2048]{1,0:T(8,128)(2,1)}, bf16[2,2048,1024]{2,1,0:T(8,128)(2,1)}, f32[1024,102...) custom-call(bf16[256,2048]{1,0:T(8,128)(2,1)} %hid_ref.3, ...), custom_call_target="tpu_custom_call" | custom-call | tf_op jit(solution)/shard_map/front/pallas_call | solution.py:1239
  124.5 1.0 copy.85.keep_ref
  125.5 1.3 copy.101
  127.5 0.8 copy.84.rank_ref
  128.4 1.0 slice.82
  129.7 1.0 copy.88
  130.9 1.0 copy.83
  133.3 1.0 compare_select_fusion
  134.8 22.0 %scan_forward.1 = (f32[1024,1024]{1,0:T(8,128)}, f32[8,16,1024]{2,1,0:T(8,128)S(1)}, f32[16,1024]{1,0:T(8,128)}, f32[1024,1024]{1,0:T(8,128)}, f32[1024,1024]{1,...) custom-call(bf16[1024,128]{1,0:T(8,128)(2,1)S(1)} %copy-done.6, bf16[128,1024]{1,0:T(8,128)(2,1)S(1)} %bitcast.64, ...), custom_call_target="tpu_custom_call" | custom-call | tf_op jit(solution)/shard_map/scan_forward/pallas_call | solution.py:70
  156.8 0.8 copy-done.9
  157.6 4.1 collective-permute-start
  161.7 1.3 reduce-window.9
  163.0 1.2 slice.85
  166.2 1.5 copy.87.scale_ref
  167.7 1.0 copy-done.10
  168.7 14.0 %scan_correct.1 = (f32[1024,1024]{1,0:T(8,128)}, f32[8,16,1024]{2,1,0:T(8,128)S(1)}, bf16[1024,1024]{1,0:T(8,128)(2,1)S(1)}) custom-call(s32[8]{0:T(128)S(1)} %compare_convert_fusion.2.alive_ref, f32[1024,1024]{1,0:T(8,128)} %get-tuple-element.59.y_ref, f32[1024,1024]{1,0:T(8,128)} %get-tuple-element.60.stepd_ref, ...), custom_call_target="tpu_custom_call" | custom-call | tf_op jit(solution)/shard_map/scan_correct/pallas_call | solution.py:268
  182.7 1.3 copy-done.5
  184.1 0.8 copy-done.7
  184.9 120.8 %middle.1 = (bf16[256,2048]{1,0:T(8,128)(2,1)}, f32[256,2048]{1,0:T(8,128)}, bf16[2048,1024]{1,0:T(8,128)(2,1)}, f32[1024,1024]{1,0:T(8,128)}, bf16[1024,1024]{1,0:T(8,128)(2,1)}) custom-call(bf16[1024,1024]{1,0:T(8,128)(2,1)} %copy-done.5, bf16[2048,1024]{1,0:T(8,128)(2,1)} %all-gather.2.cloned.1.call-done.w_ref, bf16[256,2048]{1,0:T(8,128)(2,1)} %hid_ref.3, ...), custom_call_target="tpu_custom_call" | custom-call | tf_op jit(solution)/shard_map/middle/pallas_call | solution.py:879
  305.8 1.0 copy-done.15
  306.7 0.8 pad_maximum_fusion.keep_ref
  307.6 2.2 copy-done
  309.8 10.2 %scan_entry.1 = f32[16,1024]{1,0:T(8,128)S(1)} custom-call(s32[8]{0:T(128)S(1)} %compare_convert_fusion.2.alive_ref, f32[1024,1024]{1,0:T(8,128)S(1)} %copy-done, f32[1024,1024]{1,0:T(8,128)} %get-tuple-element.73.ds_ref, f32[64,16,32]{2,1,0:T(8,128)S(1)} %pad_maximum_fusion.1.bc_ref, f32[16,1024]{1,0:T(8,128)S(1)} %negate_multiply_fusion.rate_ref), custom_call_target="tpu_custom_call" | custom-call | tf_op jit(solution)/shard_map/scan_entry/pallas_call | solution.py:315
  320.0 1.3 collective-permute-start.1
  321.5 0.8 slice.86
  322.3 0.8 reshape.206.wx_ref
  323.2 3.6 collective-permute-done.1.gin_ref
  326.8 58.4 %scan_backward.1 = (bf16[1024,1024]{1,0:T(8,128)(2,1)S(1)}, f32[1024,1024]{1,0:T(8,128)}, f32[2,128,1024]{2,1,0:T(8,128)S(1)}, f32[2,64,256]{2,1,0:T(8,128)S(1)}...) custom-call(f32[1024,1024]{1,0:T(8,128)} %get-tuple-element.60.stepd_ref, ...), custom_call_target="tpu_custom_call" | custom-call | tf_op jit(solution)/shard_map/scan_backward/pallas_call | solution.py:182
  385.1 1.3 copy-done.4
  388.3 31.0 %mix_backward.1 = (bf16[1024,1024]{1,0:T(8,128)(2,1)}, f32[160,1024]{1,0:T(8,128)}, f32[128,1024]{1,0:T(8,128)}, f32[8,1024]{1,0:T(8,128)}) custom-call(bf16[4,160,256]{2,1,0:T(8,128)(2,1)} %maximum_bitcast_fusion.part_ref, f32[1024,1024]{1,0:T(8,128)} %get-tuple-element.80.e_hbm, f32[1024,1024]{1,0:T(8,128)} %get-tuple-element.81.conv_hbm, ...), custom_call_target="tpu_custom_call" | custom-call | tf_op jit(solution)/shard_map/mix_backward/pallas_call | solution.py:1429
  419.4 1.0 slice.89
  420.3 1.1 slice.88
  421.5 2.0 concatenate.50.all_ref
  423.5 1.3 maximum_maximum_fusion.sm_ref
  424.8 90.0 %tail_sums.1 = (f32[256,2048]{1,0:T(8,128)}, f32[2,256,1024]{2,1,0:T(8,128)}, f32[40,1024]{1,0:T(8,128)}, f32[32,1024]{1,0:T(8,128)}) custom-call(bf16[1024,1024]{1,0:T(8,128)(2,1)} %get-tuple-element.84.dx_ref, bf16[1024,1024]{1,0:T(8,128)(2,1)} %get-tuple-element.85.dz_ref, bf16[2,2048,1024]{2,1,0:T(8,128)(2,1)} %get-tuple-element.86.w_hbm, ...), custom_call_target="tpu_custom_call" | custom-call | tf_op jit(solution)/shard_map/tail_sums/pallas_call | solution.py:594
  514.8 1.4 slice.92
  516.1 1.5 slice.98
  517.6 4.7 copy.95
  522.3 0.9 slice_reduce_fusion
  524.3 1.5 fusion.14
  527.1 2.0 fusion.3
  529.1 1.2 convert_bitcast_fusion
  530.3 1.3 copy.96
  531.6 1.0 copy.108
  (115 shorter events, 15.2 us)
Async XLA Ops:
  7.2 8.9 %copy-start.19 = (bf16[256,2,1024]{2,1,0:T(2,128)(2,1)S(1)}, bf16[256,2,1024]{2,1,0:T(2,128)(2,1)}, u32[]{:S(2)}) copy-start(bf16[256,2,1024]{2,1,0:T(2,128)(2,1)} %param.17) | copy-start | bytes 3145732
  7.2 10.9 %copy-start.26 = (bf16[16,1024]{1,0:T(8,128)(2,1)S(1)}, bf16[16,1024]{1,0:T(8,128)(2,1)}, u32[]{:S(2)}) copy-start(bf16[16,1024]{1,0:T(8,128)(2,1)} %param.21) | copy-start | bytes 98308
  7.2 10.9 %copy-start.25 = (bf16[1024,20]{0,1:T(8,128)(2,1)S(1)}, bf16[1024,20]{0,1:T(8,128)(2,1)}, u32[]{:S(2)}) copy-start(bf16[1024,20]{0,1:T(8,128)(2,1)} %param.20) | copy-start | bytes 122884
  7.2 177.6 %all-gather.2.cloned.1.call-start = ((), (), s32[]{:S(2)}) async-start(), calls=%async_computation.1 | async-start | bytes 4718592 | tf_op jit(solution)/shard_map/all_gather | solution.py:1514
  123.7 405.4 %reduce-scatter.2.cloned.1.call-start = ((), (), s32[]{:S(2)}) async-start(), calls=%async_computation.2 | async-start | bytes 4718592 | tf_op jit(solution)/shard_map/reduce_scatter | solution.py:1602
  131.9 0.9 copy-start.24
  131.9 1.1 copy-start.17
  131.9 1.3 copy-start.18
  132.6 1.8 copy-start.1
  132.6 2.0 copy-start.2
  132.6 2.2 copy-start.6
  132.6 2.2 copy-start.12
  134.8 32.9 %copy-start.11 = (f32[1024]{0:T(1024)S(1)}, f32[1024]{0:T(1024)}, u32[]{:S(2)}) copy-start(f32[1024]{0:T(1024)} %param.24) | copy-start | bytes 12292
  156.8 0.8 copy-start.9
  157.6 10.1 %collective-permute-start = (f32[16,1024]{1,0:T(8,128)}, f32[16,1024]{1,0:T(8,128)S(1)}, u32[]{:S(2)}, u32[]{:S(2)}) collective-permute-start(f32[16,1024]{1,0:T(8,128)} %get-tuple-element.62), channel_id=1, source_target_pairs={{0,4},{1,5},{2,6},{3,7},{8,12},{9,13},{10,14},{11,15},{16,20},{17,... | collective-permute-start | bytes 196616 | tf_op jit(solution)/shard_map/ppermute | solution.py:21
  167.7 1.0 copy-start.10
  182.7 1.3 copy-start.5
  184.1 0.8 copy-start.7
  305.7 1.0 copy-start.15
  307.6 2.2 copy-start
  309.8 11.6 %copy-start.21 = (bf16[8,48,1024]{2,1,0:T(8,128)(2,1)S(1)}, bf16[8,48,1024]{2,1,0:T(8,128)(2,1)}, u32[]{:S(2)}) copy-start(bf16[8,48,1024]{2,1,0:T(8,128)(2,1)} %get-tuple-element.57) | copy-start | bytes 2359300
  309.8 17.0 %copy-start.3 = (bf16[1024,256]{1,0:T(8,128)(2,1)S(1)}, bf16[1024,256]{1,0:T(8,128)(2,1)}, u32[]{:S(2)}) copy-start(bf16[1024,256]{1,0:T(8,128)(2,1)} %get-tuple-element.166.bdiag_ref) | copy-start | bytes 1572868
  309.8 17.0 %copy-start.8 = (f32[8,16,1024]{2,1,0:T(8,128)S(1)}, f32[8,16,1024]{2,1,0:T(8,128)}, u32[]{:S(2)}) copy-start(f32[8,16,1024]{2,1,0:T(8,128)} %copy-done.7) | copy-start | bytes 1572868
  320.0 6.8 %collective-permute-start.1 = (f32[16,1024]{1,0:T(8,128)S(1)}, f32[16,1024]{1,0:T(8,128)S(1)}, u32[]{:S(2)}, u32[]{:S(2)}) collective-permute-start(f32[16,1024]{1,0:T(8,128)S(1)} %scan_entry.1), channel_id=1, source_target_pairs={{4,0},{5,1},{6,2},{7,3},{12,8},{13,9},{14,10},{15,11},{20,16},{21,... | collective-permute-start | bytes 196616 | tf_op jit(solution)/shard_map/ppermute | solution.py:21
  385.1 1.3 copy-start.4
  419.4 4.2 copy-start.22
  517.6 5.6 %copy-start.13 = (bf16[256,2048]{1,0:T(8,128)(2,1)S(1)}, bf16[256,2048]{1,0:T(8,128)(2,1)}, u32[]{:S(2)}) copy-start(bf16[256,2048]{1,0:T(8,128)(2,1)} %hid_ref.3) | copy-start | bytes 3145732
  517.6 5.6 %copy-start.14 = (f32[256,2048]{1,0:T(8,128)S(1)}, f32[256,2048]{1,0:T(8,128)}, u32[]{:S(2)}) copy-start(f32[256,2048]{1,0:T(8,128)} %get-tuple-element.94) | copy-start | bytes 6291460
  522.3 1.4 copy-start.27
  522.3 3.5 copy-start.23
  522.3 4.8 copy-start.16
  529.1 2.6 copy-start.20
Sparse Core Ops, SparseCore 0:
  123.8 38.7 all-gather.1
  305.9 51.5 reduce-scatter.1

commit v8 on v7

--- a/solution.py
+++ b/solution.py
@@ -12,6 +12,9 @@
 LN2 = 0.6931471805599453
 FAR = 1e30
 SMALL_ROWS = 24
+N = 16
+CH = 16
+F32, BF16 = jnp.float32, jnp.bfloat16
 MESH = pl.DeviceIdType.MESH
 
 
@@ -21,22 +24,29 @@
     return lax.ppermute(x, axis, pairs)
 
 
-def silu_slope(values):
-    logistic = jax.nn.sigmoid(values)
-    return logistic * (1.0 + values * (1.0 - logistic))
-
-
-F32, BF16 = jnp.float32, jnp.bfloat16
-N = 16
-CH = 16
-
-def fwd_kernel(rank_ref, wdt_ref, bias_ref, low_ref, keep_ref, bc_ref, cdiag_ref, rate_ref,
-               y_ref, ckpt_ref, last_ref, stepd_ref, u_ref, step_ref, sig_ref, state_ref, sbf_ref, *, unroll):
+def spread(values_t):
+    tokens = values_t.shape[1]
+    name = lax.broadcasted_iota(jnp.int32, (N, CH * N), 0)
+    lane = lax.broadcasted_iota(jnp.int32, (N, CH * N), 1)
+    copies = (name == lane % N).astype(BF16)
+    wide = lax.dot_general(values_t.astype(BF16), copies, (((0,), (0,)), ((), ())), preferred_element_type=F32)
+    row = lax.broadcasted_iota(jnp.int32, (tokens, CH * N), 0)
+    place_of = lax.broadcasted_iota(jnp.int32, (tokens, CH * N), 1)
+    return jnp.where(row % CH == place_of // N, wide, 0.0).astype(BF16)
+
+
+def fwd_kernel(mix_ref, wdt_ref, bias_ref, low_ref, keep_ref, rate_ref,
+               y_ref, ckpt_ref, last_ref, stepd_ref, u_ref, step_ref, sig_ref, state_ref, sbf_ref, cdiag_ref):
     @pl.when(pl.program_id(1) == 0)
     def _():
         state_ref[...] = jnp.zeros_like(state_ref)
     ckpt_ref[0] = state_ref[...]
-    pre = jnp.dot(rank_ref[...], wdt_ref[...], preferred_element_type=F32) + bias_ref[...]
+    rank = wdt_ref.shape[0]
+    b_t, c_t = mix_ref[rank:rank + N, :], mix_ref[rank + N:rank + 2 * N, :]
+    cdiag_ref[...] = spread(c_t)
+    tn = (((0,), (0,)), ((), ()))
+    pre = lax.dot_general(mix_ref[0:rank, :].astype(BF16), wdt_ref[...], tn, preferred_element_type=F32)
+    pre = pre + bias_ref[...]
     small = jnp.exp(-jnp.abs(pre))
     step = jnp.maximum(pre, 0.0) + jnp.log1p(small)
     step_ref[...] = step
@@ -46,38 +56,33 @@
     rate = rate_ref[...]
     tb = stepd_ref.shape[0]
 
-    def chunk(c, s):
-        base = pl.multiple_of(c * CH, CH)
-        bc = bc_ref[c]
-        for k in range(CH):
-            dec = jnp.exp2(rate * stepd_ref[pl.ds(base + k, 1), :])
-            s = dec * s + bc[:, k:k + 1] * u_ref[pl.ds(base + k, 1), :]
-            sbf_ref[k * N:(k + 1) * N, :] = s.astype(BF16)
-        y_ref[pl.ds(base, CH), :] = jnp.dot(cdiag_ref[pl.ds(base, CH), :], sbf_ref[...], preferred_element_type=F32)
-        return s
-
-    s = lax.fori_loop(0, tb // CH, chunk, state_ref[...], unroll=unroll)
+    s = state_ref[...]
+    for base in range(0, tb, CH):
+        for k in range(base, base + CH):
+            dec = jnp.exp2(rate * stepd_ref[k:k + 1, :])
+            s = dec * s + b_t[:, k:k + 1] * u_ref[k:k + 1, :]
+            sbf_ref[(k - base) * N:(k - base + 1) * N, :] = s.astype(BF16)
+        y_ref[base:base + CH, :] = jnp.dot(cdiag_ref[base:base + CH, :], sbf_ref[...], preferred_element_type=F32)
     state_ref[...] = s
     last_ref[...] = s
 
-def fwd(rank, w_dt, bias, low, keep, bc, cdiag, rate, tb=128, w=512, unroll=1):
+
+def fwd(mix_t, w_dt, bias, low, keep, rate, tb=128, w=512):
     t, c = low.shape
     w = min(w, c)
     grid = (c // w, t // tb)
-    width = rank.shape[1]
+    mixed, rank = mix_t.shape[0], w_dt.shape[0]
     rows = pl.BlockSpec((tb, w), lambda j, i: (i, j))
     whole = jax.ShapeDtypeStruct((t, c), F32)
     return pl.pallas_call(
-        functools.partial(fwd_kernel, unroll=unroll),
+        fwd_kernel,
         grid=grid,
         in_specs=[
-            pl.BlockSpec((tb, width), lambda j, i: (i, 0)),
-            pl.BlockSpec((width, w), lambda j, i: (0, j)),
+            pl.BlockSpec((mixed, tb), lambda j, i: (0, i)),
+            pl.BlockSpec((rank, w), lambda j, i: (0, j)),
             pl.BlockSpec((1, w), lambda j, i: (0, j)),
             rows,
             pl.BlockSpec((tb, 1), lambda j, i: (i, 0)),
-            pl.BlockSpec((tb // CH, N, 2 * CH), lambda j, i: (i, 0, 0)),
-            pl.BlockSpec((tb, CH * N), lambda j, i: (i, 0)),
             pl.BlockSpec((N, w), lambda j, i: (0, j)),
         ],
         out_specs=[
@@ -92,16 +97,16 @@
             jax.ShapeDtypeStruct((N, c), F32),
             whole, whole, whole, whole,
         ],
-        scratch_shapes=[pltpu.VMEM((N, w), F32), pltpu.VMEM((CH * N, w), BF16)],
+        scratch_shapes=[pltpu.VMEM((N, w), F32), pltpu.VMEM((CH * N, w), BF16), pltpu.VMEM((tb, CH * N), BF16)],
         compiler_params=pltpu.CompilerParams(vmem_limit_bytes=48 << 20),
         name="scan_forward",
-    )(rank, w_dt, bias, low, keep, bc, cdiag, rate)
-
-
-def bwd_kernel(stepd_ref, u_ref, ds_ref, bc_ref, bdiag_ref, ones_ref, rate_ref, ckpt_ref, gin_ref,
+    )(mix_t, w_dt, bias, low, keep, rate)
+
+
+def bwd_kernel(stepd_ref, u_ref, ds_ref, mix_ref, rate_ref, ckpt_ref, gin_ref,
                step_ref, sig_ref, low_ref, skip_ref, wdt_ref,
                dpl_ref, e_ref, rank_ref, db_ref, dc_ref, acc_ref, bias_ref, dskip_ref,
-               g_ref, sbf_ref, abf_ref, rbf_ref, pb_ref, pc_ref, wb_ref, dn_ref, *, unroll):
+               g_ref, sbf_ref, abf_ref, rbf_ref, pb_ref, pc_ref, wb_ref, dn_ref, bdiag_ref):
     @pl.when(pl.program_id(1) == 0)
     def _():
         g_ref[...] = gin_ref[...]
@@ -122,43 +127,41 @@
     sbf_ref[0:N, :] = ckpt_ref[0].astype(BF16)
     nt = (((1,), (1,)), ((), ()))
     lanes = jnp.ones((8, 128), BF16)
-
-    def forward(c, s):
-        base = pl.multiple_of(c * CH, CH)
-        bc = bc_ref[c]
+    rank = wdt_ref.shape[0]
+    b_t, c_t = mix_ref[rank:rank + N, :], mix_ref[rank + N:rank + 2 * N, :]
+    bdiag_ref[...] = spread(b_t)
+    ones = spread(jnp.ones((N, CH), F32))
+
+    s = ckpt_ref[0]
+    for c in range(nc):
+        base = c * CH
         for k in range(CH):
-            dec = jnp.exp2(rate * stepd_ref[pl.ds(base + k, 1), :])
-            s = dec * s + bc[:, k:k + 1] * u_ref[pl.ds(base + k, 1), :]
-            sbf_ref[pl.ds(pl.multiple_of((base + k + 1) * N, N), N), :] = s.astype(BF16)
-            pc_ref[k * N:(k + 1) * N, :] = fold(s * ds_ref[pl.ds(base + k, 1), :])
+            at = base + k
+            dec = jnp.exp2(rate * stepd_ref[at:at + 1, :])
+            s = dec * s + b_t[:, at:at + 1] * u_ref[at:at + 1, :]
+            sbf_ref[(at + 1) * N:(at + 2) * N, :] = s.astype(BF16)
+            pc_ref[k * N:(k + 1) * N, :] = fold(s * ds_ref[at:at + 1, :])
         dc = lax.dot_general(lanes, pc_ref[...].astype(BF16), nt, preferred_element_type=F32)
-        dc_ref[0, pl.ds(c, 1), :] = dc[0:1]
-        return s
-
-    lax.fori_loop(0, nc, forward, ckpt_ref[0], unroll=unroll)
-
-    def backward(c, carry):
-        g, acc = carry
-        c = nc - 1 - c
-        base = pl.multiple_of(c * CH, CH)
-        bc = bc_ref[c]
+        dc_ref[0, c:c + 1, :] = dc[0:1]
+
+    g, acc = g_ref[...], acc_ref[...]
+    for c in range(nc - 1, -1, -1):
+        base = c * CH
         for k in range(CH - 1, -1, -1):
-            sd = stepd_ref[pl.ds(base + k, 1), :]
-            adj = g + bc[:, CH + k:CH + k + 1] * ds_ref[pl.ds(base + k, 1), :]
+            at = base + k
+            sd = stepd_ref[at:at + 1, :]
+            adj = g + c_t[:, at:at + 1] * ds_ref[at:at + 1, :]
             abf_ref[k * N:(k + 1) * N, :] = adj.astype(BF16)
-            pb_ref[k * N:(k + 1) * N, :] = fold(adj * u_ref[pl.ds(base + k, 1), :])
+            pb_ref[k * N:(k + 1) * N, :] = fold(adj * u_ref[at:at + 1, :])
             g = jnp.exp2(rate * sd) * adj
-            before = sbf_ref[pl.ds(pl.multiple_of((base + k) * N, N), N), :].astype(F32)
+            before = sbf_ref[at * N:(at + 1) * N, :].astype(F32)
             r = g * before * rate
             rbf_ref[k * N:(k + 1) * N, :] = r.astype(BF16)
             acc = acc + r * sd
-        wb_ref[pl.ds(base, CH), :] = jnp.dot(bdiag_ref[pl.ds(base, CH), :], abf_ref[...], preferred_element_type=F32)
-        dn_ref[pl.ds(base, CH), :] = jnp.dot(ones_ref[...], rbf_ref[...], preferred_element_type=F32)
+        wb_ref[base:base + CH, :] = jnp.dot(bdiag_ref[base:base + CH, :], abf_ref[...], preferred_element_type=F32)
+        dn_ref[base:base + CH, :] = jnp.dot(ones, rbf_ref[...], preferred_element_type=F32)
         db = lax.dot_general(lanes, pb_ref[...].astype(BF16), nt, preferred_element_type=F32)
-        db_ref[0, pl.ds(c, 1), :] = db[0:1]
-        return g, acc
-
-    g, acc = lax.fori_loop(0, nc, backward, (g_ref[...], acc_ref[...]), unroll=unroll)
+        db_ref[0, c:c + 1, :] = db[0:1]
     g_ref[...] = g
     acc_ref[...] = acc
 
@@ -172,7 +175,7 @@
     rank_ref[0] = lax.dot_general(wdt_ref[...], d_pre_low, nt, preferred_element_type=F32)
 
 
-def bwd(stepd, u, ds, bc, bdiag, ones, rate, ckpt, gin, step, sig, low, skip, w_dt, tb=128, w=512, unroll=1):
+def bwd(stepd, u, ds, mix_t, rate, ckpt, gin, step, sig, low, skip, w_dt, tb=128, w=512):
     t, c = stepd.shape
     w = min(w, c)
     nb = t // tb
@@ -180,13 +183,11 @@
     rank = w_dt.shape[0]
     rows = pl.BlockSpec((tb, w), lambda j, i: (nb - 1 - i, j))
     return pl.pallas_call(
-        functools.partial(bwd_kernel, unroll=unroll),
+        bwd_kernel,
         grid=grid,
         in_specs=[
             rows, rows, rows,
-            pl.BlockSpec((tb // CH, N, 2 * CH), lambda j, i: (nb - 1 - i, 0, 0)),
-            pl.BlockSpec((tb, CH * N), lambda j, i: (nb - 1 - i, 0)),
-            pl.BlockSpec((CH, CH * N), lambda j, i: (0, 0)),
+            pl.BlockSpec((mix_t.shape[0], tb), lambda j, i: (0, nb - 1 - i)),
             pl.BlockSpec((N, w), lambda j, i: (0, j)),
             pl.BlockSpec((1, N, w), lambda j, i: (nb - 1 - i, 0, j)),
             pl.BlockSpec((N, w), lambda j, i: (0, j)),
@@ -215,14 +216,14 @@
         ],
         scratch_shapes=[pltpu.VMEM((N, w), F32), pltpu.VMEM(((tb + 1) * N, w), BF16),
                         pltpu.VMEM((CH * N, w), BF16), pltpu.VMEM((CH * N, w), BF16), pltpu.VMEM((CH * N, 128), F32), pltpu.VMEM((CH * N, 128), F32),
-                        pltpu.VMEM((tb, w), F32), pltpu.VMEM((tb, w), F32)],
+                        pltpu.VMEM((tb, w), F32), pltpu.VMEM((tb, w), F32), pltpu.VMEM((tb, CH * N), BF16)],
         compiler_params=pltpu.CompilerParams(vmem_limit_bytes=48 << 20),
         name="scan_backward",
-    )(stepd, u, ds, bc, bdiag, ones, rate, ckpt, gin, step, sig, low, skip, w_dt)
-
-
-def correct_kernel(alive_ref, y_ref, stepd_ref, cdiag_ref, rate_ref, ckpt_ref, sin_ref, low_ref, skip_ref, z_ref,
-                   yo_ref, ckpto_ref, gated_ref, state_ref, sbf_ref):
+    )(stepd, u, ds, mix_t, rate, ckpt, gin, step, sig, low, skip, w_dt)
+
+
+def correct_kernel(rank, alive_ref, y_ref, stepd_ref, mix_ref, rate_ref, ckpt_ref, sin_ref, low_ref, skip_ref, z_ref,
+                   yo_ref, ckpto_ref, gated_ref, state_ref, sbf_ref, cdiag_ref):
     i = pl.program_id(1)
 
     @pl.when(i == 0)
@@ -236,17 +237,16 @@
         rate = rate_ref[...]
         ckpto_ref[0] = ckpt_ref[0] + state_ref[...]
 
-        def chunk(c, s):
-            base = pl.multiple_of(c * CH, CH)
+        cdiag_ref[...] = spread(mix_ref[rank + N:rank + 2 * N, :])
+        s = state_ref[...]
+        for base in range(0, y_ref.shape[0], CH):
             for k in range(CH):
-                s = jnp.exp2(rate * stepd_ref[pl.ds(base + k, 1), :]) * s
+                s = jnp.exp2(rate * stepd_ref[base + k:base + k + 1, :]) * s
                 sbf_ref[k * N:(k + 1) * N, :] = s.astype(BF16)
-            yo_ref[pl.ds(base, CH), :] = y_ref[pl.ds(base, CH), :] + jnp.dot(
-                cdiag_ref[pl.ds(base, CH), :], sbf_ref[...], preferred_element_type=F32
+            yo_ref[base:base + CH, :] = y_ref[base:base + CH, :] + jnp.dot(
+                cdiag_ref[base:base + CH, :], sbf_ref[...], preferred_element_type=F32
             )
-            return s
-
-        state_ref[...] = lax.fori_loop(0, y_ref.shape[0] // CH, chunk, state_ref[...], unroll=8)
+        state_ref[...] = s
 
     @pl.when(jnp.logical_not(alive))
     def _():
@@ -259,30 +259,30 @@
     gated_ref[...] = (total * (z / (1.0 + jnp.exp(-z)))).astype(BF16)
 
 
-def correct(alive, y, stepd, cdiag, rate, ckpt, state_in, low, skip, z, tb=128, w=512):
+def correct(rank, alive, y, stepd, mix_t, rate, ckpt, state_in, low, skip, z, tb=128, w=512):
     t, c = stepd.shape
     w = min(w, c)
     rows = pl.BlockSpec((tb, w), lambda j, i, _: (i, j))
     lanes = pl.BlockSpec((N, w), lambda j, i, _: (0, j))
     marks = pl.BlockSpec((1, N, w), lambda j, i, _: (i, 0, j))
     return pl.pallas_call(
-        correct_kernel,
+        functools.partial(correct_kernel, rank),
         grid_spec=pltpu.PrefetchScalarGridSpec(
             num_scalar_prefetch=1,
             grid=(c // w, t // tb),
-            in_specs=[rows, rows, pl.BlockSpec((tb, CH * N), lambda j, i, _: (i, 0)), lanes, marks, lanes,
+            in_specs=[rows, rows, pl.BlockSpec((mix_t.shape[0], tb), lambda j, i, _: (0, i)), lanes, marks, lanes,
                       rows, pl.BlockSpec((1, w), lambda j, i, _: (0, j)), rows],
             out_specs=[rows, marks, rows],
-            scratch_shapes=[pltpu.VMEM((N, w), F32), pltpu.VMEM((CH * N, w), BF16)],
+            scratch_shapes=[pltpu.VMEM((N, w), F32), pltpu.VMEM((CH * N, w), BF16), pltpu.VMEM((tb, CH * N), BF16)],
         ),
         out_shape=[jax.ShapeDtypeStruct((t, c), F32), jax.ShapeDtypeStruct(ckpt.shape, F32),
                    jax.ShapeDtypeStruct((t, c), BF16)],
         compiler_params=pltpu.CompilerParams(vmem_limit_bytes=48 << 20),
         name="scan_correct",
-    )(alive, y, stepd, cdiag, rate, ckpt, state_in, low, skip, z)
-
-
-def entry_kernel(alive_ref, stepd_ref, ds_ref, bc_ref, rate_ref, g_ref):
+    )(alive, y, stepd, mix_t, rate, ckpt, state_in, low, skip, z)
+
+
+def entry_kernel(rank, alive_ref, stepd_ref, ds_ref, mix_ref, rate_ref, g_ref):
     i = pl.program_id(1)
 
     @pl.when(i == 0)
@@ -292,38 +292,32 @@
     @pl.when(alive_ref[pl.num_programs(1) - 1 - i] != 0)
     def _():
         rate = rate_ref[...]
-        nc = stepd_ref.shape[0] // CH
-
-        def chunk(c, g):
-            c = nc - 1 - c
-            base = pl.multiple_of(c * CH, CH)
-            bc = bc_ref[c]
-            for k in range(CH - 1, -1, -1):
-                adj = g + bc[:, CH + k:CH + k + 1] * ds_ref[pl.ds(base + k, 1), :]
-                g = jnp.exp2(rate * stepd_ref[pl.ds(base + k, 1), :]) * adj
-            return g
-
-        g_ref[...] = lax.fori_loop(0, nc, chunk, g_ref[...], unroll=8)
-
-
-def entry(alive, stepd, ds, bc, rate, tb=128, w=512):
+        c_t = mix_ref[rank + N:rank + 2 * N, :]
+        g = g_ref[...]
+        for k in range(stepd_ref.shape[0] - 1, -1, -1):
+            adj = g + c_t[:, k:k + 1] * ds_ref[k:k + 1, :]
+            g = jnp.exp2(rate * stepd_ref[k:k + 1, :]) * adj
+        g_ref[...] = g
+
+
+def entry(rank, alive, stepd, ds, mix_t, rate, tb=128, w=512):
     t, c = stepd.shape
     w = min(w, c)
     nb = t // tb
     rows = pl.BlockSpec((tb, w), lambda j, i, _: (nb - 1 - i, j))
     lanes = pl.BlockSpec((N, w), lambda j, i, _: (0, j))
     return pl.pallas_call(
-        entry_kernel,
+        functools.partial(entry_kernel, rank),
         grid_spec=pltpu.PrefetchScalarGridSpec(
             num_scalar_prefetch=1,
             grid=(c // w, nb),
-            in_specs=[rows, rows, pl.BlockSpec((tb // CH, N, 2 * CH), lambda j, i, _: (nb - 1 - i, 0, 0)), lanes],
+            in_specs=[rows, rows, pl.BlockSpec((mix_t.shape[0], tb), lambda j, i, _: (0, nb - 1 - i)), lanes],
             out_specs=lanes,
         ),
         out_shape=jax.ShapeDtypeStruct((N, c), F32),
         compiler_params=pltpu.CompilerParams(vmem_limit_bytes=48 << 20),
         name="scan_entry",
-    )(alive, stepd, ds, bc, rate)
+    )(alive, stepd, ds, mix_t, rate)
 
 
 def carried(local, reach, axis, by):
@@ -333,17 +327,6 @@
     return found
 
 
-def columns(values):
-    tokens = values.shape[0]
-    return values.reshape(tokens // CH, CH, N).transpose(0, 2, 1)
-
-
-def diagonal(values):
-    tokens = values.shape[0]
-    mine = jnp.arange(CH * N)[None] // N == jnp.arange(tokens)[:, None] % CH
-    return jnp.where(mine, jnp.tile(values.astype(BF16), (1, CH)), 0)
-
-
 def mesh_copy(src, dst, send, recv, **where):
     return pltpu.make_async_remote_copy(
         src_ref=src, dst_ref=dst, send_sem=send, recv_sem=recv, device_id=where, device_id_type=MESH
@@ -355,9 +338,10 @@
     return dp, seq, mine
 
 
-def tail_kernel(n, dps, seqs, tile, lag, dx_ref, dz_ref, w_hbm, nrm_ref, sm_ref, all_ref,
+def tail_kernel(n, dps, seqs, tile, lag, rank, dx_ref, dz_ref, w_hbm, nrm_ref,
+                dwx_ref, dwdt_ref, alog_ref, conv_ref, bias_ref, skip_ref,
                 dn_ref, gin_ref, gs_ref, ga_ref,
-                gacc, gsend, grecv, all_mine,
+                sm_ref, gacc, gsend, grecv, all_mine,
                 zr, zl, w_ref, loads, one_send, one_recv, two_recv, sm_one, sm_two, all_one, all_two,
                 r_send, r_recv, l_send, l_recv, w1s, w1r, w2s, w2r, s1s, s1r, s2s, s2r, a1s, a1r, a2s, a2r, gs, gr):
     dp, seq, t = place()
@@ -427,23 +411,32 @@
         here = pl.ds(pl.multiple_of(o * rows, rows), rows)
         cols = cols_of(sub)
         nt = (((1,), (1,)), ((), ()))
-        block = lax.dot_general(
+        return lax.dot_general(
             dx_ref[here, :], w_ref[0, cols, :], nt, preferred_element_type=F32
         ) + lax.dot_general(dz_ref[here, :], w_ref[1, cols, :], nt, preferred_element_type=F32)
-        scaled = block * nrm_ref[here, cols].astype(F32)
-        gacc[:, cols] = gacc[:, cols] + jnp.sum(scaled.reshape(rows // 8, 8, tile), axis=0)
-        return block
 
     def weight_rows(p, k):
         cols = pl.ds(pl.multiple_of(p * wrows, wrows), wrows)
         tn = (((0,), (0,)), ((), ()))
         d_ref = dx_ref if k == 0 else dz_ref
-        return lax.dot_general(nrm_ref[:, cols], d_ref[...], tn, preferred_element_type=F32)
+        block = lax.dot_general(nrm_ref[:, cols], d_ref[...], tn, preferred_element_type=F32)
+        scaled = (block * w_ref[k, cols, :].astype(F32)).astype(BF16)
+        lanes = jnp.ones((8, block.shape[1]), BF16)
+        nt = (((1,), (1,)), ((), ()))
+        gacc[:, cols] = gacc[:, cols] + lax.dot_general(lanes, scaled, nt, preferred_element_type=F32)
+        return block
 
     @pl.loop(0, subs)
     def _(sub):
         load(sub).start()
 
+    parts = sm_ref.shape[0]
+    for p in range(parts):
+        here, more = rank // parts, (dwx_ref.shape[0] - rank) // parts
+        sm_ref[p, 0:here, :] = dwx_ref[p * here:(p + 1) * here, :]
+        sm_ref[p, here:2 * here, :] = dwdt_ref[p * here:(p + 1) * here, :]
+        sm_ref[p, 2 * here:2 * here + more, :] = dwx_ref[rank + p * more:rank + (p + 1) * more, :]
+        sm_ref[p, 2 * here + more:, :] = jnp.zeros((sm_ref.shape[1] - 2 * here - more, sm_ref.shape[2]), F32)
     for q in range(chips):
         s1_copy(q).start()
 
@@ -464,28 +457,34 @@
             copy(i).start()
 
     def step(g, _):
-        @pl.when(g < subs)
-        def _():
-            load(g).wait()
+        @pl.when(g == 0)
+        def _():
+            load(0).wait()
+
+        @pl.when(g == 1)
+        def _():
+            @pl.loop(1, subs)
+            def _(sub):
+                load(sub).wait()
 
         stream(g - lag * t, (n - 1 - t) * subs, t == 0, zr, r_copy, lambda k: n - 1 - k)
         stream(g - lag * (n - 1 - t), t * subs, t == n - 1, zl, l_copy, lambda k: k)
 
-        @pl.when(g < chips)
+        @pl.when(jnp.logical_and(g >= 1, g < chips + 1))
         def _():
             for k in range(2):
-                one_send[g, k] = weight_rows(owner(g, 1 - core), k).astype(BF16)
-            w1_copy(g).start()
-
-        @pl.when(jnp.logical_and(g >= chips, g < 2 * chips - 1))
-        def _():
-            q = lax.rem(chip + 1 + g - chips, chips)
+                one_send[g - 1, k] = weight_rows(owner(g - 1, 1 - core), k).astype(BF16)
+            w1_copy(g - 1).start()
+
+        @pl.when(jnp.logical_and(g >= chips + 1, g < 2 * chips))
+        def _():
+            q = lax.rem(chip + g - chips, chips)
             w1_copy(q).wait_recv()
             for k in range(2):
                 one_recv[q, k] = (weight_rows(owner(q, core), k) + one_recv[q, k].astype(F32)).astype(BF16)
             w2_copy(q, chip).start()
 
-        @pl.when(g == 2 * chips - 1)
+        @pl.when(g == 2 * chips)
         def _():
             for q in range(chips):
                 s1_copy(q).wait_recv()
@@ -497,20 +496,46 @@
             for k in range(2):
                 gin_ref[k] = weight_rows(owner(chip, core), k) + one_recv[chip, k].astype(F32)
 
-        @pl.when(jnp.logical_and(g >= 2 * chips, g < 2 * chips + subs))
-        def _():
-            dn_ref[:, cols_of(g - 2 * chips)] = partial_tile(t, g - 2 * chips)
+            share = wide // n
+            for p in range(n):
+                gsend[p] = gacc[:, p * share:(p + 1) * share]
+            for ahead in range(1, n):
+                g_copy(lax.rem(t + ahead, n), t).start()
+
+        late = 2 * chips + 1
+
+        @pl.when(jnp.logical_and(g >= late, g < late + subs))
+        def _():
+            dn_ref[:, cols_of(g - late)] = partial_tile(t, g - late)
+
+        @pl.when(g == late + subs // 2)
+        def _():
+            share = wide // n
+            plain = all_mine.shape[0] - 8
+            all_mine[0:N, :] = LN2 * alog_ref[...]
+            all_mine[N:N + 8, :] = conv_ref[...]
+            all_mine[N + 8:plain, :] = jnp.zeros((plain - N - 8, all_mine.shape[1]), F32)
+            all_mine[N + 8:N + 9, :] = bias_ref[...]
+            all_mine[N + 9:N + 10, :] = skip_ref[...]
+            all_mine[plain:, :] = jnp.zeros((8, all_mine.shape[1]), F32)
+            all_mine[plain:, 0:share] = gsend[t]
+            for ahead in range(1, n):
+                p = lax.rem(t + ahead, n)
+                g_copy(p, p).wait_recv()
+                all_mine[plain:, 0:share] = all_mine[plain:, 0:share] + grecv[p]
+            a1_copy().start()
+
+        @pl.when(g == late + subs)
+        def _():
+            a1_copy().wait_recv()
+            all_one[...] = all_one[...] + all_mine[...]
+            for ahead in range(1, chips):
+                a2_copy(lax.rem(chip + ahead, chips), chip).start()
 
         return 0
 
-    steps = max((n - 1) * max(subs, lag), 2 * chips + subs)
+    steps = max((n - 1) * max(subs, lag), 2 * chips + subs + 2)
     lax.fori_loop(0, steps, step, 0)
-
-    share = wide // n
-    for p in range(n):
-        gsend[p] = gacc[:, p * share:(p + 1) * share]
-    for ahead in range(1, n):
-        g_copy(lax.rem(t + ahead, n), t).start()
 
     @pl.loop(0, subs)
     def _(s):
@@ -528,24 +553,11 @@
             l_copy(i).wait_recv()
             dn_ref[:, cols] = dn_ref[:, cols] + zl[i].astype(F32)
 
-    plain = all_ref.shape[0]
-    all_mine[0:plain, :] = all_ref[...]
-    all_mine[plain:, :] = jnp.zeros((8, all_mine.shape[1]), F32)
-    all_mine[plain:, 0:share] = gsend[t]
-    for ahead in range(1, n):
-        p = lax.rem(t + ahead, n)
-        g_copy(p, p).wait_recv()
-        all_mine[plain:, 0:share] = all_mine[plain:, 0:share] + grecv[p]
-    a1_copy().start()
     gs_ref[...] = sm_one[chip]
     for ahead in range(1, chips):
         q = lax.rem(chip + ahead, chips)
         s2_copy(q, q).wait_recv()
         gs_ref[...] = gs_ref[...] + sm_two[q]
-    a1_copy().wait_recv()
-    all_one[...] = all_one[...] + all_mine[...]
-    for ahead in range(1, chips):
-        a2_copy(lax.rem(chip + ahead, chips), chip).start()
     ga_ref[...] = all_one[...]
     for ahead in range(1, chips):
         q = lax.rem(chip + ahead, chips)
@@ -579,9 +591,12 @@
             l_copy(i).wait_send()
 
 
-def tail(dx, dz, w_full, normed, small, whole):
+def tail(dx, dz, w_full, normed, dwx, dwdt, *singles):
     n, dps, seqs = (lax.axis_size(axis) for axis in ("tensor", "dp", "seq"))
     chips = dps // 2 * seqs
+    rank = dwdt.shape[0]
+    small_rows = -(-(rank + dwx.shape[0]) // (dps * seqs) // 8) * 8
+    all_rows = N + 24
     rows = dx.shape[0] // n
     wide, lanes = w_full.shape[1], w_full.shape[2]
     wrows = wide // (dps * seqs)
@@ -592,20 +607,21 @@
     dma = pltpu.SemaphoreType.DMA
     few = dma((chips,))
     return pl.pallas_call(
-        functools.partial(tail_kernel, n, dps, seqs, tile, 2),
+        functools.partial(tail_kernel, n, dps, seqs, tile, 2, rank),
         out_shape=[
             jax.ShapeDtypeStruct((rows, wide), F32),
             jax.ShapeDtypeStruct((2, wrows, lanes), F32),
-            jax.ShapeDtypeStruct(small.shape[1:], F32),
-            jax.ShapeDtypeStruct((whole.shape[0] + 8, lanes), F32),
+            jax.ShapeDtypeStruct((small_rows, lanes), F32),
+            jax.ShapeDtypeStruct((all_rows, lanes), F32),
         ],
-        in_specs=[vmem] * 2 + [hbm] + [vmem] * 3,
+        in_specs=[vmem] * 2 + [hbm] + [vmem] * 7,
         out_specs=[vmem] * 4,
         scratch_shapes=[
+            pltpu.VMEM((dps * seqs, small_rows, lanes), F32),
             pltpu.VMEM((8, wide), F32),
             pltpu.VMEM((n, 8, wide // n), F32),
             pltpu.VMEM((n, 8, wide // n), F32),
-            pltpu.VMEM((whole.shape[0] + 8, lanes), F32),
+            pltpu.VMEM((all_rows, lanes), F32),
             pltpu.VMEM((hops, rows, tile), BF16),
             pltpu.VMEM((hops, rows, tile), BF16),
             pltpu.VMEM((2, wide, lanes), BF16),
@@ -613,10 +629,10 @@
             pltpu.VMEM((chips, 2, wrows, lanes), BF16),
             pltpu.VMEM((chips, 2, wrows, lanes), BF16),
             pltpu.VMEM((chips, 2, wrows, lanes), BF16),
-            pltpu.VMEM((chips,) + small.shape[1:], F32),
-            pltpu.VMEM((chips,) + small.shape[1:], F32),
-            pltpu.VMEM((whole.shape[0] + 8, lanes), F32),
-            pltpu.VMEM((chips, whole.shape[0] + 8, lanes), F32),
+            pltpu.VMEM((chips, small_rows, lanes), F32),
+            pltpu.VMEM((chips, small_rows, lanes), F32),
+            pltpu.VMEM((all_rows, lanes), F32),
+            pltpu.VMEM((chips, all_rows, lanes), F32),
             dma((hops,)), dma((hops,)), dma((hops,)), dma((hops,)),
             few, few, few, few, few, few, few, few, dma, dma, few, few, dma((n,)), dma((n,)),
         ],
@@ -624,7 +640,7 @@
             collective_id=2, has_side_effects=True, vmem_limit_bytes=60 << 20
         ),
         name="tail_sums",
-    )(dx, dz, w_full, normed, small, whole)
+    )(dx, dz, w_full, normed, dwx, dwdt, *singles)
 
 
 def mid_kernel(n, tile, lag, gated_ref, w_ref, hid_ref, tea_ref, scale_ref, z_hbm, scan_hbm,
@@ -909,9 +925,9 @@
 
 
 def front_kernel(n, dps, seqs, subs, lag, hid_ref, gain_ref, seg_ref, win_ref, wsm_ref, taps_ref, keep_ref,
-                 x_out, z_out, nrm_out, w_out, conv_out, low_out, total_ref, gfull, ws_ref, mixed_ref,
+                 x_out, z_out, nrm_out, w_out, conv_out, low_out, total_ref, gfull, ws_ref, natural_ref,
                  rows_ref, gain_tile, cnt_tile, grecv, cnt_one, cnt_two, x_ref, z_ref, nrm_ref, w_ref, conv_ref, low_ref,
-                 mix_send, mix_recv, mix_own, outs, ms, mr, ns, nr,
+                 mix_send, mix_recv, mix_own, mix_rows_ref, mixed_ref, outs, ms, mr, ns, nr,
                  ar_send, ar_recv, al_send, al_recv, gs, gr, c1s, c1r, c2s, c2r, hs, hr, ls,
                  chip_send, chip_recv, core_send, core_recv):
     dp, seq, t = place()
@@ -1054,88 +1070,6 @@
                 cols = pl.ds(pl.multiple_of(j * width, width), width)
                 dst[there, cols] = jnp.dot(nrm_ref[here, :], w_ref[k, :, cols], preferred_element_type=F32)
 
-    def turn(d, o):
-        final = jnp.where(o == 0, (n - 1) * gap + 1, (n - 2 - o) * gap + lag)
-        return jnp.where(d == n - 1, final, (d - o) * gap)
-
-    weights_at = (n - 1) * gap
-
-    def step(g, _):
-        @pl.when(g == 0)
-        def _():
-            normalize(t)
-
-        @pl.when(g == weights_at)
-        def _():
-            for kind in (1, 0):
-                for ahead in range(1, chips):
-                    q = lax.rem(chip + ahead, chips)
-                    chip_copy(kind, q, owner(q, core)).wait_recv()
-                    core_copy(kind, owner(q, core), False).start()
-            for kind in (1, 0):
-                for q in range(chips):
-                    core_copy(kind, owner(q, 1 - core), True).wait_recv()
-            project(t)
-
-        @pl.loop(0, n)
-        def _(o):
-            s_right = g - turn(t, o)
-            s_left = g - turn(n - 1 - t, n - 1 - o)
-
-            @pl.when(jnp.logical_and(o < t, jnp.logical_and(s_right >= 0, s_right < subs)))
-            def _():
-                ar_copy(o, s_right).wait_recv()
-
-                @pl.when(t < n - 1)
-                def _():
-                    ar_copy(o, s_right).start()
-
-            @pl.when(jnp.logical_and(o > t, jnp.logical_and(s_left >= 0, s_left < subs)))
-            def _():
-                al_copy(o, s_left).wait_recv()
-
-                @pl.when(t > 0)
-                def _():
-                    al_copy(o, s_left).start()
-
-            landed = jnp.where(o < t, s_right, s_left) - subs + 1
-
-            @pl.when(jnp.logical_and(o != t, landed == 0))
-            def _():
-                normalize(o)
-
-            ripe = jnp.where(g == weights_at, landed >= 0, jnp.logical_and(g > weights_at, landed == 0))
-
-            @pl.when(jnp.logical_and(o != t, ripe))
-            def _():
-                project(o)
-
-        return 0
-
-    steps = weights_at + 1 + subs
-    lax.fori_loop(0, steps, step, 0)
-
-    @pl.when(seq < seqs - 1)
-    def _():
-        edge_copy().start()
-
-    @pl.when(seq == 0)
-    def _():
-        x_ref[0:8, :] = jnp.zeros((8, x_ref.shape[1]), F32)
-
-    for i in range(3):
-        written(i).start()
-
-    @pl.when(seq > 0)
-    def _():
-        edge_copy().wait_recv()
-
-    @pl.when(seq < seqs - 1)
-    def _():
-        edge_copy().wait_send()
-
-    written(3).start()
-    local_copy().wait()
     lanes = low_ref.shape[1]
     width = min(tile, lanes)
     piece = min(64, rows)
@@ -1157,26 +1091,111 @@
             low_ref[here, cols] = (total / (1.0 + jnp.exp(-total))).astype(BF16)
 
     groups, depth = ws_ref.shape[0], ws_ref.shape[1]
-    used = mix_own.shape[0] // groups
-
-    @pl.loop(0, n)
-    def _(i):
-        o = lax.rem(t + 1 + i, n)
+    live = natural_ref.shape[0] // groups
+
+    def mix_rows(o):
         convolve(o)
         nt = (((1,), (1,)), ((), ()))
         low = low_ref[pl.ds(pl.multiple_of(o * rows, rows), rows), :]
         weights = ws_ref[...].reshape(groups * depth, lanes)
         mix = lax.dot_general(weights, low, nt, preferred_element_type=F32)
-        mix = jnp.concatenate([mix[p * depth:p * depth + used] for p in range(groups)], 0)
+        for p in range(groups):
+            mix_rows_ref[p * live:(p + 1) * live, :] = mix[p * depth:p * depth + live]
 
         @pl.when(o != t)
         def _():
-            mix_send[o] = mix.astype(BF16)
+            mix_send[o] = mix_rows_ref[...].astype(BF16)
             mix_copy(o, t).start()
 
         @pl.when(o == t)
         def _():
-            mix_own[...] = mix
+            mix_own[...] = mix_rows_ref[...]
+
+    def turn(d, o):
+        final = jnp.where(o == 0, (n - 1) * gap + 1, (n - 2 - o) * gap + lag)
+        return jnp.where(d == n - 1, final, (d - o) * gap)
+
+    weights_at = (n - 1) * gap
+
+    def step(g, _):
+        @pl.when(g == 0)
+        def _():
+            normalize(t)
+
+        @pl.when(g == weights_at)
+        def _():
+            for kind in (1, 0):
+                for ahead in range(1, chips):
+                    q = lax.rem(chip + ahead, chips)
+                    chip_copy(kind, q, owner(q, core)).wait_recv()
+                    core_copy(kind, owner(q, core), False).start()
+            for kind in (1, 0):
+                for q in range(chips):
+                    core_copy(kind, owner(q, 1 - core), True).wait_recv()
+            project(t)
+
+        @pl.loop(0, n)
+        def _(o):
+            s_right = g - turn(t, o)
+            s_left = g - turn(n - 1 - t, n - 1 - o)
+
+            @pl.when(jnp.logical_and(o < t, jnp.logical_and(s_right >= 0, s_right < subs)))
+            def _():
+                ar_copy(o, s_right).wait_recv()
+
+                @pl.when(t < n - 1)
+                def _():
+                    ar_copy(o, s_right).start()
+
+            @pl.when(jnp.logical_and(o > t, jnp.logical_and(s_left >= 0, s_left < subs)))
+            def _():
+                al_copy(o, s_left).wait_recv()
+
+                @pl.when(t > 0)
+                def _():
+                    al_copy(o, s_left).start()
+
+            landed = jnp.where(o < t, s_right, s_left) - subs + 1
+
+            @pl.when(jnp.logical_and(o != t, landed == 0))
+            def _():
+                normalize(o)
+
+            ripe = jnp.where(g == weights_at, landed >= 0, jnp.logical_and(g > weights_at, landed == 0))
+
+            @pl.when(jnp.logical_and(o != t, ripe))
+            def _():
+                project(o)
+
+        return 0
+
+    steps = weights_at + 1 + subs
+    lax.fori_loop(0, steps, step, 0)
+
+    @pl.when(seq < seqs - 1)
+    def _():
+        edge_copy().start()
+
+    @pl.when(seq == 0)
+    def _():
+        x_ref[0:8, :] = jnp.zeros((8, x_ref.shape[1]), F32)
+
+    for i in range(3):
+        written(i).start()
+
+    @pl.when(seq > 0)
+    def _():
+        edge_copy().wait_recv()
+
+    @pl.when(seq < seqs - 1)
+    def _():
+        edge_copy().wait_send()
+
+    written(3).start()
+    local_copy().wait()
+    @pl.loop(0, n)
+    def _(i):
+        mix_rows(lax.rem(t + 1 + i, n))
 
     for i in range(4, 6):
         written(i).start()
@@ -1195,6 +1214,8 @@
     for ahead in range(1, n):
         p = lax.rem(t + ahead, n)
         sum_copy(p, p).wait_recv()
+    for o in range(n):
+        natural_ref[:, o * rows:(o + 1) * rows] = mixed_ref[o].astype(F32)
     for ahead in range(1, n):
         p = lax.rem(t + ahead, n)
         mix_copy(p, t).wait_send()
@@ -1224,14 +1245,14 @@
             al_copy(o, s).wait_send()
 
 
-def front(hidden, gain, segments, w_in, w_small, taps, keeps):
+def front(hidden, gain, segments, w_in, w_small, taps, keeps, x_cols):
     n, dps, seqs = (lax.axis_size(axis) for axis in ("tensor", "dp", "seq"))
     parts = dps * seqs
     chips = parts // 2
     rows, wide = hidden.shape
     lanes = w_in.shape[2]
     tokens = rows * n
-    mixed = parts * SMALL_ROWS
+    mixed = parts * x_cols
     subs = max(1, rows // 32)
     vmem, hbm = pl.BlockSpec(memory_space=pltpu.VMEM), pl.BlockSpec(memory_space=pl.ANY)
     dma = pltpu.SemaphoreType.DMA
@@ -1248,7 +1269,7 @@
             jax.ShapeDtypeStruct((8, 128), F32),
             jax.ShapeDtypeStruct((8, wide), F32),
             jax.ShapeDtypeStruct((parts,) + w_small.shape, BF16),
-            jax.ShapeDtypeStruct((n, mixed, rows), BF16),
+            jax.ShapeDtypeStruct((parts * x_cols, tokens), F32),
         ],
         in_specs=[vmem] * 7,
         out_specs=[hbm] * 6 + [vmem] * 4,
@@ -1268,6 +1289,8 @@
             pltpu.VMEM((n, mixed, rows), BF16),
             pltpu.VMEM((n, mixed, rows), BF16),
             pltpu.VMEM((mixed, rows), F32),
+            pltpu.VMEM((mixed, rows), F32),
+            pltpu.VMEM((n, mixed, rows), BF16),
             dma((6,)), peers, peers, peers, peers,
             many, many, many, many, peers, peers, dma, dma, few, few, dma, dma, dma,
             dma((2, chips)), dma((2, parts)), dma((2, parts)), dma((2, parts)),
@@ -1322,12 +1345,13 @@
     dcv_ref[0:8, :] = jnp.zeros((8, lanes), F32)
     dcv_ref[tokens + 8:, :] = jnp.zeros((8, lanes), F32)
     load(1).wait()
+    step = step_ref[0:dwdt_ref.shape[0], :].astype(BF16)
     tn = (((0,), (0,)), ((), ()))
 
     @pl.loop(0, across)
     def _(j):
         cols = pl.ds(pl.multiple_of(j * width, width), width)
-        dwdt_ref[:, cols] = jnp.dot(step_ref[...], dpl_ref[:, cols], preferred_element_type=F32)
+        dwdt_ref[:, cols] = jnp.dot(step, dpl_ref[:, cols], preferred_element_type=F32)
 
     own[...] = part_ref[t].astype(F32)
     for ahead in range(1, n):
@@ -1418,11 +1442,10 @@
     out.wait()
 
 
-def mixback(part, e, conv_sum, x_rows, x_low, d_pre_low, step_t, w_x, taps, keeps):
+def mixback(part, e, conv_sum, x_rows, x_low, d_pre_low, mix_t, w_x, taps, keeps, rank):
     n, seqs = lax.axis_size("tensor"), lax.axis_size("seq")
     tokens, lanes = x_low.shape
     mixed, rows = part.shape[1:]
-    rank = step_t.shape[0]
     vmem, hbm = pl.BlockSpec(memory_space=pltpu.VMEM), pl.BlockSpec(memory_space=pl.ANY)
     dma = pltpu.SemaphoreType.DMA
     peers = dma((n,))
@@ -1455,7 +1478,7 @@
             collective_id=4, has_side_effects=True, vmem_limit_bytes=60 << 20
         ),
         name="mix_backward",
-    )(part, e, conv_sum, x_rows, x_low, d_pre_low, step_t, w_x, taps, keeps)
+    )(part, e, conv_sum, x_rows, x_low, d_pre_low, mix_t, w_x, taps, keeps)
 
 
 def on_device(
@@ -1501,7 +1524,7 @@
     taps = jnp.concatenate(
         [conv_weight.astype(F32), conv_bias.astype(F32)[None], jnp.zeros((7 - conv_taps, chan_lanes), F32)], 0
     )
-    x_rows, z_gate, normalized_rows, w_in, conv_sum, x_low, total, gain_rows, w_small, mixed = front(
+    x_rows, z_gate, normalized_rows, w_in, conv_sum, x_low, total, gain_rows, w_small, mix_t = front(
         hidden_in,
         norm_gain[None],
         segment_ids.reshape(8, -1),
@@ -1509,6 +1532,7 @@
         w_small,
         taps,
         jnp.concatenate(tap_keeps, 1),
+        x_cols,
     )
     w_out_rows, z_gate = lax.optimization_barrier((output_projection_weight.T, z_gate))
     w_out = lax.all_gather(w_out_rows, ("dp", "seq"), axis=0, tiled=True)
@@ -1518,22 +1542,14 @@
     share_rows = hidden_in.astype(F32)
     full_gain = gain_rows[0]
     inv_share = lax.rsqrt(jnp.mean(share_rows * share_rows, axis=1, keepdims=True) + EPS)
-    mixed = mixed.reshape(-1, parts, SMALL_ROWS, row_share)[:, :, :x_cols]
-    mixed_rows = mixed.transpose(0, 3, 1, 2).reshape(tok_rows, parts * x_cols).astype(F32)
     rank_width = w_dt.shape[0]
-    state_width = (mixed_rows.shape[1] - rank_width) // 2
-    step_low = mixed_rows[:, :rank_width].astype(jnp.bfloat16)
-    b_in = mixed_rows[:, rank_width : rank_width + state_width]
-    c_out = mixed_rows[:, rank_width + state_width :]
     same_doc = (seg_float == ext_seg[back_rows - 1 : back_rows - 1 + tok_rows]).astype(jnp.float32)
     rates = -jnp.exp(a_log) * LOG2E
     block = 128
-    col_pair = jnp.concatenate([columns(b_in), columns(c_out)], -1)
-    b_diag, c_diag = diagonal(b_in), diagonal(c_out)
-    resets = jnp.sum((same_doc == 0).astype(jnp.int32).reshape(-1, block), axis=1)
-    alive = (jnp.cumsum(resets) - resets == 0).astype(jnp.int32)
+    first_reset = jnp.min(jnp.where(same_doc == 0, jnp.arange(tok_rows), tok_rows))
+    alive = (jnp.arange(0, tok_rows, block) <= first_reset).astype(jnp.int32)
     y_local, marks, state_last, stepd, inject, step_size, step_slope = fwd(
-        step_low, w_dt, dt_bias[None], x_low, same_doc[:, None], col_pair, c_diag, rates, tb=block, unroll=8
+        mix_t, w_dt, dt_bias[None], x_low, same_doc[:, None], rates, tb=block, w=1024
     )
 
     def reach():
@@ -1541,7 +1557,7 @@
 
     state_in = carried(state_last, reach, "seq", 1)
     scan_out, marks, gated_output_rows = correct(
-        alive, y_local, stepd, c_diag, rates, marks, state_in, x_low, d_skip[None], z_gate, tb=block
+        rank_width, alive, y_local, stepd, mix_t, rates, marks, state_in, x_low, d_skip[None], z_gate, tb=block, w=1024
     )
     valid_share = lax.dynamic_slice_in_dim(valid_mask, row_start, row_share, 0)
     total_tokens = float(tok_rows * lax.axis_size(("dp", "seq")))
@@ -1549,14 +1565,12 @@
     output, grad_out, d_wout, d_scan, d_z = middle(
         gated_output_rows, w_out, hidden_in, teacher, scale, z_gate, scan_out
     )
-    adjoint_first = entry(alive, stepd, d_scan, col_pair, rates, tb=block)
+    adjoint_first = entry(rank_width, alive, stepd, d_scan, mix_t, rates, tb=block, w=1024)
     adjoint_in = carried(adjoint_first, reach, "seq", -1)
-    ones = diagonal(jnp.ones((CH, N), F32))
     d_pre_low, d_direct, d_rank_t, d_b_part, d_c_part, a_log_part, dt_bias_part, d_skip_part = bwd(
-        stepd, inject, d_scan, col_pair, b_diag, ones, rates, marks, adjoint_in,
-        step_size, step_slope, x_low, d_skip[None], w_dt, tb=block, unroll=8
+        stepd, inject, d_scan, mix_t, rates, marks, adjoint_in,
+        step_size, step_slope, x_low, d_skip[None], w_dt, tb=block
     )
-    a_log_part = LN2 * a_log_part
     part = jnp.concatenate(
         [
             jnp.sum(d_rank_t, axis=0),
@@ -1568,24 +1582,13 @@
     part = part.astype(BF16).reshape(part.shape[0], -1, row_share).transpose(1, 0, 2)
     edge = jnp.zeros((8, conv_taps), F32)
     d_x, d_wx, d_wdt, conv_parts = mixback(
-        part, d_direct, conv_sum, x_rows, x_low, d_pre_low, step_low.T, w_x, taps,
+        part, d_direct, conv_sum, x_rows, x_low, d_pre_low, mix_t, w_x, taps,
         jnp.concatenate([edge] + [jnp.concatenate(tap_keeps, 1)] + [edge], 0),
+        rank_width,
     )
-    d_wx_rank, d_wx_state = d_wx[:rank_width], d_wx[rank_width:]
-    conv_weight_part, conv_bias_part = conv_parts[:conv_taps], conv_parts[conv_taps]
-    small = jnp.concatenate(
-        [
-            d_wx_rank.reshape(parts, -1, chan_lanes),
-            d_wx_state.reshape(parts, -1, chan_lanes),
-            d_wdt.reshape(parts, -1, chan_lanes),
-            jnp.zeros((parts, 4, chan_lanes), F32),
-        ],
-        1,
+    d_norm_share, g_in, g_small, g_whole = tail(
+        d_x, d_z, w_in, normalized_rows, d_wx, d_wdt, a_log_part, conv_parts, dt_bias_part, d_skip_part
     )
-    whole = jnp.concatenate(
-        [a_log_part, conv_weight_part, conv_bias_part[None], dt_bias_part, d_skip_part, d_skip_part], 0
-    )
-    d_norm_share, g_in, g_small, g_whole = tail(d_x, d_z, w_in, normalized_rows, small, whole)
     g_in = jnp.swapaxes(g_in, 0, 1)
     inner_sum = jnp.sum(d_norm_share * full_gain[None] * share_rows, axis=1, keepdims=True)
     inv_cube = inv_share * inv_share * inv_share
@@ -1595,14 +1598,14 @@
         - share_rows * inv_cube * inner_sum / model_width
     )
     rank_here = rank_width // parts
-    state_here = 2 * state_width // parts
+    state_here = 2 * N // parts
     g_x_rank = g_small[:rank_here].T
-    g_x_state = g_small[rank_here : rank_here + state_here].T
-    g_dt = g_small[rank_here + state_here : rank_here + state_here + rank_here]
+    g_dt = g_small[rank_here : 2 * rank_here]
+    g_x_state = g_small[2 * rank_here : 2 * rank_here + state_here].T
     g_out = lax.psum_scatter(d_wout, ("dp", "seq"), scatter_dimension=0, tiled=True).astype(F32).T
-    g_gain = jnp.sum(g_whole[N + conv_taps + 4 :, : norm_gain.shape[0]], axis=0) / norm_gain.astype(F32)
-    g_alog, g_conv_w = g_whole[:N], g_whole[N : N + conv_taps]
-    g_conv_b, g_bias, g_skip = g_whole[N + conv_taps], g_whole[N + conv_taps + 1], g_whole[N + conv_taps + 2]
+    g_gain = g_whole[N + 16, : norm_gain.shape[0]] / norm_gain.astype(F32)
+    g_alog, g_conv_w, g_conv_b = g_whole[:N], g_whole[N : N + conv_taps], g_whole[N + conv_taps]
+    g_bias, g_skip = g_whole[N + 8], g_whole[N + 9]
     return (
         output,
         input_grad,

time: 542 us -> 526 us (0.970)
  Pallas kernels: 451 us -> 441 us
  local copies, waits for them, and re-layouts: 45.2 us -> 38.1 us
    pallas_call x5, Pallas kernels: 195 us -> 187 us  [the longest x1 89.5 us: tail(): pl.pallas_call(functools.partial(tail_kernel, n, dps, seqs, tile, 2, rank...]
    unnamed x63 -> x65, local copies, waits for them, and re-layouts: 21 us -> 23.6 us
  transfers between devices with their start and end apart: 4 -> 4, of which waited for: 1 -> 1; matrix products, arithmetic and copies ran while one was open for 7% -> 4% of each run, Pallas kernels for 42% -> 42%
where the time goes in v8:
time: 526 us; the launch traced here: 519 us
  Pallas kernels  441 us (84%)
  local copies, waits for them, and re-layouts  38.1 us (7%)
  between operations  15.8 us (3%)
  other arithmetic  12.7 us (2%)
  waiting for transfers between devices  6.66 us (1%)
    pallas_call x1, Pallas kernels, middle(): pl.pallas_call(functools.partial(mid_kernel, n, tile, 2), out_shape=[jax....  121 us
    pallas_call x1, Pallas kernels, front(): pl.pallas_call(functools.partial(front_kernel, n, dps, seqs, subs, 2), ou...  103 us
    pallas_call x1, Pallas kernels, tail(): pl.pallas_call(functools.partial(tail_kernel, n, dps, seqs, tile, 2, rank...  89.5 us
    pallas_call x1, Pallas kernels, bwd(): pl.pallas_call(bwd_kernel, grid=grid, in_specs=[rows, rows, rows, pl.Bloc...  59 us
    pallas_call x1, Pallas kernels, mixback(): pl.pallas_call(functools.partial(mixback_kernel, n, seqs), out_shape=[jax...  29 us
    unnamed x65, local copies, waits for them, and re-layouts  23.6 us
    pallas_call x1, Pallas kernels, fwd(): pl.pallas_call(fwd_kernel, grid=grid, in_specs=[pl.BlockSpec((mixed, tb),...  22 us
  transfers between devices with their start and end apart: 4, of which 1 were waited for; matrix products, arithmetic and copies ran while one was open for 4% of the time, Pallas kernels for 42%

profile of v8, /device:TPU:0, one launch (start us, length us, event | category | flops | bytes accessed | tf_op | source)
XLA Modules:
  0.0 518.6 jit_solution(5666613669581355034)
XLA Ops:
  7.3 0.8 convert_element_type.29
  8.0 0.8 compare_convert_fusion
  9.0 1.3 broadcast_in_dim.66.gain_ref
  11.5 0.7 broadcast_in_dim.81
  12.2 0.7 convert_element_type.32
  13.2 0.8 concatenate.33.keep_ref
  14.1 2.0 copy.63
  16.1 1.2 copy.78
  17.4 0.7 maximum_maximum_fusion.1.taps_ref
  18.1 0.7 maximum_maximum_fusion.wsm_ref
  18.9 103.5 %front.1 = (f32[1032,1024]{1,0:T(8,128)}, f32[1024,1024]{1,0:T(8,128)}, bf16[1024,2048]{1,0:T(8,128)(2,1)}, bf16[2,2048,1024]{2,1,0:T(8,128)(2,1)}, f32[1024,102...) custom-call(bf16[256,2048]{1,0:T(8,128)(2,1)} %hid_ref.3, ...), custom_call_target="tpu_custom_call" | custom-call | tf_op jit(solution)/shard_map/front/pallas_call | solution.py:1260
  122.4 0.7 select_reduce_fusion
  123.3 1.0 slice.56
  124.4 1.6 copy-done.1
  126.0 22.0 %scan_forward.1 = (f32[1024,1024]{1,0:T(8,128)}, f32[8,16,1024]{2,1,0:T(8,128)S(1)}, f32[16,1024]{1,0:T(8,128)}, f32[1024,1024]{1,0:T(8,128)}, f32[1024,1024]{1,...) custom-call(f32[160,1024]{1,0:T(8,128)S(1)} %copy-done.3, bf16[128,1024]{1,0:T(8,128)(2,1)S(1)} %bitcast.35, ...), custom_call_target="tpu_custom_call" | custom-call | tf_op jit(solution)/shard_map/scan_forward/pallas_call | solution.py:77
  148.1 0.8 copy-done.9
  148.8 3.2 collective-permute-start
  152.1 1.2 slice.57
  154.1 0.8 copy.64.scale_ref
  156.2 0.8 copy-done.7
  157.0 1.0 copy-done.10
  158.0 0.8 copy-done.13
  158.9 10.2 %scan_correct.1 = (f32[1024,1024]{1,0:T(8,128)}, f32[8,16,1024]{2,1,0:T(8,128)S(1)}, bf16[1024,1024]{1,0:T(8,128)(2,1)S(1)}) custom-call(s32[8]{0:T(128)S(1)} %compare_convert_fusion.2.alive_ref, f32[1024,1024]{1,0:T(8,128)} %get-tuple-element.59.y_ref, f32[1024,1024]{1,0:T(8,128)} %get-tuple-element.60.stepd_ref, f32[160,1024]{1,0:T(8,128)S(1)} %copy-done.3, ...), custom_call_target="tpu_custom_call" | custom-call | tf_op jit(solution)/shard_map/scan_correct/pallas_call | solution.py:268
  169.1 1.3 copy-done.5
  170.4 120.9 %middle.1 = (bf16[256,2048]{1,0:T(8,128)(2,1)}, f32[256,2048]{1,0:T(8,128)}, bf16[2048,1024]{1,0:T(8,128)(2,1)}, f32[1024,1024]{1,0:T(8,128)}, bf16[1024,1024]{1,0:T(8,128)(2,1)}) custom-call(bf16[1024,1024]{1,0:T(8,128)(2,1)} %copy-done.5, bf16[2048,1024]{1,0:T(8,128)(2,1)} %all-gather.2.cloned.1.call-done.w_ref, bf16[256,2048]{1,0:T(8,128)(2,1)} %hid_ref.3, ...), custom_call_target="tpu_custom_call" | custom-call | tf_op jit(solution)/shard_map/middle/pallas_call | solution.py:895
  291.3 0.8 copy-done.8
  292.2 2.2 copy-done
  294.3 6.8 %scan_entry.1 = f32[16,1024]{1,0:T(8,128)S(1)} custom-call(s32[8]{0:T(128)S(1)} %compare_convert_fusion.2.alive_ref, f32[1024,1024]{1,0:T(8,128)S(1)} %copy-done, f32[1024,1024]{1,0:T(8,128)} %get-tuple-element.73.ds_ref, f32[160,1024]{1,0:T(8,128)S(1)} %copy-done.3, f32[16,1024]{1,0:T(8,128)S(1)} %copy-done.8), custom_call_target="tpu_custom_call" | custom-call | tf_op jit(solution)/shard_map/scan_entry/pallas_call | solution.py:309
  301.2 1.3 collective-permute-start.1
  302.5 0.8 pad_maximum_fusion.keep_ref
  303.4 0.9 slice.58
  304.2 0.8 reshape.71.wx_ref
  305.0 6.6 %collective-permute-done.1.gin_ref = f32[16,1024]{1,0:T(8,128)S(1)} collective-permute-done((f32[16,1024]{1,0:T(8,128)S(1)}, f32[16,1024]{1,0:T(8,128)S(1)}, u32[]{:S(2)}, u32[]{:S(2)}) %collective-permute-start.1) | collective-permute-done | bytes 65568 | tf_op jit(solution)/shard_map/ppermute | solution.py:24
  311.6 59.0 %scan_backward.1 = (bf16[1024,1024]{1,0:T(8,128)(2,1)S(1)}, f32[1024,1024]{1,0:T(8,128)}, f32[2,128,1024]{2,1,0:T(8,128)S(1)}, f32[2,64,256]{2,1,0:T(8,128)S(1)}...) custom-call(f32[1024,1024]{1,0:T(8,128)} %get-tuple-element.60.stepd_ref, ...), custom_call_target="tpu_custom_call" | custom-call | tf_op jit(solution)/shard_map/scan_backward/pallas_call | solution.py:185
  370.6 1.3 copy-done.4
  374.8 0.8 maximum_bitcast_fusion.part_ref
  375.6 29.0 %mix_backward.1 = (bf16[1024,1024]{1,0:T(8,128)(2,1)}, f32[160,1024]{1,0:T(8,128)}, f32[128,1024]{1,0:T(8,128)}, f32[8,1024]{1,0:T(8,128)}) custom-call(bf16[4,160,256]{2,1,0:T(8,128)(2,1)} %maximum_bitcast_fusion.part_ref, f32[1024,1024]{1,0:T(8,128)} %get-tuple-element.80.e_hbm, f32[1024,1024]{1,0:T(8,128)} %get-tuple-element.81.conv_hbm, ...), custom_call_target="tpu_custom_call" | custom-call | tf_op jit(solution)/shard_map/mix_backward/pallas_call | solution.py:1452
  404.5 89.5 %tail_sums.1 = (f32[256,2048]{1,0:T(8,128)}, f32[2,256,1024]{2,1,0:T(8,128)}, f32[40,1024]{1,0:T(8,128)}, f32[40,1024]{1,0:T(8,128)}) custom-call(bf16[1024,1024]{1,0:T(8,128)(2,1)} %get-tuple-element.84.dx_ref, bf16[1024,1024]{1,0:T(8,128)(2,1)} %get-tuple-element.85.dz_ref, bf16[2,2048,1024]{2,1,0:T(8,128)(2,1)} %get-tuple-element.86.w_hbm, ...), custom_call_target="tpu_custom_call" | custom-call | tf_op jit(solution)/shard_map/tail_sums/pallas_call | solution.py:609
  494.0 0.7 slice.60
  494.7 1.4 slice.61
  496.1 1.5 slice.67
  497.6 4.7 copy.71
  503.5 1.4 fusion.8
  505.6 0.7 fusion.9
  506.2 2.0 fusion.3
  508.2 1.2 convert_bitcast_fusion
  509.4 1.3 copy.72
  510.8 1.0 copy.80
  (91 shorter events, 7.7 us)
Async XLA Ops:
  7.2 8.9 %copy-start.22 = (bf16[256,2,1024]{2,1,0:T(2,128)(2,1)S(1)}, bf16[256,2,1024]{2,1,0:T(2,128)(2,1)}, u32[]{:S(2)}) copy-start(bf16[256,2,1024]{2,1,0:T(2,128)(2,1)} %param.17) | copy-start | bytes 3145732
  7.2 10.9 %copy-start.28 = (bf16[16,1024]{1,0:T(8,128)(2,1)S(1)}, bf16[16,1024]{1,0:T(8,128)(2,1)}, u32[]{:S(2)}) copy-start(bf16[16,1024]{1,0:T(8,128)(2,1)} %param.21) | copy-start | bytes 98308
  7.2 10.9 %copy-start.27 = (bf16[1024,20]{0,1:T(8,128)(2,1)S(1)}, bf16[1024,20]{0,1:T(8,128)(2,1)}, u32[]{:S(2)}) copy-start(bf16[1024,20]{0,1:T(8,128)(2,1)} %param.20) | copy-start | bytes 122884
  7.2 163.2 %all-gather.2.cloned.1.call-start = ((), (), s32[]{:S(2)}) async-start(), calls=%async_computation.1 | async-start | bytes 4718592 | tf_op jit(solution)/shard_map/all_gather | solution.py:1538
  18.8 105.5 %copy-start.26 = (f32[16,1024]{1,0:T(8,128)S(1)}, f32[16,1024]{1,0:T(8,128)}, u32[]{:S(2)}) copy-start(f32[16,1024]{1,0:T(8,128)} %param.23) | copy-start | bytes 196612
  18.8 105.5 %copy-start.15 = (f32[1024]{0:T(1024)S(1)}, f32[1024]{0:T(1024)}, u32[]{:S(2)}) copy-start(f32[1024]{0:T(1024)} %param.22) | copy-start | bytes 12292
  122.3 2.1 copy-start.3
  122.3 385.9 %reduce-scatter.2.cloned.1.call-start = ((), (), s32[]{:S(2)}) async-start(), calls=%async_computation.2 | async-start | bytes 4718592 | tf_op jit(solution)/shard_map/reduce_scatter | solution.py:1605
  123.3 32.8 %copy-start.14 = (f32[1024]{0:T(1024)S(1)}, f32[1024]{0:T(1024)}, u32[]{:S(2)}) copy-start(f32[1024]{0:T(1024)} %param.24) | copy-start | bytes 12292
  124.4 23.7 %copy-start.6 = (f32[16,1024]{1,0:T(8,128)}, f32[16,1024]{1,0:T(8,128)S(1)}, u32[]{:S(2)}) copy-start(f32[16,1024]{1,0:T(8,128)S(1)} %negate_multiply_fusion.rate_ref) | copy-start | bytes 196612
  124.4 1.6 copy-start.1
  126.0 30.2 %copy-start.2 = (bf16[1024,1024]{1,0:T(8,128)(2,1)S(1)}, bf16[1024,1024]{1,0:T(8,128)(2,1)}, u32[]{:S(2)}) copy-start(bf16[1024,1024]{1,0:T(8,128)(2,1)} %get-tuple-element.58.low_ref.low_hbm) | copy-start | bytes 6291460
  148.1 0.8 copy-start.9
  148.8 6.7 %collective-permute-start = (f32[16,1024]{1,0:T(8,128)}, f32[16,1024]{1,0:T(8,128)S(1)}, u32[]{:S(2)}, u32[]{:S(2)}) collective-permute-start(f32[16,1024]{1,0:T(8,128)} %get-tuple-element.62), channel_id=1, source_target_pairs={{0,4},{1,5},{2,6},{3,7},{8,12},{9,13},{10,14},{11,15},{16,20},{17,... | collective-permute-start | bytes 196616 | tf_op jit(solution)/shard_map/ppermute | solution.py:24
  155.5 0.6 copy-start.12
  156.2 0.8 copy-start.7
  157.0 1.0 copy-start.10
  158.0 0.8 copy-start.13
  169.1 1.3 copy-start.5
  291.3 0.8 copy-start.8
  292.2 2.2 copy-start
  294.3 8.1 %copy-start.20 = (f32[1024,4]{1,0:T(8,128)S(1)}, f32[1024,4]{1,0:T(8,128)}, u32[]{:S(2)}) copy-start(f32[1024,4]{1,0:T(8,128)} %concatenate.33.keep_ref) | copy-start | bytes 49156
  294.3 9.0 %copy-start.24 = (bf16[8,48,1024]{2,1,0:T(8,128)(2,1)S(1)}, bf16[8,48,1024]{2,1,0:T(8,128)(2,1)}, u32[]{:S(2)}) copy-start(bf16[8,48,1024]{2,1,0:T(8,128)(2,1)} %get-tuple-element.57) | copy-start | bytes 2359300
  301.2 10.5 %collective-permute-start.1 = (f32[16,1024]{1,0:T(8,128)S(1)}, f32[16,1024]{1,0:T(8,128)S(1)}, u32[]{:S(2)}, u32[]{:S(2)}) collective-permute-start(f32[16,1024]{1,0:T(8,128)S(1)} %scan_entry.1), channel_id=1, source_target_pairs={{4,0},{5,1},{6,2},{7,3},{12,8},{13,9},{14,10},{15,11},{20,16},{21,... | collective-permute-start | bytes 196616 | tf_op jit(solution)/shard_map/ppermute | solution.py:24
  370.6 1.3 copy-start.4
  371.9 0.6 copy-start.11
  372.5 0.6 copy-start.16
  373.1 0.6 copy-start.17
  497.6 4.7 copy-start.18
  497.6 4.7 copy-start.19
  502.2 0.7 copy-start.29
  502.2 2.7 copy-start.25
  502.2 4.0 copy-start.21
  508.2 2.6 copy-start.23
Sparse Core Ops, SparseCore 0:
  122.5 38.0 all-gather.1
  291.5 54.5 reduce-scatter.1

commit v9 on v8

--- a/solution.py
+++ b/solution.py
@@ -106,7 +106,7 @@
 def bwd_kernel(stepd_ref, u_ref, ds_ref, mix_ref, rate_ref, ckpt_ref, gin_ref,
                step_ref, sig_ref, low_ref, skip_ref, wdt_ref,
                dpl_ref, e_ref, rank_ref, db_ref, dc_ref, acc_ref, bias_ref, dskip_ref,
-               g_ref, sbf_ref, abf_ref, rbf_ref, pb_ref, pc_ref, wb_ref, dn_ref, bdiag_ref):
+               g_ref, states_ref, abf_ref, rbf_ref, pb_ref, pc_ref, wb_ref, dn_ref, bdiag_ref, dec_ref):
     @pl.when(pl.program_id(1) == 0)
     def _():
         g_ref[...] = gin_ref[...]
@@ -124,7 +124,7 @@
             p = p + v[:, q * 128:(q + 1) * 128]
         return p
 
-    sbf_ref[0:N, :] = ckpt_ref[0].astype(BF16)
+    states_ref[0:N, :] = ckpt_ref[0]
     nt = (((1,), (1,)), ((), ()))
     lanes = jnp.ones((8, 128), BF16)
     rank = wdt_ref.shape[0]
@@ -138,8 +138,9 @@
         for k in range(CH):
             at = base + k
             dec = jnp.exp2(rate * stepd_ref[at:at + 1, :])
+            dec_ref[at * N:(at + 1) * N, :] = dec
             s = dec * s + b_t[:, at:at + 1] * u_ref[at:at + 1, :]
-            sbf_ref[(at + 1) * N:(at + 2) * N, :] = s.astype(BF16)
+            states_ref[(at + 1) * N:(at + 2) * N, :] = s
             pc_ref[k * N:(k + 1) * N, :] = fold(s * ds_ref[at:at + 1, :])
         dc = lax.dot_general(lanes, pc_ref[...].astype(BF16), nt, preferred_element_type=F32)
         dc_ref[0, c:c + 1, :] = dc[0:1]
@@ -153,8 +154,8 @@
             adj = g + c_t[:, at:at + 1] * ds_ref[at:at + 1, :]
             abf_ref[k * N:(k + 1) * N, :] = adj.astype(BF16)
             pb_ref[k * N:(k + 1) * N, :] = fold(adj * u_ref[at:at + 1, :])
-            g = jnp.exp2(rate * sd) * adj
-            before = sbf_ref[at * N:(at + 1) * N, :].astype(F32)
+            g = dec_ref[at * N:(at + 1) * N, :] * adj
+            before = states_ref[at * N:(at + 1) * N, :]
             r = g * before * rate
             rbf_ref[k * N:(k + 1) * N, :] = r.astype(BF16)
             acc = acc + r * sd
@@ -214,9 +215,10 @@
             jax.ShapeDtypeStruct((1, c), F32),
             jax.ShapeDtypeStruct((1, c), F32),
         ],
-        scratch_shapes=[pltpu.VMEM((N, w), F32), pltpu.VMEM(((tb + 1) * N, w), BF16),
+        scratch_shapes=[pltpu.VMEM((N, w), F32), pltpu.VMEM(((tb + 1) * N, w), F32),
                         pltpu.VMEM((CH * N, w), BF16), pltpu.VMEM((CH * N, w), BF16), pltpu.VMEM((CH * N, 128), F32), pltpu.VMEM((CH * N, 128), F32),
-                        pltpu.VMEM((tb, w), F32), pltpu.VMEM((tb, w), F32), pltpu.VMEM((tb, CH * N), BF16)],
+                        pltpu.VMEM((tb, w), F32), pltpu.VMEM((tb, w), F32), pltpu.VMEM((tb, CH * N), BF16),
+                        pltpu.VMEM((tb * N, w), F32)],
         compiler_params=pltpu.CompilerParams(vmem_limit_bytes=48 << 20),
         name="scan_backward",
     )(stepd, u, ds, mix_t, rate, ckpt, gin, step, sig, low, skip, w_dt)
@@ -338,11 +340,11 @@
     return dp, seq, mine
 
 
-def tail_kernel(n, dps, seqs, tile, lag, rank, dx_ref, dz_ref, w_hbm, nrm_ref,
+def tail_kernel(n, dps, seqs, tile, lag, rank, dx_ref, dz_ref, w_hbm, nrm_hbm,
                 dwx_ref, dwdt_ref, alog_ref, conv_ref, bias_ref, skip_ref,
                 dn_ref, gin_ref, gs_ref, ga_ref,
                 sm_ref, gacc, gsend, grecv, all_mine,
-                zr, zl, w_ref, loads, one_send, one_recv, two_recv, sm_one, sm_two, all_one, all_two,
+                zr, zl, w_ref, nrm_ref, loads, nrm_load, one_send, one_recv, two_recv, sm_one, sm_two, all_one, all_two,
                 r_send, r_recv, l_send, l_recv, w1s, w1r, w2s, w2r, s1s, s1r, s2s, s2r, a1s, a1r, a2s, a2r, gs, gr):
     dp, seq, t = place()
     core, hi = dp % 2, dp // 2
@@ -426,9 +428,14 @@
         gacc[:, cols] = gacc[:, cols] + lax.dot_general(lanes, scaled, nt, preferred_element_type=F32)
         return block
 
+    def load_rows():
+        return pltpu.make_async_copy(nrm_hbm, nrm_ref, nrm_load)
+
     @pl.loop(0, subs)
     def _(sub):
         load(sub).start()
+
+    load_rows().start()
 
     parts = sm_ref.shape[0]
     for p in range(parts):
@@ -466,6 +473,8 @@
             @pl.loop(1, subs)
             def _(sub):
                 load(sub).wait()
+
+            load_rows().wait()
 
         stream(g - lag * t, (n - 1 - t) * subs, t == 0, zr, r_copy, lambda k: n - 1 - k)
         stream(g - lag * (n - 1 - t), t * subs, t == n - 1, zl, l_copy, lambda k: k)
@@ -614,7 +623,7 @@
             jax.ShapeDtypeStruct((small_rows, lanes), F32),
             jax.ShapeDtypeStruct((all_rows, lanes), F32),
         ],
-        in_specs=[vmem] * 2 + [hbm] + [vmem] * 7,
+        in_specs=[vmem] * 2 + [hbm] * 2 + [vmem] * 6,
         out_specs=[vmem] * 4,
         scratch_shapes=[
             pltpu.VMEM((dps * seqs, small_rows, lanes), F32),
@@ -625,7 +634,9 @@
             pltpu.VMEM((hops, rows, tile), BF16),
             pltpu.VMEM((hops, rows, tile), BF16),
             pltpu.VMEM((2, wide, lanes), BF16),
+            pltpu.VMEM(normed.shape, BF16),
             dma((subs,)),
+            dma,
             pltpu.VMEM((chips, 2, wrows, lanes), BF16),
             pltpu.VMEM((chips, 2, wrows, lanes), BF16),
             pltpu.VMEM((chips, 2, wrows, lanes), BF16),
@@ -643,9 +654,9 @@
     )(dx, dz, w_full, normed, dwx, dwdt, *singles)
 
 
-def mid_kernel(n, tile, lag, gated_ref, w_ref, hid_ref, tea_ref, scale_ref, z_hbm, scan_hbm,
+def mid_kernel(n, tile, lag, gated_ref, w_hbm, hid_ref, tea_ref, scale_ref, z_hbm, scan_hbm,
                out_ref, go_ref, dwo_hbm, dscan_hbm, dz_hbm,
-               zr, zl, dwo_ref, part_ref, piece_ref, z_ref, scan_ref, acc_ref, dz_ref, loads, stores, wstores,
+               zr, zl, w_ref, wloads, dwo_ref, part_ref, piece_ref, z_ref, scan_ref, acc_ref, dz_ref, loads, stores, wstores,
                r_send, r_recv, l_send, l_recv, ar_send, ar_recv, al_send, al_recv):
     t = lax.axis_index("tensor")
     rows, wide = hid_ref.shape
@@ -660,6 +671,14 @@
 
     def load(i):
         return pltpu.make_async_copy((z_hbm, scan_hbm)[i], (z_ref, scan_ref)[i], loads.at[i])
+
+    def load_tile(w):
+        here = pl.ds(pl.multiple_of(w * tile, tile), tile)
+        return pltpu.make_async_copy(w_hbm.at[here, :], w_ref.at[here, :], wloads.at[w])
+
+    @pl.loop(0, waves)
+    def _(w):
+        load_tile(w).start()
 
     for i in range(2):
         load(i).start()
@@ -792,6 +811,7 @@
         def _():
             cols = cols_of(g // n)
             nt = (((1,), (1,)), ((), ()))
+            load_tile(g // n).wait()
 
             @pl.loop(0, n)
             def _(o):
@@ -901,11 +921,13 @@
             jax.ShapeDtypeStruct((tokens, lanes), F32),
             jax.ShapeDtypeStruct((tokens, lanes), BF16),
         ],
-        in_specs=[vmem] * 5 + [hbm] * 2,
+        in_specs=[vmem, hbm] + [vmem] * 3 + [hbm] * 2,
         out_specs=[vmem] * 2 + [hbm] * 3,
         scratch_shapes=[
             pltpu.VMEM((hops, rows, tile), BF16),
             pltpu.VMEM((hops, rows, tile), BF16),
+            pltpu.VMEM((wide, lanes), BF16),
+            dma((waves,)),
             pltpu.VMEM((waves, tile, lanes), BF16),
             pltpu.VMEM((tokens, wide), F32),
             pltpu.VMEM((tokens, wide), BF16),

time: 526 us -> 519 us (0.987)
  Pallas kernels: 441 us -> 432 us
  transfers between devices with their start and end apart: 4 -> 4, of which waited for: 1 -> 1; matrix products, arithmetic and copies ran while one was open for 4% -> 4% of each run, Pallas kernels for 42% -> 41%
where the time goes in v9:
time: 519 us; the launch traced here: 512 us
  Pallas kernels  432 us (83%)
  local copies, waits for them, and re-layouts  38.1 us (7%)
  between operations  15.8 us (3%)
  other arithmetic  12.7 us (2%)
  waiting for transfers between devices  9.23 us (2%)
    pallas_call x1, Pallas kernels, middle(): pl.pallas_call(functools.partial(mid_kernel, n, tile, 2), out_shape=[jax....  121 us
    pallas_call x1, Pallas kernels, front(): pl.pallas_call(functools.partial(front_kernel, n, dps, seqs, subs, 2), ou...  103 us
    pallas_call x1, Pallas kernels, tail(): pl.pallas_call(functools.partial(tail_kernel, n, dps, seqs, tile, 2, rank...  85 us
    pallas_call x1, Pallas kernels, bwd(): pl.pallas_call(bwd_kernel, grid=grid, in_specs=[rows, rows, rows, pl.Bloc...  54.6 us
    pallas_call x1, Pallas kernels, mixback(): pl.pallas_call(functools.partial(mixback_kernel, n, seqs), out_shape=[jax...  29 us
    unnamed x65, local copies, waits for them, and re-layouts  23.6 us
    pallas_call x1, Pallas kernels, fwd(): pl.pallas_call(fwd_kernel, grid=grid, in_specs=[pl.BlockSpec((mixed, tb),...  22 us
  transfers between devices with their start and end apart: 4, of which 1 were waited for; matrix products, arithmetic and copies ran while one was open for 4% of the time, Pallas kernels for 41%

profile of v9, /device:TPU:0, one launch (start us, length us, event | category | flops | bytes accessed | tf_op | source)
XLA Modules:
  0.0 512.3 jit_solution(11606167613768183792)
XLA Ops:
  7.3 0.8 convert_element_type.29
  8.0 0.8 compare_convert_fusion
  9.0 1.3 broadcast_in_dim.66.gain_ref
  11.5 0.7 broadcast_in_dim.81
  12.2 0.7 convert_element_type.32
  13.2 0.8 concatenate.33.keep_ref
  14.1 2.0 copy.63
  16.1 1.2 copy.78
  17.4 0.7 maximum_maximum_fusion.1.taps_ref
  18.1 0.7 maximum_maximum_fusion.wsm_ref
  18.9 103.5 %front.1 = (f32[1032,1024]{1,0:T(8,128)}, f32[1024,1024]{1,0:T(8,128)}, bf16[1024,2048]{1,0:T(8,128)(2,1)}, bf16[2,2048,1024]{2,1,0:T(8,128)(2,1)}, f32[1024,102...) custom-call(bf16[256,2048]{1,0:T(8,128)(2,1)} %hid_ref.3, ...), custom_call_target="tpu_custom_call" | custom-call | tf_op jit(solution)/shard_map/front/pallas_call | solution.py:1282
  122.4 0.7 select_reduce_fusion
  123.3 1.0 slice.56
  124.4 1.6 copy-done.1
  126.0 22.0 %scan_forward.1 = (f32[1024,1024]{1,0:T(8,128)}, f32[8,16,1024]{2,1,0:T(8,128)S(1)}, f32[16,1024]{1,0:T(8,128)}, f32[1024,1024]{1,0:T(8,128)}, f32[1024,1024]{1,...) custom-call(f32[160,1024]{1,0:T(8,128)S(1)} %copy-done.3, bf16[128,1024]{1,0:T(8,128)(2,1)S(1)} %bitcast.35, ...), custom_call_target="tpu_custom_call" | custom-call | tf_op jit(solution)/shard_map/scan_forward/pallas_call | solution.py:77
  148.1 0.8 copy-done.9
  148.8 3.2 collective-permute-start
  152.1 1.2 slice.57
  154.1 0.8 copy.64.scale_ref
  156.2 0.8 copy-done.7
  157.0 1.0 copy-done.10
  158.0 0.8 copy-done.13
  158.9 10.2 %scan_correct.1 = (f32[1024,1024]{1,0:T(8,128)}, f32[8,16,1024]{2,1,0:T(8,128)S(1)}, bf16[1024,1024]{1,0:T(8,128)(2,1)S(1)}) custom-call(s32[8]{0:T(128)S(1)} %compare_convert_fusion.2.alive_ref, f32[1024,1024]{1,0:T(8,128)} %get-tuple-element.59.y_ref, f32[1024,1024]{1,0:T(8,128)} %get-tuple-element.60.stepd_ref, f32[160,1024]{1,0:T(8,128)S(1)} %copy-done.3, ...), custom_call_target="tpu_custom_call" | custom-call | tf_op jit(solution)/shard_map/scan_correct/pallas_call | solution.py:270
  169.1 1.3 copy-done.5
  170.4 120.8 %middle.1 = (bf16[256,2048]{1,0:T(8,128)(2,1)}, f32[256,2048]{1,0:T(8,128)}, bf16[2048,1024]{1,0:T(8,128)(2,1)}, f32[1024,1024]{1,0:T(8,128)}, bf16[1024,1024]{1,0:T(8,128)(2,1)}) custom-call(bf16[1024,1024]{1,0:T(8,128)(2,1)} %copy-done.5, bf16[2048,1024]{1,0:T(8,128)(2,1)} %all-gather.2.cloned.1.call-done.w_hbm, bf16[256,2048]{1,0:T(8,128)(2,1)} %hid_ref.3, ...), custom_call_target="tpu_custom_call" | custom-call | tf_op jit(solution)/shard_map/middle/pallas_call | solution.py:915
  291.3 0.8 copy-done.8
  292.1 2.2 copy-done
  294.3 6.8 %scan_entry.1 = f32[16,1024]{1,0:T(8,128)S(1)} custom-call(s32[8]{0:T(128)S(1)} %compare_convert_fusion.2.alive_ref, f32[1024,1024]{1,0:T(8,128)S(1)} %copy-done, f32[1024,1024]{1,0:T(8,128)} %get-tuple-element.73.ds_ref, f32[160,1024]{1,0:T(8,128)S(1)} %copy-done.3, f32[16,1024]{1,0:T(8,128)S(1)} %copy-done.8), custom_call_target="tpu_custom_call" | custom-call | tf_op jit(solution)/shard_map/scan_entry/pallas_call | solution.py:311
  301.1 1.3 collective-permute-start.1
  302.4 0.8 pad_maximum_fusion.keep_ref
  303.3 0.9 slice.58
  304.2 0.8 reshape.71.wx_ref
  304.9 9.2 %collective-permute-done.1.gin_ref = f32[16,1024]{1,0:T(8,128)S(1)} collective-permute-done((f32[16,1024]{1,0:T(8,128)S(1)}, f32[16,1024]{1,0:T(8,128)S(1)}, u32[]{:S(2)}, u32[]{:S(2)}) %collective-permute-start.1) | collective-permute-done | bytes 65568 | tf_op jit(solution)/shard_map/ppermute | solution.py:24
  314.1 54.6 %scan_backward.1 = (bf16[1024,1024]{1,0:T(8,128)(2,1)S(1)}, f32[1024,1024]{1,0:T(8,128)}, f32[2,128,1024]{2,1,0:T(8,128)S(1)}, f32[2,64,256]{2,1,0:T(8,128)S(1)}...) custom-call(f32[1024,1024]{1,0:T(8,128)} %get-tuple-element.60.stepd_ref, ...), custom_call_target="tpu_custom_call" | custom-call | tf_op jit(solution)/shard_map/scan_backward/pallas_call | solution.py:186
  368.7 1.3 copy-done.4
  373.0 0.8 maximum_bitcast_fusion.part_ref
  373.7 29.0 %mix_backward.1 = (bf16[1024,1024]{1,0:T(8,128)(2,1)}, f32[160,1024]{1,0:T(8,128)}, f32[128,1024]{1,0:T(8,128)}, f32[8,1024]{1,0:T(8,128)}) custom-call(bf16[4,160,256]{2,1,0:T(8,128)(2,1)} %maximum_bitcast_fusion.part_ref, f32[1024,1024]{1,0:T(8,128)} %get-tuple-element.80.e_hbm, f32[1024,1024]{1,0:T(8,128)} %get-tuple-element.81.conv_hbm, ...), custom_call_target="tpu_custom_call" | custom-call | tf_op jit(solution)/shard_map/mix_backward/pallas_call | solution.py:1474
  402.7 85.0 %tail_sums.1 = (f32[256,2048]{1,0:T(8,128)}, f32[2,256,1024]{2,1,0:T(8,128)}, f32[40,1024]{1,0:T(8,128)}, f32[40,1024]{1,0:T(8,128)}) custom-call(bf16[1024,1024]{1,0:T(8,128)(2,1)} %get-tuple-element.84.dx_ref, bf16[1024,1024]{1,0:T(8,128)(2,1)} %get-tuple-element.85.dz_ref, bf16[2,2048,1024]{2,1,0:T(8,128)(2,1)} %get-tuple-element.86.w_hbm, ...), custom_call_target="tpu_custom_call" | custom-call | tf_op jit(solution)/shard_map/tail_sums/pallas_call | solution.py:618
  487.7 0.7 slice.60
  488.5 1.4 slice.61
  489.8 1.5 slice.67
  491.3 4.7 copy.71
  497.2 1.4 fusion.8
  499.3 0.7 fusion.9
  500.0 2.0 fusion.3
  501.9 1.2 convert_bitcast_fusion
  503.2 1.3 copy.72
  504.5 1.0 copy.80
  (91 shorter events, 7.7 us)
Async XLA Ops:
  7.2 8.9 %copy-start.22 = (bf16[256,2,1024]{2,1,0:T(2,128)(2,1)S(1)}, bf16[256,2,1024]{2,1,0:T(2,128)(2,1)}, u32[]{:S(2)}) copy-start(bf16[256,2,1024]{2,1,0:T(2,128)(2,1)} %param.17) | copy-start | bytes 3145732
  7.2 10.9 %copy-start.28 = (bf16[16,1024]{1,0:T(8,128)(2,1)S(1)}, bf16[16,1024]{1,0:T(8,128)(2,1)}, u32[]{:S(2)}) copy-start(bf16[16,1024]{1,0:T(8,128)(2,1)} %param.21) | copy-start | bytes 98308
  7.2 10.9 %copy-start.27 = (bf16[1024,20]{0,1:T(8,128)(2,1)S(1)}, bf16[1024,20]{0,1:T(8,128)(2,1)}, u32[]{:S(2)}) copy-start(bf16[1024,20]{0,1:T(8,128)(2,1)} %param.20) | copy-start | bytes 122884
  7.2 163.2 %all-gather.2.cloned.1.call-start = ((), (), s32[]{:S(2)}) async-start(), calls=%async_computation.1 | async-start | bytes 4718592 | tf_op jit(solution)/shard_map/all_gather | solution.py:1560
  18.8 105.5 %copy-start.26 = (f32[16,1024]{1,0:T(8,128)S(1)}, f32[16,1024]{1,0:T(8,128)}, u32[]{:S(2)}) copy-start(f32[16,1024]{1,0:T(8,128)} %param.23) | copy-start | bytes 196612
  18.8 105.5 %copy-start.15 = (f32[1024]{0:T(1024)S(1)}, f32[1024]{0:T(1024)}, u32[]{:S(2)}) copy-start(f32[1024]{0:T(1024)} %param.22) | copy-start | bytes 12292
  122.3 2.1 copy-start.3
  122.3 379.6 %reduce-scatter.2.cloned.1.call-start = ((), (), s32[]{:S(2)}) async-start(), calls=%async_computation.2 | async-start | bytes 4718592 | tf_op jit(solution)/shard_map/reduce_scatter | solution.py:1627
  123.3 32.8 %copy-start.14 = (f32[1024]{0:T(1024)S(1)}, f32[1024]{0:T(1024)}, u32[]{:S(2)}) copy-start(f32[1024]{0:T(1024)} %param.24) | copy-start | bytes 12292
  124.4 23.7 %copy-start.6 = (f32[16,1024]{1,0:T(8,128)}, f32[16,1024]{1,0:T(8,128)S(1)}, u32[]{:S(2)}) copy-start(f32[16,1024]{1,0:T(8,128)S(1)} %negate_multiply_fusion.rate_ref) | copy-start | bytes 196612
  124.4 1.6 copy-start.1
  126.0 30.2 %copy-start.2 = (bf16[1024,1024]{1,0:T(8,128)(2,1)S(1)}, bf16[1024,1024]{1,0:T(8,128)(2,1)}, u32[]{:S(2)}) copy-start(bf16[1024,1024]{1,0:T(8,128)(2,1)} %get-tuple-element.58.low_ref.low_hbm) | copy-start | bytes 6291460
  148.1 0.8 copy-start.9
  148.8 6.7 %collective-permute-start = (f32[16,1024]{1,0:T(8,128)}, f32[16,1024]{1,0:T(8,128)S(1)}, u32[]{:S(2)}, u32[]{:S(2)}) collective-permute-start(f32[16,1024]{1,0:T(8,128)} %get-tuple-element.62), channel_id=1, source_target_pairs={{0,4},{1,5},{2,6},{3,7},{8,12},{9,13},{10,14},{11,15},{16,20},{17,... | collective-permute-start | bytes 196616 | tf_op jit(solution)/shard_map/ppermute | solution.py:24
  155.5 0.6 copy-start.12
  156.2 0.8 copy-start.7
  157.0 1.0 copy-start.10
  158.0 0.8 copy-start.13
  169.1 1.3 copy-start.5
  291.2 0.8 copy-start.8
  292.1 2.2 copy-start
  294.3 8.1 %copy-start.20 = (f32[1024,4]{1,0:T(8,128)S(1)}, f32[1024,4]{1,0:T(8,128)}, u32[]{:S(2)}) copy-start(f32[1024,4]{1,0:T(8,128)} %concatenate.33.keep_ref) | copy-start | bytes 49156
  294.3 9.0 %copy-start.24 = (bf16[8,48,1024]{2,1,0:T(8,128)(2,1)S(1)}, bf16[8,48,1024]{2,1,0:T(8,128)(2,1)}, u32[]{:S(2)}) copy-start(bf16[8,48,1024]{2,1,0:T(8,128)(2,1)} %get-tuple-element.57) | copy-start | bytes 2359300
  301.1 13.1 %collective-permute-start.1 = (f32[16,1024]{1,0:T(8,128)S(1)}, f32[16,1024]{1,0:T(8,128)S(1)}, u32[]{:S(2)}, u32[]{:S(2)}) collective-permute-start(f32[16,1024]{1,0:T(8,128)S(1)} %scan_entry.1), channel_id=1, source_target_pairs={{4,0},{5,1},{6,2},{7,3},{12,8},{13,9},{14,10},{15,11},{20,16},{21,... | collective-permute-start | bytes 196616 | tf_op jit(solution)/shard_map/ppermute | solution.py:24
  368.7 1.3 copy-start.4
  370.0 0.6 copy-start.11
  370.7 0.6 copy-start.16
  371.3 0.6 copy-start.17
  491.3 4.7 copy-start.18
  491.3 4.7 copy-start.19
  496.0 0.7 copy-start.29
  496.0 2.7 copy-start.25
  496.0 4.0 copy-start.21
  501.9 2.6 copy-start.23
Sparse Core Ops, SparseCore 0:
  122.5 38.0 all-gather.1
  291.4 54.1 reduce-scatter.1

commit v10 on v9

--- a/solution.py
+++ b/solution.py
@@ -616,7 +616,7 @@
     dma = pltpu.SemaphoreType.DMA
     few = dma((chips,))
     return pl.pallas_call(
-        functools.partial(tail_kernel, n, dps, seqs, tile, 2, rank),
+        functools.partial(tail_kernel, n, dps, seqs, tile, 3, rank),
         out_shape=[
             jax.ShapeDtypeStruct((rows, wide), F32),
             jax.ShapeDtypeStruct((2, wrows, lanes), F32),
@@ -1275,7 +1275,7 @@
     lanes = w_in.shape[2]
     tokens = rows * n
     mixed = parts * x_cols
-    subs = max(1, rows // 32)
+    subs = max(1, rows // 64)
     vmem, hbm = pl.BlockSpec(memory_space=pltpu.VMEM), pl.BlockSpec(memory_space=pl.ANY)
     dma = pltpu.SemaphoreType.DMA
     many, few, peers = dma((n * subs,)), dma((chips,)), dma((n,))

time: 519 us -> 514 us (level)
  no operation moved by 1% of the time
where the time goes in v10:
time: 514 us; the launch traced here: 511 us
  Pallas kernels  431 us (84%)
  local copies, waits for them, and re-layouts  38.1 us (7%)
  between operations  15.8 us (3%)
  other arithmetic  12.7 us (2%)
  waiting for transfers between devices  9.12 us (2%)
    pallas_call x1, Pallas kernels, middle(): pl.pallas_call(functools.partial(mid_kernel, n, tile, 2), out_shape=[jax....  121 us
    pallas_call x1, Pallas kernels, front(): pl.pallas_call(functools.partial(front_kernel, n, dps, seqs, subs, 2), ou...  102 us
    pallas_call x1, Pallas kernels, tail(): pl.pallas_call(functools.partial(tail_kernel, n, dps, seqs, tile, 3, rank...  85 us
    pallas_call x1, Pallas kernels, bwd(): pl.pallas_call(bwd_kernel, grid=grid, in_specs=[rows, rows, rows, pl.Bloc...  54.6 us
    pallas_call x1, Pallas kernels, mixback(): pl.pallas_call(functools.partial(mixback_kernel, n, seqs), out_shape=[jax...  28.9 us
    unnamed x65, local copies, waits for them, and re-layouts  23.6 us
    pallas_call x1, Pallas kernels, fwd(): pl.pallas_call(fwd_kernel, grid=grid, in_specs=[pl.BlockSpec((mixed, tb),...  22 us
  transfers between devices with their start and end apart: 4, of which 1 were waited for; matrix products, arithmetic and copies ran while one was open for 4% of the time, Pallas kernels for 41%

profile of v10, /device:TPU:0, one launch (start us, length us, event | category | flops | bytes accessed | tf_op | source)
XLA Modules:
  0.0 511.1 jit_solution(1916688766343059617)
XLA Ops:
  7.3 0.8 convert_element_type.29
  8.0 0.8 compare_convert_fusion
  9.0 1.3 broadcast_in_dim.66.gain_ref
  11.5 0.7 broadcast_in_dim.81
  12.2 0.7 convert_element_type.32
  13.2 0.8 concatenate.33.keep_ref
  14.1 2.0 copy.63
  16.1 1.2 copy.78
  17.4 0.7 maximum_maximum_fusion.1.taps_ref
  18.1 0.7 maximum_maximum_fusion.wsm_ref
  18.9 102.2 %front.1 = (f32[1032,1024]{1,0:T(8,128)}, f32[1024,1024]{1,0:T(8,128)}, bf16[1024,2048]{1,0:T(8,128)(2,1)}, bf16[2,2048,1024]{2,1,0:T(8,128)(2,1)}, f32[1024,102...) custom-call(bf16[256,2048]{1,0:T(8,128)(2,1)} %hid_ref.3, ...), custom_call_target="tpu_custom_call" | custom-call | tf_op jit(solution)/shard_map/front/pallas_call | solution.py:1282
  121.2 0.7 select_reduce_fusion
  122.1 1.0 slice.56
  123.2 1.6 copy-done.1
  124.8 22.0 %scan_forward.1 = (f32[1024,1024]{1,0:T(8,128)}, f32[8,16,1024]{2,1,0:T(8,128)S(1)}, f32[16,1024]{1,0:T(8,128)}, f32[1024,1024]{1,0:T(8,128)}, f32[1024,1024]{1,...) custom-call(f32[160,1024]{1,0:T(8,128)S(1)} %copy-done.3, bf16[128,1024]{1,0:T(8,128)(2,1)S(1)} %bitcast.35, ...), custom_call_target="tpu_custom_call" | custom-call | tf_op jit(solution)/shard_map/scan_forward/pallas_call | solution.py:77
  146.8 0.8 copy-done.9
  147.6 3.3 collective-permute-start
  150.9 1.2 slice.57
  152.9 0.8 copy.64.scale_ref
  155.0 0.8 copy-done.7
  155.8 1.0 copy-done.10
  156.9 0.8 copy-done.13
  157.7 10.2 %scan_correct.1 = (f32[1024,1024]{1,0:T(8,128)}, f32[8,16,1024]{2,1,0:T(8,128)S(1)}, bf16[1024,1024]{1,0:T(8,128)(2,1)S(1)}) custom-call(s32[8]{0:T(128)S(1)} %compare_convert_fusion.2.alive_ref, f32[1024,1024]{1,0:T(8,128)} %get-tuple-element.59.y_ref, f32[1024,1024]{1,0:T(8,128)} %get-tuple-element.60.stepd_ref, f32[160,1024]{1,0:T(8,128)S(1)} %copy-done.3, ...), custom_call_target="tpu_custom_call" | custom-call | tf_op jit(solution)/shard_map/scan_correct/pallas_call | solution.py:270
  167.9 1.3 copy-done.5
  169.2 120.8 %middle.1 = (bf16[256,2048]{1,0:T(8,128)(2,1)}, f32[256,2048]{1,0:T(8,128)}, bf16[2048,1024]{1,0:T(8,128)(2,1)}, f32[1024,1024]{1,0:T(8,128)}, bf16[1024,1024]{1,0:T(8,128)(2,1)}) custom-call(bf16[1024,1024]{1,0:T(8,128)(2,1)} %copy-done.5, bf16[2048,1024]{1,0:T(8,128)(2,1)} %all-gather.2.cloned.1.call-done.w_hbm, bf16[256,2048]{1,0:T(8,128)(2,1)} %hid_ref.3, ...), custom_call_target="tpu_custom_call" | custom-call | tf_op jit(solution)/shard_map/middle/pallas_call | solution.py:915
  290.0 0.8 copy-done.8
  290.8 2.2 copy-done
  293.0 7.0 %scan_entry.1 = f32[16,1024]{1,0:T(8,128)S(1)} custom-call(s32[8]{0:T(128)S(1)} %compare_convert_fusion.2.alive_ref, f32[1024,1024]{1,0:T(8,128)S(1)} %copy-done, f32[1024,1024]{1,0:T(8,128)} %get-tuple-element.73.ds_ref, f32[160,1024]{1,0:T(8,128)S(1)} %copy-done.3, f32[16,1024]{1,0:T(8,128)S(1)} %copy-done.8), custom_call_target="tpu_custom_call" | custom-call | tf_op jit(solution)/shard_map/scan_entry/pallas_call | solution.py:311
  300.1 1.3 collective-permute-start.1
  301.4 0.8 pad_maximum_fusion.keep_ref
  302.3 0.9 slice.58
  303.1 0.8 reshape.71.wx_ref
  303.9 9.1 %collective-permute-done.1.gin_ref = f32[16,1024]{1,0:T(8,128)S(1)} collective-permute-done((f32[16,1024]{1,0:T(8,128)S(1)}, f32[16,1024]{1,0:T(8,128)S(1)}, u32[]{:S(2)}, u32[]{:S(2)}) %collective-permute-start.1) | collective-permute-done | bytes 65568 | tf_op jit(solution)/shard_map/ppermute | solution.py:24
  313.0 54.6 %scan_backward.1 = (bf16[1024,1024]{1,0:T(8,128)(2,1)S(1)}, f32[1024,1024]{1,0:T(8,128)}, f32[2,128,1024]{2,1,0:T(8,128)S(1)}, f32[2,64,256]{2,1,0:T(8,128)S(1)}...) custom-call(f32[1024,1024]{1,0:T(8,128)} %get-tuple-element.60.stepd_ref, ...), custom_call_target="tpu_custom_call" | custom-call | tf_op jit(solution)/shard_map/scan_backward/pallas_call | solution.py:186
  367.6 1.3 copy-done.4
  371.8 0.8 maximum_bitcast_fusion.part_ref
  372.6 28.9 %mix_backward.1 = (bf16[1024,1024]{1,0:T(8,128)(2,1)}, f32[160,1024]{1,0:T(8,128)}, f32[128,1024]{1,0:T(8,128)}, f32[8,1024]{1,0:T(8,128)}) custom-call(bf16[4,160,256]{2,1,0:T(8,128)(2,1)} %maximum_bitcast_fusion.part_ref, f32[1024,1024]{1,0:T(8,128)} %get-tuple-element.80.e_hbm, f32[1024,1024]{1,0:T(8,128)} %get-tuple-element.81.conv_hbm, ...), custom_call_target="tpu_custom_call" | custom-call | tf_op jit(solution)/shard_map/mix_backward/pallas_call | solution.py:1474
  401.5 85.0 %tail_sums.1 = (f32[256,2048]{1,0:T(8,128)}, f32[2,256,1024]{2,1,0:T(8,128)}, f32[40,1024]{1,0:T(8,128)}, f32[40,1024]{1,0:T(8,128)}) custom-call(bf16[1024,1024]{1,0:T(8,128)(2,1)} %get-tuple-element.84.dx_ref, bf16[1024,1024]{1,0:T(8,128)(2,1)} %get-tuple-element.85.dz_ref, bf16[2,2048,1024]{2,1,0:T(8,128)(2,1)} %get-tuple-element.86.w_hbm, ...), custom_call_target="tpu_custom_call" | custom-call | tf_op jit(solution)/shard_map/tail_sums/pallas_call | solution.py:618
  486.5 0.7 slice.60
  487.2 1.4 slice.61
  488.6 1.5 slice.67
  490.0 4.7 copy.71
  496.0 1.4 fusion.8
  498.0 0.7 fusion.9
  498.7 2.0 fusion.3
  500.7 1.2 convert_bitcast_fusion
  501.9 1.3 copy.72
  503.2 1.0 copy.80
  (91 shorter events, 7.7 us)
Async XLA Ops:
  7.2 8.9 %copy-start.22 = (bf16[256,2,1024]{2,1,0:T(2,128)(2,1)S(1)}, bf16[256,2,1024]{2,1,0:T(2,128)(2,1)}, u32[]{:S(2)}) copy-start(bf16[256,2,1024]{2,1,0:T(2,128)(2,1)} %param.17) | copy-start | bytes 3145732
  7.2 10.9 %copy-start.28 = (bf16[16,1024]{1,0:T(8,128)(2,1)S(1)}, bf16[16,1024]{1,0:T(8,128)(2,1)}, u32[]{:S(2)}) copy-start(bf16[16,1024]{1,0:T(8,128)(2,1)} %param.21) | copy-start | bytes 98308
  7.2 10.9 %copy-start.27 = (bf16[1024,20]{0,1:T(8,128)(2,1)S(1)}, bf16[1024,20]{0,1:T(8,128)(2,1)}, u32[]{:S(2)}) copy-start(bf16[1024,20]{0,1:T(8,128)(2,1)} %param.20) | copy-start | bytes 122884
  7.2 162.0 %all-gather.2.cloned.1.call-start = ((), (), s32[]{:S(2)}) async-start(), calls=%async_computation.1 | async-start | bytes 4718592 | tf_op jit(solution)/shard_map/all_gather | solution.py:1560
  18.8 104.2 %copy-start.26 = (f32[16,1024]{1,0:T(8,128)S(1)}, f32[16,1024]{1,0:T(8,128)}, u32[]{:S(2)}) copy-start(f32[16,1024]{1,0:T(8,128)} %param.23) | copy-start | bytes 196612
  18.8 104.3 %copy-start.15 = (f32[1024]{0:T(1024)S(1)}, f32[1024]{0:T(1024)}, u32[]{:S(2)}) copy-start(f32[1024]{0:T(1024)} %param.22) | copy-start | bytes 12292
  121.1 2.1 copy-start.3
  121.1 379.6 %reduce-scatter.2.cloned.1.call-start = ((), (), s32[]{:S(2)}) async-start(), calls=%async_computation.2 | async-start | bytes 4718592 | tf_op jit(solution)/shard_map/reduce_scatter | solution.py:1627
  122.1 32.9 %copy-start.14 = (f32[1024]{0:T(1024)S(1)}, f32[1024]{0:T(1024)}, u32[]{:S(2)}) copy-start(f32[1024]{0:T(1024)} %param.24) | copy-start | bytes 12292
  123.1 23.7 %copy-start.6 = (f32[16,1024]{1,0:T(8,128)}, f32[16,1024]{1,0:T(8,128)S(1)}, u32[]{:S(2)}) copy-start(f32[16,1024]{1,0:T(8,128)S(1)} %negate_multiply_fusion.rate_ref) | copy-start | bytes 196612
  123.2 1.6 copy-start.1
  124.8 30.2 %copy-start.2 = (bf16[1024,1024]{1,0:T(8,128)(2,1)S(1)}, bf16[1024,1024]{1,0:T(8,128)(2,1)}, u32[]{:S(2)}) copy-start(bf16[1024,1024]{1,0:T(8,128)(2,1)} %get-tuple-element.58.low_ref.low_hbm) | copy-start | bytes 6291460
  146.8 0.8 copy-start.9
  147.6 6.7 %collective-permute-start = (f32[16,1024]{1,0:T(8,128)}, f32[16,1024]{1,0:T(8,128)S(1)}, u32[]{:S(2)}, u32[]{:S(2)}) collective-permute-start(f32[16,1024]{1,0:T(8,128)} %get-tuple-element.62), channel_id=1, source_target_pairs={{0,4},{1,5},{2,6},{3,7},{8,12},{9,13},{10,14},{11,15},{16,20},{17,... | collective-permute-start | bytes 196616 | tf_op jit(solution)/shard_map/ppermute | solution.py:24
  154.3 0.6 copy-start.12
  155.0 0.8 copy-start.7
  155.8 1.0 copy-start.10
  156.9 0.8 copy-start.13
  167.9 1.3 copy-start.5
  290.0 0.8 copy-start.8
  290.8 2.2 copy-start
  293.0 8.4 %copy-start.20 = (f32[1024,4]{1,0:T(8,128)S(1)}, f32[1024,4]{1,0:T(8,128)}, u32[]{:S(2)}) copy-start(f32[1024,4]{1,0:T(8,128)} %concatenate.33.keep_ref) | copy-start | bytes 49156
  293.0 9.2 %copy-start.24 = (bf16[8,48,1024]{2,1,0:T(8,128)(2,1)S(1)}, bf16[8,48,1024]{2,1,0:T(8,128)(2,1)}, u32[]{:S(2)}) copy-start(bf16[8,48,1024]{2,1,0:T(8,128)(2,1)} %get-tuple-element.57) | copy-start | bytes 2359300
  300.1 12.9 %collective-permute-start.1 = (f32[16,1024]{1,0:T(8,128)S(1)}, f32[16,1024]{1,0:T(8,128)S(1)}, u32[]{:S(2)}, u32[]{:S(2)}) collective-permute-start(f32[16,1024]{1,0:T(8,128)S(1)} %scan_entry.1), channel_id=1, source_target_pairs={{4,0},{5,1},{6,2},{7,3},{12,8},{13,9},{14,10},{15,11},{20,16},{21,... | collective-permute-start | bytes 196616 | tf_op jit(solution)/shard_map/ppermute | solution.py:24
  367.6 1.3 copy-start.4
  368.9 0.6 copy-start.11
  369.5 0.6 copy-start.16
  370.1 0.6 copy-start.17
  490.0 4.7 copy-start.18
  490.0 4.7 copy-start.19
  494.7 0.7 copy-start.29
  494.7 2.7 copy-start.25
  494.7 4.0 copy-start.21
  500.7 2.6 copy-start.23
Sparse Core Ops, SparseCore 0:
  121.2 37.2 all-gather.1
  290.1 53.4 reduce-scatter.1
